TPU v7x, 32 devices: a whole 2x2x4 slice. The times are simulated.
32 devices in a mesh: gx: 8 (over y, x, core), gy: 4 (over z).
Axes of the slice: x: 2, y: 2, z: 4, core: 2. Of those that a mesh axis runs over, the one named last changes fastest.
Arguments:
- atm_state: float32 [6, 196608], P(None, ('gx', 'gy')), may hold values from -6 to 6
- pair_block: int32 [8192], P(('gx', 'gy')), may hold values from 0 to 47
- pair_owner: int32 [8192, 1], P(('gx', 'gy')), may hold values from 0 to 31; in each aligned block of 256 rows (0 to 255, 256 to 511, ...) at most 16 rows name the same one
- pair_row: int32 [8192], P(('gx', 'gy')), may hold values from 0 to 63
- pair_tile: int32 [8192], P(('gx', 'gy')), may hold values from 0 to 127
- remap_weight: bfloat16 [4096, 128, 128], P(('gx', 'gy')), may hold values from 0.0014953613 to 0.029907227
- wet_mask: int32 [512, 512], P('gx', 'gy'), may hold values 0 or 1
- ocean_state: float32 [4, 16, 512, 512], P(None, None, 'gx', 'gy'), may hold values from -6 to 6
- vert_kappa: float32 [16, 512, 512], P(None, 'gx', 'gy'), may hold values from 0.05 to 3
- horiz_kappa: float32 [512, 512], P('gx', 'gy'), may hold values from 0.02 to 0.24
Outputs:
- ocean_next: float32 [4, 16, 512, 512], P(None, None, 'gx', 'gy')
- atm_surface: float32 [4, 196608], P(None, ('gx', 'gy'))
Inputs may be any that keep to these rules, and one draw needn't show every extreme that they name: `pair_owner`: the intersections of one device name one owner at most 16 times, and exactly 16 times for some owner.
All inputs are finite; a program needn't handle non-finite values. No bound on the sum of `wet_mask` on one device may be relied on, other than what follows from the above.
Results may differ from a plain program's by a relative error of at most 0.0039.
Values sent between devices are 32-bit elements; how exact they have to be, the bound alone decides.
No kernel may reach another device: no remote copies, remote signals or barrier semaphores. Data moves between devices by JAX's collectives and lax.ppermute only.
A program may use at most 64 MiB of HBM per device.

v0:
```python
import jax
import jax.numpy as jnp
from jax import lax
from jax.sharding import PartitionSpec as P


def extended(shard, sides, width):
    for axis, dim in sides:
        count, length = (lax.axis_size(axis), shard.shape[dim])
        up = [(i, (i + 1) % count) for i in range(count - 1)]
        down = [(j, i) for i, j in up]
        last = lax.slice_in_dim(shard, length - width, length, axis=dim)
        leading = lax.slice_in_dim(shard, 0, width, axis=dim)
        before = lax.ppermute(last, axis, up)
        after = lax.ppermute(leading, axis, down)
        shard = jnp.concatenate([before, shard, after], axis=dim)
    return shard


def surface_flux(atm_state):
    wind_u = atm_state[0]
    wind_v = atm_state[1]
    speed = jnp.sqrt(wind_u * wind_u + wind_v * wind_v + 0.25)
    heat_flux = 0.5 * speed * (atm_state[2] - atm_state[5])
    water_flux = atm_state[4] - 0.3 * speed * atm_state[3]
    return jnp.stack([heat_flux, water_flux, 0.2 * speed * wind_u, 0.2 * speed * wind_v]).astype(
        jnp.bfloat16
    )


def column_mix(fields, vert_kappa):
    levels = vert_kappa.shape[0]
    face_coef = 0.5 * (vert_kappa[:-1] + vert_kappa[1:])
    zero_plane = jnp.zeros_like(vert_kappa[:1])
    above = jnp.concatenate([zero_plane, face_coef], 0)
    below = jnp.concatenate([face_coef, zero_plane], 0)
    diagonal = 1.0 + above + below
    upper_list = []
    rhs_list = []
    for level_index in range(levels):
        if level_index == 0:
            pivot_inv = 1.0 / diagonal[0]
            rhs_now = fields[:, 0] * pivot_inv
        else:
            pivot_inv = 1.0 / (diagonal[level_index] + above[level_index] * upper_list[-1])
            rhs_now = (fields[:, level_index] + above[level_index] * rhs_list[-1]) * pivot_inv
        upper_list.append(-below[level_index] * pivot_inv)
        rhs_list.append(rhs_now)
    solved = [rhs_list[-1]]
    for level_index in range(levels - 2, -1, -1):
        solved.append(rhs_list[level_index] - upper_list[level_index] * solved[-1])
    return jnp.stack(solved[::-1], 1)


def shifted(array, step_x, step_y):
    size_x = array.shape[-2]
    size_y = array.shape[-1]
    return array[..., 1 + step_x : size_x - 1 + step_x, 1 + step_y : size_y - 1 + step_y]


def diffuse(padded, coefficients):
    kappa_pad = coefficients[0]
    wet_pad = coefficients[1]
    centre = shifted(padded, 0, 0)
    kappa_mid = shifted(kappa_pad, 0, 0)
    wet_mid = shifted(wet_pad, 0, 0)
    result = centre
    for step_x, step_y in ((1, 0), (-1, 0), (0, 1), (0, -1)):
        face_coef = (
            0.25
            * (kappa_mid + shifted(kappa_pad, step_x, step_y))
            * wet_mid
            * shifted(wet_pad, step_x, step_y)
        )
        result = result + face_coef * (shifted(padded, step_x, step_y) - centre)
    return result


def local(
    atm_state,
    pair_block,
    pair_owner,
    pair_row,
    pair_tile,
    remap_weight,
    wet_mask,
    ocean_state,
    vert_kappa,
    horiz_kappa,
):
    highest = lax.Precision.HIGHEST
    grid_x = lax.axis_size("gx")
    grid_y = lax.axis_size("gy")
    devices = grid_x * grid_y
    npairs = pair_block.shape[0]
    capacity = max(2, 2 * npairs // devices)
    slot_count = devices * capacity
    tile_rows = ocean_state.shape[2]
    patch_width = ocean_state.shape[3]
    block_cols = remap_weight.shape[1]
    fluxes = surface_flux(atm_state)
    nblocks = fluxes.shape[1] // block_cols
    blocks = fluxes.reshape(4, nblocks, block_cols).transpose(1, 0, 2)
    tile_weights = remap_weight[pair_tile]
    contrib = jnp.einsum(
        "pca,pab->pcb", blocks[pair_block], tile_weights, preferred_element_type=jnp.float32
    )
    owner_ids = pair_owner[:, 0]
    owner_hits = (owner_ids[:, None] == jnp.arange(devices, dtype=jnp.int32)[None, :]).astype(
        jnp.int32
    )
    slot_rank = jnp.sum(owner_hits * (jnp.cumsum(owner_hits, 0) - 1), 1)
    send_slot = owner_ids * capacity + slot_rank
    outgoing = jnp.zeros((slot_count, 4, patch_width), jnp.float32).at[send_slot].set(contrib)
    out_rows = jnp.zeros((slot_count,), jnp.int32).at[send_slot].set(pair_row)
    arrived, in_rows = (
        lax.all_to_all(outgoing, ("gx", "gy"), split_axis=0, concat_axis=0, tiled=True),
        lax.all_to_all(out_rows, ("gx", "gy"), split_axis=0, concat_axis=0, tiled=True),
    )
    placing = (jnp.arange(tile_rows, dtype=jnp.int32)[:, None] == in_rows[None, :]).astype(
        jnp.float32
    )
    forcing = jnp.dot(
        placing,
        arrived.reshape(slot_count, 4 * patch_width),
        precision=highest,
        preferred_element_type=jnp.float32,
    )
    forcing = forcing.reshape(tile_rows, 4, patch_width).transpose(1, 0, 2)
    wet_frac = wet_mask.astype(jnp.float32)
    forced = ocean_state.at[:, 0].add(forcing * wet_frac[None])
    coef_pad = extended(jnp.stack([horiz_kappa, wet_frac]), (("gx", 1), ("gy", 2)), 2)
    coef_near = coef_pad[:, 1:-1, 1:-1]
    mixed = column_mix(forced, vert_kappa)
    tracers = mixed[:2]
    for pass_index in range(2):
        padded = extended(tracers, (("gx", 2), ("gy", 3)), 1)
        tracers = diffuse(padded, coef_near)
    ocean_next = jnp.concatenate([tracers, mixed[2:]], 0)
    surface = jnp.concatenate([ocean_next[:, 0] * wet_frac[None], wet_frac[None]], 0)
    sendback = surface.transpose(1, 0, 2)[in_rows]
    returned = lax.all_to_all(sendback, ("gx", "gy"), split_axis=0, concat_axis=0, tiled=True)
    picks = returned[send_slot]
    picks_high = picks.astype(jnp.bfloat16)
    picks_low = (picks - picks_high.astype(jnp.float32)).astype(jnp.bfloat16)
    back = jnp.einsum("pab,pcb->pca", tile_weights, picks_high, preferred_element_type=jnp.float32)
    back = back + jnp.einsum(
        "pab,pcb->pca", tile_weights, picks_low, preferred_element_type=jnp.float32
    )
    member = (jnp.arange(nblocks, dtype=jnp.int32)[:, None] == pair_block[None, :]).astype(
        jnp.float32
    )
    sums = jnp.dot(
        member,
        back.reshape(npairs, 5 * block_cols),
        precision=highest,
        preferred_element_type=jnp.float32,
    )
    sums = sums.reshape(nblocks, 5, block_cols)
    values = sums[:, :4] / jnp.maximum(sums[:, 4:5], 0.1)
    atm_surface = values.transpose(1, 0, 2).reshape(4, nblocks * block_cols)
    return (ocean_next, atm_surface)


def solution(mesh):
    placed = (
        P(None, ("gx", "gy")),
        P(("gx", "gy")),
        P(("gx", "gy"), None),
        P(("gx", "gy")),
        P(("gx", "gy")),
        P(("gx", "gy"), None, None),
        P("gx", "gy"),
        P(None, None, "gx", "gy"),
        P(None, "gx", "gy"),
        P("gx", "gy"),
    )
    return jax.shard_map(
        local,
        mesh=mesh,
        in_specs=placed,
        out_specs=(P(None, None, "gx", "gy"), P(None, ("gx", "gy"))),
        check_vma=False,
    )
```

profile of v0, /device:TPU:1, one launch (start us, length us, event | category | flops | bytes accessed | tf_op | source)
XLA Modules:
  0.0 234.3 jit_solution(1108116299046325999)
XLA Ops:
  5.9 7.1 %all-to-all-start = ((s32[32,16,1]{1,2,0:T(1,128)}), s32[32,16,1]{1,2,0:T(1,128)S(1)}, u32[]{:S(2)}, u32[]{:S(2)}) async-start(s32[32,16,1]{1,2,0:T(1,128)} %bitcast.5), calls=%async_computation | async-start | bytes 32768 | tf_op jit(solution)/shard_map/all_to_all | solution.py:118
  14.5 3.5 %collective-permute-start = (f32[2,2,128]{2,1,0:T(2,128)S(1)}, f32[2,2,128]{2,1,0:T(2,128)S(1)}, u32[]{:S(2)}, u32[]{:S(2)}) collective-permute-start(f32[2,2,128]{2,1,0:T(2,128)S(1)} %get-tuple-element.104), channel_id=1, source_target_pairs={{0,4},{4,8},{8,12},{12,16},{16,20},{20,24},{24,28},{1,5},{5,9},{9,... | collective-permute-start | bytes 6152 | tf_op jit(solution)/shard_map/ppermute | solution.py:14
  26.0 10.9 %gather_fusion.1 = bf16[256,128,128]{2,1,0:T(8,128)(2,1)} fusion(bf16[128,128,128]{2,1,0:T(8,128)(2,1)} %param.17, s32[1024]{0:T(1024)S(1)} %get-tuple-element.109), kind=kCustom, calls=%fused_computation.1 | custom fusion | bytes 16778240 | tf_op jit(solution)/shard_map/gather | solution.py:104
  36.9 5.6 %fusion.137 = f32[256,4,128]{2,1,0:T(4,128)S(1)} fusion(bf16[256,4,128]{2,1,0:T(4,128)(2,1)S(1)} %gather_fusion, bf16[256,128,128]{2,1,0:T(8,128)(2,1)} %gather_fusion.1), kind=kOutput, calls=%fused_computation.270 | convolution fusion | flops 33554432 | bytes 9175040 | tf_op jit(solution)/shard_map/pca,pab->pcb/dot_general | solution.py:105
  43.7 25.9 %scatter_fusion = f32[512,4,128]{2,1,0:T(4,128)} fusion(f32[512,4,128]{2,1,0:T(4,128)} %broadcast_in_dim.8, s32[256]{0:T(256)S(1)} %bitcast.304, f32[256,4,128]{2,1,0:T(4,128)S(1)} %fusion.137), kind=kCustom, calls=%fused_computation.5 | custom fusion | bytes 1573888 | tf_op jit(solution)/shard_map/scatter | solution.py:114
  69.6 5.9 %all-to-all-start.1 = ((f32[512,4,128]{2,1,0:T(4,128)}), f32[512,4,128]{2,1,0:T(4,128)S(1)}, u32[]{:S(2)}, u32[]{:S(2)}) async-start(f32[512,4,128]{2,1,0:T(4,128)} %scatter_fusion), calls=%async_computation.1 | async-start | bytes 2097152 | tf_op jit(solution)/shard_map/all_to_all | solution.py:117
  79.0 3.3 %collective-permute-start.2 = (f32[2,68,2]{2,1,0:T(8,128)S(1)}, f32[2,68,2]{2,1,0:T(8,128)S(1)}, u32[]{:S(2)}, u32[]{:S(2)}) collective-permute-start(f32[2,68,2]{2,1,0:T(8,128)S(1)} %get-tuple-element.102), channel_id=1, source_target_pairs={{0,1},{1,2},{2,3},{4,5},{5,6},{6,7},{8,9},{9,10},{10,11},{12,13},{... | collective-permute-start | bytes 3272 | tf_op jit(solution)/shard_map/ppermute | solution.py:14
  84.5 9.8 %collective-permute-done.2 = f32[2,68,2]{2,1,0:T(8,128)S(1)} collective-permute-done((f32[2,68,2]{2,1,0:T(8,128)S(1)}, f32[2,68,2]{2,1,0:T(8,128)S(1)}, u32[]{:S(2)}, u32[]{:S(2)}) %collective-permute-start.2) | collective-permute-done | bytes 1120 | tf_op jit(solution)/shard_map/ppermute | solution.py:14
  95.9 6.1 %all-to-all-done.1 = f32[512,4,128]{2,1,0:T(4,128)S(1)} async-done(((f32[512,4,128]{2,1,0:T(4,128)}), f32[512,4,128]{2,1,0:T(4,128)S(1)}, u32[]{:S(2)}, u32[]{:S(2)}) %all-to-all-start.1) | async-done | bytes 1048608 | tf_op jit(solution)/shard_map/all_to_all | solution.py:117
  102.6 3.0 %subtract_dynamic-update-slice_fusion = (f32[4,16,64,128]{3,2,0,1:T(8,128)S(1)}, f32[4,1,64,128]{3,2,0,1:T(8,128)S(1)}, f32[4,1,64,128]{3,2,0,1:T(8,128)S(1)}, f...) fusion(f32[64,128]{1,0:T(8,128)S(1)} %copy-done.25, ...), kind=kOutput, calls=%fused_computation.99 | convolution fusion | flops 203915264 | bytes 6653952 | tf_op jit(solution)/shard_map/dot_general | solution.py:123
  107.6 1.9 collective-permute-start.4
  109.5 3.6 %collective-permute-start.5 = (f32[2,16,1,128]{3,2,0,1:T(1,128)S(1)}, f32[2,16,1,128]{3,2,0,1:T(1,128)S(1)}, u32[]{:S(2)}, u32[]{:S(2)}) collective-permute-start(f32[2,16,1,128]{3,2,0,1:T(1,128)S(1)} %get-tuple-element.59), channel_id=1, source_target_pairs={{0,4},{4,8},{8,12},{12,16},{16,20},{20,24},{24,28},{1,5},{5,9},{9,... | collective-permute-start | bytes 49160 | tf_op jit(solution)/shard_map/ppermute | solution.py:14
  119.6 5.5 %collective-permute-start.7 = (f32[2,16,66,1]{2,1,3,0:T(8,128)}, f32[2,16,66,1]{2,1,3,0:T(8,128)S(1)}, u32[]{:S(2)}, u32[]{:S(2)}) collective-permute-start(f32[2,16,66,1]{2,1,3,0:T(8,128)} %copy.74), channel_id=1, source_target_pairs={{0,1},{1,2},{2,3},{4,5},{5,6},{6,7},{8,9},{9,10},{10,11},{12,13},{... | collective-permute-start | bytes 25352 | tf_op jit(solution)/shard_map/ppermute | solution.py:14
  128.2 2.8 %fusion.17 = f32[2,16,64,128]{3,2,0,1:T(8,128)S(1)} fusion(f32[2,16,64,128]{3,2,0,1:T(8,128)S(1)} %get-tuple-element.61, f32[2,16,66,1]{3,2,0,1:T(8,128)} %copy.75, f32[2,16,1,128]{3,2,0,1:T(1,128)S(1)} %collective-permute-done.4, f32[2,16,1,128]{3,2,0,1:T(1,128)S(1)} %collective-permute-done.5, f32[2,16,66,1]{3,2,0,1:T(8,128)} %copy.73, ...), kind=kLoop, calls=%fused_computation.39 | loop fusion | flops 5242880 | bytes 2277888 | tf_op jit(solution)/shard_map/add | solution.py:75
  131.0 1.9 collective-permute-start.8
  133.0 4.5 %collective-permute-start.9 = (f32[2,16,1,128]{3,2,0,1:T(1,128)S(1)}, f32[2,16,1,128]{3,2,0,1:T(1,128)S(1)}, u32[]{:S(2)}, u32[]{:S(2)}) collective-permute-start(f32[2,16,1,128]{3,2,0,1:T(1,128)S(1)} %get-tuple-element.67), channel_id=1, source_target_pairs={{0,4},{4,8},{8,12},{12,16},{16,20},{20,24},{24,28},{1,5},{5,9},{9,... | collective-permute-start | bytes 49160 | tf_op jit(solution)/shard_map/ppermute | solution.py:14
  144.9 4.4 %collective-permute-start.11 = (f32[2,16,66,1]{2,1,3,0:T(8,128)S(1)}, f32[2,16,66,1]{2,1,3,0:T(8,128)S(1)}, u32[]{:S(2)}, u32[]{:S(2)}) collective-permute-start(f32[2,16,66,1]{2,1,3,0:T(8,128)S(1)} %copy.78), channel_id=1, source_target_pairs={{0,1},{1,2},{2,3},{4,5},{5,6},{6,7},{8,9},{9,10},{10,11},{12,13},{... | collective-permute-start | bytes 25352 | tf_op jit(solution)/shard_map/ppermute | solution.py:14
  152.3 2.8 %fusion.5 = f32[2,16,64,128]{3,2,0,1:T(8,128)S(1)} fusion(f32[2,16,64,128]{3,2,0,1:T(8,128)S(1)} %fusion.17, f32[2,16,66,1]{3,2,0,1:T(8,128)} %copy.79, f32[2,16,1,128]{3,2,0,1:T(1,128)S(1)} %collective-permute-done.8, f32[2,16,1,128]{3,2,0,1:T(1,128)S(1)} %collective-permute-done.9, f32[2,16,66,1]{3,2,0,1:T(8,128)} %copy.77, ...), kind=kLoop, calls=%fused_computation.19 | loop fusion | flops 5242880 | bytes 2277888 | tf_op jit(solution)/shard_map/add | solution.py:75
  155.7 2.8 %gather_fusion.2 = f32[512,5,128]{2,1,0:T(8,128)} fusion(f32[64,5,128]{2,1,0:T(8,128)S(1)} %copy.80, s32[1024]{0:T(1024)S(1)} %copy-done.32), kind=kCustom, calls=%fused_computation.2 | custom fusion | bytes 2623488 | tf_op jit(solution)/shard_map/gather | solution.py:141
  158.5 10.2 %all-to-all-start.2 = ((f32[512,5,128]{2,1,0:T(8,128)}), f32[512,5,128]{2,1,0:T(8,128)}, u32[]{:S(2)}, u32[]{:S(2)}) async-start(f32[512,5,128]{2,1,0:T(8,128)} %gather_fusion.2), calls=%async_computation.2 | async-start | bytes 4194304 | tf_op jit(solution)/shard_map/all_to_all | solution.py:142
  170.3 46.7 %all-to-all-done.2 = f32[512,5,128]{2,1,0:T(8,128)} async-done(((f32[512,5,128]{2,1,0:T(8,128)}), f32[512,5,128]{2,1,0:T(8,128)}, u32[]{:S(2)}, u32[]{:S(2)}) %all-to-all-start.2) | async-done | bytes 1310752 | tf_op jit(solution)/shard_map/all_to_all | solution.py:142
  217.0 2.3 %gather_fusion.3 = f32[256,5,128]{2,1,0:T(8,128)S(1)} fusion(f32[512,5,128]{2,1,0:T(8,128)} %all-to-all-done.2, s32[1024]{0:T(1024)S(1)} %pad_clamp_fusion), kind=kCustom, calls=%fused_computation.3 | custom fusion | bytes 1311744 | tf_op jit(solution)/shard_map/gather | solution.py:143
  219.3 6.7 %fusion.31 = f32[256,5,128]{2,1,0:T(8,128)S(1)} fusion(bf16[256,128,128]{2,1,0:T(8,128)(2,1)} %gather_fusion.1, f32[256,5,128]{2,1,0:T(8,128)S(1)} %gather_fusion.3), kind=kOutput, calls=%fused_computation.63 | convolution fusion | flops 42106880 | bytes 9699328 | tf_op jit(solution)/shard_map/pab,pcb->pca/dot_general | solution.py:146
  226.0 6.7 %convolution_add_fusion = f32[256,5,128]{2,1,0:T(8,128)S(1)} fusion(f32[256,5,128]{2,1,0:T(8,128)S(1)} %fusion.31, bf16[256,128,128]{2,1,0:T(8,128)(2,1)} %gather_fusion.1, f32[256,5,128]{2,1,0:T(8,128)S(1)} %gather_fusion.3), kind=kOutput, calls=%fused_computation.9 | convolution fusion | flops 42762240 | bytes 10354688 | tf_op jit(solution)/shard_map/pab,pcb->pca/dot_general | solution.py:147
  (176 shorter events, 48.7 us)
Async XLA Ops:
  3.7 40.0 %copy-start.33 = (s32[256,1]{0,1:T(1,128)}, s32[256,1]{0,1:T(1,128)S(1)}, u32[]{:S(2)}) copy-start(s32[256,1]{0,1:T(1,128)S(1)} %compare_select_fusion.1) | copy-start | bytes 3076
  5.9 19.4 %all-to-all-start = ((s32[32,16,1]{1,2,0:T(1,128)}), s32[32,16,1]{1,2,0:T(1,128)S(1)}, u32[]{:S(2)}, u32[]{:S(2)}) async-start(s32[32,16,1]{1,2,0:T(1,128)} %bitcast.5), calls=%async_computation | async-start | bytes 32768 | tf_op jit(solution)/shard_map/all_to_all | solution.py:118
  14.5 64.4 %collective-permute-start = (f32[2,2,128]{2,1,0:T(2,128)S(1)}, f32[2,2,128]{2,1,0:T(2,128)S(1)}, u32[]{:S(2)}, u32[]{:S(2)}) collective-permute-start(f32[2,2,128]{2,1,0:T(2,128)S(1)} %get-tuple-element.104), channel_id=1, source_target_pairs={{0,4},{4,8},{8,12},{12,16},{16,20},{20,24},{24,28},{1,5},{5,9},{9,... | collective-permute-start | bytes 6152 | tf_op jit(solution)/shard_map/ppermute | solution.py:14
  18.0 60.9 %collective-permute-start.1 = (f32[2,2,128]{2,1,0:T(2,128)S(1)}, f32[2,2,128]{2,1,0:T(2,128)S(1)}, u32[]{:S(2)}, u32[]{:S(2)}) collective-permute-start(f32[2,2,128]{2,1,0:T(2,128)S(1)} %get-tuple-element.105), channel_id=1, source_target_pairs={{4,0},{8,4},{12,8},{16,12},{20,16},{24,20},{28,24},{5,1},{9,5},{13... | collective-permute-start | bytes 6152 | tf_op jit(solution)/shard_map/ppermute | solution.py:15
  23.3 60.4 %copy-start.1 = (f32[1,64,128]{2,1,0:T(8,128)}, f32[1,64,128]{2,1,0:T(8,128)S(1)}, u32[]{:S(2)}) copy-start(f32[1,64,128]{2,1,0:T(8,128)S(1)} %get-tuple-element.42) | copy-start | bytes 98308
  23.9 51.6 %copy-start.5 = (f32[1,64,128]{2,1,0:T(8,128)}, f32[1,64,128]{2,1,0:T(8,128)S(1)}, u32[]{:S(2)}) copy-start(f32[1,64,128]{2,1,0:T(8,128)S(1)} %get-tuple-element.44) | copy-start | bytes 98308
  23.9 59.7 %copy-start.6 = (f32[1,64,128]{2,1,0:T(8,128)}, f32[1,64,128]{2,1,0:T(8,128)S(1)}, u32[]{:S(2)}) copy-start(f32[1,64,128]{2,1,0:T(8,128)S(1)} %get-tuple-element.45) | copy-start | bytes 98308
  69.6 32.4 %all-to-all-start.1 = ((f32[512,4,128]{2,1,0:T(4,128)}), f32[512,4,128]{2,1,0:T(4,128)S(1)}, u32[]{:S(2)}, u32[]{:S(2)}) async-start(f32[512,4,128]{2,1,0:T(4,128)} %scatter_fusion), calls=%async_computation.1 | async-start | bytes 2097152 | tf_op jit(solution)/shard_map/all_to_all | solution.py:117
  76.2 26.2 %copy-start.9 = (f32[1,64,128]{2,1,0:T(8,128)}, f32[1,64,128]{2,1,0:T(8,128)S(1)}, u32[]{:S(2)}) copy-start(f32[1,64,128]{2,1,0:T(8,128)S(1)} %get-tuple-element.47) | copy-start | bytes 98308
  76.2 26.2 %copy-start.10 = (f32[1,64,128]{2,1,0:T(8,128)}, f32[1,64,128]{2,1,0:T(8,128)S(1)}, u32[]{:S(2)}) copy-start(f32[1,64,128]{2,1,0:T(8,128)S(1)} %get-tuple-element.48) | copy-start | bytes 98308
  76.8 25.6 %copy-start.11 = (f32[1,64,128]{2,1,0:T(8,128)}, f32[1,64,128]{2,1,0:T(8,128)S(1)}, u32[]{:S(2)}) copy-start(f32[1,64,128]{2,1,0:T(8,128)S(1)} %get-tuple-element.50) | copy-start | bytes 98308
  76.8 25.6 %copy-start.12 = (f32[1,64,128]{2,1,0:T(8,128)}, f32[1,64,128]{2,1,0:T(8,128)S(1)}, u32[]{:S(2)}) copy-start(f32[1,64,128]{2,1,0:T(8,128)S(1)} %get-tuple-element.51) | copy-start | bytes 98308
  77.4 25.0 %copy-start.15 = (f32[1,64,128]{2,1,0:T(8,128)}, f32[1,64,128]{2,1,0:T(8,128)S(1)}, u32[]{:S(2)}) copy-start(f32[1,64,128]{2,1,0:T(8,128)S(1)} %get-tuple-element.53) | copy-start | bytes 98308
  79.0 15.3 %collective-permute-start.2 = (f32[2,68,2]{2,1,0:T(8,128)S(1)}, f32[2,68,2]{2,1,0:T(8,128)S(1)}, u32[]{:S(2)}, u32[]{:S(2)}) collective-permute-start(f32[2,68,2]{2,1,0:T(8,128)S(1)} %get-tuple-element.102), channel_id=1, source_target_pairs={{0,1},{1,2},{2,3},{4,5},{5,6},{6,7},{8,9},{9,10},{10,11},{12,13},{... | collective-permute-start | bytes 3272 | tf_op jit(solution)/shard_map/ppermute | solution.py:14
  82.3 12.0 %collective-permute-start.3 = (f32[2,68,2]{2,1,0:T(8,128)S(1)}, f32[2,68,2]{2,1,0:T(8,128)S(1)}, u32[]{:S(2)}, u32[]{:S(2)}) collective-permute-start(f32[2,68,2]{2,1,0:T(8,128)S(1)} %get-tuple-element.103), channel_id=1, source_target_pairs={{1,0},{2,1},{3,2},{5,4},{6,5},{7,6},{9,8},{10,9},{11,10},{13,12},{... | collective-permute-start | bytes 3272 | tf_op jit(solution)/shard_map/ppermute | solution.py:15
  107.6 5.8 %collective-permute-start.4 = (f32[2,16,1,128]{3,2,0,1:T(1,128)S(1)}, f32[2,16,1,128]{3,2,0,1:T(1,128)S(1)}, u32[]{:S(2)}, u32[]{:S(2)}) collective-permute-start(f32[2,16,1,128]{3,2,0,1:T(1,128)S(1)} %get-tuple-element.60), channel_id=1, source_target_pairs={{4,0},{8,4},{12,8},{16,12},{20,16},{24,20},{28,24},{5,1},{9,5},{13... | collective-permute-start | bytes 49160 | tf_op jit(solution)/shard_map/ppermute | solution.py:15
  109.5 4.5 %collective-permute-start.5 = (f32[2,16,1,128]{3,2,0,1:T(1,128)S(1)}, f32[2,16,1,128]{3,2,0,1:T(1,128)S(1)}, u32[]{:S(2)}, u32[]{:S(2)}) collective-permute-start(f32[2,16,1,128]{3,2,0,1:T(1,128)S(1)} %get-tuple-element.59), channel_id=1, source_target_pairs={{0,4},{4,8},{8,12},{12,16},{16,20},{20,24},{24,28},{1,5},{5,9},{9,... | collective-permute-start | bytes 49160 | tf_op jit(solution)/shard_map/ppermute | solution.py:14
  117.2 8.0 %collective-permute-start.6 = (f32[2,16,66,1]{2,1,3,0:T(8,128)S(1)}, f32[2,16,66,1]{2,1,3,0:T(8,128)S(1)}, u32[]{:S(2)}, u32[]{:S(2)}) collective-permute-start(f32[2,16,66,1]{2,1,3,0:T(8,128)S(1)} %copy.72), channel_id=1, source_target_pairs={{1,0},{2,1},{3,2},{5,4},{6,5},{7,6},{9,8},{10,9},{11,10},{13,12},{... | collective-permute-start | bytes 25352 | tf_op jit(solution)/shard_map/ppermute | solution.py:15
  119.6 7.1 %collective-permute-start.7 = (f32[2,16,66,1]{2,1,3,0:T(8,128)}, f32[2,16,66,1]{2,1,3,0:T(8,128)S(1)}, u32[]{:S(2)}, u32[]{:S(2)}) collective-permute-start(f32[2,16,66,1]{2,1,3,0:T(8,128)} %copy.74), channel_id=1, source_target_pairs={{0,1},{1,2},{2,3},{4,5},{5,6},{6,7},{8,9},{9,10},{10,11},{12,13},{... | collective-permute-start | bytes 25352 | tf_op jit(solution)/shard_map/ppermute | solution.py:14
  131.0 6.4 %collective-permute-start.8 = (f32[2,16,1,128]{3,2,0,1:T(1,128)S(1)}, f32[2,16,1,128]{3,2,0,1:T(1,128)S(1)}, u32[]{:S(2)}, u32[]{:S(2)}) collective-permute-start(f32[2,16,1,128]{3,2,0,1:T(1,128)S(1)} %get-tuple-element.68), channel_id=1, source_target_pairs={{4,0},{8,4},{12,8},{16,12},{20,16},{24,20},{28,24},{5,1},{9,5},{13... | collective-permute-start | bytes 49160 | tf_op jit(solution)/shard_map/ppermute | solution.py:15
  133.0 5.3 %collective-permute-start.9 = (f32[2,16,1,128]{3,2,0,1:T(1,128)S(1)}, f32[2,16,1,128]{3,2,0,1:T(1,128)S(1)}, u32[]{:S(2)}, u32[]{:S(2)}) collective-permute-start(f32[2,16,1,128]{3,2,0,1:T(1,128)S(1)} %get-tuple-element.67), channel_id=1, source_target_pairs={{0,4},{4,8},{8,12},{12,16},{16,20},{20,24},{24,28},{1,5},{5,9},{9,... | collective-permute-start | bytes 49160 | tf_op jit(solution)/shard_map/ppermute | solution.py:14
  141.9 7.4 %collective-permute-start.10 = (f32[2,16,66,1]{2,1,3,0:T(8,128)S(1)}, f32[2,16,66,1]{2,1,3,0:T(8,128)S(1)}, u32[]{:S(2)}, u32[]{:S(2)}) collective-permute-start(f32[2,16,66,1]{2,1,3,0:T(8,128)S(1)} %copy.76), channel_id=1, source_target_pairs={{1,0},{2,1},{3,2},{5,4},{6,5},{7,6},{9,8},{10,9},{11,10},{13,12},{... | collective-permute-start | bytes 25352 | tf_op jit(solution)/shard_map/ppermute | solution.py:15
  144.9 5.9 %collective-permute-start.11 = (f32[2,16,66,1]{2,1,3,0:T(8,128)S(1)}, f32[2,16,66,1]{2,1,3,0:T(8,128)S(1)}, u32[]{:S(2)}, u32[]{:S(2)}) collective-permute-start(f32[2,16,66,1]{2,1,3,0:T(8,128)S(1)} %copy.78), channel_id=1, source_target_pairs={{0,1},{1,2},{2,3},{4,5},{5,6},{6,7},{8,9},{9,10},{10,11},{12,13},{... | collective-permute-start | bytes 25352 | tf_op jit(solution)/shard_map/ppermute | solution.py:14
  158.5 58.5 %all-to-all-start.2 = ((f32[512,5,128]{2,1,0:T(8,128)}), f32[512,5,128]{2,1,0:T(8,128)}, u32[]{:S(2)}, u32[]{:S(2)}) async-start(f32[512,5,128]{2,1,0:T(8,128)} %gather_fusion.2), calls=%async_computation.2 | async-start | bytes 4194304 | tf_op jit(solution)/shard_map/all_to_all | solution.py:142
  (29 other events, 343.3 us)
where the time goes:
time: 236 us; the launch traced here: 234 us
  local copies, waits for them, and re-layouts  67 us (28%)
  waiting for transfers between devices  64.1 us (27%)
  starting transfers between devices  57.7 us (24%)
  matrix products  22.5 us (10%)
  other arithmetic  21.4 us (9%)
    all_to_all x1, waiting for transfers between devices, local(): lax.all_to_all(sendback, ('gx', 'gy'), split_axis=0, concat_axis=0, tiled...  46.7 us
    scatter x1, local copies, waits for them, and re-layouts, local(): jnp.zeros((slot_count, 4, patch_width), jnp.float32).at[send_slot]  25.9 us
    ppermute x6, starting transfers between devices, extended(): before = lax.ppermute(last, axis, up)  24.8 us
    ppermute x6, waiting for transfers between devices, extended(): before = lax.ppermute(last, axis, up)  11.3 us
    gather x1, local copies, waits for them, and re-layouts, local(): tile_weights = remap_weight[pair_tile]  10.9 us
    all_to_all x1, starting transfers between devices, local(): lax.all_to_all(sendback, ('gx', 'gy'), split_axis=0, concat_axis=0, tiled...  10.2 us
    ppermute x6, starting transfers between devices, extended(): after = lax.ppermute(leading, axis, down)  9.67 us
    all_to_all x1, starting transfers between devices, local(): lax.all_to_all(out_rows, ('gx', 'gy'), split_axis=0, concat_axis=0, tiled...  7.1 us
  transfers between devices with their start and end apart: 15, of which 5 were waited for; matrix products, arithmetic and copies ran while one was open for 27% of the time, Pallas kernels for 0%

commit v1 on v0

v1 whole, which is shorter than its diff:
```python
import functools

import jax
import jax.numpy as jnp
from jax import lax
from jax.experimental import pallas as pl
from jax.experimental.pallas import tpu as pltpu
from jax.sharding import PartitionSpec as P

F32 = jnp.float32
BF16 = jnp.bfloat16
VMEM = pltpu.VMEM
SMEM = pltpu.SMEM


def remap_out_kernel(capacity, block_s, owner_s, row_s, tile_s, atm, weights, out, slot_o, rows_o, flux, fill):
    npairs = block_s.shape[0]
    nblocks = flux.shape[0]
    devices = fill.shape[0]
    out[...] = jnp.zeros_like(out)

    def clear_rows(i, carry):
        rows_o[i] = -1
        return carry

    lax.fori_loop(0, rows_o.shape[0], clear_rows, 0, unroll=16)

    def clear_fill(i, carry):
        fill[i] = 0
        return carry

    lax.fori_loop(0, devices, clear_fill, 0, unroll=16)
    wind_u = atm[0:1, :]
    wind_v = atm[1:2, :]
    speed = jnp.sqrt(wind_u * wind_u + wind_v * wind_v + 0.25)
    heat = 0.5 * speed * (atm[2:3, :] - atm[5:6, :])
    water = atm[4:5, :] - 0.3 * speed * atm[3:4, :]
    planes = jnp.concatenate(
        [heat, water, 0.2 * speed * wind_u, 0.2 * speed * wind_v, jnp.zeros((12, wind_u.shape[1]), F32)], 0
    ).astype(BF16)
    for b in range(nblocks):
        flux[b] = planes[:, b * 128 : (b + 1) * 128]

    def pair(p, carry):
        owner = owner_s[p]
        rank = fill[owner]
        fill[owner] = rank + 1
        slot = owner * capacity + rank
        slot_o[p] = slot
        rows_o[slot] = row_s[p]
        value = jnp.dot(flux[block_s[p]], weights[tile_s[p]], preferred_element_type=F32)
        out[slot] = value[0:4]
        return carry

    lax.fori_loop(0, npairs, pair, 0, unroll=8)


def remap_out(capacity, devices, atm_state, pair_block, owner, pair_row, pair_tile, remap_weight):
    npairs = pair_block.shape[0]
    slots = devices * capacity
    nblocks = atm_state.shape[1] // 128
    smem = pl.BlockSpec(memory_space=SMEM)
    vmem = pl.BlockSpec(memory_space=VMEM)
    return pl.pallas_call(
        functools.partial(remap_out_kernel, capacity),
        out_shape=(
            jax.ShapeDtypeStruct((slots, 4, 128), F32),
            jax.ShapeDtypeStruct((npairs,), jnp.int32),
            jax.ShapeDtypeStruct((slots,), jnp.int32),
        ),
        in_specs=[smem] * 4 + [vmem] * 2,
        out_specs=(vmem, smem, smem),
        scratch_shapes=[pltpu.VMEM((nblocks, 16, 128), BF16), pltpu.SMEM((devices,), jnp.int32)],
        compiler_params=pltpu.CompilerParams(vmem_limit_bytes=24 * 1024 * 1024),
        cost_estimate=pl.CostEstimate(flops=2 * npairs * 16 * 128 * 128, bytes_accessed=6 << 20, transcendentals=0),
    )(pair_block, owner, pair_row, pair_tile, atm_state, remap_weight)


def remap_back_kernel(block_s, tile_s, slot_s, cell_s, returned, wet, weights, out, total):
    npairs = block_s.shape[0]
    nblocks = total.shape[0]
    total[...] = jnp.zeros_like(total)

    def pair(p, carry):
        rows = returned[slot_s[p]]
        mask = wet[pl.ds(cell_s[p], 1), :].astype(F32)
        full = jnp.concatenate([rows, mask, jnp.zeros((3, 128), F32)], 0)
        high = full.astype(BF16)
        low = (full - high.astype(F32)).astype(BF16)
        both = jnp.concatenate([high, low], 0)
        value = lax.dot_general(
            both, weights[tile_s[p]], (((1,), (1,)), ((), ())), preferred_element_type=F32
        )
        b = block_s[p]
        total[b] = total[b] + (value[0:8] + value[8:16])
        return carry

    lax.fori_loop(0, npairs, pair, 0, unroll=8)
    for b in range(nblocks):
        sums = total[b]
        out[:, b * 128 : (b + 1) * 128] = sums[0:4] / jnp.maximum(sums[4:5], 0.1)


def remap_back(pair_block, pair_tile, slot, cell, returned, wet_all, remap_weight, nblocks):
    npairs = pair_block.shape[0]
    smem = pl.BlockSpec(memory_space=SMEM)
    vmem = pl.BlockSpec(memory_space=VMEM)
    return pl.pallas_call(
        remap_back_kernel,
        out_shape=jax.ShapeDtypeStruct((4, nblocks * 128), F32),
        in_specs=[smem] * 4 + [vmem] * 3,
        out_specs=vmem,
        scratch_shapes=[pltpu.VMEM((nblocks, 8, 128), F32)],
        compiler_params=pltpu.CompilerParams(vmem_limit_bytes=24 * 1024 * 1024),
        cost_estimate=pl.CostEstimate(flops=2 * npairs * 16 * 128 * 128, bytes_accessed=6 << 20, transcendentals=0),
    )(pair_block, pair_tile, slot, cell, returned, wet_all, remap_weight)


def extended(shard, sides, width):
    for axis, dim in sides:
        count, length = (lax.axis_size(axis), shard.shape[dim])
        up = [(i, (i + 1) % count) for i in range(count - 1)]
        down = [(j, i) for i, j in up]
        last = lax.slice_in_dim(shard, length - width, length, axis=dim)
        leading = lax.slice_in_dim(shard, 0, width, axis=dim)
        before = lax.ppermute(last, axis, up)
        after = lax.ppermute(leading, axis, down)
        shard = jnp.concatenate([before, shard, after], axis=dim)
    return shard


def column_mix(fields, vert_kappa):
    levels = vert_kappa.shape[0]
    face_coef = 0.5 * (vert_kappa[:-1] + vert_kappa[1:])
    zero_plane = jnp.zeros_like(vert_kappa[:1])
    above = jnp.concatenate([zero_plane, face_coef], 0)
    below = jnp.concatenate([face_coef, zero_plane], 0)
    diagonal = 1.0 + above + below
    upper_list = []
    rhs_list = []
    for level_index in range(levels):
        if level_index == 0:
            pivot_inv = 1.0 / diagonal[0]
            rhs_now = fields[:, 0] * pivot_inv
        else:
            pivot_inv = 1.0 / (diagonal[level_index] + above[level_index] * upper_list[-1])
            rhs_now = (fields[:, level_index] + above[level_index] * rhs_list[-1]) * pivot_inv
        upper_list.append(-below[level_index] * pivot_inv)
        rhs_list.append(rhs_now)
    solved = [rhs_list[-1]]
    for level_index in range(levels - 2, -1, -1):
        solved.append(rhs_list[level_index] - upper_list[level_index] * solved[-1])
    return jnp.stack(solved[::-1], 1)


def shifted(array, step_x, step_y):
    size_x = array.shape[-2]
    size_y = array.shape[-1]
    return array[..., 1 + step_x : size_x - 1 + step_x, 1 + step_y : size_y - 1 + step_y]


def diffuse(padded, coefficients):
    kappa_pad = coefficients[0]
    wet_pad = coefficients[1]
    centre = shifted(padded, 0, 0)
    kappa_mid = shifted(kappa_pad, 0, 0)
    wet_mid = shifted(wet_pad, 0, 0)
    result = centre
    for step_x, step_y in ((1, 0), (-1, 0), (0, 1), (0, -1)):
        face_coef = (
            0.25
            * (kappa_mid + shifted(kappa_pad, step_x, step_y))
            * wet_mid
            * shifted(wet_pad, step_x, step_y)
        )
        result = result + face_coef * (shifted(padded, step_x, step_y) - centre)
    return result


def local(
    atm_state,
    pair_block,
    pair_owner,
    pair_row,
    pair_tile,
    remap_weight,
    wet_mask,
    ocean_state,
    vert_kappa,
    horiz_kappa,
):
    highest = lax.Precision.HIGHEST
    grid_x = lax.axis_size("gx")
    grid_y = lax.axis_size("gy")
    devices = grid_x * grid_y
    npairs = pair_block.shape[0]
    capacity = max(2, 2 * npairs // devices)
    slot_count = devices * capacity
    tile_rows = ocean_state.shape[2]
    nblocks = atm_state.shape[1] // 128
    me = lax.axis_index("gx") * grid_y + lax.axis_index("gy")
    owner = pair_owner.reshape(npairs)
    wet_all = lax.all_gather(wet_mask, ("gx", "gy"), axis=0, tiled=True)
    outgoing, slot, out_rows = remap_out(
        capacity, devices, atm_state, pair_block, owner, pair_row, pair_tile, remap_weight
    )
    arrived = lax.all_to_all(outgoing, ("gx", "gy"), split_axis=0, concat_axis=0, tiled=True)
    rows_all = lax.all_gather(out_rows, ("gx", "gy"), axis=0, tiled=True)
    in_rows = lax.dynamic_slice_in_dim(rows_all.reshape(devices, devices, capacity), me, 1, 1).reshape(slot_count)
    placing = (jnp.arange(tile_rows, dtype=jnp.int32)[:, None] == in_rows[None, :]).astype(F32)
    forcing = jnp.dot(
        placing,
        arrived.reshape(slot_count, 4 * 128),
        precision=highest,
        preferred_element_type=F32,
    )
    forcing = forcing.reshape(tile_rows, 4, 128).transpose(1, 0, 2)
    wet_frac = wet_mask.astype(F32)
    forced = ocean_state.at[:, 0].add(forcing * wet_frac[None])
    coef_pad = extended(jnp.stack([horiz_kappa, wet_frac]), (("gx", 1), ("gy", 2)), 2)
    mixed = column_mix(forced, vert_kappa)
    tracers = extended(mixed[:2], (("gx", 2), ("gy", 3)), 2)
    tracers = diffuse(tracers, coef_pad)
    tracers = diffuse(tracers, coef_pad[:, 1:-1, 1:-1])
    ocean_next = jnp.concatenate([tracers, mixed[2:]], 0)
    surface = ocean_next[:, 0] * wet_frac[None]
    sendback = surface.transpose(1, 0, 2)[jnp.maximum(in_rows, 0)]
    returned = lax.all_to_all(sendback, ("gx", "gy"), split_axis=0, concat_axis=0, tiled=True)
    atm_surface = remap_back(
        pair_block, pair_tile, slot, owner * tile_rows + pair_row, returned, wet_all, remap_weight, nblocks
    )
    return (ocean_next, atm_surface)


def solution(mesh):
    placed = (
        P(None, ("gx", "gy")),
        P(("gx", "gy")),
        P(("gx", "gy"), None),
        P(("gx", "gy")),
        P(("gx", "gy")),
        P(("gx", "gy"), None, None),
        P("gx", "gy"),
        P(None, None, "gx", "gy"),
        P(None, "gx", "gy"),
        P("gx", "gy"),
    )
    return jax.shard_map(
        local,
        mesh=mesh,
        in_specs=placed,
        out_specs=(P(None, None, "gx", "gy"), P(None, ("gx", "gy"))),
        check_vma=False,
    )
```

time: 236 us -> 209 us (0.89)
  blocking collectives: 0 us -> 72.1 us
  local copies, waits for them, and re-layouts: 67 us -> 21 us
  waiting for transfers between devices: 64.1 us -> 27.2 us
  matrix products: 22.5 us -> 2.75 us
  starting transfers between devices: 57.7 us -> 39.7 us
  Pallas kernels: 0 us -> 17.7 us
  between operations: 1.58 us -> 14.8 us
  other arithmetic: 21.4 us -> 12.8 us
    all_gather x0 -> x1, blocking collectives: none -> 72.1 us  [local(): rows_all = lax.all_gather(out_rows, ('gx', 'gy'), axis=0, tiled=True)]
    scatter x2 -> x0, local copies, waits for them, and re-layouts: 27.4 us -> none  [the longest x1 25.9 us: local(): jnp.zeros((slot_count, 4, patch_width), jnp.float32).at[send_slot]]
    all_to_all x1, waiting for transfers between devices: 46.7 us -> 24.7 us  [local(): lax.all_to_all(sendback, ('gx', 'gy'), split_axis=0, concat_axis=0, tiled...]
    dot_general x5 -> x1, matrix products: 22.5 us -> 2.75 us  [local(): jnp.dot(placing, arrived.reshape(slot_count, 4 * 128), precision=highest,...]
    pallas_call x0 -> x2, Pallas kernels: none -> 17.7 us  [the longest x1 9.51 us: remap_back(): pl.pallas_call(remap_back_kernel, out_shape=jax.ShapeDtypeStruct((4, nblo...]
    gather x4 -> x1, local copies, waits for them, and re-layouts: 17 us -> 2.64 us  [local(): sendback = surface.transpose(1, 0, 2)[jnp.maximum(in_rows, 0)]]
    ppermute x6 -> x4, starting transfers between devices: 24.8 us -> 13.3 us  [extended(): before = lax.ppermute(last, axis, up)]
    ppermute x6 -> x4, waiting for transfers between devices: 11.3 us -> 0.73 us  [extended(): before = lax.ppermute(last, axis, up)]
  transfers between devices with their start and end apart: 15 -> 11, of which waited for: 5 -> 4; matrix products, arithmetic and copies ran while one was open for 27% -> 13% of each run, Pallas kernels for 0% -> 0%
where the time goes in v1:
time: 209 us; the launch traced here: 208 us
  blocking collectives  72.1 us (34%)
  starting transfers between devices  39.7 us (19%)
  waiting for transfers between devices  27.2 us (13%)
  local copies, waits for them, and re-layouts  21 us (10%)
  Pallas kernels  17.7 us (8%)
  between operations  14.8 us (7%)
  other arithmetic  12.8 us (6%)
  matrix products  2.75 us (1%)
    all_gather x1, blocking collectives, local(): rows_all = lax.all_gather(out_rows, ('gx', 'gy'), axis=0, tiled=True)  72.1 us
    all_to_all x1, waiting for transfers between devices, local(): lax.all_to_all(sendback, ('gx', 'gy'), split_axis=0, concat_axis=0, tiled...  24.7 us
    ppermute x4, starting transfers between devices, extended(): before = lax.ppermute(last, axis, up)  13.3 us
    ppermute x4, starting transfers between devices, extended(): after = lax.ppermute(leading, axis, down)  13.2 us
    unnamed x79, local copies, waits for them, and re-layouts  11.4 us
    pallas_call x1, Pallas kernels, remap_back(): pl.pallas_call(remap_back_kernel, out_shape=jax.ShapeDtypeStruct((4, nblo...  9.51 us
    pallas_call x1, Pallas kernels, remap_out(): pl.pallas_call(functools.partial(remap_out_kernel, capacity), out_shape=(...  8.2 us
    all_to_all x1, starting transfers between devices, local(): lax.all_to_all(outgoing, ('gx', 'gy'), split_axis=0, concat_axis=0, tiled...  7.11 us
  transfers between devices with their start and end apart: 11, of which 4 were waited for; matrix products, arithmetic and copies ran while one was open for 13% of the time, Pallas kernels for 0%

profile of v1, /device:TPU:1, one launch (start us, length us, event | category | flops | bytes accessed | tf_op | source)
XLA Modules:
  0.0 208.1 jit_solution(18100907446133046551)
XLA Ops:
  7.2 2.2 %copy-done = bf16[128,128,128]{2,1,0:T(8,128)(2,1)S(1)} copy-done((bf16[128,128,128]{2,1,0:T(8,128)(2,1)S(1)}, bf16[128,128,128]{2,1,0:T(8,128)(2,1)}, u32[]{:S(2)}) %copy-start) | copy-done | bytes 4194328
  13.0 8.2 %shard_map.113 = (f32[512,4,128]{2,1,0:T(4,128)}, s32[256]{0:T(256)S(1)}, s32[512]{0:T(512)S(1)}) custom-call(s32[256]{0:T(256)S(1)} %copy-done.8, s32[256]{0:T(256)S(1)} %bitcast.239, s32[256]{0:T(256)S(1)} %copy-done.6, s32[256]{0:T(256)S(1)} %copy-done.10, f32[6,6144]{1,0:T(8,128)S(1)} %copy-done.3, bf16[128,128,128]{2,1,0:T(8,128)(2,1)S(1)} %copy-done), custom_call_target="tpu_custom_call" | custom-call | flops 134217728 | bytes 6291456 | tf_op jit(solution)/shard_map/pallas_call | solution.py:64
  21.2 7.1 %all-to-all-start = ((f32[512,4,128]{2,1,0:T(4,128)}), f32[512,4,128]{2,1,0:T(4,128)S(1)}, u32[]{:S(2)}, u32[]{:S(2)}) async-start(f32[512,4,128]{2,1,0:T(4,128)} %get-tuple-element.18), calls=%async_computation | async-start | bytes 2097152 | tf_op jit(solution)/shard_map/all_to_all | solution.py:207
  29.7 2.2 %collective-permute-start.5 = (f32[2,2,128]{2,1,0:T(2,128)}, f32[2,2,128]{2,1,0:T(2,128)S(1)}, u32[]{:S(2)}, u32[]{:S(2)}) collective-permute-start(f32[2,2,128]{2,1,0:T(2,128)} %get-tuple-element.112), channel_id=1, source_target_pairs={{4,0},{8,4},{12,8},{16,12},{20,16},{24,20},{28,24},{5,1},{9,5},{13... | collective-permute-start | bytes 6152 | tf_op jit(solution)/shard_map/ppermute | solution.py:127
  31.9 3.4 %collective-permute-start.4 = (f32[2,2,128]{2,1,0:T(2,128)}, f32[2,2,128]{2,1,0:T(2,128)S(1)}, u32[]{:S(2)}, u32[]{:S(2)}) collective-permute-start(f32[2,2,128]{2,1,0:T(2,128)} %get-tuple-element.111), channel_id=1, source_target_pairs={{0,4},{4,8},{8,12},{12,16},{16,20},{20,24},{24,28},{1,5},{5,9},{9,... | collective-permute-start | bytes 6152 | tf_op jit(solution)/shard_map/ppermute | solution.py:126
  35.6 72.1 %all-gather = s32[32,1,512]{2,1,0:T(1,128)S(1)} all-gather(s32[1,1,512]{2,1,0:T(1,128)S(1)} %bitcast.241), channel_id=1, replica_groups=mesh['gx'=8,'gy'=4] {'gx','gy'}, dimensions={0}, use_global_device_ids=true | all-gather | bytes 67584 | tf_op jit(solution)/shard_map/all_gather | solution.py:208
  109.6 1.3 collective-permute-start.7
  110.9 4.0 %collective-permute-start.6 = (f32[2,68,2]{2,1,0:T(8,128)S(1)}, f32[2,68,2]{2,1,0:T(8,128)S(1)}, u32[]{:S(2)}, u32[]{:S(2)}) collective-permute-start(f32[2,68,2]{2,1,0:T(8,128)S(1)} %get-tuple-element.109), channel_id=1, source_target_pairs={{0,1},{1,2},{2,3},{4,5},{5,6},{6,7},{8,9},{9,10},{10,11},{12,13},{... | collective-permute-start | bytes 3272 | tf_op jit(solution)/shard_map/ppermute | solution.py:126
  119.7 2.8 %subtract_dynamic-update-slice_fusion = (f32[4,16,64,128]{3,2,0,1:T(8,128)S(1)}, f32[4,1,64,128]{3,2,0,1:T(8,128)S(1)}, f32[4,1,64,128]{3,2,0,1:T(8,128)S(1)}, f...) fusion(f32[64,128]{1,0:T(8,128)S(1)} %get-tuple-element.74, ...), kind=kOutput, calls=%fused_computation.77 | convolution fusion | flops 203915264 | bytes 6653952 | tf_op jit(solution)/shard_map/dot_general | solution.py:211
  123.8 8.4 %collective-permute-start.1 = (f32[2,16,2,128]{3,2,0,1:T(2,128)S(1)}, f32[2,16,2,128]{3,2,0,1:T(2,128)S(1)}, u32[]{:S(2)}, u32[]{:S(2)}) collective-permute-start(f32[2,16,2,128]{3,2,0,1:T(2,128)S(1)} %get-tuple-element.68), channel_id=1, source_target_pairs={{4,0},{8,4},{12,8},{16,12},{20,16},{24,20},{28,24},{5,1},{9,5},{13... | collective-permute-start | bytes 98312 | tf_op jit(solution)/shard_map/ppermute | solution.py:127
  132.2 1.9 collective-permute-start
  136.9 4.0 %collective-permute-start.2 = (f32[2,16,68,2]{2,1,3,0:T(8,128)}, f32[2,16,68,2]{2,1,3,0:T(8,128)S(1)}, u32[]{:S(2)}, u32[]{:S(2)}) collective-permute-start(f32[2,16,68,2]{2,1,3,0:T(8,128)} %copy.92), channel_id=1, source_target_pairs={{0,1},{1,2},{2,3},{4,5},{5,6},{6,7},{8,9},{9,10},{10,11},{12,13},{... | collective-permute-start | bytes 52232 | tf_op jit(solution)/shard_map/ppermute | solution.py:126
  141.3 1.3 collective-permute-start.3
  142.6 1.8 slice_multiply_fusion.7
  146.1 1.3 copy.95
  148.6 3.2 %fusion.2 = f32[2,16,66,130]{3,2,0,1:T(8,128)S(1)} fusion(f32[2,16,68,2]{3,2,0,1:T(8,128)S(1)} %copy.94, f32[2,16,2,128]{3,2,0,1:T(2,128)S(1)} %collective-permute-done.1, f32[2,16,64,128]{3,2,0,1:T(8,128)S(1)} %get-tuple-element.69, f32[2,16,2,128]{3,2,0,1:T(2,128)S(1)} %collective-permute-done, f32[2,16,68,2]{3,2,0,1:T(8,128)S(1)} %copy.95, ...), kind=kLoop, calls=%fused_computation.7 | loop fusion | flops 4942080 | bytes 5679168 | tf_op jit(solution)/shard_map/add | solution.py:176
  151.9 1.1 fusion.14
  153.2 2.6 %gather_fusion = f32[512,4,128]{2,1,0:T(4,128)} fusion(f32[64,4,128]{2,1,0:T(4,128)S(1)} %copy.99, s32[1024]{0:T(1024)S(1)} %pad_clamp_fusion), kind=kCustom, calls=%fused_computation | custom fusion | bytes 2099200 | tf_op jit(solution)/shard_map/gather | solution.py:227
  155.9 6.1 %all-to-all-start.1 = ((f32[512,4,128]{2,1,0:T(4,128)}), f32[512,4,128]{2,1,0:T(4,128)S(1)}, u32[]{:S(2)}, u32[]{:S(2)}) async-start(f32[512,4,128]{2,1,0:T(4,128)} %gather_fusion), calls=%async_computation.1 | async-start | bytes 2097152 | tf_op jit(solution)/shard_map/all_to_all | solution.py:228
  162.2 1.5 copy.100
  163.6 24.7 %all-to-all-done.1.returned = f32[512,4,128]{2,1,0:T(4,128)S(1)} async-done(((f32[512,4,128]{2,1,0:T(4,128)}), f32[512,4,128]{2,1,0:T(4,128)S(1)}, u32[]{:S(2)}, u32[]{:S(2)}) %all-to-all-start.1) | async-done | bytes 1048608 | tf_op jit(solution)/shard_map/all_to_all | solution.py:228
  188.3 2.2 %copy-done.1 = bf16[128,128,128]{2,1,0:T(8,128)(2,1)S(1)} copy-done((bf16[128,128,128]{2,1,0:T(8,128)(2,1)S(1)}, bf16[128,128,128]{2,1,0:T(8,128)(2,1)}, u32[]{:S(2)}) %copy-start.1) | copy-done | bytes 4194328
  190.5 1.2 copy-done.2
  191.7 9.5 %shard_map.114 = f32[4,6144]{1,0:T(4,128)} custom-call(s32[256]{0:T(256)S(1)} %copy-done.9, s32[256]{0:T(256)S(1)} %copy-done.11, s32[256]{0:T(256)S(1)} %get-tuple-element.19.slot_s, s32[256]{0:T(256)S(1)} %multiply_add_fusion.cell_s, f32[512,4,128]{2,1,0:T(4,128)S(1)} %all-to-all-done.1.returned, s32[2048,128]{1,0:T(8,128)S(1)} %copy-done.2, ...), custom_call_target="tpu_custom_call" | custom-call | flops 134217728 | bytes 6291456 | tf_op jit(solution)/shard_map/pallas_call | solution.py:108
  (135 shorter events, 19.3 us)
Async XLA Ops:
  7.2 2.2 %copy-start = (bf16[128,128,128]{2,1,0:T(8,128)(2,1)S(1)}, bf16[128,128,128]{2,1,0:T(8,128)(2,1)}, u32[]{:S(2)}) copy-start(bf16[128,128,128]{2,1,0:T(8,128)(2,1)} %weights.3) | copy-start | bytes 12582916
  21.2 7.9 %copy-start.33 = (s32[64,128]{1,0:T(8,128)S(1)}, s32[64,128]{1,0:T(8,128)}, u32[]{:S(2)}) copy-start(s32[64,128]{1,0:T(8,128)} %param.18) | copy-start | bytes 98308
  21.2 7.9 %copy-start.20 = (f32[64,128]{1,0:T(8,128)S(1)}, f32[64,128]{1,0:T(8,128)}, u32[]{:S(2)}) copy-start(f32[64,128]{1,0:T(8,128)} %param.21) | copy-start | bytes 98308
  21.2 14.1 %copy-start.13 = (f32[16,64,128]{2,1,0:T(8,128)S(1)}, f32[16,64,128]{2,1,0:T(8,128)}, u32[]{:S(2)}) copy-start(f32[16,64,128]{2,1,0:T(8,128)} %param.20) | copy-start | bytes 1572868
  21.2 97.5 %all-to-all-start = ((f32[512,4,128]{2,1,0:T(4,128)}), f32[512,4,128]{2,1,0:T(4,128)S(1)}, u32[]{:S(2)}, u32[]{:S(2)}) async-start(f32[512,4,128]{2,1,0:T(4,128)} %get-tuple-element.18), calls=%async_computation | async-start | bytes 2097152 | tf_op jit(solution)/shard_map/all_to_all | solution.py:207
  28.4 135.3 %all-gather.3.cloned.1.call-start = ((), (), s32[]{:S(2)}) async-start(), calls=%async_computation.2 | async-start | bytes 1081344 | tf_op jit(solution)/shard_map/all_gather | solution.py:203
  29.1 90.2 %copy-start.14 = (f32[64,128]{1,0:T(8,128)}, f32[64,128]{1,0:T(8,128)S(1)}, u32[]{:S(2)}) copy-start(f32[64,128]{1,0:T(8,128)S(1)} %get-tuple-element.114) | copy-start | bytes 98308
  29.7 79.8 %collective-permute-start.5 = (f32[2,2,128]{2,1,0:T(2,128)}, f32[2,2,128]{2,1,0:T(2,128)S(1)}, u32[]{:S(2)}, u32[]{:S(2)}) collective-permute-start(f32[2,2,128]{2,1,0:T(2,128)} %get-tuple-element.112), channel_id=1, source_target_pairs={{4,0},{8,4},{12,8},{16,12},{20,16},{24,20},{28,24},{5,1},{9,5},{13... | collective-permute-start | bytes 6152 | tf_op jit(solution)/shard_map/ppermute | solution.py:127
  31.9 77.6 %collective-permute-start.4 = (f32[2,2,128]{2,1,0:T(2,128)}, f32[2,2,128]{2,1,0:T(2,128)S(1)}, u32[]{:S(2)}, u32[]{:S(2)}) collective-permute-start(f32[2,2,128]{2,1,0:T(2,128)} %get-tuple-element.111), channel_id=1, source_target_pairs={{0,4},{4,8},{8,12},{12,16},{16,20},{20,24},{24,28},{1,5},{5,9},{9,... | collective-permute-start | bytes 6152 | tf_op jit(solution)/shard_map/ppermute | solution.py:126
  109.6 6.0 %collective-permute-start.7 = (f32[2,68,2]{2,1,0:T(8,128)S(1)}, f32[2,68,2]{2,1,0:T(8,128)S(1)}, u32[]{:S(2)}, u32[]{:S(2)}) collective-permute-start(f32[2,68,2]{2,1,0:T(8,128)S(1)} %get-tuple-element.110), channel_id=1, source_target_pairs={{1,0},{2,1},{3,2},{5,4},{6,5},{7,6},{9,8},{10,9},{11,10},{13,12},{... | collective-permute-start | bytes 3272 | tf_op jit(solution)/shard_map/ppermute | solution.py:127
  110.9 5.4 %collective-permute-start.6 = (f32[2,68,2]{2,1,0:T(8,128)S(1)}, f32[2,68,2]{2,1,0:T(8,128)S(1)}, u32[]{:S(2)}, u32[]{:S(2)}) collective-permute-start(f32[2,68,2]{2,1,0:T(8,128)S(1)} %get-tuple-element.109), channel_id=1, source_target_pairs={{0,1},{1,2},{2,3},{4,5},{5,6},{6,7},{8,9},{9,10},{10,11},{12,13},{... | collective-permute-start | bytes 3272 | tf_op jit(solution)/shard_map/ppermute | solution.py:126
  123.8 11.5 %collective-permute-start.1 = (f32[2,16,2,128]{3,2,0,1:T(2,128)S(1)}, f32[2,16,2,128]{3,2,0,1:T(2,128)S(1)}, u32[]{:S(2)}, u32[]{:S(2)}) collective-permute-start(f32[2,16,2,128]{3,2,0,1:T(2,128)S(1)} %get-tuple-element.68), channel_id=1, source_target_pairs={{4,0},{8,4},{12,8},{16,12},{20,16},{24,20},{28,24},{5,1},{9,5},{13... | collective-permute-start | bytes 98312 | tf_op jit(solution)/shard_map/ppermute | solution.py:127
  132.2 3.1 %collective-permute-start = (f32[2,16,2,128]{3,2,0,1:T(2,128)S(1)}, f32[2,16,2,128]{3,2,0,1:T(2,128)S(1)}, u32[]{:S(2)}, u32[]{:S(2)}) collective-permute-start(f32[2,16,2,128]{3,2,0,1:T(2,128)S(1)} %get-tuple-element.67), channel_id=1, source_target_pairs={{0,4},{4,8},{8,12},{12,16},{16,20},{20,24},{24,28},{1,5},{5,9},{9,... | collective-permute-start | bytes 98312 | tf_op jit(solution)/shard_map/ppermute | solution.py:126
  136.9 7.5 %collective-permute-start.2 = (f32[2,16,68,2]{2,1,3,0:T(8,128)}, f32[2,16,68,2]{2,1,3,0:T(8,128)S(1)}, u32[]{:S(2)}, u32[]{:S(2)}) collective-permute-start(f32[2,16,68,2]{2,1,3,0:T(8,128)} %copy.92), channel_id=1, source_target_pairs={{0,1},{1,2},{2,3},{4,5},{5,6},{6,7},{8,9},{9,10},{10,11},{12,13},{... | collective-permute-start | bytes 52232 | tf_op jit(solution)/shard_map/ppermute | solution.py:126
  141.3 4.8 %collective-permute-start.3 = (f32[2,16,68,2]{2,1,3,0:T(8,128)S(1)}, f32[2,16,68,2]{2,1,3,0:T(8,128)}, u32[]{:S(2)}, u32[]{:S(2)}) collective-permute-start(f32[2,16,68,2]{2,1,3,0:T(8,128)S(1)} %copy.93), channel_id=1, source_target_pairs={{1,0},{2,1},{3,2},{5,4},{6,5},{7,6},{9,8},{10,9},{11,10},{13,12},{... | collective-permute-start | bytes 52232 | tf_op jit(solution)/shard_map/ppermute | solution.py:127
  148.6 3.2 %copy-start.21 = (f32[64,128]{1,0:T(8,128)S(1)}, f32[64,128]{1,0:T(8,128)}, u32[]{:S(2)}) copy-start(f32[64,128]{1,0:T(8,128)} %get-tuple-element.97) | copy-start | bytes 98308
  148.6 3.2 %copy-start.22 = (f32[64,128]{1,0:T(8,128)S(1)}, f32[64,128]{1,0:T(8,128)}, u32[]{:S(2)}) copy-start(f32[64,128]{1,0:T(8,128)} %get-tuple-element.98) | copy-start | bytes 98308
  148.6 3.2 %copy-start.23 = (f32[64,128]{1,0:T(8,128)S(1)}, f32[64,128]{1,0:T(8,128)}, u32[]{:S(2)}) copy-start(f32[64,128]{1,0:T(8,128)} %get-tuple-element.99) | copy-start | bytes 98308
  148.6 3.2 %copy-start.24 = (f32[64,128]{1,0:T(8,128)S(1)}, f32[64,128]{1,0:T(8,128)}, u32[]{:S(2)}) copy-start(f32[64,128]{1,0:T(8,128)} %get-tuple-element.100) | copy-start | bytes 98308
  153.2 8.8 %copy-start.5 = (s32[256,1]{0,1:T(1,128)S(1)}, s32[256,1]{0,1:T(1,128)}, u32[]{:S(2)}) copy-start(s32[256,1]{0,1:T(1,128)} %param.14) | copy-start | bytes 3076
  153.2 8.8 %copy-start.7 = (s32[256]{0:T(256)S(1)}, s32[256]{0:T(256)}, u32[]{:S(2)}) copy-start(s32[256]{0:T(256)} %row_s.1) | copy-start | bytes 3076
  155.9 32.5 %all-to-all-start.1 = ((f32[512,4,128]{2,1,0:T(4,128)}), f32[512,4,128]{2,1,0:T(4,128)S(1)}, u32[]{:S(2)}, u32[]{:S(2)}) async-start(f32[512,4,128]{2,1,0:T(4,128)} %gather_fusion), calls=%async_computation.1 | async-start | bytes 2097152 | tf_op jit(solution)/shard_map/all_to_all | solution.py:228
  162.1 26.2 %copy-start.9 = (s32[256]{0:T(256)S(1)}, s32[256]{0:T(256)}, u32[]{:S(2)}) copy-start(s32[256]{0:T(256)} %block_s.3) | copy-start | bytes 3076
  162.2 26.2 %copy-start.11 = (s32[256]{0:T(256)S(1)}, s32[256]{0:T(256)}, u32[]{:S(2)}) copy-start(s32[256]{0:T(256)} %tile_s.3) | copy-start | bytes 3076
  (22 other events, 22.0 us)
Sparse Core Ops, SparseCore 0:
  32.2 55.7 all-gather.2

commit v2 on v1

v2 whole, which is shorter than its diff:
```python
import functools

import jax
import jax.numpy as jnp
from jax import lax
from jax.experimental import pallas as pl
from jax.experimental.pallas import tpu as pltpu
from jax.sharding import PartitionSpec as P

F32 = jnp.float32
BF16 = jnp.bfloat16
I32 = jnp.int32
VMEM = pltpu.VMEM
SMEM = pltpu.SMEM
LANES = 128
EDGE = 16
HALO = 8


def iota(shape, dim):
    return lax.broadcasted_iota(I32, shape, dim)


def pick(mask, value):
    return jnp.where(mask, value, 0.0)


def split(value):
    high = value.astype(BF16)
    return high, (value - high.astype(F32)).astype(BF16)


def back_rows(capacity):
    return 4 * capacity + max(8, capacity)


def remap_out_kernel(
    capacity, grid_y, tile_rows, block_h, owner_h, row_h, tile_h, atm_h, weights_h,
    out, field_o, wet_o, block_s, owner_s, row_s, tile_s, atm, weights, flux, fill, rows_acc, cols_acc, sems,
):
    devices = fill.shape[0]
    npairs = block_s.shape[0]
    nblocks = flux.shape[0]
    message = 4 * capacity + EDGE
    copies = [
        pltpu.make_async_copy(src, dst, sems.at[n])
        for n, (src, dst) in enumerate(
            [(atm_h, atm), (block_h, block_s), (owner_h, owner_s), (row_h, row_s), (tile_h, tile_s), (weights_h, weights)]
        )
    ]
    for copy in copies:
        copy.start()
    out[...] = jnp.zeros_like(out)
    rows_acc[...] = jnp.zeros_like(rows_acc)
    cols_acc[...] = jnp.zeros_like(cols_acc)

    def clear_fill(i, carry):
        fill[i] = 0
        return carry

    lax.fori_loop(0, devices, clear_fill, 0, unroll=16)
    copies[0].wait()
    wind_u = atm[0:1, :]
    wind_v = atm[1:2, :]
    speed = jnp.sqrt(wind_u * wind_u + wind_v * wind_v + 0.25)
    heat = 0.5 * speed * (atm[2:3, :] - atm[5:6, :])
    water = atm[4:5, :] - 0.3 * speed * atm[3:4, :]
    planes = jnp.concatenate(
        [heat, water, 0.2 * speed * wind_u, 0.2 * speed * wind_v, jnp.zeros((4, wind_u.shape[1]), F32)]
        + [heat] * 4
        + [water] * 4,
        0,
    ).astype(BF16)
    for b in range(nblocks):
        flux[b] = planes[:, b * LANES : (b + 1) * LANES]
    for copy in copies[1:]:
        copy.wait()

    sub = iota((8, LANES), 0)
    lane = iota((8, LANES), 1)
    part = sub % 4
    edge_row = jnp.where(part == 0, 0, jnp.where(part == 1, 1, tile_rows - 4 + part))
    edge_col = lane == jnp.where(part == 0, 0, jnp.where(part == 1, 1, LANES - 4 + part))
    col_lane = lane - 64 * (sub // 4)
    id_rank = jnp.where((sub == 0) & (lane >= 64), (lane - 64) // 4, -1)

    def pair(p, carry):
        owner = owner_s[p]
        row = row_s[p]
        rank = fill[owner]
        fill[owner] = rank + 1
        field_o[p] = owner * back_rows(capacity) + 4 * rank
        wet_o[p] = owner * back_rows(capacity) + 4 * capacity + rank
        value = jnp.dot(flux[block_s[p]], weights[tile_s[p]], preferred_element_type=F32)
        out[pl.ds(owner * message + 4 * rank, 4), :] = value[0:4]
        tracer = value[8:16]
        rows_acc[owner] = rows_acc[owner] + pick(edge_row == row, tracer)
        column = jnp.sum(pick(edge_col, tracer), axis=1, keepdims=True)
        number = (row + 1).astype(F32)
        cols_acc[owner] = cols_acc[owner] + (
            pick(col_lane == row, column) + pick(id_rank == rank, number)
        )
        return carry

    lax.fori_loop(0, npairs, pair, 0, unroll=8)

    grid_x = devices // grid_y
    zero = jnp.zeros((8, LANES), F32)
    inside = ((sub < 4) & (lane < 64)) | (sub >= 4)

    def folded(d):
        kept = pick(inside, cols_acc[d])
        return kept + pltpu.roll(kept, 4, 0)

    folds = {}

    def fold(i, j):
        if not (0 <= i < grid_x and 0 <= j < grid_y):
            return zero
        return folds_ref(i * grid_y + j)

    def folds_ref(d):
        if d not in folds:
            folds[d] = folded(d)
        return folds[d]

    last = (lane == tile_rows - 1) | (lane == 64 + tile_rows - 1)
    first = (lane == 0) | (lane == 64)
    for d in range(devices):
        i, j = d // grid_y, d % grid_y
        below = rows_acc[d + grid_y] if i < grid_x - 1 else zero
        above = rows_acc[d - grid_y] if i > 0 else zero
        base = d * message + 4 * capacity
        out[base : base + 8, :] = jnp.where(part < 2, below, above)
        if i > 1:
            folds.pop(d - 2 * grid_y, None)
        right, left = fold(i, j + 1), fold(i, j - 1)
        tile = pick(sub < 2, right) + pick((sub == 2) | (sub == 3), left)
        tile = tile + pick((sub == 4) & last, fold(i - 1, j + 1)) + pick((sub == 4) & first, fold(i + 1, j + 1))
        tile = tile + pick((sub == 7) & last, fold(i - 1, j - 1)) + pick((sub == 7) & first, fold(i + 1, j - 1))
        numbers = pltpu.roll(cols_acc[d], 5, 0)
        tile = tile + pick((sub == 5) & (lane >= 64), numbers)
        out[base + 8 : base + 16, :] = tile


def remap_out(capacity, grid_y, devices, tile_rows, atm_state, pair_block, owner, pair_row, pair_tile, remap_weight):
    npairs = pair_block.shape[0]
    nblocks = atm_state.shape[1] // LANES
    message = 4 * capacity + EDGE
    vmem = pl.BlockSpec(memory_space=VMEM)
    smem = pl.BlockSpec(memory_space=SMEM)
    return pl.pallas_call(
        functools.partial(remap_out_kernel, capacity, grid_y, tile_rows),
        out_shape=(
            jax.ShapeDtypeStruct((devices * message, LANES), F32),
            jax.ShapeDtypeStruct((npairs,), I32),
            jax.ShapeDtypeStruct((npairs,), I32),
        ),
        in_specs=[pl.BlockSpec(memory_space=pl.ANY)] * 6,
        out_specs=(vmem, smem, smem),
        scratch_shapes=[pltpu.SMEM((npairs,), I32)] * 4
        + [
            pltpu.VMEM(atm_state.shape, F32),
            pltpu.VMEM(remap_weight.shape, BF16),
            pltpu.VMEM((nblocks, 16, LANES), BF16),
            pltpu.SMEM((devices,), I32),
            pltpu.VMEM((devices, 8, LANES), F32),
            pltpu.VMEM((devices, 8, LANES), F32),
            pltpu.SemaphoreType.DMA((6,)),
        ],
        compiler_params=pltpu.CompilerParams(vmem_limit_bytes=24 << 20),
        cost_estimate=pl.CostEstimate(flops=2 * npairs * 16 * LANES * LANES, bytes_accessed=6 << 20, transcendentals=0),
    )(pair_block, owner, pair_row, pair_tile, atm_state, remap_weight)


def solve_kernel(state, kappa, horiz, wet, tracer, currents, edge_up, edge_down):
    levels = kappa.shape[0]
    rows_all = kappa.shape[1]
    planes = tracer.shape[0]

    def chunk(c, carry):
        rows = pl.ds(pl.multiple_of(c * 8, 8), 8)
        column = [kappa[l, rows, :] for l in range(levels)]
        face = [0.5 * (column[l] + column[l + 1]) for l in range(levels - 1)]
        upper = []
        now = None
        for l in range(levels):
            diagonal = 1.0
            if l > 0:
                diagonal = diagonal + face[l - 1]
            if l < levels - 1:
                diagonal = diagonal + face[l]
            if l > 0:
                diagonal = diagonal + face[l - 1] * upper[-1]
            inverse = 1.0 / diagonal
            if l == 0:
                now = [state[f, 0, rows, :] * inverse for f in range(4)] + [inverse]
            else:
                pull = face[l - 1] * inverse
                now = [state[f, l, rows, :] * inverse + pull * now[f] for f in range(4)] + [pull * now[4]]
            upper.append(-face[l] * inverse if l < levels - 1 else None)
            store(l, rows, now)
        for l in range(levels - 2, -1, -1):
            here = load(l, rows)
            now = [here[f] - upper[l] * now[f] for f in range(5)]
            store(l, rows, now)
        return carry

    def store(l, rows, now):
        tracer[l, rows, :] = now[0]
        tracer[levels + l, rows, :] = now[1]
        currents[0, l, rows, :] = now[2]
        currents[1, l, rows, :] = now[3]
        tracer[2 * levels + l, rows, :] = now[4]

    def load(l, rows):
        return [
            tracer[l, rows, :],
            tracer[levels + l, rows, :],
            currents[0, l, rows, :],
            currents[1, l, rows, :],
            tracer[2 * levels + l, rows, :],
        ]

    lax.fori_loop(0, rows_all // 8, chunk, 0)
    tracer[3 * levels] = horiz[...]
    tracer[3 * levels + 1] = wet[...].astype(F32)
    for k in range(planes):
        edge_up[k] = tracer[k, 0:8, :]
        edge_down[k] = tracer[k, rows_all - 8 : rows_all, :]


def solve(ocean_state, vert_kappa, horiz_kappa, wet_mask):
    levels, rows, _ = vert_kappa.shape
    planes = 3 * levels + 2
    vmem = pl.BlockSpec(memory_space=VMEM)
    return pl.pallas_call(
        solve_kernel,
        out_shape=(
            jax.ShapeDtypeStruct((planes, rows, LANES), F32),
            jax.ShapeDtypeStruct((2, levels, rows, LANES), F32),
            jax.ShapeDtypeStruct((planes, 8, LANES), F32),
            jax.ShapeDtypeStruct((planes, 8, LANES), F32),
        ),
        in_specs=[vmem] * 4,
        out_specs=(vmem,) * 4,
        compiler_params=pltpu.CompilerParams(vmem_limit_bytes=24 << 20),
        cost_estimate=pl.CostEstimate(flops=20 << 20, bytes_accessed=6 << 20, transcendentals=0),
    )(ocean_state, vert_kappa, horiz_kappa, wet_mask)


def pack_kernel(levels, tracer, above, below, wide, to_left, to_right):
    planes, rows, _ = tracer.shape
    for k in range(planes):
        wide[k, 0:HALO, :] = above[k]
        wide[k, HALO : HALO + rows, :] = tracer[k]
        wide[k, HALO + rows : 2 * HALO + rows, :] = below[k]
    lane = iota((8, LANES), 1)

    def chunk(c, carry):
        at = pl.ds(pl.multiple_of(c * 8, 8), 8)

        def place(values, lanes):
            left = [jnp.zeros((8, LANES), F32)] * 1
            left, right = jnp.zeros((8, LANES), F32), jnp.zeros((8, LANES), F32)
            for k, (near, far) in zip(values, lanes):
                value = wide[k, at, :]
                left = jnp.where(lane == near, pltpu.roll(value, near, 1), left)
                left = jnp.where(lane == far, pltpu.roll(value, far - 1, 1), left)
                right = jnp.where(lane == near + 1, pltpu.roll(value, (near + 2) % LANES, 1), right)
                right = jnp.where(lane == far + 1, pltpu.roll(value, (far + 3) % LANES, 1), right)
            return left, right

        left, right = place(range(2 * levels), [(2 * k, 64 + 2 * k) for k in range(2 * levels)])
        to_left[0, at, :] = left
        to_right[0, at, :] = right
        lanes = [(2 * l, 64 + 2 * l) for l in range(levels)]
        lanes += [(2 * levels, 2 * levels + 2), (2 * levels + 4, 2 * levels + 6)]
        left, right = place(range(2 * levels, 3 * levels + 2), lanes)
        to_left[1, at, :] = left
        to_right[1, at, :] = right
        return carry

    lax.fori_loop(0, (rows + 2 * HALO) // 8, chunk, 0)


def pack(levels, tracer, above, below):
    planes, rows, _ = tracer.shape
    tall = rows + 2 * HALO
    vmem = pl.BlockSpec(memory_space=VMEM)
    return pl.pallas_call(
        functools.partial(pack_kernel, levels),
        out_shape=(
            jax.ShapeDtypeStruct((planes, tall, LANES), F32),
            jax.ShapeDtypeStruct((2, tall, LANES), F32),
            jax.ShapeDtypeStruct((2, tall, LANES), F32),
        ),
        in_specs=[vmem] * 3,
        out_specs=(vmem,) * 3,
        compiler_params=pltpu.CompilerParams(vmem_limit_bytes=24 << 20),
        cost_estimate=pl.CostEstimate(flops=8 << 20, bytes_accessed=4 << 20, transcendentals=0),
    )(tracer, above, below)


def faces_kernel(levels, horiz, wet, own_left, own_right, from_left, from_right, faces, packed):
    tall = horiz.shape[0]
    lane = iota((tall, LANES), 1)
    odd = lane % 2 == 1
    twice = lane % 64 < 2 * levels
    tracer = jnp.where(odd, from_left[0], from_right[0])
    other = jnp.where(odd, from_left[1], from_right[1])
    at = 2 * levels

    def column(offset):
        return other[:, at + offset : at + offset + 1], other[:, at + offset + 1 : at + offset + 2]

    kappa_right, kappa_left = column(0)
    kappa_far_right, kappa_far_left = column(2)
    wet_right, wet_left = column(4)
    wet_far_right, wet_far_left = column(6)
    h = horiz[...]
    w = wet[...]

    kappa_near = jnp.where(odd, kappa_left, kappa_right)
    kappa_far = jnp.where(odd, kappa_far_left, kappa_far_right)
    wet_near = jnp.where(odd, wet_left, wet_right)
    wet_far = jnp.where(odd, wet_far_left, wet_far_right)
    kappa_own = jnp.where(odd, h[:, 0:1], h[:, LANES - 1 : LANES])
    wet_own = jnp.where(odd, w[:, 0:1], w[:, LANES - 1 : LANES])

    def face(kappa_a, wet_a, kappa_b, wet_b):
        return 0.25 * (kappa_a + kappa_b) * wet_a * wet_b

    unit = jnp.where(twice, other, pltpu.roll(other, 2 * levels, 1))
    packed[0] = tracer
    packed[1] = unit * jnp.where(lane < 64, wet_near, wet_far)
    packed[2] = jnp.where(odd, pltpu.roll(own_left[0], 1, 1), pltpu.roll(own_right[0], LANES - 1, 1))
    own = jnp.where(odd, pltpu.roll(own_left[1], 1, 1), pltpu.roll(own_right[1], LANES - 1, 1))
    packed[3] = jnp.where(twice, own, pltpu.roll(own, 2 * levels, 1)) * wet_own
    north = face(kappa_near, wet_near, pltpu.roll(kappa_near, 1, 0), pltpu.roll(wet_near, 1, 0))
    packed[4] = north
    packed[5] = pltpu.roll(north, tall - 1, 0)
    packed[6] = face(kappa_near, wet_near, kappa_far, wet_far)
    packed[7] = face(kappa_near, wet_near, kappa_own, wet_own)

    north = face(h, w, pltpu.roll(h, 1, 0), pltpu.roll(w, 1, 0))
    faces[0] = north
    faces[1] = pltpu.roll(north, tall - 1, 0)
    west = face(
        h, w, jnp.where(lane == 0, kappa_left, pltpu.roll(h, 1, 1)), jnp.where(lane == 0, wet_left, pltpu.roll(w, 1, 1))
    )
    faces[2] = west
    faces[3] = jnp.where(lane == LANES - 1, face(h, w, kappa_right, wet_right), pltpu.roll(west, LANES - 1, 1))


def face_values(levels, wide, own_left, own_right, from_left, from_right):
    tall = wide.shape[1]
    vmem = pl.BlockSpec(memory_space=VMEM)
    return pl.pallas_call(
        functools.partial(faces_kernel, levels),
        out_shape=(
            jax.ShapeDtypeStruct((4, tall, LANES), F32),
            jax.ShapeDtypeStruct((8, tall, LANES), F32),
        ),
        in_specs=[vmem] * 6,
        out_specs=(vmem,) * 2,
        cost_estimate=pl.CostEstimate(flops=1 << 20, bytes_accessed=1 << 20, transcendentals=0),
    )(wide[3 * levels], wide[3 * levels + 1], own_left, own_right, from_left, from_right)


def one_pass(value, faces, beside, shift):
    tall = value.shape[0]
    lane = iota(value.shape, 1)
    moved = pltpu.roll(beside, shift, 1)
    west = jnp.where(lane == 0, moved, pltpu.roll(value, 1, 1))
    east = jnp.where(lane == LANES - 1, moved, pltpu.roll(value, LANES - 1, 1))
    result = value + faces[1] * (pltpu.roll(value, tall - 1, 0) - value)
    result = result + faces[0] * (pltpu.roll(value, 1, 0) - value)
    result = result + faces[3] * (east - value)
    return result + faces[2] * (west - value)


def middle_kernel(
    capacity, levels, arrived, top, currents, wet_wide, faces, packed, sent, forcing, near_o,
    placing, values, number_t,
):
    devices, message, _ = arrived.shape
    rows_all = currents.shape[1]
    tall = rows_all + 2 * HALO
    span = 4 * capacity
    group = LANES // span
    groups = devices // group
    sub8 = iota((8, LANES), 0)
    lane8 = iota((8, LANES), 1)

    lane1 = iota((1, LANES), 1)
    numbers = []
    for m in range(groups):
        line = jnp.zeros((1, LANES), F32)
        for g in range(group):
            ids = arrived[m * group + g, span + 13 : span + 14, :]
            moved = pltpu.roll(ids, (g * span - 64) % LANES, 1)
            line = jnp.where(lane1 // span == g, moved, line)
        numbers.append(line)
    number_t[...] = jnp.transpose(
        jnp.concatenate(numbers + [jnp.zeros((LANES - groups, LANES), F32)], 0)
    )

    row_number = iota((rows_all, LANES), 0).astype(F32) + 1.0
    lane_field = iota((rows_all, LANES), 1) % 4
    for m in range(groups):
        hit = numbers[m] == row_number
        for f in range(4):
            placing[f * rows_all : (f + 1) * rows_all, m * LANES : (m + 1) * LANES] = jnp.where(
                hit & (lane_field == f), 1.0, 0.0
            ).astype(BF16)
    edge_rows = jnp.zeros((8, LANES), F32)
    edge_cols = jnp.zeros((8, LANES), F32)
    for s in range(devices):
        high, low = split(arrived[s, 0:span, :])
        values[s * span : (s + 1) * span, 0:LANES] = high
        values[s * span : (s + 1) * span, LANES : 2 * LANES] = low
        edge_rows = edge_rows + arrived[s, span : span + 8, :]
        edge_cols = edge_cols + arrived[s, span + 8 : span + 16, :]
    total = jnp.dot(placing[...], values[...], preferred_element_type=F32)
    total = total[:, 0:LANES] + total[:, LANES : 2 * LANES]

    def plane(f):
        return total[f * rows_all : (f + 1) * rows_all]

    wide = []
    for f in range(2):
        before = pick(sub8 >= 6, edge_rows if f == 1 else pltpu.roll(edge_rows, 4, 0))
        after = pick(sub8 < 2, edge_rows if f == 0 else pltpu.roll(edge_rows, 4, 0))
        wide.append(jnp.concatenate([before, plane(f), after], 0))
        forcing[f] = wide[f]
    wet = wet_wide[HALO : HALO + rows_all, :]
    for f in range(2, 4):
        forcing[f, 0:HALO, :] = jnp.zeros((HALO, LANES), F32)
        forcing[f, HALO : HALO + rows_all, :] = plane(f) * wet
        forcing[f, HALO + rows_all : tall, :] = jnp.zeros((HALO, LANES), F32)

    corner = pick((sub8 == 0) | (sub8 == 3), pltpu.roll(edge_cols, 4, 0))
    side = pick(sub8 < 4, edge_cols)
    within = (lane8 >= HALO) & (lane8 < HALO + rows_all)
    ends = (lane8 == HALO - 1) | (lane8 == HALO + rows_all)
    halves = []
    for f in range(2):
        body = pltpu.roll(side, (HALO - 64 * f) % LANES, 1)
        tips = pltpu.roll(corner, (HALO + rows_all - 64 * f) % LANES, 1)
        halves.append((pick(within, body) + pick(ends, tips))[0:4])
    columns = jnp.concatenate(halves, 0)
    upright = jnp.transpose(jnp.concatenate([columns, jnp.zeros((LANES - 8, LANES), F32)], 0))[0:tall]
    lane = iota((tall, LANES), 1)
    odd = lane % 2 == 1
    heat = lane % 64 < 2 * levels
    close = lane < 64

    def chosen(right_near, left_near, right_far, left_far):
        near = jnp.where(odd, left_near, right_near)
        far = jnp.where(odd, left_far, right_far)
        return jnp.where(close, near, far)

    def of_field(f):
        return [upright[:, 4 * f + e : 4 * f + e + 1] for e in (0, 3, 1, 2)]

    beside = jnp.where(heat, chosen(*of_field(0)), chosen(*of_field(1)))
    both = packed[0] + packed[1] * beside
    far = pltpu.roll(both, 64, 1)
    ends_of = [jnp.where(odd, w[:, 0:1], w[:, LANES - 1 : LANES]) for w in wide]
    own = packed[2] + packed[3] * jnp.where(heat, ends_of[0], ends_of[1])
    near = both + packed[5] * (pltpu.roll(both, tall - 1, 0) - both)
    near = near + packed[4] * (pltpu.roll(both, 1, 0) - both)
    near = near + packed[6] * (far - both)
    near = near + packed[7] * (own - both)
    near_o[0] = both
    near_o[1] = near

    surface = []
    unit = top[2] * wet_wide[...]
    for f in range(2):
        value = top[f] + unit * wide[f]
        shift = LANES - (2 * levels * f + 1)
        value = one_pass(value, faces, both, shift)
        value = one_pass(value, faces, near, shift)
        surface.append(value[HALO : HALO + rows_all] * wet)
    for f in range(2):
        surface.append(
            (currents[f] + top[2, HALO : HALO + rows_all, :] * forcing[2 + f, HALO : HALO + rows_all, :]) * wet
        )
    high, low = split(jnp.concatenate(surface, 0))
    source = jnp.concatenate([high, low], 1)
    lane_t = iota((LANES, 4 * rows_all), 1)
    sub_t = iota((LANES, 4 * rows_all), 0)
    target = jnp.where(sub_t % 4 == lane_t // rows_all, lane_t % rows_all + 1, -1).astype(F32)
    mask = jnp.concatenate([wet, jnp.zeros((LANES - rows_all, LANES), F32)], 0).astype(BF16)
    per = LANES // 4
    slot_number = number_t[pl.ds(0, per, stride=4), :]
    lane_s = (iota((per, LANES), 1) + 1).astype(F32)
    height = back_rows(capacity)
    for m in range(groups):
        chosen_rows = jnp.where(number_t[:, m : m + 1] == target, 1.0, 0.0).astype(BF16)
        rows = jnp.dot(chosen_rows, source, preferred_element_type=F32)
        rows = rows[:, 0:LANES] + rows[:, LANES : 2 * LANES]
        slots = jnp.where(slot_number[:, m : m + 1] == lane_s, 1.0, 0.0).astype(BF16)
        masks = jnp.dot(slots, mask, preferred_element_type=F32)
        for g in range(group):
            s = m * group + g
            sent[s, 0:span, :] = rows[g * span : (g + 1) * span]
            sent[s, span : span + capacity, :] = masks[g * capacity : (g + 1) * capacity]
            if height > span + capacity:
                sent[s, span + capacity : height, :] = jnp.zeros((height - span - capacity, LANES), F32)


def middle(capacity, levels, arrived, top, currents, wet_wide, faces, packed):
    devices = arrived.shape[0]
    rows = currents.shape[1]
    tall = rows + 2 * HALO
    vmem = pl.BlockSpec(memory_space=VMEM)
    return pl.pallas_call(
        functools.partial(middle_kernel, capacity, levels),
        out_shape=(
            jax.ShapeDtypeStruct((devices, back_rows(capacity), LANES), F32),
            jax.ShapeDtypeStruct((4, tall, LANES), F32),
            jax.ShapeDtypeStruct((2, tall, LANES), F32),
        ),
        in_specs=[vmem] * 6,
        out_specs=(vmem,) * 3,
        scratch_shapes=[
            pltpu.VMEM((4 * rows, 4 * capacity * devices), BF16),
            pltpu.VMEM((4 * capacity * devices, 2 * LANES), BF16),
            pltpu.VMEM((LANES, LANES), F32),
        ],
        compiler_params=pltpu.CompilerParams(vmem_limit_bytes=24 << 20),
        cost_estimate=pl.CostEstimate(flops=200 << 20, bytes_accessed=4 << 20, transcendentals=0),
    )(arrived, top, currents, wet_wide, faces, packed)


def finish_kernel(levels, wide, currents, faces, forcing, near, ocean):
    rows_all = currents.shape[2]
    inner = slice(HALO, HALO + rows_all)

    def level(l, carry):
        unit = wide[2 * levels + l]
        masked = unit * wide[3 * levels + 1]
        for f in range(2):
            value = wide[f * levels + l] + masked * forcing[f]
            shift = LANES - 1 - 2 * (levels * f + l)
            value = one_pass(value, faces, near[0], shift)
            value = one_pass(value, faces, near[1], shift)
            ocean[f, l] = value[inner]
            ocean[2 + f, l] = currents[f, l] + unit[inner] * forcing[2 + f][inner]
        return carry

    lax.fori_loop(0, levels, level, 0)


def finish(levels, wide, currents, faces, forcing, near):
    rows = currents.shape[2]
    vmem = pl.BlockSpec(memory_space=VMEM)
    return pl.pallas_call(
        functools.partial(finish_kernel, levels),
        out_shape=jax.ShapeDtypeStruct((4, levels, rows, LANES), F32),
        in_specs=[vmem] * 5,
        out_specs=vmem,
        compiler_params=pltpu.CompilerParams(vmem_limit_bytes=24 << 20),
        cost_estimate=pl.CostEstimate(flops=40 << 20, bytes_accessed=6 << 20, transcendentals=0),
    )(wide, currents, faces, forcing, near)


def remap_back_kernel(block_h, tile_h, field_h, wet_h, returned, weights, out, block_s, tile_s, field_s, wet_s, total, sems):
    npairs = block_s.shape[0]
    nblocks = total.shape[0]
    copies = [
        pltpu.make_async_copy(src, dst, sems.at[n])
        for n, (src, dst) in enumerate([(block_h, block_s), (tile_h, tile_s), (field_h, field_s), (wet_h, wet_s)])
    ]
    for copy in copies:
        copy.start()
    total[...] = jnp.zeros_like(total)
    for copy in copies:
        copy.wait()

    def pair(p, carry):
        rows = returned[pl.ds(field_s[p], 4), :]
        mask = returned[pl.ds(wet_s[p], 1), :]
        full = jnp.concatenate([rows, mask, jnp.zeros((3, LANES), F32)], 0)
        high, low = split(full)
        value = lax.dot_general(
            jnp.concatenate([high, low], 0),
            weights[tile_s[p]],
            (((1,), (1,)), ((), ())),
            preferred_element_type=F32,
        )
        b = block_s[p]
        total[b] = total[b] + (value[0:8] + value[8:16])
        return carry

    lax.fori_loop(0, npairs, pair, 0, unroll=8)
    for b in range(nblocks):
        sums = total[b]
        out[:, b * LANES : (b + 1) * LANES] = sums[0:4] / jnp.maximum(sums[4:5], 0.1)


def remap_back(pair_block, pair_tile, field_at, wet_at, returned, remap_weight, nblocks):
    npairs = pair_block.shape[0]
    vmem = pl.BlockSpec(memory_space=VMEM)
    return pl.pallas_call(
        remap_back_kernel,
        out_shape=jax.ShapeDtypeStruct((4, nblocks * LANES), F32),
        in_specs=[pl.BlockSpec(memory_space=pl.ANY)] * 4 + [vmem] * 2,
        out_specs=vmem,
        scratch_shapes=[pltpu.SMEM((npairs,), I32)] * 4
        + [pltpu.VMEM((nblocks, 8, LANES), F32), pltpu.SemaphoreType.DMA((4,))],
        compiler_params=pltpu.CompilerParams(vmem_limit_bytes=24 << 20),
        cost_estimate=pl.CostEstimate(flops=2 * npairs * 16 * LANES * LANES, bytes_accessed=6 << 20, transcendentals=0),
    )(pair_block, pair_tile, field_at, wet_at, returned, remap_weight)


def local(
    atm_state,
    pair_block,
    pair_owner,
    pair_row,
    pair_tile,
    remap_weight,
    wet_mask,
    ocean_state,
    vert_kappa,
    horiz_kappa,
):
    grid_x = lax.axis_size("gx")
    grid_y = lax.axis_size("gy")
    devices = grid_x * grid_y
    npairs = pair_block.shape[0]
    capacity = max(2, 2 * npairs // devices)
    levels, tile_rows, _ = vert_kappa.shape
    nblocks = atm_state.shape[1] // LANES
    owner = pair_owner.reshape(npairs)
    message = 4 * capacity + EDGE
    outgoing, field_at, wet_at = remap_out(
        capacity, grid_y, devices, tile_rows, atm_state, pair_block, owner, pair_row, pair_tile, remap_weight
    )
    arrived = lax.all_to_all(
        outgoing.reshape(devices, message, LANES), ("gx", "gy"), split_axis=0, concat_axis=0, tiled=True
    )
    tracer, currents, edge_up, edge_down = solve(ocean_state, vert_kappa, horiz_kappa, wet_mask)
    rise_x = [(i, i + 1) for i in range(grid_x - 1)]
    fall_x = [(b, a) for a, b in rise_x]
    rise_y = [(i, i + 1) for i in range(grid_y - 1)]
    fall_y = [(b, a) for a, b in rise_y]
    above = lax.ppermute(edge_down, "gx", rise_x)
    below = lax.ppermute(edge_up, "gx", fall_x)
    wide, to_left, to_right = pack(levels, tracer, above, below)
    from_left = lax.ppermute(to_right, "gy", rise_y)
    from_right = lax.ppermute(to_left, "gy", fall_y)
    faces, packed = face_values(levels, wide, to_left, to_right, from_left, from_right)
    top = jnp.stack([wide[0], wide[levels], wide[2 * levels]])
    sent, forcing, near = middle(
        capacity, levels, arrived, top, currents[:, 0], wide[3 * levels + 1], faces, packed
    )
    returned = lax.all_to_all(sent, ("gx", "gy"), split_axis=0, concat_axis=0, tiled=True)
    ocean_next = finish(levels, wide, currents, faces, forcing, near)
    atm_surface = remap_back(
        pair_block, pair_tile, field_at, wet_at, returned.reshape(-1, LANES), remap_weight, nblocks
    )
    return (ocean_next, atm_surface)


def solution(mesh):
    placed = (
        P(None, ("gx", "gy")),
        P(("gx", "gy")),
        P(("gx", "gy"), None),
        P(("gx", "gy")),
        P(("gx", "gy")),
        P(("gx", "gy"), None, None),
        P("gx", "gy"),
        P(None, None, "gx", "gy"),
        P(None, "gx", "gy"),
        P("gx", "gy"),
    )
    return jax.shard_map(
        local,
        mesh=mesh,
        in_specs=placed,
        out_specs=(P(None, None, "gx", "gy"), P(None, ("gx", "gy"))),
        check_vma=False,
    )
```

time: 209 us -> 118 us (0.56)
  blocking collectives: 72.1 us -> 0 us
  starting transfers between devices: 39.7 us -> 24.1 us
  Pallas kernels: 17.7 us -> 33 us
  between operations: 14.8 us -> 0.82 us
  other arithmetic: 12.8 us -> 0.66 us
  waiting for transfers between devices: 27.2 us -> 35.3 us
  matrix products: 2.75 us -> 0 us
    all_gather x1 -> x0, blocking collectives: 72.1 us -> none  [local(): rows_all = lax.all_gather(out_rows, ('gx', 'gy'), axis=0, tiled=True)]
    ppermute x8 -> x4, starting transfers between devices: 26.5 us -> 9.75 us  [the longest x1 3.54 us: local(): above = lax.ppermute(edge_down, 'gx', rise_x)]
    pallas_call x1 -> x6, Pallas kernels: 8.2 us -> 23.5 us  [the longest x1 9.93 us: remap_out(): pl.pallas_call(functools.partial(remap_out_kernel, capacity, grid_y, tile...]
    unnamed x79 -> x62, local copies, waits for them, and re-layouts: 11.4 us -> 21.6 us
    ppermute x8 -> x4, waiting for transfers between devices: 1.87 us -> 11.3 us  [the longest x1 7.26 us: local(): below = lax.ppermute(edge_up, 'gx', fall_x)]
    mul x13 -> x0, other arithmetic: 4.37 us -> none  [the longest x2 2.72 us: diffuse(): 0.25 * (kappa_mid + shifted(kappa_pad, step_x, step_y)) * wet_mid]
    add x4 -> x0, other arithmetic: 4.37 us -> none  [the longest x2 4.32 us: diffuse(): result = result + face_coef * (shifted(padded, step_x, step_y) - centre)]
    dot_general x1 -> x0, matrix products: 2.75 us -> none  [local(): jnp.dot(placing, arrived.reshape(slot_count, 4 * 128), precision=highest,...]
  transfers between devices with their start and end apart: 11 -> 6, of which waited for: 4 -> 4; matrix products, arithmetic and copies ran while one was open for 13% -> 2% of each run, Pallas kernels for 0% -> 10%
where the time goes in v2:
time: 118 us; the launch traced here: 117 us
  waiting for transfers between devices  35.3 us (30%)
  Pallas kernels  33 us (28%)
  starting transfers between devices  24.1 us (20%)
  local copies, waits for them, and re-layouts  22.8 us (19%)
    all_to_all x1, waiting for transfers between devices, local(): lax.all_to_all(sent, ('gx', 'gy'), split_axis=0, concat_axis=0, tiled=True)  24 us
    unnamed x62, local copies, waits for them, and re-layouts  21.6 us
    pallas_call x1, Pallas kernels, remap_out(): pl.pallas_call(functools.partial(remap_out_kernel, capacity, grid_y, tile...  9.93 us
    pallas_call x1, Pallas kernels, remap_back(): pl.pallas_call(remap_back_kernel, out_shape=jax.ShapeDtypeStruct((4, nblo...  9.52 us
    ppermute x1, waiting for transfers between devices, local(): below = lax.ppermute(edge_up, 'gx', fall_x)  7.26 us
    all_to_all x1, starting transfers between devices, local(): lax.all_to_all(sent, ('gx', 'gy'), split_axis=0, concat_axis=0, tiled=True)  7.24 us
    all_to_all x1, starting transfers between devices, local(): lax.all_to_all(outgoing.reshape(devices, message, LANES), ('gx', 'gy'), s...  7.09 us
    pallas_call x1, Pallas kernels, finish(): pl.pallas_call(functools.partial(finish_kernel, levels), out_shape=jax.Sh...  4.86 us
  transfers between devices with their start and end apart: 6, of which 4 were waited for; matrix products, arithmetic and copies ran while one was open for 2% of the time, Pallas kernels for 10%

profile of v2, /device:TPU:1, one launch (start us, length us, event | category | flops | bytes accessed | tf_op | source)
XLA Modules:
  0.0 116.7 jit_solution(8576171907679013023)
XLA Ops:
  0.6 2.2 %copy-done = bf16[128,128,128]{2,1,0:T(8,128)(2,1)S(1)} copy-done((bf16[128,128,128]{2,1,0:T(8,128)(2,1)S(1)}, bf16[128,128,128]{2,1,0:T(8,128)(2,1)}, u32[]{:S(2)}) %copy-start) | copy-done | bytes 4194328
  6.5 9.9 %shard_map.116 = (f32[2560,128]{1,0:T(8,128)S(1)}, s32[256]{0:T(256)S(1)}, s32[256]{0:T(256)S(1)}) custom-call(s32[256]{0:T(256)S(1)} %copy-done.23, s32[256]{0:T(256)S(1)} %bitcast.11, s32[256]{0:T(256)S(1)} %copy-done.28, s32[256]{0:T(256)S(1)} %copy-done.25, f32[6,6144]{1,0:T(8,128)S(1)} %copy-done.14, bf16[128,128,128]{2,1,0:T(8,128)(2,1)S(1)} %copy-done), custom_call_target="tpu_custom_call" | custom-call | flops 134217728 | bytes 6291456 | tf_op jit(solution)/shard_map/pallas_call | solution.py:152
  16.4 1.0 copy-done.3
  17.5 7.1 %all-to-all-start = ((f32[32,80,128]{2,1,0:T(8,128)}), f32[32,80,128]{2,1,0:T(8,128)S(1)}, u32[]{:S(2)}, u32[]{:S(2)}) async-start(f32[32,80,128]{2,1,0:T(8,128)} %bitcast.10), calls=%async_computation | async-start | bytes 2621440 | tf_op jit(solution)/shard_map/all_to_all | solution.py:644
  24.6 1.0 copy-done.9
  25.6 1.7 %shard_map.113 = (f32[50,64,128]{2,1,0:T(8,128)S(1)}, f32[2,16,64,128]{3,2,1,0:T(8,128)S(1)}, f32[50,8,128]{2,1,0:T(8,128)S(1)}, f32[50,8,128]{2,1,0:T(8,128)S(1)}) custom-call(f32[4,16,64,128]{3,2,1,0:T(8,128)S(1)} %copy-done.2, f32[16,64,128]{2,1,0:T(8,128)S(1)} %copy-done.9, f32[64,128]{1,0:T(8,128)S(1)} %copy-done.21, s32[64,128]{1,0:T(8,128)S(1)} %copy-done.22), custom_call_target="tpu_custom_call" | custom-call | flops 20971520 | bytes 6291456 | tf_op jit(solution)/shard_map/pallas_call | solution.py:237
  27.4 3.5 %collective-permute-start = (f32[50,8,128]{2,1,0:T(8,128)S(1)}, f32[50,8,128]{2,1,0:T(8,128)S(1)}, u32[]{:S(2)}, u32[]{:S(2)}) collective-permute-start(f32[50,8,128]{2,1,0:T(8,128)S(1)} %get-tuple-element.18), channel_id=1, source_target_pairs={{0,4},{4,8},{8,12},{12,16},{16,20},{20,24},{24,28},{1,5},{5,9},{9,... | collective-permute-start | bytes 614408 | tf_op jit(solution)/shard_map/ppermute | solution.py:652
  30.9 1.9 %collective-permute-start.1 = (f32[50,8,128]{2,1,0:T(8,128)S(1)}, f32[50,8,128]{2,1,0:T(8,128)S(1)}, u32[]{:S(2)}, u32[]{:S(2)}) collective-permute-start(f32[50,8,128]{2,1,0:T(8,128)S(1)} %get-tuple-element.19), channel_id=1, source_target_pairs={{4,0},{8,4},{12,8},{16,12},{20,16},{24,20},{28,24},{5,1},{9,5},{13... | collective-permute-start | bytes 614408 | tf_op jit(solution)/shard_map/ppermute | solution.py:653
  33.5 1.0 copy-done.5
  34.7 7.3 %collective-permute-done.1.below = f32[50,8,128]{2,1,0:T(8,128)S(1)} collective-permute-done((f32[50,8,128]{2,1,0:T(8,128)S(1)}, f32[50,8,128]{2,1,0:T(8,128)S(1)}, u32[]{:S(2)}, u32[]{:S(2)}) %collective-permute-start.1) | collective-permute-done | bytes 204832 | tf_op jit(solution)/shard_map/ppermute | solution.py:653
  42.0 2.9 %shard_map.114 = (f32[50,80,128]{2,1,0:T(8,128)S(1)}, f32[2,80,128]{2,1,0:T(8,128)S(1)}, f32[2,80,128]{2,1,0:T(8,128)S(1)}) custom-call(f32[50,64,128]{2,1,0:T(8,128)S(1)} %get-tuple-element.17.tracer, f32[50,8,128]{2,1,0:T(8,128)S(1)} %collective-permute-done.above, f32[50,8,128]{2,1,0:T(8,128)S(1)} %collective-permute-done.1.below), custom_call_target="tpu_custom_call" | custom-call | flops 8388608 | bytes 4194304 | tf_op jit(solution)/shard_map/pallas_call | solution.py:291
  44.9 3.0 %collective-permute-start.2 = (f32[2,80,128]{2,1,0:T(8,128)S(1)}, f32[2,80,128]{2,1,0:T(8,128)S(1)}, u32[]{:S(2)}, u32[]{:S(2)}) collective-permute-start(f32[2,80,128]{2,1,0:T(8,128)S(1)} %get-tuple-element.23.own_right), channel_id=1, source_target_pairs={{0,1},{1,2},{2,3},{4,5},{5,6},{6,7},{8,9},{9,10},{10,11},{12,13},{... | collective-permute-start | bytes 245768 | tf_op jit(solution)/shard_map/ppermute | solution.py:655
  47.9 1.3 %collective-permute-start.3 = (f32[2,80,128]{2,1,0:T(8,128)S(1)}, f32[2,80,128]{2,1,0:T(8,128)S(1)}, u32[]{:S(2)}, u32[]{:S(2)}) collective-permute-start(f32[2,80,128]{2,1,0:T(8,128)S(1)} %get-tuple-element.22.own_left), channel_id=1, source_target_pairs={{1,0},{2,1},{3,2},{5,4},{6,5},{7,6},{9,8},{10,9},{11,10},{13,12},{... | collective-permute-start | bytes 245768 | tf_op jit(solution)/shard_map/ppermute | solution.py:656
  50.5 3.8 %collective-permute-done.3.from_right = f32[2,80,128]{2,1,0:T(8,128)S(1)} collective-permute-done((f32[2,80,128]{2,1,0:T(8,128)S(1)}, f32[2,80,128]{2,1,0:T(8,128)S(1)}, u32[]{:S(2)}, u32[]{:S(2)}) %collective-permute-start.3) | collective-permute-done | bytes 81952 | tf_op jit(solution)/shard_map/ppermute | solution.py:656
  54.9 2.2 %shard_map.115 = (f32[4,80,128]{2,1,0:T(8,128)}, f32[8,80,128]{2,1,0:T(8,128)}) custom-call(f32[80,128]{1,0:T(8,128)} %get-tuple-element.36.horiz, f32[80,128]{1,0:T(8,128)} %get-tuple-element.35.wet.wet_wide, f32[2,80,128]{2,1,0:T(8,128)} %copy-done.17, f32[2,80,128]{2,1,0:T(8,128)} %copy-done.18, f32[2,80,128]{2,1,0:T(8,128)} %copy-done.29, ...), custom_call_target="tpu_custom_call" | custom-call | flops 1048576 | bytes 1048576 | tf_op jit(solution)/shard_map/pallas_call | solution.py:359
  59.7 1.0 copy-done.12
  61.6 1.9 %shard_map.117 = (f32[32,80,128]{2,1,0:T(8,128)S(1)}, f32[4,80,128]{2,1,0:T(8,128)S(1)}, f32[2,80,128]{2,1,0:T(8,128)S(1)}) custom-call(f32[32,80,128]{2,1,0:T(8,128)S(1)} %all-to-all-done.arrived, f32[3,80,128]{2,1,0:T(8,128)S(1)} %copy-done.10, f32[2,64,128]{2,1,0:T(8,128)S(1)} %copy-done.13, f32[80,128]{1,0:T(8,128)S(1)} %copy-done.11, ...), custom_call_target="tpu_custom_call" | custom-call | flops 209715200 | bytes 4194304 | tf_op jit(solution)/shard_map/pallas_call | solution.py:520
  63.5 1.1 copy-done.4
  65.9 7.2 %all-to-all-start.1 = ((f32[32,80,128]{2,1,0:T(8,128)}), f32[32,80,128]{2,1,0:T(8,128)S(1)}, u32[]{:S(2)}, u32[]{:S(2)}) async-start(f32[32,80,128]{2,1,0:T(8,128)} %copy-done.4), calls=%async_computation.1 | async-start | bytes 2621440 | tf_op jit(solution)/shard_map/all_to_all | solution.py:662
  73.1 1.2 %copy-done.6 = f32[2,16,64,128]{3,2,1,0:T(8,128)S(1)} copy-done((f32[2,16,64,128]{3,2,1,0:T(8,128)S(1)}, f32[2,16,64,128]{3,2,1,0:T(8,128)}, u32[]{:S(2)}) %copy-start.6) | copy-done | bytes 1048600
  76.1 4.9 %shard_map.118 = f32[4,16,64,128]{3,2,1,0:T(8,128)} custom-call(f32[50,80,128]{2,1,0:T(8,128)S(1)} %get-tuple-element.20.wide, f32[2,16,64,128]{3,2,1,0:T(8,128)S(1)} %copy-done.6, f32[4,80,128]{2,1,0:T(8,128)S(1)} %copy-done.8, f32[4,80,128]{2,1,0:T(8,128)S(1)} %copy-done.16, f32[2,80,128]{2,1,0:T(8,128)S(1)} %copy-done.20), custom_call_target="tpu_custom_call" | custom-call | flops 41943040 | bytes 6291456 | tf_op jit(solution)/shard_map/pallas_call | solution.py:561
  81.0 24.0 %all-to-all-done.1 = f32[32,80,128]{2,1,0:T(8,128)S(1)} async-done(((f32[32,80,128]{2,1,0:T(8,128)}), f32[32,80,128]{2,1,0:T(8,128)S(1)}, u32[]{:S(2)}, u32[]{:S(2)}) %all-to-all-start.1) | async-done | bytes 1310752 | tf_op jit(solution)/shard_map/all_to_all | solution.py:662
  105.0 2.2 %copy-done.1 = bf16[128,128,128]{2,1,0:T(8,128)(2,1)S(1)} copy-done((bf16[128,128,128]{2,1,0:T(8,128)(2,1)S(1)}, bf16[128,128,128]{2,1,0:T(8,128)(2,1)}, u32[]{:S(2)}) %copy-start.1) | copy-done | bytes 4194328
  107.2 9.5 %shard_map.119 = f32[4,6144]{1,0:T(4,128)} custom-call(s32[256]{0:T(256)S(1)} %copy-done.24, s32[256]{0:T(256)S(1)} %copy-done.26, s32[256]{0:T(256)S(1)} %get-tuple-element.29.field_h, s32[256]{0:T(256)S(1)} %get-tuple-element.30.wet_h, f32[2560,128]{1,0:T(8,128)S(1)} %bitcast.9, bf16[128,128,128]{2,1,0:T(8,128)(2,1)S(1)} %copy-done.1), custom_call_target="tpu_custom_call" | custom-call | flops 134217728 | bytes 6291456 | tf_op jit(solution)/shard_map/pallas_call | solution.py:608
  (60 shorter events, 13.1 us)
Async XLA Ops:
  0.6 2.2 %copy-start = (bf16[128,128,128]{2,1,0:T(8,128)(2,1)S(1)}, bf16[128,128,128]{2,1,0:T(8,128)(2,1)}, u32[]{:S(2)}) copy-start(bf16[128,128,128]{2,1,0:T(8,128)(2,1)} %weights.1) | copy-start | bytes 12582916
  2.8 0.9 copy-start.14
  16.4 1.1 copy-start.3
  17.5 7.1 %copy-start.2 = (f32[4,16,64,128]{3,2,1,0:T(8,128)S(1)}, f32[4,16,64,128]{3,2,1,0:T(8,128)}, u32[]{:S(2)}) copy-start(f32[4,16,64,128]{3,2,1,0:T(8,128)} %state.1) | copy-start | bytes 6291460
  17.5 7.1 %copy-start.21 = (f32[64,128]{1,0:T(8,128)S(1)}, f32[64,128]{1,0:T(8,128)}, u32[]{:S(2)}) copy-start(f32[64,128]{1,0:T(8,128)} %horiz.1) | copy-start | bytes 98308
  17.5 7.1 %copy-start.22 = (s32[64,128]{1,0:T(8,128)S(1)}, s32[64,128]{1,0:T(8,128)}, u32[]{:S(2)}) copy-start(s32[64,128]{1,0:T(8,128)} %wet.1) | copy-start | bytes 98308
  17.5 39.7 %all-to-all-start = ((f32[32,80,128]{2,1,0:T(8,128)}), f32[32,80,128]{2,1,0:T(8,128)S(1)}, u32[]{:S(2)}, u32[]{:S(2)}) async-start(f32[32,80,128]{2,1,0:T(8,128)} %bitcast.10), calls=%async_computation | async-start | bytes 2621440 | tf_op jit(solution)/shard_map/all_to_all | solution.py:644
  24.6 1.0 copy-start.9
  27.4 7.4 %collective-permute-start = (f32[50,8,128]{2,1,0:T(8,128)S(1)}, f32[50,8,128]{2,1,0:T(8,128)S(1)}, u32[]{:S(2)}, u32[]{:S(2)}) collective-permute-start(f32[50,8,128]{2,1,0:T(8,128)S(1)} %get-tuple-element.18), channel_id=1, source_target_pairs={{0,4},{4,8},{8,12},{12,16},{16,20},{20,24},{24,28},{1,5},{5,9},{9,... | collective-permute-start | bytes 614408 | tf_op jit(solution)/shard_map/ppermute | solution.py:652
  30.9 11.1 %collective-permute-start.1 = (f32[50,8,128]{2,1,0:T(8,128)S(1)}, f32[50,8,128]{2,1,0:T(8,128)S(1)}, u32[]{:S(2)}, u32[]{:S(2)}) collective-permute-start(f32[50,8,128]{2,1,0:T(8,128)S(1)} %get-tuple-element.19), channel_id=1, source_target_pairs={{4,0},{8,4},{12,8},{16,12},{20,16},{24,20},{28,24},{5,1},{9,5},{13... | collective-permute-start | bytes 614408 | tf_op jit(solution)/shard_map/ppermute | solution.py:653
  33.5 1.0 copy-start.5
  44.9 10.0 %copy-start.17 = (f32[2,80,128]{2,1,0:T(8,128)}, f32[2,80,128]{2,1,0:T(8,128)S(1)}, u32[]{:S(2)}) copy-start(f32[2,80,128]{2,1,0:T(8,128)S(1)} %get-tuple-element.22.own_left) | copy-start | bytes 245764
  44.9 10.0 %copy-start.18 = (f32[2,80,128]{2,1,0:T(8,128)}, f32[2,80,128]{2,1,0:T(8,128)S(1)}, u32[]{:S(2)}) copy-start(f32[2,80,128]{2,1,0:T(8,128)S(1)} %get-tuple-element.23.own_right) | copy-start | bytes 245764
  44.9 5.6 %collective-permute-start.2 = (f32[2,80,128]{2,1,0:T(8,128)S(1)}, f32[2,80,128]{2,1,0:T(8,128)S(1)}, u32[]{:S(2)}, u32[]{:S(2)}) collective-permute-start(f32[2,80,128]{2,1,0:T(8,128)S(1)} %get-tuple-element.23.own_right), channel_id=1, source_target_pairs={{0,1},{1,2},{2,3},{4,5},{5,6},{6,7},{8,9},{9,10},{10,11},{12,13},{... | collective-permute-start | bytes 245768 | tf_op jit(solution)/shard_map/ppermute | solution.py:655
  47.9 6.4 %collective-permute-start.3 = (f32[2,80,128]{2,1,0:T(8,128)S(1)}, f32[2,80,128]{2,1,0:T(8,128)S(1)}, u32[]{:S(2)}, u32[]{:S(2)}) collective-permute-start(f32[2,80,128]{2,1,0:T(8,128)S(1)} %get-tuple-element.22.own_left), channel_id=1, source_target_pairs={{1,0},{2,1},{3,2},{5,4},{6,5},{7,6},{9,8},{10,9},{11,10},{13,12},{... | collective-permute-start | bytes 245768 | tf_op jit(solution)/shard_map/ppermute | solution.py:656
  50.5 3.8 %copy-start.29 = (f32[2,80,128]{2,1,0:T(8,128)}, f32[2,80,128]{2,1,0:T(8,128)S(1)}, u32[]{:S(2)}) copy-start(f32[2,80,128]{2,1,0:T(8,128)S(1)} %collective-permute-done.2.from_left) | copy-start | bytes 245764
  59.7 1.0 copy-start.12
  61.5 11.6 %copy-start.8 = (f32[4,80,128]{2,1,0:T(8,128)S(1)}, f32[4,80,128]{2,1,0:T(8,128)}, u32[]{:S(2)}) copy-start(f32[4,80,128]{2,1,0:T(8,128)} %get-tuple-element.24.faces) | copy-start | bytes 491524
  63.5 1.1 copy-start.4
  65.9 39.1 %all-to-all-start.1 = ((f32[32,80,128]{2,1,0:T(8,128)}), f32[32,80,128]{2,1,0:T(8,128)S(1)}, u32[]{:S(2)}, u32[]{:S(2)}) async-start(f32[32,80,128]{2,1,0:T(8,128)} %copy-done.4), calls=%async_computation.1 | async-start | bytes 2621440 | tf_op jit(solution)/shard_map/all_to_all | solution.py:662
  73.1 1.2 %copy-start.6 = (f32[2,16,64,128]{3,2,1,0:T(8,128)S(1)}, f32[2,16,64,128]{3,2,1,0:T(8,128)}, u32[]{:S(2)}) copy-start(f32[2,16,64,128]{3,2,1,0:T(8,128)} %copy-done.5) | copy-start | bytes 3145732
  76.1 28.8 %copy-start.24 = (s32[256]{0:T(256)S(1)}, s32[256]{0:T(256)}, u32[]{:S(2)}) copy-start(s32[256]{0:T(256)} %block_h.3) | copy-start | bytes 3076
  76.1 28.8 %copy-start.26 = (s32[256]{0:T(256)S(1)}, s32[256]{0:T(256)}, u32[]{:S(2)}) copy-start(s32[256]{0:T(256)} %tile_h.3) | copy-start | bytes 3076
  105.0 2.2 %copy-start.1 = (bf16[128,128,128]{2,1,0:T(8,128)(2,1)S(1)}, bf16[128,128,128]{2,1,0:T(8,128)(2,1)}, u32[]{:S(2)}) copy-start(bf16[128,128,128]{2,1,0:T(8,128)(2,1)} %weights.1) | copy-start | bytes 12582916
  (13 other events, 9.9 us)

commit v3 on v2

--- a/solution.py
+++ b/solution.py
@@ -15,6 +15,31 @@
 LANES = 128
 EDGE = 16
 HALO = 8
+PARTS = 8
+
+
+def hbm():
+    return pl.BlockSpec(memory_space=pltpu.HBM)
+
+
+def vmem():
+    return pl.BlockSpec(memory_space=VMEM)
+
+
+def pin(*arrays):
+    return [pltpu.with_memory_space_constraint(a, pltpu.HBM) for a in arrays]
+
+
+def start_all(pairs, sems, first=0):
+    copies = [pltpu.make_async_copy(src, dst, sems.at[first + n]) for n, (src, dst) in enumerate(pairs)]
+    for copy in copies:
+        copy.start()
+    return copies
+
+
+def wait_all(copies):
+    for copy in copies:
+        copy.wait()
 
 
 def iota(shape, dim):
@@ -35,21 +60,28 @@
 
 
 def remap_out_kernel(
-    capacity, grid_y, tile_rows, block_h, owner_h, row_h, tile_h, atm_h, weights_h,
-    out, field_o, wet_o, block_s, owner_s, row_s, tile_s, atm, weights, flux, fill, rows_acc, cols_acc, sems,
+    capacity, grid_y, tile_rows, block_h, owner_h, row_h, tile_h, atm_h, weights_h, out_h,
+    out, block_s, owner_s, row_s, tile_s, atm, weights, flux, every, fill, rows_acc, cols_acc, sems, weight_sems, out_sems,
 ):
     devices = fill.shape[0]
     npairs = block_s.shape[0]
-    nblocks = flux.shape[0]
+    tiles = weights.shape[0]
+    four = flux.shape[0]
+    nblocks = four // 4
     message = 4 * capacity + EDGE
     copies = [
         pltpu.make_async_copy(src, dst, sems.at[n])
         for n, (src, dst) in enumerate(
-            [(atm_h, atm), (block_h, block_s), (owner_h, owner_s), (row_h, row_s), (tile_h, tile_s), (weights_h, weights)]
+            [(atm_h, atm), (block_h, block_s), (owner_h, owner_s), (row_h, row_s), (tile_h, tile_s)]
         )
     ]
     for copy in copies:
         copy.start()
+    part_tiles = tiles // PARTS
+    parts = [pl.ds(n * part_tiles, part_tiles) for n in range(PARTS)]
+    loads = [pltpu.make_async_copy(weights_h.at[at], weights.at[at], weight_sems.at[n]) for n, at in enumerate(parts)]
+    for load in loads:
+        load.start()
     out[...] = jnp.zeros_like(out)
     rows_acc[...] = jnp.zeros_like(rows_acc)
     cols_acc[...] = jnp.zeros_like(cols_acc)
@@ -65,14 +97,21 @@
     speed = jnp.sqrt(wind_u * wind_u + wind_v * wind_v + 0.25)
     heat = 0.5 * speed * (atm[2:3, :] - atm[5:6, :])
     water = atm[4:5, :] - 0.3 * speed * atm[3:4, :]
-    planes = jnp.concatenate(
-        [heat, water, 0.2 * speed * wind_u, 0.2 * speed * wind_v, jnp.zeros((4, wind_u.shape[1]), F32)]
-        + [heat] * 4
-        + [water] * 4,
-        0,
-    ).astype(BF16)
-    for b in range(nblocks):
-        flux[b] = planes[:, b * LANES : (b + 1) * LANES]
+    for f, plane in enumerate([heat, water, 0.2 * speed * wind_u, 0.2 * speed * wind_v]):
+        for b in range(nblocks):
+            flux[f * nblocks + b : f * nblocks + b + 1, :] = plane[:, b * LANES : (b + 1) * LANES]
+    source = flux[...].astype(BF16)
+
+    for n in range(PARTS):
+        loads[n].wait()
+
+        def tile_step(t, carry):
+            every[pl.ds(pl.multiple_of(t * four, 8), four), :] = jnp.dot(
+                source, weights[t], preferred_element_type=F32
+            )
+            return carry
+
+        lax.fori_loop(n * part_tiles, (n + 1) * part_tiles, tile_step, 0, unroll=4)
     for copy in copies[1:]:
         copy.wait()
 
@@ -89,11 +128,11 @@
         row = row_s[p]
         rank = fill[owner]
         fill[owner] = rank + 1
-        field_o[p] = owner * back_rows(capacity) + 4 * rank
-        wet_o[p] = owner * back_rows(capacity) + 4 * capacity + rank
-        value = jnp.dot(flux[block_s[p]], weights[tile_s[p]], preferred_element_type=F32)
-        out[pl.ds(owner * message + 4 * rank, 4), :] = value[0:4]
-        tracer = value[8:16]
+        first = tile_s[p] * four + block_s[p]
+        lines = [every[pl.ds(first + f * nblocks, 1), :] for f in range(4)]
+        for f in range(4):
+            out[pl.ds(owner * message + 4 * rank + f, 1), :] = lines[f]
+        tracer = jnp.where(sub < 4, lines[0], lines[1])
         rows_acc[owner] = rows_acc[owner] + pick(edge_row == row, tracer)
         column = jnp.sum(pick(edge_col, tracer), axis=1, keepdims=True)
         number = (row + 1).astype(F32)
@@ -107,25 +146,21 @@
     grid_x = devices // grid_y
     zero = jnp.zeros((8, LANES), F32)
     inside = ((sub < 4) & (lane < 64)) | (sub >= 4)
-
-    def folded(d):
-        kept = pick(inside, cols_acc[d])
-        return kept + pltpu.roll(kept, 4, 0)
-
     folds = {}
 
     def fold(i, j):
         if not (0 <= i < grid_x and 0 <= j < grid_y):
             return zero
-        return folds_ref(i * grid_y + j)
-
-    def folds_ref(d):
+        d = i * grid_y + j
         if d not in folds:
-            folds[d] = folded(d)
+            kept = pick(inside, cols_acc[d])
+            folds[d] = kept + pltpu.roll(kept, 4, 0)
         return folds[d]
 
     last = (lane == tile_rows - 1) | (lane == 64 + tile_rows - 1)
     first = (lane == 0) | (lane == 64)
+    send = devices // 4
+    stores = []
     for d in range(devices):
         i, j = d // grid_y, d % grid_y
         below = rows_acc[d + grid_y] if i < grid_x - 1 else zero
@@ -141,39 +176,47 @@
         numbers = pltpu.roll(cols_acc[d], 5, 0)
         tile = tile + pick((sub == 5) & (lane >= 64), numbers)
         out[base + 8 : base + 16, :] = tile
+        if d % send == send - 1:
+            n = d // send
+            at = pl.ds(n * send * message, send * message)
+            stores.append(pltpu.make_async_copy(out.at[at], out_h.at[at], out_sems.at[n]))
+            stores[-1].start()
+    for store in stores:
+        store.wait()
 
 
 def remap_out(capacity, grid_y, devices, tile_rows, atm_state, pair_block, owner, pair_row, pair_tile, remap_weight):
     npairs = pair_block.shape[0]
     nblocks = atm_state.shape[1] // LANES
     message = 4 * capacity + EDGE
-    vmem = pl.BlockSpec(memory_space=VMEM)
-    smem = pl.BlockSpec(memory_space=SMEM)
+    tiles = remap_weight.shape[0]
     return pl.pallas_call(
         functools.partial(remap_out_kernel, capacity, grid_y, tile_rows),
-        out_shape=(
-            jax.ShapeDtypeStruct((devices * message, LANES), F32),
-            jax.ShapeDtypeStruct((npairs,), I32),
-            jax.ShapeDtypeStruct((npairs,), I32),
-        ),
-        in_specs=[pl.BlockSpec(memory_space=pl.ANY)] * 6,
-        out_specs=(vmem, smem, smem),
-        scratch_shapes=[pltpu.SMEM((npairs,), I32)] * 4
+        out_shape=pltpu.HBM((devices * message, LANES), F32),
+        in_specs=[hbm()] * 6,
+        out_specs=hbm(),
+        scratch_shapes=[pltpu.VMEM((devices * message, LANES), F32)]
+        + [pltpu.SMEM((npairs,), I32)] * 4
         + [
             pltpu.VMEM(atm_state.shape, F32),
             pltpu.VMEM(remap_weight.shape, BF16),
-            pltpu.VMEM((nblocks, 16, LANES), BF16),
+            pltpu.VMEM((4 * nblocks, LANES), F32),
+            pltpu.VMEM((tiles * 4 * nblocks, LANES), F32),
             pltpu.SMEM((devices,), I32),
             pltpu.VMEM((devices, 8, LANES), F32),
             pltpu.VMEM((devices, 8, LANES), F32),
-            pltpu.SemaphoreType.DMA((6,)),
+            pltpu.SemaphoreType.DMA((5,)),
+            pltpu.SemaphoreType.DMA((PARTS,)),
+            pltpu.SemaphoreType.DMA((4,)),
         ],
-        compiler_params=pltpu.CompilerParams(vmem_limit_bytes=24 << 20),
-        cost_estimate=pl.CostEstimate(flops=2 * npairs * 16 * LANES * LANES, bytes_accessed=6 << 20, transcendentals=0),
-    )(pair_block, owner, pair_row, pair_tile, atm_state, remap_weight)
-
-
-def solve_kernel(state, kappa, horiz, wet, tracer, currents, edge_up, edge_down):
+        compiler_params=pltpu.CompilerParams(vmem_limit_bytes=40 << 20),
+        cost_estimate=pl.CostEstimate(
+            flops=2 * tiles * 4 * nblocks * LANES * LANES, bytes_accessed=6 << 20, transcendentals=0
+        ),
+    )(*pin(pair_block, owner, pair_row, pair_tile, atm_state, remap_weight))
+
+
+def solve_kernel(state, kappa, horiz, wet, tracer, currents_h, edge_up, edge_down, currents, sems):
     levels = kappa.shape[0]
     rows_all = kappa.shape[1]
     planes = tracer.shape[0]
@@ -223,45 +266,47 @@
         ]
 
     lax.fori_loop(0, rows_all // 8, chunk, 0)
+    out = start_all([(currents, currents_h)], sems)
     tracer[3 * levels] = horiz[...]
     tracer[3 * levels + 1] = wet[...].astype(F32)
     for k in range(planes):
         edge_up[k] = tracer[k, 0:8, :]
         edge_down[k] = tracer[k, rows_all - 8 : rows_all, :]
+    wait_all(out)
 
 
 def solve(ocean_state, vert_kappa, horiz_kappa, wet_mask):
     levels, rows, _ = vert_kappa.shape
     planes = 3 * levels + 2
-    vmem = pl.BlockSpec(memory_space=VMEM)
     return pl.pallas_call(
         solve_kernel,
         out_shape=(
             jax.ShapeDtypeStruct((planes, rows, LANES), F32),
-            jax.ShapeDtypeStruct((2, levels, rows, LANES), F32),
+            pltpu.HBM((2, levels, rows, LANES), F32),
             jax.ShapeDtypeStruct((planes, 8, LANES), F32),
             jax.ShapeDtypeStruct((planes, 8, LANES), F32),
         ),
-        in_specs=[vmem] * 4,
-        out_specs=(vmem,) * 4,
+        in_specs=[vmem()] * 4,
+        out_specs=(vmem(), hbm(), vmem(), vmem()),
+        scratch_shapes=[pltpu.VMEM((2, levels, rows, LANES), F32), pltpu.SemaphoreType.DMA((1,))],
         compiler_params=pltpu.CompilerParams(vmem_limit_bytes=24 << 20),
         cost_estimate=pl.CostEstimate(flops=20 << 20, bytes_accessed=6 << 20, transcendentals=0),
     )(ocean_state, vert_kappa, horiz_kappa, wet_mask)
 
 
-def pack_kernel(levels, tracer, above, below, wide, to_left, to_right):
+def pack_kernel(levels, tracer, above, below, wide_h, to_left, to_right, wide, sems):
     planes, rows, _ = tracer.shape
     for k in range(planes):
         wide[k, 0:HALO, :] = above[k]
         wide[k, HALO : HALO + rows, :] = tracer[k]
         wide[k, HALO + rows : 2 * HALO + rows, :] = below[k]
+    out = start_all([(wide, wide_h)], sems)
     lane = iota((8, LANES), 1)
 
     def chunk(c, carry):
         at = pl.ds(pl.multiple_of(c * 8, 8), 8)
 
         def place(values, lanes):
-            left = [jnp.zeros((8, LANES), F32)] * 1
             left, right = jnp.zeros((8, LANES), F32), jnp.zeros((8, LANES), F32)
             for k, (near, far) in zip(values, lanes):
                 value = wide[k, at, :]
@@ -282,27 +327,44 @@
         return carry
 
     lax.fori_loop(0, (rows + 2 * HALO) // 8, chunk, 0)
+    wait_all(out)
 
 
 def pack(levels, tracer, above, below):
     planes, rows, _ = tracer.shape
     tall = rows + 2 * HALO
-    vmem = pl.BlockSpec(memory_space=VMEM)
     return pl.pallas_call(
         functools.partial(pack_kernel, levels),
         out_shape=(
-            jax.ShapeDtypeStruct((planes, tall, LANES), F32),
+            pltpu.HBM((planes, tall, LANES), F32),
             jax.ShapeDtypeStruct((2, tall, LANES), F32),
             jax.ShapeDtypeStruct((2, tall, LANES), F32),
         ),
-        in_specs=[vmem] * 3,
-        out_specs=(vmem,) * 3,
+        in_specs=[vmem()] * 3,
+        out_specs=(hbm(), vmem(), vmem()),
+        scratch_shapes=[pltpu.VMEM((planes, tall, LANES), F32), pltpu.SemaphoreType.DMA((1,))],
         compiler_params=pltpu.CompilerParams(vmem_limit_bytes=24 << 20),
         cost_estimate=pl.CostEstimate(flops=8 << 20, bytes_accessed=4 << 20, transcendentals=0),
     )(tracer, above, below)
 
 
-def faces_kernel(levels, horiz, wet, own_left, own_right, from_left, from_right, faces, packed):
+def faces_kernel(
+    levels, wide_h, own_left_h, own_right_h, from_left_h, from_right_h, faces_h, packed_h,
+    coef, own_left, own_right, from_left, from_right, faces, packed, sems,
+):
+    wait_all(
+        start_all(
+            [
+                (wide_h.at[pl.ds(3 * levels, 2)], coef),
+                (own_left_h, own_left),
+                (own_right_h, own_right),
+                (from_left_h, from_left),
+                (from_right_h, from_right),
+            ],
+            sems,
+        )
+    )
+    horiz, wet = coef.at[0], coef.at[1]
     tall = horiz.shape[0]
     lane = iota((tall, LANES), 1)
     odd = lane % 2 == 1
@@ -351,21 +413,24 @@
     )
     faces[2] = west
     faces[3] = jnp.where(lane == LANES - 1, face(h, w, kappa_right, wet_right), pltpu.roll(west, LANES - 1, 1))
+    wait_all(start_all([(faces, faces_h), (packed, packed_h)], sems, 5))
 
 
 def face_values(levels, wide, own_left, own_right, from_left, from_right):
     tall = wide.shape[1]
-    vmem = pl.BlockSpec(memory_space=VMEM)
     return pl.pallas_call(
         functools.partial(faces_kernel, levels),
         out_shape=(
-            jax.ShapeDtypeStruct((4, tall, LANES), F32),
-            jax.ShapeDtypeStruct((8, tall, LANES), F32),
+            pltpu.HBM((4, tall, LANES), F32),
+            pltpu.HBM((8, tall, LANES), F32),
         ),
-        in_specs=[vmem] * 6,
-        out_specs=(vmem,) * 2,
+        in_specs=[hbm()] + [pl.BlockSpec(memory_space=pl.ANY)] * 4,
+        out_specs=(hbm(),) * 2,
+        scratch_shapes=[pltpu.VMEM((2, tall, LANES), F32)] * 5
+        + [pltpu.VMEM((4, tall, LANES), F32), pltpu.VMEM((8, tall, LANES), F32), pltpu.SemaphoreType.DMA((7,))],
+        compiler_params=pltpu.CompilerParams(vmem_limit_bytes=24 << 20),
         cost_estimate=pl.CostEstimate(flops=1 << 20, bytes_accessed=1 << 20, transcendentals=0),
-    )(wide[3 * levels], wide[3 * levels + 1], own_left, own_right, from_left, from_right)
+    )(*pin(wide), own_left, own_right, from_left, from_right)
 
 
 def one_pass(value, faces, beside, shift):
@@ -381,12 +446,23 @@
 
 
 def middle_kernel(
-    capacity, levels, arrived, top, currents, wet_wide, faces, packed, sent, forcing, near_o,
-    placing, values, number_t,
+    capacity, levels, arrived, wide_h, currents_h, faces_h, packed_h, sent_h, forcing_h, near_h,
+    placing, values, number_t, top, currents, faces, packed, sent, forcing, near_o, sems, sent_sems,
 ):
     devices, message, _ = arrived.shape
     rows_all = currents.shape[1]
     tall = rows_all + 2 * HALO
+    loads = start_all(
+        [(wide_h.at[levels * k], top.at[k]) for k in range(3)]
+        + [
+            (wide_h.at[3 * levels + 1], top.at[3]),
+            (currents_h.at[0, 0], currents.at[0]),
+            (currents_h.at[1, 0], currents.at[1]),
+            (faces_h, faces),
+            (packed_h, packed),
+        ],
+        sems,
+    )
     span = 4 * capacity
     group = LANES // span
     groups = devices // group
@@ -425,6 +501,9 @@
     total = jnp.dot(placing[...], values[...], preferred_element_type=F32)
     total = total[:, 0:LANES] + total[:, LANES : 2 * LANES]
 
+    wait_all(loads)
+    wet_wide = top[3]
+
     def plane(f):
         return total[f * rows_all : (f + 1) * rows_all]
 
@@ -434,7 +513,7 @@
         after = pick(sub8 < 2, edge_rows if f == 0 else pltpu.roll(edge_rows, 4, 0))
         wide.append(jnp.concatenate([before, plane(f), after], 0))
         forcing[f] = wide[f]
-    wet = wet_wide[HALO : HALO + rows_all, :]
+    wet = wet_wide[HALO : HALO + rows_all]
     for f in range(2, 4):
         forcing[f, 0:HALO, :] = jnp.zeros((HALO, LANES), F32)
         forcing[f, HALO : HALO + rows_all, :] = plane(f) * wet
@@ -475,9 +554,10 @@
     near = near + packed[7] * (own - both)
     near_o[0] = both
     near_o[1] = near
+    stores = start_all([(forcing, forcing_h), (near_o, near_h)], sems, 8)
 
     surface = []
-    unit = top[2] * wet_wide[...]
+    unit = top[2] * wet_wide
     for f in range(2):
         value = top[f] + unit * wide[f]
         shift = LANES - (2 * levels * f + 1)
@@ -510,34 +590,53 @@
             sent[s, span : span + capacity, :] = masks[g * capacity : (g + 1) * capacity]
             if height > span + capacity:
                 sent[s, span + capacity : height, :] = jnp.zeros((height - span - capacity, LANES), F32)
-
-
-def middle(capacity, levels, arrived, top, currents, wet_wide, faces, packed):
+        at = pl.ds(m * group, group)
+        stores += start_all([(sent.at[at], sent_h.at[at])], sent_sems, m)
+    wait_all(stores)
+
+
+def middle(capacity, levels, arrived, wide, currents, faces, packed):
     devices = arrived.shape[0]
-    rows = currents.shape[1]
+    rows = currents.shape[2]
     tall = rows + 2 * HALO
-    vmem = pl.BlockSpec(memory_space=VMEM)
+    height = back_rows(capacity)
     return pl.pallas_call(
         functools.partial(middle_kernel, capacity, levels),
         out_shape=(
-            jax.ShapeDtypeStruct((devices, back_rows(capacity), LANES), F32),
-            jax.ShapeDtypeStruct((4, tall, LANES), F32),
-            jax.ShapeDtypeStruct((2, tall, LANES), F32),
+            pltpu.HBM((devices, height, LANES), F32),
+            pltpu.HBM((4, tall, LANES), F32),
+            pltpu.HBM((2, tall, LANES), F32),
         ),
-        in_specs=[vmem] * 6,
-        out_specs=(vmem,) * 3,
+        in_specs=[vmem()] + [hbm()] * 4,
+        out_specs=(hbm(),) * 3,
         scratch_shapes=[
             pltpu.VMEM((4 * rows, 4 * capacity * devices), BF16),
             pltpu.VMEM((4 * capacity * devices, 2 * LANES), BF16),
             pltpu.VMEM((LANES, LANES), F32),
+            pltpu.VMEM((4, tall, LANES), F32),
+            pltpu.VMEM((2, rows, LANES), F32),
+            pltpu.VMEM((4, tall, LANES), F32),
+            pltpu.VMEM((8, tall, LANES), F32),
+            pltpu.VMEM((devices, height, LANES), F32),
+            pltpu.VMEM((4, tall, LANES), F32),
+            pltpu.VMEM((2, tall, LANES), F32),
+            pltpu.SemaphoreType.DMA((10,)),
+            pltpu.SemaphoreType.DMA((4 * capacity * devices // LANES,)),
         ],
         compiler_params=pltpu.CompilerParams(vmem_limit_bytes=24 << 20),
         cost_estimate=pl.CostEstimate(flops=200 << 20, bytes_accessed=4 << 20, transcendentals=0),
-    )(arrived, top, currents, wet_wide, faces, packed)
-
-
-def finish_kernel(levels, wide, currents, faces, forcing, near, ocean):
+    )(arrived, *pin(wide, currents, faces, packed))
+
+
+def finish_kernel(
+    levels, wide_h, currents_h, faces_h, forcing_h, near_h, ocean, wide, currents, faces, forcing, near, sems
+):
     rows_all = currents.shape[2]
+    wait_all(
+        start_all(
+            [(wide_h, wide), (currents_h, currents), (faces_h, faces), (forcing_h, forcing), (near_h, near)], sems
+        )
+    )
     inner = slice(HALO, HALO + rows_all)
 
     def level(l, carry):
@@ -557,64 +656,85 @@
 
 def finish(levels, wide, currents, faces, forcing, near):
     rows = currents.shape[2]
-    vmem = pl.BlockSpec(memory_space=VMEM)
     return pl.pallas_call(
         functools.partial(finish_kernel, levels),
         out_shape=jax.ShapeDtypeStruct((4, levels, rows, LANES), F32),
-        in_specs=[vmem] * 5,
-        out_specs=vmem,
+        in_specs=[hbm()] * 5,
+        out_specs=vmem(),
+        scratch_shapes=[pltpu.VMEM(a.shape, F32) for a in (wide, currents, faces, forcing, near)]
+        + [pltpu.SemaphoreType.DMA((5,))],
         compiler_params=pltpu.CompilerParams(vmem_limit_bytes=24 << 20),
         cost_estimate=pl.CostEstimate(flops=40 << 20, bytes_accessed=6 << 20, transcendentals=0),
-    )(wide, currents, faces, forcing, near)
-
-
-def remap_back_kernel(block_h, tile_h, field_h, wet_h, returned, weights, out, block_s, tile_s, field_s, wet_s, total, sems):
+    )(*pin(wide, currents, faces, forcing, near))
+
+
+def remap_back_kernel(
+    capacity, block_h, tile_h, owner_h, returned, weights_h, out,
+    block_s, tile_s, owner_s, fill, weights, picked, total, sems, weight_sems,
+):
     npairs = block_s.shape[0]
     nblocks = total.shape[0]
-    copies = [
-        pltpu.make_async_copy(src, dst, sems.at[n])
-        for n, (src, dst) in enumerate([(block_h, block_s), (tile_h, tile_s), (field_h, field_s), (wet_h, wet_s)])
-    ]
-    for copy in copies:
-        copy.start()
+    devices = fill.shape[0]
+    height = back_rows(capacity)
+    scalars = start_all([(owner_h, owner_s), (block_h, block_s), (tile_h, tile_s)], sems)
+    part_tiles = weights.shape[0] // PARTS
+    parts = [pl.ds(n * part_tiles, part_tiles) for n in range(PARTS)]
+    loads = start_all([(weights_h.at[at], weights.at[at]) for at in parts], weight_sems)
     total[...] = jnp.zeros_like(total)
-    for copy in copies:
-        copy.wait()
+
+    def clear_fill(i, carry):
+        fill[i] = 0
+        return carry
+
+    lax.fori_loop(0, devices, clear_fill, 0, unroll=16)
+    wait_all(scalars)
+
+    def gather(p, carry):
+        owner = owner_s[p]
+        rank = fill[owner]
+        fill[owner] = rank + 1
+        rows = returned[pl.ds(owner * height + 4 * rank, 4), :]
+        mask = returned[pl.ds(owner * height + 4 * capacity + rank, 1), :]
+        high, low = split(jnp.concatenate([rows, mask, jnp.zeros((3, LANES), F32)], 0))
+        picked[p] = jnp.concatenate([high, low], 0)
+        return carry
+
+    lax.fori_loop(0, npairs, gather, 0, unroll=8)
+    wait_all(loads)
 
     def pair(p, carry):
-        rows = returned[pl.ds(field_s[p], 4), :]
-        mask = returned[pl.ds(wet_s[p], 1), :]
-        full = jnp.concatenate([rows, mask, jnp.zeros((3, LANES), F32)], 0)
-        high, low = split(full)
         value = lax.dot_general(
-            jnp.concatenate([high, low], 0),
-            weights[tile_s[p]],
-            (((1,), (1,)), ((), ())),
-            preferred_element_type=F32,
+            picked[p], weights[tile_s[p]], (((1,), (1,)), ((), ())), preferred_element_type=F32
         )
         b = block_s[p]
         total[b] = total[b] + (value[0:8] + value[8:16])
         return carry
 
-    lax.fori_loop(0, npairs, pair, 0, unroll=8)
+    lax.fori_loop(0, npairs, pair, 0, unroll=16)
     for b in range(nblocks):
         sums = total[b]
         out[:, b * LANES : (b + 1) * LANES] = sums[0:4] / jnp.maximum(sums[4:5], 0.1)
 
 
-def remap_back(pair_block, pair_tile, field_at, wet_at, returned, remap_weight, nblocks):
+def remap_back(capacity, devices, pair_block, pair_tile, owner, returned, remap_weight, nblocks):
     npairs = pair_block.shape[0]
-    vmem = pl.BlockSpec(memory_space=VMEM)
     return pl.pallas_call(
-        remap_back_kernel,
+        functools.partial(remap_back_kernel, capacity),
         out_shape=jax.ShapeDtypeStruct((4, nblocks * LANES), F32),
-        in_specs=[pl.BlockSpec(memory_space=pl.ANY)] * 4 + [vmem] * 2,
-        out_specs=vmem,
-        scratch_shapes=[pltpu.SMEM((npairs,), I32)] * 4
-        + [pltpu.VMEM((nblocks, 8, LANES), F32), pltpu.SemaphoreType.DMA((4,))],
+        in_specs=[hbm()] * 3 + [vmem(), hbm()],
+        out_specs=vmem(),
+        scratch_shapes=[pltpu.SMEM((npairs,), I32)] * 3
+        + [
+            pltpu.SMEM((devices,), I32),
+            pltpu.VMEM(remap_weight.shape, BF16),
+            pltpu.VMEM((npairs, 16, LANES), BF16),
+            pltpu.VMEM((nblocks, 8, LANES), F32),
+            pltpu.SemaphoreType.DMA((3,)),
+            pltpu.SemaphoreType.DMA((PARTS,)),
+        ],
         compiler_params=pltpu.CompilerParams(vmem_limit_bytes=24 << 20),
         cost_estimate=pl.CostEstimate(flops=2 * npairs * 16 * LANES * LANES, bytes_accessed=6 << 20, transcendentals=0),
-    )(pair_block, pair_tile, field_at, wet_at, returned, remap_weight)
+    )(*pin(pair_block, pair_tile, owner), returned, *pin(remap_weight))
 
 
 def local(
@@ -638,7 +758,7 @@
     nblocks = atm_state.shape[1] // LANES
     owner = pair_owner.reshape(npairs)
     message = 4 * capacity + EDGE
-    outgoing, field_at, wet_at = remap_out(
+    outgoing = remap_out(
         capacity, grid_y, devices, tile_rows, atm_state, pair_block, owner, pair_row, pair_tile, remap_weight
     )
     arrived = lax.all_to_all(
@@ -655,14 +775,11 @@
     from_left = lax.ppermute(to_right, "gy", rise_y)
     from_right = lax.ppermute(to_left, "gy", fall_y)
     faces, packed = face_values(levels, wide, to_left, to_right, from_left, from_right)
-    top = jnp.stack([wide[0], wide[levels], wide[2 * levels]])
-    sent, forcing, near = middle(
-        capacity, levels, arrived, top, currents[:, 0], wide[3 * levels + 1], faces, packed
-    )
+    sent, forcing, near = middle(capacity, levels, arrived, wide, currents, faces, packed)
     returned = lax.all_to_all(sent, ("gx", "gy"), split_axis=0, concat_axis=0, tiled=True)
     ocean_next = finish(levels, wide, currents, faces, forcing, near)
     atm_surface = remap_back(
-        pair_block, pair_tile, field_at, wet_at, returned.reshape(-1, LANES), remap_weight, nblocks
+        capacity, devices, pair_block, pair_tile, owner, returned.reshape(-1, LANES), remap_weight, nblocks
     )
     return (ocean_next, atm_surface)
 

time: 118 us -> 105 us (0.89)
  local copies, waits for them, and re-layouts: 22.8 us -> 1.06 us
  Pallas kernels: 33 us -> 40.8 us
  waiting for transfers between devices: 35.3 us -> 37.4 us
    unnamed x62 -> x8, local copies, waits for them, and re-layouts: 21.6 us -> 1.06 us
    pallas_call x1, Pallas kernels: 9.93 us -> 12.7 us  [remap_out(): pl.pallas_call(functools.partial(remap_out_kernel, capacity, grid_y, tile...]
    ppermute x1, waiting for transfers between devices: 3.76 us -> 1.05 us  [local(): from_right = lax.ppermute(to_left, 'gy', fall_y)]
    all_to_all x1, waiting for transfers between devices: 0.01 us -> 2.33 us  [local(): lax.all_to_all(outgoing.reshape(devices, message, LANES), ('gx', 'gy'), s...]
    pallas_call x1, Pallas kernels: 1.9 us -> 4.01 us  [middle(): pl.pallas_call(functools.partial(middle_kernel, capacity, levels), out_sh...]
    pallas_call x1, Pallas kernels: 4.86 us -> 6.85 us  [finish(): pl.pallas_call(functools.partial(finish_kernel, levels), out_shape=jax.Sh...]
    ppermute x1, waiting for transfers between devices: 0.29 us -> 2.03 us  [local(): above = lax.ppermute(edge_down, 'gx', rise_x)]
  transfers between devices with their start and end apart: 6 -> 6, of which waited for: 4 -> 6; matrix products, arithmetic and copies ran while one was open for 2% -> 0% of each run, Pallas kernels for 10% -> 14%
where the time goes in v3:
time: 105 us; the launch traced here: 104 us
  Pallas kernels  40.8 us (39%)
  waiting for transfers between devices  37.4 us (36%)
  starting transfers between devices  24.4 us (23%)
  local copies, waits for them, and re-layouts  1.06 us (1%)
    all_to_all x1, waiting for transfers between devices, local(): lax.all_to_all(sent, ('gx', 'gy'), split_axis=0, concat_axis=0, tiled=True)  25 us
    pallas_call x1, Pallas kernels, remap_out(): pl.pallas_call(functools.partial(remap_out_kernel, capacity, grid_y, tile...  12.7 us
    pallas_call x1, Pallas kernels, remap_back(): pl.pallas_call(functools.partial(remap_back_kernel, capacity), out_shape=...  9.59 us
    all_to_all x1, starting transfers between devices, local(): lax.all_to_all(outgoing.reshape(devices, message, LANES), ('gx', 'gy'), s...  7.1 us
    pallas_call x1, Pallas kernels, finish(): pl.pallas_call(functools.partial(finish_kernel, levels), out_shape=jax.Sh...  6.85 us
    all_to_all x1, starting transfers between devices, local(): lax.all_to_all(sent, ('gx', 'gy'), split_axis=0, concat_axis=0, tiled=True)  6.58 us
    ppermute x1, waiting for transfers between devices, local(): below = lax.ppermute(edge_up, 'gx', fall_x)  6.55 us
    pallas_call x1, Pallas kernels, middle(): pl.pallas_call(functools.partial(middle_kernel, capacity, levels), out_sh...  4.01 us
  transfers between devices with their start and end apart: 6, of which 6 were waited for; matrix products, arithmetic and copies ran while one was open for 0% of the time, Pallas kernels for 14%

profile of v3, /device:TPU:1, one launch (start us, length us, event | category | flops | bytes accessed | tf_op | source)
XLA Modules:
  0.0 104.5 jit_solution(15942429930081285544)
XLA Ops:
  0.6 12.7 %shard_map.116 = f32[2560,128]{1,0:T(8,128)} custom-call(s32[256]{0:T(256)} %block_h.3, s32[256]{0:T(256)} %bitcast.5, s32[256]{0:T(256)} %row_h.1, s32[256]{0:T(256)} %tile_h.3, f32[6,6144]{1,0:T(8,128)} %atm_h.1, bf16[128,128,128]{2,1,0:T(8,128)(2,1)} %weights_h.3), custom_call_target="tpu_custom_call" | custom-call | flops 805306368 | bytes 6291456 | tf_op jit(solution)/shard_map/pallas_call | solution.py:193
  13.3 0.0 copy-start
  13.3 0.0 copy-start.2
  13.4 0.0 copy-start.3
  13.4 7.1 %all-to-all-start = ((f32[32,80,128]{2,1,0:T(8,128)}), f32[32,80,128]{2,1,0:T(8,128)S(1)}, u32[]{:S(2)}, u32[]{:S(2)}) async-start(f32[32,80,128]{2,1,0:T(8,128)} %bitcast.4), calls=%async_computation | async-start | bytes 2621440 | tf_op jit(solution)/shard_map/all_to_all | solution.py:764
  20.5 0.0 copy-start.1
  20.5 1.0 copy-done.1
  21.6 2.7 %shard_map.113 = (f32[50,64,128]{2,1,0:T(8,128)S(1)}, f32[2,16,64,128]{3,2,1,0:T(8,128)}, f32[50,8,128]{2,1,0:T(8,128)S(1)}, f32[50,8,128]{2,1,0:T(8,128)S(1)}) custom-call(f32[4,16,64,128]{3,2,1,0:T(8,128)S(1)} %copy-done, f32[16,64,128]{2,1,0:T(8,128)S(1)} %copy-done.1, f32[64,128]{1,0:T(8,128)S(1)} %copy-done.2, s32[64,128]{1,0:T(8,128)S(1)} %copy-done.3), custom_call_target="tpu_custom_call" | custom-call | flops 20971520 | bytes 6291456 | tf_op jit(solution)/shard_map/pallas_call | solution.py:281
  24.2 3.5 %collective-permute-start = (f32[50,8,128]{2,1,0:T(8,128)S(1)}, f32[50,8,128]{2,1,0:T(8,128)S(1)}, u32[]{:S(2)}, u32[]{:S(2)}) collective-permute-start(f32[50,8,128]{2,1,0:T(8,128)S(1)} %get-tuple-element.15), channel_id=1, source_target_pairs={{0,4},{4,8},{8,12},{12,16},{16,20},{20,24},{24,28},{1,5},{5,9},{9,... | collective-permute-start | bytes 614408 | tf_op jit(solution)/shard_map/ppermute | solution.py:772
  27.8 1.9 %collective-permute-start.1 = (f32[50,8,128]{2,1,0:T(8,128)S(1)}, f32[50,8,128]{2,1,0:T(8,128)S(1)}, u32[]{:S(2)}, u32[]{:S(2)}) collective-permute-start(f32[50,8,128]{2,1,0:T(8,128)S(1)} %get-tuple-element.16), channel_id=1, source_target_pairs={{4,0},{8,4},{12,8},{16,12},{20,16},{24,20},{28,24},{5,1},{9,5},{13... | collective-permute-start | bytes 614408 | tf_op jit(solution)/shard_map/ppermute | solution.py:773
  29.7 2.0 %collective-permute-done.above = f32[50,8,128]{2,1,0:T(8,128)S(1)} collective-permute-done((f32[50,8,128]{2,1,0:T(8,128)S(1)}, f32[50,8,128]{2,1,0:T(8,128)S(1)}, u32[]{:S(2)}, u32[]{:S(2)}) %collective-permute-start) | collective-permute-done | bytes 204832 | tf_op jit(solution)/shard_map/ppermute | solution.py:772
  31.7 6.6 %collective-permute-done.1.below = f32[50,8,128]{2,1,0:T(8,128)S(1)} collective-permute-done((f32[50,8,128]{2,1,0:T(8,128)S(1)}, f32[50,8,128]{2,1,0:T(8,128)S(1)}, u32[]{:S(2)}, u32[]{:S(2)}) %collective-permute-start.1) | collective-permute-done | bytes 204832 | tf_op jit(solution)/shard_map/ppermute | solution.py:773
  38.3 2.9 %shard_map.114 = (f32[50,80,128]{2,1,0:T(8,128)}, f32[2,80,128]{2,1,0:T(8,128)S(1)}, f32[2,80,128]{2,1,0:T(8,128)S(1)}) custom-call(f32[50,64,128]{2,1,0:T(8,128)S(1)} %get-tuple-element.14.tracer, f32[50,8,128]{2,1,0:T(8,128)S(1)} %collective-permute-done.above, f32[50,8,128]{2,1,0:T(8,128)S(1)} %collective-permute-done.1.below), custom_call_target="tpu_custom_call" | custom-call | flops 8388608 | bytes 4194304 | tf_op jit(solution)/shard_map/pallas_call | solution.py:336
  41.2 1.3 %collective-permute-start.3 = (f32[2,80,128]{2,1,0:T(8,128)S(1)}, f32[2,80,128]{2,1,0:T(8,128)S(1)}, u32[]{:S(2)}, u32[]{:S(2)}) collective-permute-start(f32[2,80,128]{2,1,0:T(8,128)S(1)} %get-tuple-element.19.own_left_h), channel_id=1, source_target_pairs={{1,0},{2,1},{3,2},{5,4},{6,5},{7,6},{9,8},{10,9},{11,10},{13,12},{... | collective-permute-start | bytes 245768 | tf_op jit(solution)/shard_map/ppermute | solution.py:776
  42.5 4.0 %collective-permute-start.2 = (f32[2,80,128]{2,1,0:T(8,128)S(1)}, f32[2,80,128]{2,1,0:T(8,128)S(1)}, u32[]{:S(2)}, u32[]{:S(2)}) collective-permute-start(f32[2,80,128]{2,1,0:T(8,128)S(1)} %get-tuple-element.20.own_right_h), channel_id=1, source_target_pairs={{0,1},{1,2},{2,3},{4,5},{5,6},{6,7},{8,9},{9,10},{10,11},{12,13},{... | collective-permute-start | bytes 245768 | tf_op jit(solution)/shard_map/ppermute | solution.py:775
  46.5 1.1 %collective-permute-done.3.from_right_h = f32[2,80,128]{2,1,0:T(8,128)S(1)} collective-permute-done((f32[2,80,128]{2,1,0:T(8,128)S(1)}, f32[2,80,128]{2,1,0:T(8,128)S(1)}, u32[]{:S(2)}, u32[]{:S(2)}) %collective-permute-start.3) | collective-permute-done | bytes 81952 | tf_op jit(solution)/shard_map/ppermute | solution.py:776
  47.6 0.4 collective-permute-done.2.from_left_h
  48.0 2.1 %shard_map.115 = (f32[4,80,128]{2,1,0:T(8,128)}, f32[8,80,128]{2,1,0:T(8,128)}) custom-call(f32[50,80,128]{2,1,0:T(8,128)} %get-tuple-element.17.wide_h, f32[2,80,128]{2,1,0:T(8,128)S(1)} %get-tuple-element.19.own_left_h, f32[2,80,128]{2,1,0:T(8,128)S(1)} %get-tuple-element.20.own_right_h, f32[2,80,128]{2,1,0:T(8,128)S(1)} %collective-permute-done.2.from_left_h, ...), custom_call_target="tpu_custom_call" | custom-call | flops 1048576 | bytes 1048576 | tf_op jit(solution)/shard_map/pallas_call | solution.py:421
  50.1 2.3 %all-to-all-done.arrived = f32[32,80,128]{2,1,0:T(8,128)S(1)} async-done(((f32[32,80,128]{2,1,0:T(8,128)}), f32[32,80,128]{2,1,0:T(8,128)S(1)}, u32[]{:S(2)}, u32[]{:S(2)}) %all-to-all-start) | async-done | bytes 1310752 | tf_op jit(solution)/shard_map/all_to_all | solution.py:764
  52.4 4.0 %shard_map.117 = (f32[32,80,128]{2,1,0:T(8,128)}, f32[4,80,128]{2,1,0:T(8,128)}, f32[2,80,128]{2,1,0:T(8,128)}) custom-call(f32[32,80,128]{2,1,0:T(8,128)S(1)} %all-to-all-done.arrived, f32[50,80,128]{2,1,0:T(8,128)} %get-tuple-element.17.wide_h, f32[2,16,64,128]{3,2,1,0:T(8,128)} %get-tuple-element.18.currents_h, f32[4,80,128]{2,1,0:T(8,128)} %get-tuple-element.21.faces_h, ...), custom_call_target="tpu_custom_call" | custom-call | flops 209715200 | bytes 4194304 | tf_op jit(solution)/shard_map/pallas_call | solution.py:603
  56.4 6.6 %all-to-all-start.1 = ((f32[32,80,128]{2,1,0:T(8,128)}), f32[32,80,128]{2,1,0:T(8,128)S(1)}, u32[]{:S(2)}, u32[]{:S(2)}) async-start(f32[32,80,128]{2,1,0:T(8,128)} %get-tuple-element.25), calls=%async_computation.1 | async-start | bytes 2621440 | tf_op jit(solution)/shard_map/all_to_all | solution.py:779
  63.0 6.8 %shard_map.118 = f32[4,16,64,128]{3,2,1,0:T(8,128)} custom-call(f32[50,80,128]{2,1,0:T(8,128)} %get-tuple-element.17.wide_h, f32[2,16,64,128]{3,2,1,0:T(8,128)} %get-tuple-element.18.currents_h, f32[4,80,128]{2,1,0:T(8,128)} %get-tuple-element.21.faces_h, f32[4,80,128]{2,1,0:T(8,128)} %get-tuple-element.23.forcing_h, f32[2,80,128]{2,1,0:T(8,128)} %get-tuple-element.24.near_h), custom_call_target="tpu_custom_call" | custom-call | flops 41943040 | bytes 6291456 | tf_op jit(solution)/shard_map/pallas_call | solution.py:659
  69.9 25.0 %all-to-all-done.1 = f32[32,80,128]{2,1,0:T(8,128)S(1)} async-done(((f32[32,80,128]{2,1,0:T(8,128)}), f32[32,80,128]{2,1,0:T(8,128)S(1)}, u32[]{:S(2)}, u32[]{:S(2)}) %all-to-all-start.1) | async-done | bytes 1310752 | tf_op jit(solution)/shard_map/all_to_all | solution.py:779
  94.9 9.6 %shard_map.119 = f32[4,6144]{1,0:T(4,128)} custom-call(s32[256]{0:T(256)} %block_h.3, s32[256]{0:T(256)} %tile_h.3, s32[256]{0:T(256)} %bitcast.6, f32[2560,128]{1,0:T(8,128)S(1)} %bitcast.3, bf16[128,128,128]{2,1,0:T(8,128)(2,1)} %weights_h.3), custom_call_target="tpu_custom_call" | custom-call | flops 134217728 | bytes 6291456 | tf_op jit(solution)/shard_map/pallas_call | solution.py:721
  (3 shorter events, 0.0 us)
Async XLA Ops:
  13.3 7.2 %copy-start = (f32[4,16,64,128]{3,2,1,0:T(8,128)S(1)}, f32[4,16,64,128]{3,2,1,0:T(8,128)}, u32[]{:S(2)}) copy-start(f32[4,16,64,128]{3,2,1,0:T(8,128)} %state.1) | copy-start | bytes 6291460
  13.3 7.1 %copy-start.2 = (f32[64,128]{1,0:T(8,128)S(1)}, f32[64,128]{1,0:T(8,128)}, u32[]{:S(2)}) copy-start(f32[64,128]{1,0:T(8,128)} %horiz.1) | copy-start | bytes 98308
  13.4 7.1 %copy-start.3 = (s32[64,128]{1,0:T(8,128)S(1)}, s32[64,128]{1,0:T(8,128)}, u32[]{:S(2)}) copy-start(s32[64,128]{1,0:T(8,128)} %wet.1) | copy-start | bytes 98308
  13.4 39.0 %all-to-all-start = ((f32[32,80,128]{2,1,0:T(8,128)}), f32[32,80,128]{2,1,0:T(8,128)S(1)}, u32[]{:S(2)}, u32[]{:S(2)}) async-start(f32[32,80,128]{2,1,0:T(8,128)} %bitcast.4), calls=%async_computation | async-start | bytes 2621440 | tf_op jit(solution)/shard_map/all_to_all | solution.py:764
  20.5 1.0 copy-start.1
  24.2 7.5 %collective-permute-start = (f32[50,8,128]{2,1,0:T(8,128)S(1)}, f32[50,8,128]{2,1,0:T(8,128)S(1)}, u32[]{:S(2)}, u32[]{:S(2)}) collective-permute-start(f32[50,8,128]{2,1,0:T(8,128)S(1)} %get-tuple-element.15), channel_id=1, source_target_pairs={{0,4},{4,8},{8,12},{12,16},{16,20},{20,24},{24,28},{1,5},{5,9},{9,... | collective-permute-start | bytes 614408 | tf_op jit(solution)/shard_map/ppermute | solution.py:772
  27.8 10.5 %collective-permute-start.1 = (f32[50,8,128]{2,1,0:T(8,128)S(1)}, f32[50,8,128]{2,1,0:T(8,128)S(1)}, u32[]{:S(2)}, u32[]{:S(2)}) collective-permute-start(f32[50,8,128]{2,1,0:T(8,128)S(1)} %get-tuple-element.16), channel_id=1, source_target_pairs={{4,0},{8,4},{12,8},{16,12},{20,16},{24,20},{28,24},{5,1},{9,5},{13... | collective-permute-start | bytes 614408 | tf_op jit(solution)/shard_map/ppermute | solution.py:773
  41.2 6.4 %collective-permute-start.3 = (f32[2,80,128]{2,1,0:T(8,128)S(1)}, f32[2,80,128]{2,1,0:T(8,128)S(1)}, u32[]{:S(2)}, u32[]{:S(2)}) collective-permute-start(f32[2,80,128]{2,1,0:T(8,128)S(1)} %get-tuple-element.19.own_left_h), channel_id=1, source_target_pairs={{1,0},{2,1},{3,2},{5,4},{6,5},{7,6},{9,8},{10,9},{11,10},{13,12},{... | collective-permute-start | bytes 245768 | tf_op jit(solution)/shard_map/ppermute | solution.py:776
  42.5 5.5 %collective-permute-start.2 = (f32[2,80,128]{2,1,0:T(8,128)S(1)}, f32[2,80,128]{2,1,0:T(8,128)S(1)}, u32[]{:S(2)}, u32[]{:S(2)}) collective-permute-start(f32[2,80,128]{2,1,0:T(8,128)S(1)} %get-tuple-element.20.own_right_h), channel_id=1, source_target_pairs={{0,1},{1,2},{2,3},{4,5},{5,6},{6,7},{8,9},{9,10},{10,11},{12,13},{... | collective-permute-start | bytes 245768 | tf_op jit(solution)/shard_map/ppermute | solution.py:775
  56.4 38.5 %all-to-all-start.1 = ((f32[32,80,128]{2,1,0:T(8,128)}), f32[32,80,128]{2,1,0:T(8,128)S(1)}, u32[]{:S(2)}, u32[]{:S(2)}) async-start(f32[32,80,128]{2,1,0:T(8,128)} %get-tuple-element.25), calls=%async_computation.1 | async-start | bytes 2621440 | tf_op jit(solution)/shard_map/all_to_all | solution.py:779

commit v4 on v3

v4 whole, which is shorter than its diff:
```python
import functools

import jax
import jax.numpy as jnp
from jax import lax
from jax.experimental import pallas as pl
from jax.experimental.pallas import tpu as pltpu
from jax.sharding import PartitionSpec as P

F32 = jnp.float32
BF16 = jnp.bfloat16
I32 = jnp.int32
VMEM = pltpu.VMEM
SMEM = pltpu.SMEM
LANES = 128
EDGE = 16
HALO = 8
PARTS = 8


def hbm():
    return pl.BlockSpec(memory_space=pltpu.HBM)


def vmem():
    return pl.BlockSpec(memory_space=VMEM)


def pin(*arrays):
    return [pltpu.with_memory_space_constraint(a, pltpu.HBM) for a in arrays]


def start_all(pairs, sems, first=0):
    copies = [pltpu.make_async_copy(src, dst, sems.at[first + n]) for n, (src, dst) in enumerate(pairs)]
    for copy in copies:
        copy.start()
    return copies


def wait_all(copies):
    for copy in copies:
        copy.wait()


def iota(shape, dim):
    return lax.broadcasted_iota(I32, shape, dim)


def pick(mask, value):
    return jnp.where(mask, value, 0.0)


def split(value):
    high = value.astype(BF16)
    return high, (value - high.astype(F32)).astype(BF16)


def back_rows(capacity):
    return 2 * capacity + max(8, capacity)


def remap_out_kernel(
    capacity, grid_y, tile_rows, block_h, owner_h, row_h, tile_h, atm_h, weights_h, out_h, winds_h,
    out, winds, block_s, owner_s, row_s, tile_s, atm, weights, flux, every, fill, rows_acc, cols_acc, sems, weight_sems, out_sems,
):
    devices = fill.shape[0]
    npairs = block_s.shape[0]
    tiles = weights.shape[0]
    four = flux.shape[0]
    nblocks = four // 4
    span = 2 * capacity
    message = span + EDGE
    copies = [
        pltpu.make_async_copy(src, dst, sems.at[n])
        for n, (src, dst) in enumerate(
            [(atm_h, atm), (block_h, block_s), (owner_h, owner_s), (row_h, row_s), (tile_h, tile_s)]
        )
    ]
    for copy in copies:
        copy.start()
    part_tiles = tiles // PARTS
    parts = [pl.ds(n * part_tiles, part_tiles) for n in range(PARTS)]
    loads = [pltpu.make_async_copy(weights_h.at[at], weights.at[at], weight_sems.at[n]) for n, at in enumerate(parts)]
    for load in loads:
        load.start()
    out[...] = jnp.zeros_like(out)
    winds[...] = jnp.zeros_like(winds)
    rows_acc[...] = jnp.zeros_like(rows_acc)
    cols_acc[...] = jnp.zeros_like(cols_acc)

    def clear_fill(i, carry):
        fill[i] = 0
        return carry

    lax.fori_loop(0, devices, clear_fill, 0, unroll=16)
    copies[0].wait()
    wind_u = atm[0:1, :]
    wind_v = atm[1:2, :]
    speed = jnp.sqrt(wind_u * wind_u + wind_v * wind_v + 0.25)
    heat = 0.5 * speed * (atm[2:3, :] - atm[5:6, :])
    water = atm[4:5, :] - 0.3 * speed * atm[3:4, :]
    for f, plane in enumerate([heat, water, 0.2 * speed * wind_u, 0.2 * speed * wind_v]):
        for b in range(nblocks):
            flux[f * nblocks + b : f * nblocks + b + 1, :] = plane[:, b * LANES : (b + 1) * LANES]
    source = flux[...].astype(BF16)

    for n in range(PARTS):
        loads[n].wait()

        def tile_step(t, carry):
            every[pl.ds(pl.multiple_of(t * four, 8), four), :] = jnp.dot(
                source, weights[t], preferred_element_type=F32
            )
            return carry

        lax.fori_loop(n * part_tiles, (n + 1) * part_tiles, tile_step, 0, unroll=4)
    for copy in copies[1:]:
        copy.wait()

    sub = iota((8, LANES), 0)
    lane = iota((8, LANES), 1)
    part = sub % 4
    edge_row = jnp.where(part == 0, 0, jnp.where(part == 1, 1, tile_rows - 4 + part))
    edge_col = lane == jnp.where(part == 0, 0, jnp.where(part == 1, 1, LANES - 4 + part))
    col_lane = lane - 64 * (sub // 4)
    id_rank = jnp.where((sub == 0) & (lane >= 64), (lane - 64) // 2, -1)

    def pair(p, carry):
        owner = owner_s[p]
        row = row_s[p]
        rank = fill[owner]
        fill[owner] = rank + 1
        first = tile_s[p] * four + block_s[p]
        lines = [every[pl.ds(first + f * nblocks, 1), :] for f in range(4)]
        for f in range(2):
            out[pl.ds(owner * message + 2 * rank + f, 1), :] = lines[f]
            winds[pl.ds(owner * span + 2 * rank + f, 1), :] = lines[2 + f]
        tracer = jnp.where(sub < 4, lines[0], lines[1])
        rows_acc[owner] = rows_acc[owner] + pick(edge_row == row, tracer)
        column = jnp.sum(pick(edge_col, tracer), axis=1, keepdims=True)
        number = (row + 1).astype(F32)
        cols_acc[owner] = cols_acc[owner] + (
            pick(col_lane == row, column) + pick(id_rank == rank, number)
        )
        return carry

    lax.fori_loop(0, npairs, pair, 0, unroll=8)
    stores = start_all([(winds, winds_h)], out_sems, 4)

    grid_x = devices // grid_y
    zero = jnp.zeros((8, LANES), F32)
    inside = ((sub < 4) & (lane < 64)) | (sub >= 4)
    folds = {}

    def fold(i, j):
        if not (0 <= i < grid_x and 0 <= j < grid_y):
            return zero
        d = i * grid_y + j
        if d not in folds:
            kept = pick(inside, cols_acc[d])
            folds[d] = kept + pltpu.roll(kept, 4, 0)
        return folds[d]

    last = (lane == tile_rows - 1) | (lane == 64 + tile_rows - 1)
    first = (lane == 0) | (lane == 64)
    send = devices // 4
    for d in range(devices):
        i, j = d // grid_y, d % grid_y
        below = rows_acc[d + grid_y] if i < grid_x - 1 else zero
        above = rows_acc[d - grid_y] if i > 0 else zero
        base = d * message + span
        out[base : base + 8, :] = jnp.where(part < 2, below, above)
        if i > 1:
            folds.pop(d - 2 * grid_y, None)
        right, left = fold(i, j + 1), fold(i, j - 1)
        tile = pick(sub < 2, right) + pick((sub == 2) | (sub == 3), left)
        tile = tile + pick((sub == 4) & last, fold(i - 1, j + 1)) + pick((sub == 4) & first, fold(i + 1, j + 1))
        tile = tile + pick((sub == 7) & last, fold(i - 1, j - 1)) + pick((sub == 7) & first, fold(i + 1, j - 1))
        numbers = pltpu.roll(cols_acc[d], 5, 0)
        tile = tile + pick((sub == 5) & (lane >= 64), numbers)
        out[base + 8 : base + 16, :] = tile
        if d % send == send - 1:
            n = d // send
            at = pl.ds(n * send * message, send * message)
            stores.append(pltpu.make_async_copy(out.at[at], out_h.at[at], out_sems.at[n]))
            stores[-1].start()
    for store in stores:
        store.wait()


def remap_out(capacity, grid_y, devices, tile_rows, atm_state, pair_block, owner, pair_row, pair_tile, remap_weight):
    npairs = pair_block.shape[0]
    nblocks = atm_state.shape[1] // LANES
    span = 2 * capacity
    message = span + EDGE
    tiles = remap_weight.shape[0]
    return pl.pallas_call(
        functools.partial(remap_out_kernel, capacity, grid_y, tile_rows),
        out_shape=(pltpu.HBM((devices * message, LANES), F32), pltpu.HBM((devices * span, LANES), F32)),
        in_specs=[hbm()] * 6,
        out_specs=(hbm(), hbm()),
        scratch_shapes=[pltpu.VMEM((devices * message, LANES), F32), pltpu.VMEM((devices * span, LANES), F32)]
        + [pltpu.SMEM((npairs,), I32)] * 4
        + [
            pltpu.VMEM(atm_state.shape, F32),
            pltpu.VMEM(remap_weight.shape, BF16),
            pltpu.VMEM((4 * nblocks, LANES), F32),
            pltpu.VMEM((tiles * 4 * nblocks, LANES), F32),
            pltpu.SMEM((devices,), I32),
            pltpu.VMEM((devices, 8, LANES), F32),
            pltpu.VMEM((devices, 8, LANES), F32),
            pltpu.SemaphoreType.DMA((5,)),
            pltpu.SemaphoreType.DMA((PARTS,)),
            pltpu.SemaphoreType.DMA((5,)),
        ],
        compiler_params=pltpu.CompilerParams(vmem_limit_bytes=40 << 20),
        cost_estimate=pl.CostEstimate(
            flops=2 * tiles * 4 * nblocks * LANES * LANES, bytes_accessed=6 << 20, transcendentals=0
        ),
    )(*pin(pair_block, owner, pair_row, pair_tile, atm_state, remap_weight))


def solve_kernel(
    state, kappa, horiz, wet, tracer, top, currents_h, edge_up, edge_down, top_up, top_down, currents, sems
):
    levels = kappa.shape[0]
    rows_all = kappa.shape[1]
    planes = tracer.shape[0]

    def chunk(c, carry):
        rows = pl.ds(pl.multiple_of(c * 8, 8), 8)
        column = [kappa[l, rows, :] for l in range(levels)]
        face = [0.5 * (column[l] + column[l + 1]) for l in range(levels - 1)]
        upper = []
        now = None
        for l in range(levels):
            diagonal = 1.0
            if l > 0:
                diagonal = diagonal + face[l - 1]
            if l < levels - 1:
                diagonal = diagonal + face[l]
            if l > 0:
                diagonal = diagonal + face[l - 1] * upper[-1]
            inverse = 1.0 / diagonal
            if l == 0:
                now = [state[f, 0, rows, :] * inverse for f in range(4)] + [inverse]
            else:
                pull = face[l - 1] * inverse
                now = [state[f, l, rows, :] * inverse + pull * now[f] for f in range(4)] + [pull * now[4]]
            upper.append(-face[l] * inverse if l < levels - 1 else None)
            store(l, rows, now)
        for l in range(levels - 2, -1, -1):
            here = load(l, rows)
            now = [here[f] - upper[l] * now[f] for f in range(5)]
            store(l, rows, now)
        return carry

    def store(l, rows, now):
        tracer[l, rows, :] = now[0]
        tracer[levels + l, rows, :] = now[1]
        currents[0, l, rows, :] = now[2]
        currents[1, l, rows, :] = now[3]
        tracer[2 * levels + l, rows, :] = now[4]

    def load(l, rows):
        return [
            tracer[l, rows, :],
            tracer[levels + l, rows, :],
            currents[0, l, rows, :],
            currents[1, l, rows, :],
            tracer[2 * levels + l, rows, :],
        ]

    lax.fori_loop(0, rows_all // 8, chunk, 0)
    out = start_all([(currents, currents_h)], sems)
    tracer[3 * levels] = horiz[...]
    tracer[3 * levels + 1] = wet[...].astype(F32)
    for k in range(planes):
        edge_up[k] = tracer[k, 0:8, :]
        edge_down[k] = tracer[k, rows_all - 8 : rows_all, :]
    for n, k in enumerate([0, levels, 2 * levels, 3 * levels, 3 * levels + 1]):
        top[n] = tracer[k]
        top_up[n] = edge_up[k]
        top_down[n] = edge_down[k]
    wait_all(out)


def solve(ocean_state, vert_kappa, horiz_kappa, wet_mask):
    levels, rows, _ = vert_kappa.shape
    planes = 3 * levels + 2
    return pl.pallas_call(
        solve_kernel,
        out_shape=(
            jax.ShapeDtypeStruct((planes, rows, LANES), F32),
            jax.ShapeDtypeStruct((5, rows, LANES), F32),
            pltpu.HBM((2, levels, rows, LANES), F32),
            jax.ShapeDtypeStruct((planes, 8, LANES), F32),
            jax.ShapeDtypeStruct((planes, 8, LANES), F32),
            jax.ShapeDtypeStruct((5, 8, LANES), F32),
            jax.ShapeDtypeStruct((5, 8, LANES), F32),
        ),
        in_specs=[vmem()] * 4,
        out_specs=(vmem(), vmem(), hbm()) + (vmem(),) * 4,
        scratch_shapes=[pltpu.VMEM((2, levels, rows, LANES), F32), pltpu.SemaphoreType.DMA((1,))],
        compiler_params=pltpu.CompilerParams(vmem_limit_bytes=24 << 20),
        cost_estimate=pl.CostEstimate(flops=20 << 20, bytes_accessed=6 << 20, transcendentals=0),
    )(ocean_state, vert_kappa, horiz_kappa, wet_mask)


def pack_kernel(levels, tracer, above, below, wide_h, to_left, to_right, wide, sems):
    planes, rows, _ = tracer.shape
    for k in range(planes):
        wide[k, 0:HALO, :] = above[k]
        wide[k, HALO : HALO + rows, :] = tracer[k]
        wide[k, HALO + rows : 2 * HALO + rows, :] = below[k]
    out = start_all([(wide, wide_h)], sems)
    lane = iota((8, LANES), 1)

    def chunk(c, carry):
        at = pl.ds(pl.multiple_of(c * 8, 8), 8)

        def place(values, lanes):
            left, right = jnp.zeros((8, LANES), F32), jnp.zeros((8, LANES), F32)
            for k, (near, far) in zip(values, lanes):
                value = wide[k, at, :]
                left = jnp.where(lane == near, pltpu.roll(value, near, 1), left)
                left = jnp.where(lane == far, pltpu.roll(value, far - 1, 1), left)
                right = jnp.where(lane == near + 1, pltpu.roll(value, (near + 2) % LANES, 1), right)
                right = jnp.where(lane == far + 1, pltpu.roll(value, (far + 3) % LANES, 1), right)
            return left, right

        left, right = place(range(2 * levels), [(2 * k, 64 + 2 * k) for k in range(2 * levels)])
        lanes = [(2 * l, 64 + 2 * l) for l in range(levels)]
        lanes += [(2 * levels, 2 * levels + 2), (2 * levels + 4, 2 * levels + 6)]
        left_unit, right_unit = place(range(2 * levels, 3 * levels + 2), lanes)
        if to_left.shape[0] == 1:
            to_left[0, at, :] = left + pltpu.roll(left_unit, 32, 1)
            to_right[0, at, :] = right + pltpu.roll(right_unit, 32, 1)
        else:
            to_left[0, at, :], to_left[1, at, :] = left, left_unit
            to_right[0, at, :], to_right[1, at, :] = right, right_unit
        return carry

    lax.fori_loop(0, (rows + 2 * HALO) // 8, chunk, 0)
    wait_all(out)


def pack(levels, tracer, above, below):
    planes, rows, _ = tracer.shape
    tall = rows + 2 * HALO
    arrays = 1 if levels == 1 else 2
    return pl.pallas_call(
        functools.partial(pack_kernel, levels),
        out_shape=(
            pltpu.HBM((planes, tall, LANES), F32),
            jax.ShapeDtypeStruct((arrays, tall, LANES), F32),
            jax.ShapeDtypeStruct((arrays, tall, LANES), F32),
        ),
        in_specs=[vmem()] * 3,
        out_specs=(hbm(), vmem(), vmem()),
        scratch_shapes=[pltpu.VMEM((planes, tall, LANES), F32), pltpu.SemaphoreType.DMA((1,))],
        compiler_params=pltpu.CompilerParams(vmem_limit_bytes=24 << 20),
        cost_estimate=pl.CostEstimate(flops=8 << 20, bytes_accessed=4 << 20, transcendentals=0),
    )(tracer, above, below)


def packed_pair(ref):
    value = ref[0]
    if ref.shape[0] > 1:
        return value, ref[1]
    return value, pltpu.roll(value, LANES - 32, 1)


def set_faces(levels, h, w, own_left, own_right, from_left, from_right, faces, packed):
    tall = h.shape[0]
    lane = iota((tall, LANES), 1)
    odd = lane % 2 == 1
    twice = lane % 64 < 2 * levels
    (left, left_unit), (right, right_unit) = packed_pair(from_left), packed_pair(from_right)
    other = jnp.where(odd, left_unit, right_unit)
    at = 2 * levels

    def column(offset):
        return other[:, at + offset : at + offset + 1], other[:, at + offset + 1 : at + offset + 2]

    kappa_right, kappa_left = column(0)
    kappa_far_right, kappa_far_left = column(2)
    wet_right, wet_left = column(4)
    wet_far_right, wet_far_left = column(6)

    kappa_near = jnp.where(odd, kappa_left, kappa_right)
    kappa_far = jnp.where(odd, kappa_far_left, kappa_far_right)
    wet_near = jnp.where(odd, wet_left, wet_right)
    wet_far = jnp.where(odd, wet_far_left, wet_far_right)
    kappa_own = jnp.where(odd, h[:, 0:1], h[:, LANES - 1 : LANES])
    wet_own = jnp.where(odd, w[:, 0:1], w[:, LANES - 1 : LANES])

    def face(kappa_a, wet_a, kappa_b, wet_b):
        return 0.25 * (kappa_a + kappa_b) * wet_a * wet_b

    unit = jnp.where(twice, other, pltpu.roll(other, 2 * levels, 1))
    packed[0] = jnp.where(odd, left, right)
    packed[1] = unit * jnp.where(lane < 64, wet_near, wet_far)
    (left, left_unit), (right, right_unit) = packed_pair(own_left), packed_pair(own_right)
    packed[2] = jnp.where(odd, pltpu.roll(left, 1, 1), pltpu.roll(right, LANES - 1, 1))
    own = jnp.where(odd, pltpu.roll(left_unit, 1, 1), pltpu.roll(right_unit, LANES - 1, 1))
    packed[3] = jnp.where(twice, own, pltpu.roll(own, 2 * levels, 1)) * wet_own
    north = face(kappa_near, wet_near, pltpu.roll(kappa_near, 1, 0), pltpu.roll(wet_near, 1, 0))
    packed[4] = north
    packed[5] = pltpu.roll(north, tall - 1, 0)
    packed[6] = face(kappa_near, wet_near, kappa_far, wet_far)
    packed[7] = face(kappa_near, wet_near, kappa_own, wet_own)

    north = face(h, w, pltpu.roll(h, 1, 0), pltpu.roll(w, 1, 0))
    faces[0] = north
    faces[1] = pltpu.roll(north, tall - 1, 0)
    west = face(
        h, w, jnp.where(lane == 0, kappa_left, pltpu.roll(h, 1, 1)), jnp.where(lane == 0, wet_left, pltpu.roll(w, 1, 1))
    )
    faces[2] = west
    faces[3] = jnp.where(lane == LANES - 1, face(h, w, kappa_right, wet_right), pltpu.roll(west, LANES - 1, 1))


def set_beside(levels, upright, wide, packed, beside):
    tall = upright.shape[0]
    lane = iota((tall, LANES), 1)
    odd = lane % 2 == 1
    heat = lane % 64 < 2 * levels

    def chosen(f):
        right_near, right_far, left_far, left_near = [upright[:, 4 * f + e : 4 * f + e + 1] for e in range(4)]
        near = jnp.where(odd, left_near, right_near)
        return jnp.where(lane < 64, near, jnp.where(odd, left_far, right_far))

    both = packed[0] + packed[1] * jnp.where(heat, chosen(0), chosen(1))
    far = pltpu.roll(both, 64, 1)
    ends_of = [jnp.where(odd, w[:, 0:1], w[:, LANES - 1 : LANES]) for w in wide]
    own = packed[2] + packed[3] * jnp.where(heat, ends_of[0], ends_of[1])
    near = both + packed[5] * (pltpu.roll(both, tall - 1, 0) - both)
    near = near + packed[4] * (pltpu.roll(both, 1, 0) - both)
    near = near + packed[6] * (far - both)
    near = near + packed[7] * (own - both)
    beside[0] = both
    beside[1] = near


def one_pass(value, faces, beside, shift):
    tall = value.shape[0]
    lane = iota(value.shape, 1)
    moved = pltpu.roll(beside, shift, 1)
    west = jnp.where(lane == 0, moved, pltpu.roll(value, 1, 1))
    east = jnp.where(lane == LANES - 1, moved, pltpu.roll(value, LANES - 1, 1))
    result = value + faces[1] * (pltpu.roll(value, tall - 1, 0) - value)
    result = result + faces[0] * (pltpu.roll(value, 1, 0) - value)
    result = result + faces[3] * (east - value)
    return result + faces[2] * (west - value)


def set_forcing(span, numbers, rows_all, arrived, placing, values):
    devices = arrived.shape[0]
    row_number = iota((rows_all, LANES), 0).astype(F32) + 1.0
    lane_field = iota((rows_all, LANES), 1) % 2
    for m, line in enumerate(numbers):
        hit = line == row_number
        for f in range(2):
            placing[f * rows_all : (f + 1) * rows_all, m * LANES : (m + 1) * LANES] = jnp.where(
                hit & (lane_field == f), 1.0, 0.0
            ).astype(BF16)
    for s in range(0, devices, 16 // min(16, span)):
        many = 16 // min(16, span)
        high, low = split(jnp.concatenate([arrived[s + n, 0:span, :] for n in range(many)], 0))
        values[s * span : (s + many) * span, 0:LANES] = high
        values[s * span : (s + many) * span, LANES : 2 * LANES] = low
    total = jnp.dot(placing[...], values[...], preferred_element_type=F32)
    total = total[:, 0:LANES] + total[:, LANES : 2 * LANES]
    return [total[f * rows_all : (f + 1) * rows_all] for f in range(2)]


def wanted(rows_all):
    lane_t = iota((LANES, 2 * rows_all), 1)
    sub_t = iota((LANES, 2 * rows_all), 0)
    return jnp.where(sub_t % 2 == lane_t // rows_all, lane_t % rows_all + 1, -1).astype(F32)


def picked_rows(column, target, source):
    rows = jnp.dot(jnp.where(column == target, 1.0, 0.0).astype(BF16), source, preferred_element_type=F32)
    return rows[:, 0:LANES] + rows[:, LANES : 2 * LANES]


def two_parts(surface):
    high, low = split(jnp.concatenate(surface, 0))
    return jnp.concatenate([high, low], 1)


def tracer_kernel(
    capacity, arrived, wide_h, own_left, own_right, from_left, from_right,
    sent_h, forcing_h, upright_h, numbers_h, number_t_h,
    placing, values, number_t, lines, top, faces, packed, beside, sent, forcing, upright, sems, sent_sems,
):
    devices = arrived.shape[0]
    tall = top.shape[1]
    rows_all = tall - 2 * HALO
    span = 2 * capacity
    group = LANES // span
    groups = devices // group
    sub8 = iota((8, LANES), 0)
    lane8 = iota((8, LANES), 1)
    loads = start_all([(wide_h, top)], sems)

    lane1 = iota((1, LANES), 1)
    numbers = []
    for m in range(groups):
        line = jnp.zeros((1, LANES), F32)
        for g in range(group):
            ids = arrived[m * group + g, span + 13 : span + 14, :]
            moved = pltpu.roll(ids, (g * span - 64) % LANES, 1)
            line = jnp.where(lane1 // span == g, moved, line)
        numbers.append(line)
        lines[m : m + 1, :] = line
    number_t[...] = jnp.transpose(
        jnp.concatenate(numbers + [jnp.zeros((LANES - groups, LANES), F32)], 0)
    )
    stores = start_all([(lines, numbers_h), (number_t, number_t_h)], sems, 1)

    planes = set_forcing(span, numbers, rows_all, arrived, placing, values)
    edge_rows = jnp.zeros((8, LANES), F32)
    edge_cols = jnp.zeros((8, LANES), F32)
    for s in range(devices):
        edge_rows = edge_rows + arrived[s, span : span + 8, :]
        edge_cols = edge_cols + arrived[s, span + 8 : span + 16, :]
    wide = []
    for f in range(2):
        before = pick(sub8 >= 6, edge_rows if f == 1 else pltpu.roll(edge_rows, 4, 0))
        after = pick(sub8 < 2, edge_rows if f == 0 else pltpu.roll(edge_rows, 4, 0))
        wide.append(jnp.concatenate([before, planes[f], after], 0))
        forcing[f] = wide[f]

    corner = pick((sub8 == 0) | (sub8 == 3), pltpu.roll(edge_cols, 4, 0))
    side = pick(sub8 < 4, edge_cols)
    within = (lane8 >= HALO) & (lane8 < HALO + rows_all)
    ends = (lane8 == HALO - 1) | (lane8 == HALO + rows_all)
    halves = []
    for f in range(2):
        body = pltpu.roll(side, (HALO - 64 * f) % LANES, 1)
        tips = pltpu.roll(corner, (HALO + rows_all - 64 * f) % LANES, 1)
        halves.append((pick(within, body) + pick(ends, tips))[0:4])
    columns = jnp.concatenate(halves, 0)
    upright[...] = jnp.transpose(jnp.concatenate([columns, jnp.zeros((LANES - 8, LANES), F32)], 0))[0:tall]
    stores += start_all([(forcing, forcing_h), (upright, upright_h)], sems, 3)

    wait_all(loads)
    set_faces(1, top[3], top[4], own_left, own_right, from_left, from_right, faces, packed)
    set_beside(1, upright[...], wide, packed, beside)
    wet = top[4, HALO : HALO + rows_all, :]
    unit = top[2] * top[4]
    surface = []
    for f in range(2):
        value = top[f] + unit * wide[f]
        shift = LANES - (2 * f + 1)
        value = one_pass(value, faces, beside[0], shift)
        value = one_pass(value, faces, beside[1], shift)
        surface.append(value[HALO : HALO + rows_all] * wet)
    source = two_parts(surface)
    target = wanted(rows_all)
    mask = jnp.concatenate([wet, jnp.zeros((LANES - rows_all, LANES), F32)], 0).astype(BF16)
    per = LANES // 2
    slot_number = number_t[pl.ds(0, per, stride=2), :]
    lane_s = (iota((per, LANES), 1) + 1).astype(F32)
    height = back_rows(capacity)
    for m in range(groups):
        rows = picked_rows(number_t[:, m : m + 1], target, source)
        slots = jnp.where(slot_number[:, m : m + 1] == lane_s, 1.0, 0.0).astype(BF16)
        masks = jnp.dot(slots, mask, preferred_element_type=F32)
        for g in range(group):
            s = m * group + g
            sent[s, 0:span, :] = rows[g * span : (g + 1) * span]
            sent[s, span : span + capacity, :] = masks[g * capacity : (g + 1) * capacity]
            if height > span + capacity:
                sent[s, span + capacity : height, :] = jnp.zeros((height - span - capacity, LANES), F32)
        at = pl.ds(m * group, group)
        stores += start_all([(sent.at[at], sent_h.at[at])], sent_sems, m)
    wait_all(stores)


def tracer_surface(capacity, arrived, wide, own_left, own_right, from_left, from_right):
    devices = arrived.shape[0]
    tall = wide.shape[1]
    rows = tall - 2 * HALO
    height = back_rows(capacity)
    slots = 2 * capacity * devices
    groups = slots // LANES
    return pl.pallas_call(
        functools.partial(tracer_kernel, capacity),
        out_shape=(
            pltpu.HBM((devices, height, LANES), F32),
            pltpu.HBM((2, tall, LANES), F32),
            pltpu.HBM((tall, LANES), F32),
            pltpu.HBM((groups, LANES), F32),
            pltpu.HBM((LANES, LANES), F32),
        ),
        in_specs=[vmem(), hbm()] + [vmem()] * 4,
        out_specs=(hbm(),) * 5,
        scratch_shapes=[
            pltpu.VMEM((2 * rows, slots), BF16),
            pltpu.VMEM((slots, 2 * LANES), BF16),
            pltpu.VMEM((LANES, LANES), F32),
            pltpu.VMEM((groups, LANES), F32),
            pltpu.VMEM((5, tall, LANES), F32),
            pltpu.VMEM((4, tall, LANES), F32),
            pltpu.VMEM((8, tall, LANES), F32),
            pltpu.VMEM((2, tall, LANES), F32),
            pltpu.VMEM((devices, height, LANES), F32),
            pltpu.VMEM((2, tall, LANES), F32),
            pltpu.VMEM((tall, LANES), F32),
            pltpu.SemaphoreType.DMA((5,)),
            pltpu.SemaphoreType.DMA((groups,)),
        ],
        compiler_params=pltpu.CompilerParams(vmem_limit_bytes=24 << 20),
        cost_estimate=pl.CostEstimate(flops=100 << 20, bytes_accessed=4 << 20, transcendentals=0),
    )(arrived, *pin(wide), own_left, own_right, from_left, from_right)


def current_kernel(
    capacity, arrived, wide_h, currents_h, numbers_h, number_t_h, sent_h, forcing_h,
    placing, values, lines, number_t, top, base, sent, forcing, sems, sent_sems,
):
    devices = arrived.shape[0]
    rows_all = base.shape[1]
    span = 2 * capacity
    group = LANES // span
    groups = devices // group
    loads = start_all(
        [
            (numbers_h, lines),
            (number_t_h, number_t),
            (wide_h.at[pl.ds(2, 3)], top),
            (currents_h.at[0, 0], base.at[0]),
            (currents_h.at[1, 0], base.at[1]),
        ],
        sems,
    )
    wait_all(loads)
    planes = set_forcing(span, [lines[m : m + 1, :] for m in range(groups)], rows_all, arrived, placing, values)
    wet = top[2, HALO : HALO + rows_all, :]
    unit = top[0, HALO : HALO + rows_all, :]
    surface = []
    for f in range(2):
        forcing[f] = planes[f] * wet
        surface.append((base[f] + unit * forcing[f]) * wet)
    stores = start_all([(forcing, forcing_h)], sems, 5)
    source = two_parts(surface)
    target = wanted(rows_all)
    for m in range(groups):
        rows = picked_rows(number_t[:, m : m + 1], target, source)
        for g in range(group):
            sent[m * group + g] = rows[g * span : (g + 1) * span]
        at = pl.ds(m * group, group)
        stores += start_all([(sent.at[at], sent_h.at[at])], sent_sems, m)
    wait_all(stores)


def current_surface(capacity, arrived, wide, currents, numbers, number_t):
    devices, span, _ = arrived.shape
    rows = currents.shape[2]
    tall = rows + 2 * HALO
    slots = span * devices
    groups = slots // LANES
    return pl.pallas_call(
        functools.partial(current_kernel, capacity),
        out_shape=(pltpu.HBM((devices, span, LANES), F32), pltpu.HBM((2, rows, LANES), F32)),
        in_specs=[vmem()] + [hbm()] * 4,
        out_specs=(hbm(),) * 2,
        scratch_shapes=[
            pltpu.VMEM((2 * rows, slots), BF16),
            pltpu.VMEM((slots, 2 * LANES), BF16),
            pltpu.VMEM((groups, LANES), F32),
            pltpu.VMEM((LANES, LANES), F32),
            pltpu.VMEM((3, tall, LANES), F32),
            pltpu.VMEM((2, rows, LANES), F32),
            pltpu.VMEM((devices, span, LANES), F32),
            pltpu.VMEM((2, rows, LANES), F32),
            pltpu.SemaphoreType.DMA((6,)),
            pltpu.SemaphoreType.DMA((groups,)),
        ],
        compiler_params=pltpu.CompilerParams(vmem_limit_bytes=24 << 20),
        cost_estimate=pl.CostEstimate(flops=100 << 20, bytes_accessed=3 << 20, transcendentals=0),
    )(arrived, *pin(wide, currents, numbers, number_t))


def finish_kernel(
    levels, wide_h, currents_h, forcing_h, push_h, upright_h, own_left, own_right, from_left, from_right, ocean,
    wide, currents, forcing, push, upright, faces, packed, beside, sems,
):
    rows_all = currents.shape[2]
    inner = slice(HALO, HALO + rows_all)
    wait_all(
        start_all(
            [(wide_h, wide), (currents_h, currents), (forcing_h, forcing), (push_h, push), (upright_h, upright)], sems
        )
    )
    set_faces(
        levels, wide[3 * levels], wide[3 * levels + 1], own_left, own_right, from_left, from_right, faces, packed
    )
    set_beside(levels, upright[...], [forcing[0], forcing[1]], packed, beside)

    def level(l, carry):
        unit = wide[2 * levels + l]
        masked = unit * wide[3 * levels + 1]
        for f in range(2):
            value = wide[f * levels + l] + masked * forcing[f]
            shift = LANES - 1 - 2 * (levels * f + l)
            value = one_pass(value, faces, beside[0], shift)
            value = one_pass(value, faces, beside[1], shift)
            ocean[f, l] = value[inner]
            ocean[2 + f, l] = currents[f, l] + unit[inner] * push[f]
        return carry

    lax.fori_loop(0, levels, level, 0)


def finish(levels, wide, currents, forcing, push, upright, own_left, own_right, from_left, from_right):
    rows = currents.shape[2]
    tall = rows + 2 * HALO
    return pl.pallas_call(
        functools.partial(finish_kernel, levels),
        out_shape=jax.ShapeDtypeStruct((4, levels, rows, LANES), F32),
        in_specs=[hbm()] * 5 + [vmem()] * 4,
        out_specs=vmem(),
        scratch_shapes=[pltpu.VMEM(a.shape, F32) for a in (wide, currents, forcing, push, upright)]
        + [pltpu.VMEM((n, tall, LANES), F32) for n in (4, 8, 2)]
        + [pltpu.SemaphoreType.DMA((5,))],
        compiler_params=pltpu.CompilerParams(vmem_limit_bytes=24 << 20),
        cost_estimate=pl.CostEstimate(flops=40 << 20, bytes_accessed=6 << 20, transcendentals=0),
    )(*pin(wide, currents, forcing, push, upright), own_left, own_right, from_left, from_right)


def remap_back_kernel(
    capacity, last, block_h, tile_h, owner_h, returned, weights_h, *refs
):
    if last:
        before_h, out, before = refs[0], refs[1], refs[-1]
        refs = refs[2:-1]
    else:
        out, refs = refs[0], refs[1:]
    block_s, tile_s, owner_s, fill, weights, picked, total, sems, weight_sems = refs
    npairs = block_s.shape[0]
    nblocks = total.shape[0]
    devices = fill.shape[0]
    span = 2 * capacity
    height = span if last else back_rows(capacity)
    scalars = start_all([(owner_h, owner_s), (block_h, block_s), (tile_h, tile_s)], sems)
    part_tiles = weights.shape[0] // PARTS
    parts = [pl.ds(n * part_tiles, part_tiles) for n in range(PARTS)]
    loads = start_all([(weights_h.at[at], weights.at[at]) for at in parts], weight_sems)
    if last:
        loads += start_all([(before_h, before)], sems, 3)
    total[...] = jnp.zeros_like(total)

    def clear_fill(i, carry):
        fill[i] = 0
        return carry

    lax.fori_loop(0, devices, clear_fill, 0, unroll=16)
    wait_all(scalars)

    def gather(p, carry):
        owner = owner_s[p]
        rank = fill[owner]
        fill[owner] = rank + 1
        rows = [returned[pl.ds(owner * height + 2 * rank, 2), :]]
        if not last:
            rows.append(returned[pl.ds(owner * height + span + rank, 1), :])
        rows.append(jnp.zeros((6 if last else 5, LANES), F32))
        high, low = split(jnp.concatenate(rows, 0))
        picked[p] = jnp.concatenate([high, low], 0)
        return carry

    lax.fori_loop(0, npairs, gather, 0, unroll=8)
    wait_all(loads)

    def pair(p, carry):
        value = lax.dot_general(
            picked[p], weights[tile_s[p]], (((1,), (1,)), ((), ())), preferred_element_type=F32
        )
        b = block_s[p]
        total[b] = total[b] + (value[0:8] + value[8:16])
        return carry

    lax.fori_loop(0, npairs, pair, 0, unroll=16)
    if not last:
        wait_all(start_all([(total, out)], sems, 3))
        return
    for b in range(nblocks):
        sums = jnp.concatenate([before[b, 0:2, :], total[b, 0:2, :]], 0)
        out[:, b * LANES : (b + 1) * LANES] = sums / jnp.maximum(before[b, 2:3, :], 0.1)


def remap_back(capacity, devices, pair_block, pair_tile, owner, returned, remap_weight, nblocks, before=None):
    npairs = pair_block.shape[0]
    last = before is not None
    sums = (nblocks, 8, LANES)
    return pl.pallas_call(
        functools.partial(remap_back_kernel, capacity, last),
        out_shape=jax.ShapeDtypeStruct((4, nblocks * LANES), F32) if last else pltpu.HBM(sums, F32),
        in_specs=[hbm()] * 3 + [vmem(), hbm()] + [hbm()] * last,
        out_specs=vmem() if last else hbm(),
        scratch_shapes=[pltpu.SMEM((npairs,), I32)] * 3
        + [
            pltpu.SMEM((devices,), I32),
            pltpu.VMEM(remap_weight.shape, BF16),
            pltpu.VMEM((npairs, 16, LANES), BF16),
            pltpu.VMEM(sums, F32),
            pltpu.SemaphoreType.DMA((4,)),
            pltpu.SemaphoreType.DMA((PARTS,)),
        ]
        + [pltpu.VMEM(sums, F32)] * last,
        compiler_params=pltpu.CompilerParams(vmem_limit_bytes=24 << 20),
        cost_estimate=pl.CostEstimate(flops=2 * npairs * 16 * LANES * LANES, bytes_accessed=6 << 20, transcendentals=0),
    )(*pin(pair_block, pair_tile, owner), returned, *pin(remap_weight), *(pin(before) if last else []))


def local(
    atm_state,
    pair_block,
    pair_owner,
    pair_row,
    pair_tile,
    remap_weight,
    wet_mask,
    ocean_state,
    vert_kappa,
    horiz_kappa,
):
    grid_x = lax.axis_size("gx")
    grid_y = lax.axis_size("gy")
    devices = grid_x * grid_y
    npairs = pair_block.shape[0]
    capacity = max(2, 2 * npairs // devices)
    levels, tile_rows, _ = vert_kappa.shape
    nblocks = atm_state.shape[1] // LANES
    owner = pair_owner.reshape(npairs)
    span = 2 * capacity

    def exchange(array, rows):
        array = array.reshape(devices, rows, LANES)
        return lax.all_to_all(array, ("gx", "gy"), split_axis=0, concat_axis=0, tiled=True)

    def both_ways(axis, count, backward, forward):
        rise = [(i, i + 1) for i in range(count - 1)]
        return lax.ppermute(forward, axis, rise), lax.ppermute(backward, axis, [(b, a) for a, b in rise])

    outgoing, outgoing_winds = remap_out(
        capacity, grid_y, devices, tile_rows, atm_state, pair_block, owner, pair_row, pair_tile, remap_weight
    )
    arrived = exchange(outgoing, span + EDGE)
    arrived_winds = exchange(outgoing_winds, span)
    tracer, top, currents, edge_up, edge_down, top_up, top_down = solve(
        ocean_state, vert_kappa, horiz_kappa, wet_mask
    )
    above, below = both_ways("gx", grid_x, top_up, top_down)
    top_wide, *top_own = pack(1, top, above, below)
    top_beside = both_ways("gy", grid_y, *top_own)
    sent, forcing, upright, numbers, number_t = tracer_surface(capacity, arrived, top_wide, *top_own, *top_beside)
    returned = exchange(sent, back_rows(capacity))
    above, below = both_ways("gx", grid_x, edge_up, edge_down)
    wide, *own = pack(levels, tracer, above, below)
    beside = both_ways("gy", grid_y, *own)
    sent_winds, push = current_surface(capacity, arrived_winds, top_wide, currents, numbers, number_t)
    returned_winds = exchange(sent_winds, span)
    ocean_next = finish(levels, wide, currents, forcing, push, upright, *own, *beside)
    pairs = (capacity, devices, pair_block, pair_tile, owner)
    sums = remap_back(*pairs, returned.reshape(-1, LANES), remap_weight, nblocks)
    atm_surface = remap_back(*pairs, returned_winds.reshape(-1, LANES), remap_weight, nblocks, sums)
    return (ocean_next, atm_surface)


def solution(mesh):
    placed = (
        P(None, ("gx", "gy")),
        P(("gx", "gy")),
        P(("gx", "gy"), None),
        P(("gx", "gy")),
        P(("gx", "gy")),
        P(("gx", "gy"), None, None),
        P("gx", "gy"),
        P(None, None, "gx", "gy"),
        P(None, "gx", "gy"),
        P("gx", "gy"),
    )
    return jax.shard_map(
        local,
        mesh=mesh,
        in_specs=placed,
        out_specs=(P(None, None, "gx", "gy"), P(None, ("gx", "gy"))),
        check_vma=False,
    )
```

time: 105 us -> 150 us (1.43)
  blocking collectives: 0 us -> 27.9 us
  Pallas kernels: 40.8 us -> 51.7 us
  starting transfers between devices: 24.4 us -> 34.2 us
  waiting for transfers between devices: 37.4 us -> 31.2 us
  local copies, waits for them, and re-layouts: 1.06 us -> 2.92 us
    all_to_all x0 -> x1, blocking collectives: none -> 27.9 us  [exchange(): lax.all_to_all(array, ('gx', 'gy'), split_axis=0, concat_axis=0, tiled=True)]
    ppermute x4 -> x8, starting transfers between devices: 10.7 us -> 21.8 us  [the longest x4 15.4 us: both_ways(): lax.ppermute(forward, axis, rise)]
    all_to_all x2 -> x3, waiting for transfers between devices: 27.4 us -> 18.4 us  [exchange(): lax.all_to_all(array, ('gx', 'gy'), split_axis=0, concat_axis=0, tiled=True)]
    pallas_call x3 -> x4, Pallas kernels: 15.7 us -> 24.5 us  [the longest x2 19 us: remap_back(): pl.pallas_call(functools.partial(remap_back_kernel, capacity, last), out_...]
    ppermute x4 -> x8, waiting for transfers between devices: 10 us -> 12.8 us  [the longest x4 8.31 us: both_ways(): lax.ppermute(backward, axis, [(b, a) for a, b in rise])]
    unnamed x8 -> x20, local copies, waits for them, and re-layouts: 1.06 us -> 2.92 us
    pallas_call x1 -> x2, Pallas kernels: 2.92 us -> 4.45 us  [pack(): pl.pallas_call(functools.partial(pack_kernel, levels), out_shape=(pltpu.H...]
    all_to_all x2 -> x3, starting transfers between devices: 13.7 us -> 12.4 us  [exchange(): lax.all_to_all(array, ('gx', 'gy'), split_axis=0, concat_axis=0, tiled=True)]
  transfers between devices with their start and end apart: 6 -> 11, of which waited for: 6 -> 6; matrix products, arithmetic and copies ran while one was open for 0% -> 0% of each run, Pallas kernels for 14% -> 20%
where the time goes in v4:
time: 150 us; the launch traced here: 149 us
  Pallas kernels  51.7 us (34%)
  starting transfers between devices  34.2 us (23%)
  waiting for transfers between devices  31.2 us (21%)
  blocking collectives  27.9 us (19%)
  local copies, waits for them, and re-layouts  2.92 us (2%)
    all_to_all x1, blocking collectives, exchange(): lax.all_to_all(array, ('gx', 'gy'), split_axis=0, concat_axis=0, tiled=True)  27.9 us
    pallas_call x2, Pallas kernels, remap_back(): pl.pallas_call(functools.partial(remap_back_kernel, capacity, last), out_...  19 us
    all_to_all x3, waiting for transfers between devices, exchange(): lax.all_to_all(array, ('gx', 'gy'), split_axis=0, concat_axis=0, tiled=True)  18.4 us
    ppermute x4, starting transfers between devices, both_ways(): lax.ppermute(forward, axis, rise)  15.4 us
    pallas_call x1, Pallas kernels, remap_out(): pl.pallas_call(functools.partial(remap_out_kernel, capacity, grid_y, tile...  12.8 us
    all_to_all x3, starting transfers between devices, exchange(): lax.all_to_all(array, ('gx', 'gy'), split_axis=0, concat_axis=0, tiled=True)  12.4 us
    ppermute x4, waiting for transfers between devices, both_ways(): lax.ppermute(backward, axis, [(b, a) for a, b in rise])  8.31 us
    pallas_call x1, Pallas kernels, finish(): pl.pallas_call(functools.partial(finish_kernel, levels), out_shape=jax.Sh...  7.39 us
  transfers between devices with their start and end apart: 11, of which 6 were waited for; matrix products, arithmetic and copies ran while one was open for 0% of the time, Pallas kernels for 20%

profile of v4, /device:TPU:1, one launch (start us, length us, event | category | flops | bytes accessed | tf_op | source)
XLA Modules:
  0.0 148.9 jit_solution(3290357833949704990)
XLA Ops:
  0.6 12.8 %shard_map.115 = (f32[1536,128]{1,0:T(8,128)}, f32[1024,128]{1,0:T(8,128)}) custom-call(s32[256]{0:T(256)} %block_h.5, s32[256]{0:T(256)} %bitcast.9, s32[256]{0:T(256)} %row_h.1, s32[256]{0:T(256)} %tile_h.5, f32[6,6144]{1,0:T(8,128)} %atm_h.1, bf16[128,128,128]{2,1,0:T(8,128)(2,1)} %weights_h.5), custom_call_target="tpu_custom_call" | custom-call | flops 805306368 | bytes 6291456 | tf_op jit(solution)/shard_map/pallas_call | solution.py:197
  13.4 27.9 %all_to_all.20.arrived = f32[32,48,128]{2,1,0:T(8,128)S(1)} all-to-all(f32[32,48,128]{2,1,0:T(8,128)} %bitcast.7), channel_id=1, replica_groups=mesh['gx'=8,'gy'=4] {'gx','gy'}, dimensions={0} | all-to-all | bytes 1572864 | tf_op jit(solution)/shard_map/all_to_all | solution.py:846
  41.4 3.2 %all-to-all-start.1 = ((f32[32,32,128]{2,1,0:T(8,128)}), f32[32,32,128]{2,1,0:T(8,128)S(1)}, u32[]{:S(2)}, u32[]{:S(2)}) async-start(f32[32,32,128]{2,1,0:T(8,128)} %bitcast.8), calls=%async_computation.1 | async-start | bytes 1048576 | tf_op jit(solution)/shard_map/all_to_all | solution.py:846
  45.6 2.6 %shard_map.113 = (f32[50,64,128]{2,1,0:T(8,128)S(1)}, f32[5,64,128]{2,1,0:T(8,128)S(1)}, f32[2,16,64,128]{3,2,1,0:T(8,128)}, f32[50,8,128]{2,1,0:T(8,128)S(1)}, ...) custom-call(f32[4,16,64,128]{3,2,1,0:T(8,128)S(1)} %copy-done, ...), custom_call_target="tpu_custom_call" | custom-call | flops 20971520 | bytes 6291456 | tf_op jit(solution)/shard_map/pallas_call | solution.py:291
  50.1 3.5 %collective-permute-start.2 = (f32[5,8,128]{2,1,0:T(8,128)S(1)}, f32[5,8,128]{2,1,0:T(8,128)S(1)}, u32[]{:S(2)}, u32[]{:S(2)}) collective-permute-start(f32[5,8,128]{2,1,0:T(8,128)S(1)} %get-tuple-element.31), channel_id=1, source_target_pairs={{0,4},{4,8},{8,12},{12,16},{16,20},{20,24},{24,28},{1,5},{5,9},{9,... | collective-permute-start | bytes 61448 | tf_op jit(solution)/shard_map/ppermute | solution.py:850
  53.6 1.9 %collective-permute-start.3 = (f32[5,8,128]{2,1,0:T(8,128)S(1)}, f32[5,8,128]{2,1,0:T(8,128)S(1)}, u32[]{:S(2)}, u32[]{:S(2)}) collective-permute-start(f32[5,8,128]{2,1,0:T(8,128)S(1)} %get-tuple-element.32), channel_id=1, source_target_pairs={{4,0},{8,4},{12,8},{16,12},{20,16},{24,20},{28,24},{5,1},{9,5},{13... | collective-permute-start | bytes 61448 | tf_op jit(solution)/shard_map/ppermute | solution.py:850
  55.6 3.3 %collective-permute-done.3.below = f32[5,8,128]{2,1,0:T(8,128)S(1)} collective-permute-done((f32[5,8,128]{2,1,0:T(8,128)S(1)}, f32[5,8,128]{2,1,0:T(8,128)S(1)}, u32[]{:S(2)}, u32[]{:S(2)}) %collective-permute-start.3) | collective-permute-done | bytes 20512 | tf_op jit(solution)/shard_map/ppermute | solution.py:850
  58.9 1.5 %shard_map.116 = (f32[5,80,128]{2,1,0:T(8,128)}, f32[1,80,128]{2,1,0:T(8,128)S(1)}, f32[1,80,128]{2,1,0:T(8,128)S(1)}) custom-call(f32[5,64,128]{2,1,0:T(8,128)S(1)} %get-tuple-element.30.tracer, f32[5,8,128]{2,1,0:T(8,128)S(1)} %collective-permute-done.2.above, f32[5,8,128]{2,1,0:T(8,128)S(1)} %collective-permute-done.3.below), custom_call_target="tpu_custom_call" | custom-call | flops 8388608 | bytes 4194304 | tf_op jit(solution)/shard_map/pallas_call | solution.py:352
  61.7 4.0 %collective-permute-start.4 = (f32[1,80,128]{2,1,0:T(8,128)S(1)}, f32[1,80,128]{2,1,0:T(8,128)S(1)}, u32[]{:S(2)}, u32[]{:S(2)}) collective-permute-start(f32[1,80,128]{2,1,0:T(8,128)S(1)} %get-tuple-element.35.own_right), channel_id=1, source_target_pairs={{0,1},{1,2},{2,3},{4,5},{5,6},{6,7},{8,9},{9,10},{10,11},{12,13},{... | collective-permute-start | bytes 122888 | tf_op jit(solution)/shard_map/ppermute | solution.py:850
  66.8 3.1 %shard_map.117 = (f32[32,48,128]{2,1,0:T(8,128)}, f32[2,80,128]{2,1,0:T(8,128)}, f32[80,128]{1,0:T(8,128)}, f32[8,128]{1,0:T(8,128)}, f32[128,128]{1,0:T(8,128)}) custom-call(f32[32,48,128]{2,1,0:T(8,128)S(1)} %all_to_all.20.arrived, f32[5,80,128]{2,1,0:T(8,128)} %get-tuple-element.33.wide_h, f32[1,80,128]{2,1,0:T(8,128)S(1)} %get-tuple-element.34.own_left, ...), custom_call_target="tpu_custom_call" | custom-call | flops 104857600 | bytes 4194304 | tf_op jit(solution)/shard_map/pallas_call | solution.py:592
  69.9 6.0 %all-to-all-start.3 = ((f32[32,48,128]{2,1,0:T(8,128)}), f32[32,48,128]{2,1,0:T(8,128)S(1)}, u32[]{:S(2)}, u32[]{:S(2)}) async-start(f32[32,48,128]{2,1,0:T(8,128)} %get-tuple-element.45), calls=%async_computation.3 | async-start | bytes 1572864 | tf_op jit(solution)/shard_map/all_to_all | solution.py:846
  76.0 2.4 %shard_map.118 = (f32[32,32,128]{2,1,0:T(8,128)}, f32[2,64,128]{2,1,0:T(8,128)}) custom-call(f32[32,32,128]{2,1,0:T(8,128)S(1)} %all-to-all-done.1.arrived, f32[5,80,128]{2,1,0:T(8,128)} %get-tuple-element.33.wide_h, f32[2,16,64,128]{3,2,1,0:T(8,128)} %get-tuple-element.28.currents_h, f32[8,128]{1,0:T(8,128)} %get-tuple-element.38.numbers_h, ...), custom_call_target="tpu_custom_call" | custom-call | flops 104857600 | bytes 3145728 | tf_op jit(solution)/shard_map/pallas_call | solution.py:668
  78.4 18.4 %all-to-all-done.3 = f32[32,48,128]{2,1,0:T(8,128)S(1)} async-done(((f32[32,48,128]{2,1,0:T(8,128)}), f32[32,48,128]{2,1,0:T(8,128)S(1)}, u32[]{:S(2)}, u32[]{:S(2)}) %all-to-all-start.3) | async-done | bytes 786464 | tf_op jit(solution)/shard_map/all_to_all | solution.py:846
  96.8 3.2 %all-to-all-start.2 = ((f32[32,32,128]{2,1,0:T(8,128)}), f32[32,32,128]{2,1,0:T(8,128)S(1)}, u32[]{:S(2)}, u32[]{:S(2)}) async-start(f32[32,32,128]{2,1,0:T(8,128)} %get-tuple-element.44), calls=%async_computation.2 | async-start | bytes 1048576 | tf_op jit(solution)/shard_map/all_to_all | solution.py:846
  100.0 3.5 %collective-permute-start = (f32[50,8,128]{2,1,0:T(8,128)S(1)}, f32[50,8,128]{2,1,0:T(8,128)S(1)}, u32[]{:S(2)}, u32[]{:S(2)}) collective-permute-start(f32[50,8,128]{2,1,0:T(8,128)S(1)} %copy-done.9), channel_id=1, source_target_pairs={{0,4},{4,8},{8,12},{12,16},{16,20},{20,24},{24,28},{1,5},{5,9},{9,... | collective-permute-start | bytes 614408 | tf_op jit(solution)/shard_map/ppermute | solution.py:850
  103.5 1.9 %collective-permute-start.1 = (f32[50,8,128]{2,1,0:T(8,128)S(1)}, f32[50,8,128]{2,1,0:T(8,128)S(1)}, u32[]{:S(2)}, u32[]{:S(2)}) collective-permute-start(f32[50,8,128]{2,1,0:T(8,128)S(1)} %copy-done.7), channel_id=1, source_target_pairs={{4,0},{8,4},{12,8},{16,12},{20,16},{24,20},{28,24},{5,1},{9,5},{13... | collective-permute-start | bytes 614408 | tf_op jit(solution)/shard_map/ppermute | solution.py:850
  105.5 1.9 %collective-permute-done.above = f32[50,8,128]{2,1,0:T(8,128)S(1)} collective-permute-done((f32[50,8,128]{2,1,0:T(8,128)S(1)}, f32[50,8,128]{2,1,0:T(8,128)S(1)}, u32[]{:S(2)}, u32[]{:S(2)}) %collective-permute-start) | collective-permute-done | bytes 204832 | tf_op jit(solution)/shard_map/ppermute | solution.py:850
  107.4 5.0 %collective-permute-done.1.below = f32[50,8,128]{2,1,0:T(8,128)S(1)} collective-permute-done((f32[50,8,128]{2,1,0:T(8,128)S(1)}, f32[50,8,128]{2,1,0:T(8,128)S(1)}, u32[]{:S(2)}, u32[]{:S(2)}) %collective-permute-start.1) | collective-permute-done | bytes 204832 | tf_op jit(solution)/shard_map/ppermute | solution.py:850
  112.4 2.9 %shard_map.114 = (f32[50,80,128]{2,1,0:T(8,128)}, f32[2,80,128]{2,1,0:T(8,128)S(1)}, f32[2,80,128]{2,1,0:T(8,128)S(1)}) custom-call(f32[50,64,128]{2,1,0:T(8,128)S(1)} %copy-done.2, f32[50,8,128]{2,1,0:T(8,128)S(1)} %collective-permute-done.above, f32[50,8,128]{2,1,0:T(8,128)S(1)} %collective-permute-done.1.below), custom_call_target="tpu_custom_call" | custom-call | flops 8388608 | bytes 4194304 | tf_op jit(solution)/shard_map/pallas_call | solution.py:352
  116.7 4.3 %collective-permute-start.6 = (f32[2,80,128]{2,1,0:T(8,128)S(1)}, f32[2,80,128]{2,1,0:T(8,128)S(1)}, u32[]{:S(2)}, u32[]{:S(2)}) collective-permute-start(f32[2,80,128]{2,1,0:T(8,128)S(1)} %get-tuple-element.43.own_right), channel_id=1, source_target_pairs={{0,1},{1,2},{2,3},{4,5},{5,6},{6,7},{8,9},{9,10},{10,11},{12,13},{... | collective-permute-start | bytes 245768 | tf_op jit(solution)/shard_map/ppermute | solution.py:850
  121.0 1.5 collective-permute-done.6.from_left
  122.5 7.4 %shard_map.119 = f32[4,16,64,128]{3,2,1,0:T(8,128)} custom-call(f32[50,80,128]{2,1,0:T(8,128)} %get-tuple-element.27.wide_h, f32[2,16,64,128]{3,2,1,0:T(8,128)} %get-tuple-element.28.currents_h, f32[2,80,128]{2,1,0:T(8,128)} %get-tuple-element.36.forcing_h, f32[2,64,128]{2,1,0:T(8,128)} %get-tuple-element.40.push_h, f32[80,128]{1,0:T(8,128)} %get-tuple-element.41.upright_h, ...), custom_call_target="tpu_custom_call" | custom-call | flops 41943040 | bytes 6291456 | tf_op jit(solution)/shard_map/pallas_call | solution.py:724
  129.9 9.6 %shard_map.120.refs_0_ = f32[48,8,128]{2,1,0:T(8,128)} custom-call(s32[256]{0:T(256)} %block_h.5, s32[256]{0:T(256)} %tile_h.5, s32[256]{0:T(256)} %bitcast.10, f32[1536,128]{1,0:T(8,128)S(1)} %bitcast.5, bf16[128,128,128]{2,1,0:T(8,128)(2,1)} %weights_h.5), custom_call_target="tpu_custom_call" | custom-call | flops 134217728 | bytes 6291456 | tf_op jit(solution)/shard_map/pallas_call | solution.py:802
  139.5 9.4 %shard_map.121 = f32[4,6144]{1,0:T(4,128)} custom-call(s32[256]{0:T(256)} %block_h.5, s32[256]{0:T(256)} %tile_h.5, s32[256]{0:T(256)} %bitcast.11, f32[1024,128]{1,0:T(8,128)S(1)} %bitcast.6, bf16[128,128,128]{2,1,0:T(8,128)(2,1)} %weights_h.5, f32[48,8,128]{2,1,0:T(8,128)} %shard_map.120.refs_0_), custom_call_target="tpu_custom_call" | custom-call | flops 134217728 | bytes 6291456 | tf_op jit(solution)/shard_map/pallas_call | solution.py:802
  (28 shorter events, 6.6 us)
Async XLA Ops:
  13.4 31.1 %copy-start = (f32[4,16,64,128]{3,2,1,0:T(8,128)S(1)}, f32[4,16,64,128]{3,2,1,0:T(8,128)}, u32[]{:S(2)}) copy-start(f32[4,16,64,128]{3,2,1,0:T(8,128)} %state.1) | copy-start | bytes 6291460
  13.4 31.1 %copy-start.4 = (f32[64,128]{1,0:T(8,128)S(1)}, f32[64,128]{1,0:T(8,128)}, u32[]{:S(2)}) copy-start(f32[64,128]{1,0:T(8,128)} %horiz.1) | copy-start | bytes 98308
  13.4 31.1 %copy-start.5 = (s32[64,128]{1,0:T(8,128)S(1)}, s32[64,128]{1,0:T(8,128)}, u32[]{:S(2)}) copy-start(s32[64,128]{1,0:T(8,128)} %wet.1) | copy-start | bytes 98308
  41.4 28.5 %all-to-all-start.1 = ((f32[32,32,128]{2,1,0:T(8,128)}), f32[32,32,128]{2,1,0:T(8,128)S(1)}, u32[]{:S(2)}, u32[]{:S(2)}) async-start(f32[32,32,128]{2,1,0:T(8,128)} %bitcast.8), calls=%async_computation.1 | async-start | bytes 1048576 | tf_op jit(solution)/shard_map/all_to_all | solution.py:846
  44.6 1.0 copy-start.3
  48.3 1.2 copy-start.1
  49.4 0.7 copy-start.8
  50.1 16.7 %copy-start.6 = (f32[50,8,128]{2,1,0:T(8,128)}, f32[50,8,128]{2,1,0:T(8,128)S(1)}, u32[]{:S(2)}) copy-start(f32[50,8,128]{2,1,0:T(8,128)S(1)} %get-tuple-element.26) | copy-start | bytes 614404
  50.1 5.5 %collective-permute-start.2 = (f32[5,8,128]{2,1,0:T(8,128)S(1)}, f32[5,8,128]{2,1,0:T(8,128)S(1)}, u32[]{:S(2)}, u32[]{:S(2)}) collective-permute-start(f32[5,8,128]{2,1,0:T(8,128)S(1)} %get-tuple-element.31), channel_id=1, source_target_pairs={{0,4},{4,8},{8,12},{12,16},{16,20},{20,24},{24,28},{1,5},{5,9},{9,... | collective-permute-start | bytes 61448 | tf_op jit(solution)/shard_map/ppermute | solution.py:850
  53.6 5.2 %collective-permute-start.3 = (f32[5,8,128]{2,1,0:T(8,128)S(1)}, f32[5,8,128]{2,1,0:T(8,128)S(1)}, u32[]{:S(2)}, u32[]{:S(2)}) collective-permute-start(f32[5,8,128]{2,1,0:T(8,128)S(1)} %get-tuple-element.32), channel_id=1, source_target_pairs={{4,0},{8,4},{12,8},{16,12},{20,16},{24,20},{28,24},{5,1},{9,5},{13... | collective-permute-start | bytes 61448 | tf_op jit(solution)/shard_map/ppermute | solution.py:850
  60.4 5.3 %collective-permute-start.5 = (f32[1,80,128]{2,1,0:T(8,128)S(1)}, f32[1,80,128]{2,1,0:T(8,128)S(1)}, u32[]{:S(2)}, u32[]{:S(2)}) collective-permute-start(f32[1,80,128]{2,1,0:T(8,128)S(1)} %get-tuple-element.34.own_left), channel_id=1, source_target_pairs={{1,0},{2,1},{3,2},{5,4},{6,5},{7,6},{9,8},{10,9},{11,10},{13,12},{... | collective-permute-start | bytes 122888 | tf_op jit(solution)/shard_map/ppermute | solution.py:850
  61.7 5.1 %collective-permute-start.4 = (f32[1,80,128]{2,1,0:T(8,128)S(1)}, f32[1,80,128]{2,1,0:T(8,128)S(1)}, u32[]{:S(2)}, u32[]{:S(2)}) collective-permute-start(f32[1,80,128]{2,1,0:T(8,128)S(1)} %get-tuple-element.35.own_right), channel_id=1, source_target_pairs={{0,1},{1,2},{2,3},{4,5},{5,6},{6,7},{8,9},{9,10},{10,11},{12,13},{... | collective-permute-start | bytes 122888 | tf_op jit(solution)/shard_map/ppermute | solution.py:850
  69.9 30.1 %copy-start.9 = (f32[50,8,128]{2,1,0:T(8,128)S(1)}, f32[50,8,128]{2,1,0:T(8,128)}, u32[]{:S(2)}) copy-start(f32[50,8,128]{2,1,0:T(8,128)} %copy-done.8) | copy-start | bytes 614404
  69.9 33.6 %copy-start.7 = (f32[50,8,128]{2,1,0:T(8,128)S(1)}, f32[50,8,128]{2,1,0:T(8,128)}, u32[]{:S(2)}) copy-start(f32[50,8,128]{2,1,0:T(8,128)} %copy-done.6) | copy-start | bytes 614404
  69.9 42.5 %copy-start.2 = (f32[50,64,128]{2,1,0:T(8,128)S(1)}, f32[50,64,128]{2,1,0:T(8,128)}, u32[]{:S(2)}) copy-start(f32[50,64,128]{2,1,0:T(8,128)} %copy-done.1) | copy-start | bytes 4915204
  69.9 26.9 %all-to-all-start.3 = ((f32[32,48,128]{2,1,0:T(8,128)}), f32[32,48,128]{2,1,0:T(8,128)S(1)}, u32[]{:S(2)}, u32[]{:S(2)}) async-start(f32[32,48,128]{2,1,0:T(8,128)} %get-tuple-element.45), calls=%async_computation.3 | async-start | bytes 1572864 | tf_op jit(solution)/shard_map/all_to_all | solution.py:846
  96.8 42.7 %all-to-all-start.2 = ((f32[32,32,128]{2,1,0:T(8,128)}), f32[32,32,128]{2,1,0:T(8,128)S(1)}, u32[]{:S(2)}, u32[]{:S(2)}) async-start(f32[32,32,128]{2,1,0:T(8,128)} %get-tuple-element.44), calls=%async_computation.2 | async-start | bytes 1048576 | tf_op jit(solution)/shard_map/all_to_all | solution.py:846
  100.0 7.4 %collective-permute-start = (f32[50,8,128]{2,1,0:T(8,128)S(1)}, f32[50,8,128]{2,1,0:T(8,128)S(1)}, u32[]{:S(2)}, u32[]{:S(2)}) collective-permute-start(f32[50,8,128]{2,1,0:T(8,128)S(1)} %copy-done.9), channel_id=1, source_target_pairs={{0,4},{4,8},{8,12},{12,16},{16,20},{20,24},{24,28},{1,5},{5,9},{9,... | collective-permute-start | bytes 614408 | tf_op jit(solution)/shard_map/ppermute | solution.py:850
  103.5 8.9 %collective-permute-start.1 = (f32[50,8,128]{2,1,0:T(8,128)S(1)}, f32[50,8,128]{2,1,0:T(8,128)S(1)}, u32[]{:S(2)}, u32[]{:S(2)}) collective-permute-start(f32[50,8,128]{2,1,0:T(8,128)S(1)} %copy-done.7), channel_id=1, source_target_pairs={{4,0},{8,4},{12,8},{16,12},{20,16},{24,20},{28,24},{5,1},{9,5},{13... | collective-permute-start | bytes 614408 | tf_op jit(solution)/shard_map/ppermute | solution.py:850
  115.4 5.7 %collective-permute-start.7 = (f32[2,80,128]{2,1,0:T(8,128)S(1)}, f32[2,80,128]{2,1,0:T(8,128)S(1)}, u32[]{:S(2)}, u32[]{:S(2)}) collective-permute-start(f32[2,80,128]{2,1,0:T(8,128)S(1)} %get-tuple-element.42.own_left), channel_id=1, source_target_pairs={{1,0},{2,1},{3,2},{5,4},{6,5},{7,6},{9,8},{10,9},{11,10},{13,12},{... | collective-permute-start | bytes 245768 | tf_op jit(solution)/shard_map/ppermute | solution.py:850
  116.7 5.8 %collective-permute-start.6 = (f32[2,80,128]{2,1,0:T(8,128)S(1)}, f32[2,80,128]{2,1,0:T(8,128)S(1)}, u32[]{:S(2)}, u32[]{:S(2)}) collective-permute-start(f32[2,80,128]{2,1,0:T(8,128)S(1)} %get-tuple-element.43.own_right), channel_id=1, source_target_pairs={{0,1},{1,2},{2,3},{4,5},{5,6},{6,7},{8,9},{9,10},{10,11},{12,13},{... | collective-permute-start | bytes 245768 | tf_op jit(solution)/shard_map/ppermute | solution.py:850

commit v5 on v3

--- a/solution.py
+++ b/solution.py
@@ -15,6 +15,8 @@
 LANES = 128
 EDGE = 16
 HALO = 8
+NUMBERS = 72
+CORNERS = 112
 PARTS = 8
 
 
@@ -61,7 +63,7 @@
 
 def remap_out_kernel(
     capacity, grid_y, tile_rows, block_h, owner_h, row_h, tile_h, atm_h, weights_h, out_h,
-    out, block_s, owner_s, row_s, tile_s, atm, weights, flux, every, fill, rows_acc, cols_acc, sems, weight_sems, out_sems,
+    out, block_s, owner_s, row_s, tile_s, atm, weights, flux, every, fill, row_slots, col_slots, rows_acc, cols_acc, sems, weight_sems, out_sems,
 ):
     devices = fill.shape[0]
     npairs = block_s.shape[0]
@@ -83,8 +85,8 @@
     for load in loads:
         load.start()
     out[...] = jnp.zeros_like(out)
-    rows_acc[...] = jnp.zeros_like(rows_acc)
-    cols_acc[...] = jnp.zeros_like(cols_acc)
+    row_slots[...] = jnp.zeros_like(row_slots)
+    col_slots[...] = jnp.zeros_like(col_slots)
 
     def clear_fill(i, carry):
         fill[i] = 0
@@ -111,7 +113,7 @@
             )
             return carry
 
-        lax.fori_loop(n * part_tiles, (n + 1) * part_tiles, tile_step, 0, unroll=4)
+        lax.fori_loop(n * part_tiles, (n + 1) * part_tiles, tile_step, 0, unroll=16)
     for copy in copies[1:]:
         copy.wait()
 
@@ -119,9 +121,8 @@
     lane = iota((8, LANES), 1)
     part = sub % 4
     edge_row = jnp.where(part == 0, 0, jnp.where(part == 1, 1, tile_rows - 4 + part))
-    edge_col = lane == jnp.where(part == 0, 0, jnp.where(part == 1, 1, LANES - 4 + part))
-    col_lane = lane - 64 * (sub // 4)
-    id_rank = jnp.where((sub == 0) & (lane >= 64), (lane - 64) // 4, -1)
+    band = ((lane - part) >> 2) * 4 + part
+    id_rank = jnp.where(sub == 0, lane - NUMBERS, -1)
 
     def pair(p, carry):
         owner = owner_s[p]
@@ -133,32 +134,38 @@
         for f in range(4):
             out[pl.ds(owner * message + 4 * rank + f, 1), :] = lines[f]
         tracer = jnp.where(sub < 4, lines[0], lines[1])
-        rows_acc[owner] = rows_acc[owner] + pick(edge_row == row, tracer)
-        column = jnp.sum(pick(edge_col, tracer), axis=1, keepdims=True)
+        slot = owner * capacity + rank
+        row_slots[slot] = pick(edge_row == row, tracer)
         number = (row + 1).astype(F32)
-        cols_acc[owner] = cols_acc[owner] + (
-            pick(col_lane == row, column) + pick(id_rank == rank, number)
-        )
-        return carry
-
-    lax.fori_loop(0, npairs, pair, 0, unroll=8)
+        col_slots[slot] = pick(band == row, pltpu.roll(tracer, row + 2, 1)) + pick(id_rank == rank, number)
+        return carry
+
+    lax.fori_loop(0, npairs, pair, 0, unroll=32)
+
+    def owner_step(d, carry):
+        rows = row_slots[d * capacity]
+        cols = col_slots[d * capacity]
+        for r in range(1, capacity):
+            rows = rows + row_slots[d * capacity + r]
+            cols = cols + col_slots[d * capacity + r]
+        rows_acc[d] = rows
+        cols_acc[d] = cols
+        return carry
+
+    lax.fori_loop(0, devices, owner_step, 0, unroll=8)
 
     grid_x = devices // grid_y
     zero = jnp.zeros((8, LANES), F32)
-    inside = ((sub < 4) & (lane < 64)) | (sub >= 4)
-    folds = {}
-
-    def fold(i, j):
+
+    def columns_of(i, j):
         if not (0 <= i < grid_x and 0 <= j < grid_y):
             return zero
-        d = i * grid_y + j
-        if d not in folds:
-            kept = pick(inside, cols_acc[d])
-            folds[d] = kept + pltpu.roll(kept, 4, 0)
-        return folds[d]
-
-    last = (lane == tile_rows - 1) | (lane == 64 + tile_rows - 1)
-    first = (lane == 0) | (lane == 64)
+        return cols_acc[i * grid_y + j]
+
+    from_left = (lane - sub) % 4 < 2
+    in_band = lane < tile_rows + 4
+    in_ids = (sub == 0) & (lane >= NUMBERS) & (lane < NUMBERS + capacity)
+    last, first = part == 3, part == 0
     send = devices // 4
     stores = []
     for d in range(devices):
@@ -167,14 +174,13 @@
         above = rows_acc[d - grid_y] if i > 0 else zero
         base = d * message + 4 * capacity
         out[base : base + 8, :] = jnp.where(part < 2, below, above)
-        if i > 1:
-            folds.pop(d - 2 * grid_y, None)
-        right, left = fold(i, j + 1), fold(i, j - 1)
-        tile = pick(sub < 2, right) + pick((sub == 2) | (sub == 3), left)
-        tile = tile + pick((sub == 4) & last, fold(i - 1, j + 1)) + pick((sub == 4) & first, fold(i + 1, j + 1))
-        tile = tile + pick((sub == 7) & last, fold(i - 1, j - 1)) + pick((sub == 7) & first, fold(i + 1, j - 1))
-        numbers = pltpu.roll(cols_acc[d], 5, 0)
-        tile = tile + pick((sub == 5) & (lane >= 64), numbers)
+        tile = pick(in_band, jnp.where(from_left, columns_of(i, j - 1), columns_of(i, j + 1)))
+        upper = pick(last & (lane == tile_rows), columns_of(i - 1, j - 1))
+        upper = upper + pick(last & (lane == tile_rows + 1), columns_of(i - 1, j + 1))
+        lower = pick(first & (lane == 1), columns_of(i + 1, j - 1))
+        lower = lower + pick(first & (lane == 2), columns_of(i + 1, j + 1))
+        tile = tile + pltpu.roll(upper, CORNERS - tile_rows, 1) + pltpu.roll(lower, CORNERS + 1, 1)
+        tile = tile + pick(in_ids, cols_acc[d])
         out[base + 8 : base + 16, :] = tile
         if d % send == send - 1:
             n = d // send
@@ -203,6 +209,8 @@
             pltpu.VMEM((4 * nblocks, LANES), F32),
             pltpu.VMEM((tiles * 4 * nblocks, LANES), F32),
             pltpu.SMEM((devices,), I32),
+            pltpu.VMEM((devices * capacity, 8, LANES), F32),
+            pltpu.VMEM((devices * capacity, 8, LANES), F32),
             pltpu.VMEM((devices, 8, LANES), F32),
             pltpu.VMEM((devices, 8, LANES), F32),
             pltpu.SemaphoreType.DMA((5,)),
@@ -348,29 +356,13 @@
     )(tracer, above, below)
 
 
-def faces_kernel(
-    levels, wide_h, own_left_h, own_right_h, from_left_h, from_right_h, faces_h, packed_h,
-    coef, own_left, own_right, from_left, from_right, faces, packed, sems,
-):
-    wait_all(
-        start_all(
-            [
-                (wide_h.at[pl.ds(3 * levels, 2)], coef),
-                (own_left_h, own_left),
-                (own_right_h, own_right),
-                (from_left_h, from_left),
-                (from_right_h, from_right),
-            ],
-            sems,
-        )
-    )
-    horiz, wet = coef.at[0], coef.at[1]
-    tall = horiz.shape[0]
+def set_faces(levels, h, w, own_left, own_right, from_left, from_right, faces, packed):
+    tall = h.shape[0]
     lane = iota((tall, LANES), 1)
     odd = lane % 2 == 1
     twice = lane % 64 < 2 * levels
-    tracer = jnp.where(odd, from_left[0], from_right[0])
-    other = jnp.where(odd, from_left[1], from_right[1])
+    left, left_unit, right, right_unit = from_left[0], from_left[1], from_right[0], from_right[1]
+    other = jnp.where(odd, left_unit, right_unit)
     at = 2 * levels
 
     def column(offset):
@@ -380,8 +372,6 @@
     kappa_far_right, kappa_far_left = column(2)
     wet_right, wet_left = column(4)
     wet_far_right, wet_far_left = column(6)
-    h = horiz[...]
-    w = wet[...]
 
     kappa_near = jnp.where(odd, kappa_left, kappa_right)
     kappa_far = jnp.where(odd, kappa_far_left, kappa_far_right)
@@ -394,10 +384,11 @@
         return 0.25 * (kappa_a + kappa_b) * wet_a * wet_b
 
     unit = jnp.where(twice, other, pltpu.roll(other, 2 * levels, 1))
-    packed[0] = tracer
+    packed[0] = jnp.where(odd, left, right)
     packed[1] = unit * jnp.where(lane < 64, wet_near, wet_far)
-    packed[2] = jnp.where(odd, pltpu.roll(own_left[0], 1, 1), pltpu.roll(own_right[0], LANES - 1, 1))
-    own = jnp.where(odd, pltpu.roll(own_left[1], 1, 1), pltpu.roll(own_right[1], LANES - 1, 1))
+    left, left_unit, right, right_unit = own_left[0], own_left[1], own_right[0], own_right[1]
+    packed[2] = jnp.where(odd, pltpu.roll(left, 1, 1), pltpu.roll(right, LANES - 1, 1))
+    own = jnp.where(odd, pltpu.roll(left_unit, 1, 1), pltpu.roll(right_unit, LANES - 1, 1))
     packed[3] = jnp.where(twice, own, pltpu.roll(own, 2 * levels, 1)) * wet_own
     north = face(kappa_near, wet_near, pltpu.roll(kappa_near, 1, 0), pltpu.roll(wet_near, 1, 0))
     packed[4] = north
@@ -413,24 +404,29 @@
     )
     faces[2] = west
     faces[3] = jnp.where(lane == LANES - 1, face(h, w, kappa_right, wet_right), pltpu.roll(west, LANES - 1, 1))
-    wait_all(start_all([(faces, faces_h), (packed, packed_h)], sems, 5))
-
-
-def face_values(levels, wide, own_left, own_right, from_left, from_right):
-    tall = wide.shape[1]
-    return pl.pallas_call(
-        functools.partial(faces_kernel, levels),
-        out_shape=(
-            pltpu.HBM((4, tall, LANES), F32),
-            pltpu.HBM((8, tall, LANES), F32),
-        ),
-        in_specs=[hbm()] + [pl.BlockSpec(memory_space=pl.ANY)] * 4,
-        out_specs=(hbm(),) * 2,
-        scratch_shapes=[pltpu.VMEM((2, tall, LANES), F32)] * 5
-        + [pltpu.VMEM((4, tall, LANES), F32), pltpu.VMEM((8, tall, LANES), F32), pltpu.SemaphoreType.DMA((7,))],
-        compiler_params=pltpu.CompilerParams(vmem_limit_bytes=24 << 20),
-        cost_estimate=pl.CostEstimate(flops=1 << 20, bytes_accessed=1 << 20, transcendentals=0),
-    )(*pin(wide), own_left, own_right, from_left, from_right)
+
+
+def set_beside(levels, upright, wide, packed, beside):
+    tall = upright.shape[0]
+    lane = iota((tall, LANES), 1)
+    odd = lane % 2 == 1
+    heat = lane % 64 < 2 * levels
+
+    def chosen(f):
+        left_far, left_near, right_near, right_far = [upright[:, 4 * f + e : 4 * f + e + 1] for e in range(4)]
+        near = jnp.where(odd, left_near, right_near)
+        return jnp.where(lane < 64, near, jnp.where(odd, left_far, right_far))
+
+    both = packed[0] + packed[1] * jnp.where(heat, chosen(0), chosen(1))
+    far = pltpu.roll(both, 64, 1)
+    ends_of = [jnp.where(odd, w[:, 0:1], w[:, LANES - 1 : LANES]) for w in wide]
+    own = packed[2] + packed[3] * jnp.where(heat, ends_of[0], ends_of[1])
+    near = both + packed[5] * (pltpu.roll(both, tall - 1, 0) - both)
+    near = near + packed[4] * (pltpu.roll(both, 1, 0) - both)
+    near = near + packed[6] * (far - both)
+    near = near + packed[7] * (own - both)
+    beside[0] = both
+    beside[1] = near
 
 
 def one_pass(value, faces, beside, shift):
@@ -446,8 +442,10 @@
 
 
 def middle_kernel(
-    capacity, levels, arrived, wide_h, currents_h, faces_h, packed_h, sent_h, forcing_h, near_h,
-    placing, values, number_t, top, currents, faces, packed, sent, forcing, near_o, sems, sent_sems,
+    capacity, levels, arrived, wide_h, currents_h, own_left_h, own_right_h, from_left_h, from_right_h,
+    sent_h, forcing_h, near_h, faces_h,
+    placing, values, number_t, top, currents, own_left, own_right, from_left, from_right,
+    faces, packed, sent, forcing, near_o, sems, sent_sems,
 ):
     devices, message, _ = arrived.shape
     rows_all = currents.shape[1]
@@ -455,11 +453,13 @@
     loads = start_all(
         [(wide_h.at[levels * k], top.at[k]) for k in range(3)]
         + [
-            (wide_h.at[3 * levels + 1], top.at[3]),
+            (wide_h.at[pl.ds(3 * levels, 2)], top.at[pl.ds(3, 2)]),
             (currents_h.at[0, 0], currents.at[0]),
             (currents_h.at[1, 0], currents.at[1]),
-            (faces_h, faces),
-            (packed_h, packed),
+            (own_left_h, own_left),
+            (own_right_h, own_right),
+            (from_left_h, from_left),
+            (from_right_h, from_right),
         ],
         sems,
     )
@@ -470,13 +470,15 @@
     lane8 = iota((8, LANES), 1)
 
     lane1 = iota((1, LANES), 1)
+    spread = (iota((LANES, LANES), 0) - NUMBERS) == iota((LANES, LANES), 1) % span // 4
+    every = jnp.concatenate([arrived[s, span + 8 : span + 9, :] for s in range(devices)], 0).astype(BF16)
+    every = jnp.dot(every, jnp.where(spread, 1.0, 0.0).astype(BF16), preferred_element_type=F32)
     numbers = []
     for m in range(groups):
         line = jnp.zeros((1, LANES), F32)
         for g in range(group):
-            ids = arrived[m * group + g, span + 13 : span + 14, :]
-            moved = pltpu.roll(ids, (g * span - 64) % LANES, 1)
-            line = jnp.where(lane1 // span == g, moved, line)
+            s = m * group + g
+            line = jnp.where(lane1 // span == g, every[s : s + 1], line)
         numbers.append(line)
     number_t[...] = jnp.transpose(
         jnp.concatenate(numbers + [jnp.zeros((LANES - groups, LANES), F32)], 0)
@@ -502,7 +504,8 @@
     total = total[:, 0:LANES] + total[:, LANES : 2 * LANES]
 
     wait_all(loads)
-    wet_wide = top[3]
+    set_faces(levels, top[3], top[4], own_left, own_right, from_left, from_right, faces, packed)
+    wet_wide = top[4]
 
     def plane(f):
         return total[f * rows_all : (f + 1) * rows_all]
@@ -519,50 +522,30 @@
         forcing[f, HALO : HALO + rows_all, :] = plane(f) * wet
         forcing[f, HALO + rows_all : tall, :] = jnp.zeros((HALO, LANES), F32)
 
-    corner = pick((sub8 == 0) | (sub8 == 3), pltpu.roll(edge_cols, 4, 0))
-    side = pick(sub8 < 4, edge_cols)
-    within = (lane8 >= HALO) & (lane8 < HALO + rows_all)
-    ends = (lane8 == HALO - 1) | (lane8 == HALO + rows_all)
-    halves = []
-    for f in range(2):
-        body = pltpu.roll(side, (HALO - 64 * f) % LANES, 1)
-        tips = pltpu.roll(corner, (HALO + rows_all - 64 * f) % LANES, 1)
-        halves.append((pick(within, body) + pick(ends, tips))[0:4])
-    columns = jnp.concatenate(halves, 0)
+    part8 = sub8 % 4
+    within = (part8 == lane8 % 4) & (lane8 >= HALO) & (lane8 < HALO + rows_all)
+    upper = (part8 == 3) & (lane8 == HALO - 1)
+    lower = (part8 == 0) & (lane8 == HALO + rows_all)
+    halves = [[], []]
+    for k in range(4):
+        column = pick(within, pltpu.roll(edge_cols, HALO - k, 1))
+        if k in (1, 2):
+            column = column + pick(upper, pltpu.roll(edge_cols, (HALO - CORNERS - k) % LANES, 1))
+            column = column + pick(lower, pltpu.roll(edge_cols, (HALO + rows_all - CORNERS - 1 - k) % LANES, 1))
+        for f in range(2):
+            halves[f].append(jnp.sum(column[4 * f : 4 * f + 4], axis=0, keepdims=True))
+    columns = jnp.concatenate(halves[0] + halves[1], 0)
     upright = jnp.transpose(jnp.concatenate([columns, jnp.zeros((LANES - 8, LANES), F32)], 0))[0:tall]
-    lane = iota((tall, LANES), 1)
-    odd = lane % 2 == 1
-    heat = lane % 64 < 2 * levels
-    close = lane < 64
-
-    def chosen(right_near, left_near, right_far, left_far):
-        near = jnp.where(odd, left_near, right_near)
-        far = jnp.where(odd, left_far, right_far)
-        return jnp.where(close, near, far)
-
-    def of_field(f):
-        return [upright[:, 4 * f + e : 4 * f + e + 1] for e in (0, 3, 1, 2)]
-
-    beside = jnp.where(heat, chosen(*of_field(0)), chosen(*of_field(1)))
-    both = packed[0] + packed[1] * beside
-    far = pltpu.roll(both, 64, 1)
-    ends_of = [jnp.where(odd, w[:, 0:1], w[:, LANES - 1 : LANES]) for w in wide]
-    own = packed[2] + packed[3] * jnp.where(heat, ends_of[0], ends_of[1])
-    near = both + packed[5] * (pltpu.roll(both, tall - 1, 0) - both)
-    near = near + packed[4] * (pltpu.roll(both, 1, 0) - both)
-    near = near + packed[6] * (far - both)
-    near = near + packed[7] * (own - both)
-    near_o[0] = both
-    near_o[1] = near
-    stores = start_all([(forcing, forcing_h), (near_o, near_h)], sems, 8)
+    set_beside(levels, upright, wide, packed, near_o)
+    stores = start_all([(forcing, forcing_h), (near_o, near_h), (faces, faces_h)], sems, 10)
 
     surface = []
     unit = top[2] * wet_wide
     for f in range(2):
         value = top[f] + unit * wide[f]
         shift = LANES - (2 * levels * f + 1)
-        value = one_pass(value, faces, both, shift)
-        value = one_pass(value, faces, near, shift)
+        value = one_pass(value, faces, near_o[0], shift)
+        value = one_pass(value, faces, near_o[1], shift)
         surface.append(value[HALO : HALO + rows_all] * wet)
     for f in range(2):
         surface.append(
@@ -595,7 +578,7 @@
     wait_all(stores)
 
 
-def middle(capacity, levels, arrived, wide, currents, faces, packed):
+def middle(capacity, levels, arrived, wide, currents, *columns):
     devices = arrived.shape[0]
     rows = currents.shape[2]
     tall = rows + 2 * HALO
@@ -606,26 +589,30 @@
             pltpu.HBM((devices, height, LANES), F32),
             pltpu.HBM((4, tall, LANES), F32),
             pltpu.HBM((2, tall, LANES), F32),
+            pltpu.HBM((4, tall, LANES), F32),
         ),
-        in_specs=[vmem()] + [hbm()] * 4,
-        out_specs=(hbm(),) * 3,
+        in_specs=[vmem()] + [hbm()] * 2 + [pl.BlockSpec(memory_space=pl.ANY)] * 4,
+        out_specs=(hbm(),) * 4,
         scratch_shapes=[
             pltpu.VMEM((4 * rows, 4 * capacity * devices), BF16),
             pltpu.VMEM((4 * capacity * devices, 2 * LANES), BF16),
             pltpu.VMEM((LANES, LANES), F32),
-            pltpu.VMEM((4, tall, LANES), F32),
+            pltpu.VMEM((5, tall, LANES), F32),
             pltpu.VMEM((2, rows, LANES), F32),
+        ]
+        + [pltpu.VMEM((2, tall, LANES), F32)] * 4
+        + [
             pltpu.VMEM((4, tall, LANES), F32),
             pltpu.VMEM((8, tall, LANES), F32),
             pltpu.VMEM((devices, height, LANES), F32),
             pltpu.VMEM((4, tall, LANES), F32),
             pltpu.VMEM((2, tall, LANES), F32),
-            pltpu.SemaphoreType.DMA((10,)),
+            pltpu.SemaphoreType.DMA((13,)),
             pltpu.SemaphoreType.DMA((4 * capacity * devices // LANES,)),
         ],
         compiler_params=pltpu.CompilerParams(vmem_limit_bytes=24 << 20),
         cost_estimate=pl.CostEstimate(flops=200 << 20, bytes_accessed=4 << 20, transcendentals=0),
-    )(arrived, *pin(wide, currents, faces, packed))
+    )(arrived, *pin(wide, currents), *columns)
 
 
 def finish_kernel(
@@ -699,7 +686,7 @@
         picked[p] = jnp.concatenate([high, low], 0)
         return carry
 
-    lax.fori_loop(0, npairs, gather, 0, unroll=8)
+    lax.fori_loop(0, npairs, gather, 0, unroll=32)
     wait_all(loads)
 
     def pair(p, carry):
@@ -710,7 +697,7 @@
         total[b] = total[b] + (value[0:8] + value[8:16])
         return carry
 
-    lax.fori_loop(0, npairs, pair, 0, unroll=16)
+    lax.fori_loop(0, npairs, pair, 0, unroll=64)
     for b in range(nblocks):
         sums = total[b]
         out[:, b * LANES : (b + 1) * LANES] = sums[0:4] / jnp.maximum(sums[4:5], 0.1)
@@ -774,8 +761,9 @@
     wide, to_left, to_right = pack(levels, tracer, above, below)
     from_left = lax.ppermute(to_right, "gy", rise_y)
     from_right = lax.ppermute(to_left, "gy", fall_y)
-    faces, packed = face_values(levels, wide, to_left, to_right, from_left, from_right)
-    sent, forcing, near = middle(capacity, levels, arrived, wide, currents, faces, packed)
+    sent, forcing, near, faces = middle(
+        capacity, levels, arrived, wide, currents, to_left, to_right, from_left, from_right
+    )
     returned = lax.all_to_all(sent, ("gx", "gy"), split_axis=0, concat_axis=0, tiled=True)
     ocean_next = finish(levels, wide, currents, faces, forcing, near)
     atm_surface = remap_back(

time: 105 us -> 96.7 us (0.921)
  Pallas kernels: 40.8 us -> 32.7 us
  waiting for transfers between devices: 37.4 us -> 39.5 us
  starting transfers between devices: 24.4 us -> 22.3 us
    pallas_call x1, Pallas kernels: 12.7 us -> 8.3 us  [remap_out(): pl.pallas_call(functools.partial(remap_out_kernel, capacity, grid_y, tile...]
    all_to_all x1, starting transfers between devices: 6.58 us -> 4.48 us  [local(): lax.all_to_all(sent, ('gx', 'gy'), split_axis=0, concat_axis=0, tiled=True)]
    pallas_call x1 -> x0, Pallas kernels: 2.1 us -> none  [face_values(): pl.pallas_call(functools.partial(faces_kernel, levels), out_shape=(pltpu....]
    all_to_all x1, waiting for transfers between devices: 2.33 us -> 4.13 us  [local(): lax.all_to_all(outgoing.reshape(devices, message, LANES), ('gx', 'gy'), s...]
    pallas_call x1, Pallas kernels: 9.59 us -> 7.86 us  [remap_back(): pl.pallas_call(functools.partial(remap_back_kernel, capacity), out_shape=...]
  transfers between devices with their start and end apart: 6 -> 6, of which waited for: 6 -> 6; matrix products, arithmetic and copies ran while one was open for 0% -> 0% of each run, Pallas kernels for 14% -> 13%
where the time goes in v5:
time: 96.7 us; the launch traced here: 96.4 us
  waiting for transfers between devices  39.5 us (41%)
  Pallas kernels  32.7 us (34%)
  starting transfers between devices  22.3 us (23%)
  local copies, waits for them, and re-layouts  1.06 us (1%)
    all_to_all x1, waiting for transfers between devices, local(): lax.all_to_all(sent, ('gx', 'gy'), split_axis=0, concat_axis=0, tiled=True)  25 us
    pallas_call x1, Pallas kernels, remap_out(): pl.pallas_call(functools.partial(remap_out_kernel, capacity, grid_y, tile...  8.3 us
    pallas_call x1, Pallas kernels, remap_back(): pl.pallas_call(functools.partial(remap_back_kernel, capacity), out_shape=...  7.86 us
    all_to_all x1, starting transfers between devices, local(): lax.all_to_all(outgoing.reshape(devices, message, LANES), ('gx', 'gy'), s...  7.1 us
    ppermute x1, waiting for transfers between devices, local(): below = lax.ppermute(edge_up, 'gx', fall_x)  6.92 us
    pallas_call x1, Pallas kernels, finish(): pl.pallas_call(functools.partial(finish_kernel, levels), out_shape=jax.Sh...  6.85 us
    all_to_all x1, starting transfers between devices, local(): lax.all_to_all(sent, ('gx', 'gy'), split_axis=0, concat_axis=0, tiled=True)  4.48 us
    all_to_all x1, waiting for transfers between devices, local(): lax.all_to_all(outgoing.reshape(devices, message, LANES), ('gx', 'gy'), s...  4.13 us
  transfers between devices with their start and end apart: 6, of which 6 were waited for; matrix products, arithmetic and copies ran while one was open for 0% of the time, Pallas kernels for 13%

profile of v5, /device:TPU:1, one launch (start us, length us, event | category | flops | bytes accessed | tf_op | source)
XLA Modules:
  0.0 96.4 jit_solution(1365009518250223597)
XLA Ops:
  0.6 8.3 %shard_map.115 = f32[2560,128]{1,0:T(8,128)} custom-call(s32[256]{0:T(256)} %block_h.3, s32[256]{0:T(256)} %bitcast.5, s32[256]{0:T(256)} %row_h.1, s32[256]{0:T(256)} %tile_h.3, f32[6,6144]{1,0:T(8,128)} %atm_h.1, bf16[128,128,128]{2,1,0:T(8,128)(2,1)} %weights_h.3), custom_call_target="tpu_custom_call" | custom-call | flops 805306368 | bytes 6291456 | tf_op jit(solution)/shard_map/pallas_call | solution.py:199
  8.9 0.0 copy-start
  9.0 0.0 copy-start.2
  9.0 0.0 copy-start.3
  9.0 7.1 %all-to-all-start = ((f32[32,80,128]{2,1,0:T(8,128)}), f32[32,80,128]{2,1,0:T(8,128)S(1)}, u32[]{:S(2)}, u32[]{:S(2)}) async-start(f32[32,80,128]{2,1,0:T(8,128)} %bitcast.4), calls=%async_computation | async-start | bytes 2621440 | tf_op jit(solution)/shard_map/all_to_all | solution.py:751
  16.1 0.0 copy-done
  16.1 0.0 copy-start.1
  16.1 1.0 %copy-done.1 = f32[16,64,128]{2,1,0:T(8,128)S(1)} copy-done((f32[16,64,128]{2,1,0:T(8,128)S(1)}, f32[16,64,128]{2,1,0:T(8,128)}, u32[]{:S(2)}) %copy-start.1) | copy-done | bytes 524312
  17.2 2.6 %shard_map.113 = (f32[50,64,128]{2,1,0:T(8,128)S(1)}, f32[2,16,64,128]{3,2,1,0:T(8,128)}, f32[50,8,128]{2,1,0:T(8,128)S(1)}, f32[50,8,128]{2,1,0:T(8,128)S(1)}) custom-call(f32[4,16,64,128]{3,2,1,0:T(8,128)S(1)} %copy-done, f32[16,64,128]{2,1,0:T(8,128)S(1)} %copy-done.1, f32[64,128]{1,0:T(8,128)S(1)} %copy-done.2, s32[64,128]{1,0:T(8,128)S(1)} %copy-done.3), custom_call_target="tpu_custom_call" | custom-call | flops 20971520 | bytes 6291456 | tf_op jit(solution)/shard_map/pallas_call | solution.py:289
  19.8 3.5 %collective-permute-start = (f32[50,8,128]{2,1,0:T(8,128)S(1)}, f32[50,8,128]{2,1,0:T(8,128)S(1)}, u32[]{:S(2)}, u32[]{:S(2)}) collective-permute-start(f32[50,8,128]{2,1,0:T(8,128)S(1)} %get-tuple-element.14), channel_id=1, source_target_pairs={{0,4},{4,8},{8,12},{12,16},{16,20},{20,24},{24,28},{1,5},{5,9},{9,... | collective-permute-start | bytes 614408 | tf_op jit(solution)/shard_map/ppermute | solution.py:759
  23.4 1.9 %collective-permute-start.1 = (f32[50,8,128]{2,1,0:T(8,128)S(1)}, f32[50,8,128]{2,1,0:T(8,128)S(1)}, u32[]{:S(2)}, u32[]{:S(2)}) collective-permute-start(f32[50,8,128]{2,1,0:T(8,128)S(1)} %get-tuple-element.15), channel_id=1, source_target_pairs={{4,0},{8,4},{12,8},{16,12},{20,16},{24,20},{28,24},{5,1},{9,5},{13... | collective-permute-start | bytes 614408 | tf_op jit(solution)/shard_map/ppermute | solution.py:760
  25.3 2.0 %collective-permute-done.above = f32[50,8,128]{2,1,0:T(8,128)S(1)} collective-permute-done((f32[50,8,128]{2,1,0:T(8,128)S(1)}, f32[50,8,128]{2,1,0:T(8,128)S(1)}, u32[]{:S(2)}, u32[]{:S(2)}) %collective-permute-start) | collective-permute-done | bytes 204832 | tf_op jit(solution)/shard_map/ppermute | solution.py:759
  27.3 6.9 %collective-permute-done.1.below = f32[50,8,128]{2,1,0:T(8,128)S(1)} collective-permute-done((f32[50,8,128]{2,1,0:T(8,128)S(1)}, f32[50,8,128]{2,1,0:T(8,128)S(1)}, u32[]{:S(2)}, u32[]{:S(2)}) %collective-permute-start.1) | collective-permute-done | bytes 204832 | tf_op jit(solution)/shard_map/ppermute | solution.py:760
  34.2 2.9 %shard_map.114 = (f32[50,80,128]{2,1,0:T(8,128)}, f32[2,80,128]{2,1,0:T(8,128)S(1)}, f32[2,80,128]{2,1,0:T(8,128)S(1)}) custom-call(f32[50,64,128]{2,1,0:T(8,128)S(1)} %get-tuple-element.13.tracer, f32[50,8,128]{2,1,0:T(8,128)S(1)} %collective-permute-done.above, f32[50,8,128]{2,1,0:T(8,128)S(1)} %collective-permute-done.1.below), custom_call_target="tpu_custom_call" | custom-call | flops 8388608 | bytes 4194304 | tf_op jit(solution)/shard_map/pallas_call | solution.py:344
  37.1 1.3 %collective-permute-start.3 = (f32[2,80,128]{2,1,0:T(8,128)S(1)}, f32[2,80,128]{2,1,0:T(8,128)S(1)}, u32[]{:S(2)}, u32[]{:S(2)}) collective-permute-start(f32[2,80,128]{2,1,0:T(8,128)S(1)} %get-tuple-element.18.own_left_h), channel_id=1, source_target_pairs={{1,0},{2,1},{3,2},{5,4},{6,5},{7,6},{9,8},{10,9},{11,10},{13,12},{... | collective-permute-start | bytes 245768 | tf_op jit(solution)/shard_map/ppermute | solution.py:763
  38.4 4.0 %collective-permute-start.2 = (f32[2,80,128]{2,1,0:T(8,128)S(1)}, f32[2,80,128]{2,1,0:T(8,128)S(1)}, u32[]{:S(2)}, u32[]{:S(2)}) collective-permute-start(f32[2,80,128]{2,1,0:T(8,128)S(1)} %get-tuple-element.19.own_right_h), channel_id=1, source_target_pairs={{0,1},{1,2},{2,3},{4,5},{5,6},{6,7},{8,9},{9,10},{10,11},{12,13},{... | collective-permute-start | bytes 245768 | tf_op jit(solution)/shard_map/ppermute | solution.py:762
  42.4 1.1 %collective-permute-done.3.from_right_h = f32[2,80,128]{2,1,0:T(8,128)S(1)} collective-permute-done((f32[2,80,128]{2,1,0:T(8,128)S(1)}, f32[2,80,128]{2,1,0:T(8,128)S(1)}, u32[]{:S(2)}, u32[]{:S(2)}) %collective-permute-start.3) | collective-permute-done | bytes 81952 | tf_op jit(solution)/shard_map/ppermute | solution.py:763
  43.5 0.4 collective-permute-done.2.from_left_h
  43.9 4.1 %all-to-all-done.arrived = f32[32,80,128]{2,1,0:T(8,128)S(1)} async-done(((f32[32,80,128]{2,1,0:T(8,128)}), f32[32,80,128]{2,1,0:T(8,128)S(1)}, u32[]{:S(2)}, u32[]{:S(2)}) %all-to-all-start) | async-done | bytes 1310752 | tf_op jit(solution)/shard_map/all_to_all | solution.py:751
  48.0 4.1 %shard_map.116 = (f32[32,80,128]{2,1,0:T(8,128)}, f32[4,80,128]{2,1,0:T(8,128)}, f32[2,80,128]{2,1,0:T(8,128)}, f32[4,80,128]{2,1,0:T(8,128)}) custom-call(f32[32,80,128]{2,1,0:T(8,128)S(1)} %all-to-all-done.arrived, f32[50,80,128]{2,1,0:T(8,128)} %get-tuple-element.16.wide_h, f32[2,16,64,128]{3,2,1,0:T(8,128)} %get-tuple-element.17.currents_h, ...), custom_call_target="tpu_custom_call" | custom-call | flops 209715200 | bytes 4194304 | tf_op jit(solution)/shard_map/pallas_call | solution.py:586
  52.1 4.5 %all-to-all-start.1 = ((f32[32,80,128]{2,1,0:T(8,128)}), f32[32,80,128]{2,1,0:T(8,128)S(1)}, u32[]{:S(2)}, u32[]{:S(2)}) async-start(f32[32,80,128]{2,1,0:T(8,128)} %get-tuple-element.23), calls=%async_computation.1 | async-start | bytes 2621440 | tf_op jit(solution)/shard_map/all_to_all | solution.py:767
  56.6 6.8 %shard_map.117 = f32[4,16,64,128]{3,2,1,0:T(8,128)} custom-call(f32[50,80,128]{2,1,0:T(8,128)} %get-tuple-element.16.wide_h, f32[2,16,64,128]{3,2,1,0:T(8,128)} %get-tuple-element.17.currents_h, f32[4,80,128]{2,1,0:T(8,128)} %get-tuple-element.20.faces_h, f32[4,80,128]{2,1,0:T(8,128)} %get-tuple-element.21.forcing_h, f32[2,80,128]{2,1,0:T(8,128)} %get-tuple-element.22.near_h), custom_call_target="tpu_custom_call" | custom-call | flops 41943040 | bytes 6291456 | tf_op jit(solution)/shard_map/pallas_call | solution.py:646
  63.5 25.0 %all-to-all-done.1 = f32[32,80,128]{2,1,0:T(8,128)S(1)} async-done(((f32[32,80,128]{2,1,0:T(8,128)}), f32[32,80,128]{2,1,0:T(8,128)S(1)}, u32[]{:S(2)}, u32[]{:S(2)}) %all-to-all-start.1) | async-done | bytes 1310752 | tf_op jit(solution)/shard_map/all_to_all | solution.py:767
  88.5 7.9 %shard_map.118 = f32[4,6144]{1,0:T(4,128)} custom-call(s32[256]{0:T(256)} %block_h.3, s32[256]{0:T(256)} %tile_h.3, s32[256]{0:T(256)} %bitcast.6, f32[2560,128]{1,0:T(8,128)S(1)} %bitcast.3, bf16[128,128,128]{2,1,0:T(8,128)(2,1)} %weights_h.3), custom_call_target="tpu_custom_call" | custom-call | flops 134217728 | bytes 6291456 | tf_op jit(solution)/shard_map/pallas_call | solution.py:708
  (2 shorter events, 0.0 us)
Async XLA Ops:
  8.9 7.1 %copy-start = (f32[4,16,64,128]{3,2,1,0:T(8,128)S(1)}, f32[4,16,64,128]{3,2,1,0:T(8,128)}, u32[]{:S(2)}) copy-start(f32[4,16,64,128]{3,2,1,0:T(8,128)} %state.1) | copy-start | bytes 6291460
  9.0 7.1 %copy-start.2 = (f32[64,128]{1,0:T(8,128)S(1)}, f32[64,128]{1,0:T(8,128)}, u32[]{:S(2)}) copy-start(f32[64,128]{1,0:T(8,128)} %horiz.1) | copy-start | bytes 98308
  9.0 7.1 %copy-start.3 = (s32[64,128]{1,0:T(8,128)S(1)}, s32[64,128]{1,0:T(8,128)}, u32[]{:S(2)}) copy-start(s32[64,128]{1,0:T(8,128)} %wet.1) | copy-start | bytes 98308
  9.0 39.0 %all-to-all-start = ((f32[32,80,128]{2,1,0:T(8,128)}), f32[32,80,128]{2,1,0:T(8,128)S(1)}, u32[]{:S(2)}, u32[]{:S(2)}) async-start(f32[32,80,128]{2,1,0:T(8,128)} %bitcast.4), calls=%async_computation | async-start | bytes 2621440 | tf_op jit(solution)/shard_map/all_to_all | solution.py:751
  16.1 1.0 %copy-start.1 = (f32[16,64,128]{2,1,0:T(8,128)S(1)}, f32[16,64,128]{2,1,0:T(8,128)}, u32[]{:S(2)}) copy-start(f32[16,64,128]{2,1,0:T(8,128)} %kappa.1) | copy-start | bytes 1572868
  19.8 7.4 %collective-permute-start = (f32[50,8,128]{2,1,0:T(8,128)S(1)}, f32[50,8,128]{2,1,0:T(8,128)S(1)}, u32[]{:S(2)}, u32[]{:S(2)}) collective-permute-start(f32[50,8,128]{2,1,0:T(8,128)S(1)} %get-tuple-element.14), channel_id=1, source_target_pairs={{0,4},{4,8},{8,12},{12,16},{16,20},{20,24},{24,28},{1,5},{5,9},{9,... | collective-permute-start | bytes 614408 | tf_op jit(solution)/shard_map/ppermute | solution.py:759
  23.4 10.8 %collective-permute-start.1 = (f32[50,8,128]{2,1,0:T(8,128)S(1)}, f32[50,8,128]{2,1,0:T(8,128)S(1)}, u32[]{:S(2)}, u32[]{:S(2)}) collective-permute-start(f32[50,8,128]{2,1,0:T(8,128)S(1)} %get-tuple-element.15), channel_id=1, source_target_pairs={{4,0},{8,4},{12,8},{16,12},{20,16},{24,20},{28,24},{5,1},{9,5},{13... | collective-permute-start | bytes 614408 | tf_op jit(solution)/shard_map/ppermute | solution.py:760
  37.1 6.4 %collective-permute-start.3 = (f32[2,80,128]{2,1,0:T(8,128)S(1)}, f32[2,80,128]{2,1,0:T(8,128)S(1)}, u32[]{:S(2)}, u32[]{:S(2)}) collective-permute-start(f32[2,80,128]{2,1,0:T(8,128)S(1)} %get-tuple-element.18.own_left_h), channel_id=1, source_target_pairs={{1,0},{2,1},{3,2},{5,4},{6,5},{7,6},{9,8},{10,9},{11,10},{13,12},{... | collective-permute-start | bytes 245768 | tf_op jit(solution)/shard_map/ppermute | solution.py:763
  38.4 5.5 %collective-permute-start.2 = (f32[2,80,128]{2,1,0:T(8,128)S(1)}, f32[2,80,128]{2,1,0:T(8,128)S(1)}, u32[]{:S(2)}, u32[]{:S(2)}) collective-permute-start(f32[2,80,128]{2,1,0:T(8,128)S(1)} %get-tuple-element.19.own_right_h), channel_id=1, source_target_pairs={{0,1},{1,2},{2,3},{4,5},{5,6},{6,7},{8,9},{9,10},{10,11},{12,13},{... | collective-permute-start | bytes 245768 | tf_op jit(solution)/shard_map/ppermute | solution.py:762
  52.1 36.4 %all-to-all-start.1 = ((f32[32,80,128]{2,1,0:T(8,128)}), f32[32,80,128]{2,1,0:T(8,128)S(1)}, u32[]{:S(2)}, u32[]{:S(2)}) async-start(f32[32,80,128]{2,1,0:T(8,128)} %get-tuple-element.23), calls=%async_computation.1 | async-start | bytes 2621440 | tf_op jit(solution)/shard_map/all_to_all | solution.py:767

commit v6 on v5

--- a/solution.py
+++ b/solution.py
@@ -55,10 +55,6 @@
 def split(value):
     high = value.astype(BF16)
     return high, (value - high.astype(F32)).astype(BF16)
-
-
-def back_rows(capacity):
-    return 4 * capacity + max(8, capacity)
 
 
 def remap_out_kernel(
@@ -556,23 +552,12 @@
     lane_t = iota((LANES, 4 * rows_all), 1)
     sub_t = iota((LANES, 4 * rows_all), 0)
     target = jnp.where(sub_t % 4 == lane_t // rows_all, lane_t % rows_all + 1, -1).astype(F32)
-    mask = jnp.concatenate([wet, jnp.zeros((LANES - rows_all, LANES), F32)], 0).astype(BF16)
-    per = LANES // 4
-    slot_number = number_t[pl.ds(0, per, stride=4), :]
-    lane_s = (iota((per, LANES), 1) + 1).astype(F32)
-    height = back_rows(capacity)
     for m in range(groups):
         chosen_rows = jnp.where(number_t[:, m : m + 1] == target, 1.0, 0.0).astype(BF16)
         rows = jnp.dot(chosen_rows, source, preferred_element_type=F32)
         rows = rows[:, 0:LANES] + rows[:, LANES : 2 * LANES]
-        slots = jnp.where(slot_number[:, m : m + 1] == lane_s, 1.0, 0.0).astype(BF16)
-        masks = jnp.dot(slots, mask, preferred_element_type=F32)
         for g in range(group):
-            s = m * group + g
-            sent[s, 0:span, :] = rows[g * span : (g + 1) * span]
-            sent[s, span : span + capacity, :] = masks[g * capacity : (g + 1) * capacity]
-            if height > span + capacity:
-                sent[s, span + capacity : height, :] = jnp.zeros((height - span - capacity, LANES), F32)
+            sent[m * group + g] = rows[g * span : (g + 1) * span]
         at = pl.ds(m * group, group)
         stores += start_all([(sent.at[at], sent_h.at[at])], sent_sems, m)
     wait_all(stores)
@@ -582,7 +567,7 @@
     devices = arrived.shape[0]
     rows = currents.shape[2]
     tall = rows + 2 * HALO
-    height = back_rows(capacity)
+    height = 4 * capacity
     return pl.pallas_call(
         functools.partial(middle_kernel, capacity, levels),
         out_shape=(
@@ -656,14 +641,16 @@
 
 
 def remap_back_kernel(
-    capacity, block_h, tile_h, owner_h, returned, weights_h, out,
-    block_s, tile_s, owner_s, fill, weights, picked, total, sems, weight_sems,
+    capacity, tile_rows, block_h, tile_h, owner_h, row_h, returned, wet_h, weights_h, out,
+    block_s, tile_s, owner_s, row_s, fill, wet, weights, picked, total, sems, weight_sems,
 ):
     npairs = block_s.shape[0]
     nblocks = total.shape[0]
     devices = fill.shape[0]
-    height = back_rows(capacity)
-    scalars = start_all([(owner_h, owner_s), (block_h, block_s), (tile_h, tile_s)], sems)
+    height = 4 * capacity
+    scalars = start_all(
+        [(owner_h, owner_s), (row_h, row_s), (block_h, block_s), (tile_h, tile_s), (wet_h, wet)], sems
+    )
     part_tiles = weights.shape[0] // PARTS
     parts = [pl.ds(n * part_tiles, part_tiles) for n in range(PARTS)]
     loads = start_all([(weights_h.at[at], weights.at[at]) for at in parts], weight_sems)
@@ -681,7 +668,7 @@
         rank = fill[owner]
         fill[owner] = rank + 1
         rows = returned[pl.ds(owner * height + 4 * rank, 4), :]
-        mask = returned[pl.ds(owner * height + 4 * capacity + rank, 1), :]
+        mask = wet[pl.ds(owner * tile_rows + row_s[p], 1), :].astype(F32)
         high, low = split(jnp.concatenate([rows, mask, jnp.zeros((3, LANES), F32)], 0))
         picked[p] = jnp.concatenate([high, low], 0)
         return carry
@@ -703,25 +690,26 @@
         out[:, b * LANES : (b + 1) * LANES] = sums[0:4] / jnp.maximum(sums[4:5], 0.1)
 
 
-def remap_back(capacity, devices, pair_block, pair_tile, owner, returned, remap_weight, nblocks):
+def remap_back(capacity, devices, tile_rows, pair_block, pair_tile, owner, pair_row, returned, wet, remap_weight, nblocks):
     npairs = pair_block.shape[0]
     return pl.pallas_call(
-        functools.partial(remap_back_kernel, capacity),
+        functools.partial(remap_back_kernel, capacity, tile_rows),
         out_shape=jax.ShapeDtypeStruct((4, nblocks * LANES), F32),
-        in_specs=[hbm()] * 3 + [vmem(), hbm()],
+        in_specs=[hbm()] * 4 + [vmem(), hbm(), hbm()],
         out_specs=vmem(),
-        scratch_shapes=[pltpu.SMEM((npairs,), I32)] * 3
+        scratch_shapes=[pltpu.SMEM((npairs,), I32)] * 4
         + [
             pltpu.SMEM((devices,), I32),
+            pltpu.VMEM(wet.shape, I32),
             pltpu.VMEM(remap_weight.shape, BF16),
             pltpu.VMEM((npairs, 16, LANES), BF16),
             pltpu.VMEM((nblocks, 8, LANES), F32),
-            pltpu.SemaphoreType.DMA((3,)),
+            pltpu.SemaphoreType.DMA((5,)),
             pltpu.SemaphoreType.DMA((PARTS,)),
         ],
         compiler_params=pltpu.CompilerParams(vmem_limit_bytes=24 << 20),
         cost_estimate=pl.CostEstimate(flops=2 * npairs * 16 * LANES * LANES, bytes_accessed=6 << 20, transcendentals=0),
-    )(*pin(pair_block, pair_tile, owner), returned, *pin(remap_weight))
+    )(*pin(pair_block, pair_tile, owner, pair_row), returned, *pin(wet, remap_weight))
 
 
 def local(
@@ -745,6 +733,8 @@
     nblocks = atm_state.shape[1] // LANES
     owner = pair_owner.reshape(npairs)
     message = 4 * capacity + EDGE
+    wet_all = lax.all_gather(wet_mask, "gy", axis=0, tiled=True)
+    wet_all = lax.all_gather(wet_all, "gx", axis=0, tiled=True)
     outgoing = remap_out(
         capacity, grid_y, devices, tile_rows, atm_state, pair_block, owner, pair_row, pair_tile, remap_weight
     )
@@ -767,7 +757,8 @@
     returned = lax.all_to_all(sent, ("gx", "gy"), split_axis=0, concat_axis=0, tiled=True)
     ocean_next = finish(levels, wide, currents, faces, forcing, near)
     atm_surface = remap_back(
-        capacity, devices, pair_block, pair_tile, owner, returned.reshape(-1, LANES), remap_weight, nblocks
+        capacity, devices, tile_rows, pair_block, pair_tile, owner, pair_row,
+        returned.reshape(-1, LANES), wet_all, remap_weight, nblocks,
     )
     return (ocean_next, atm_surface)
 

time: 96.7 us -> 136 us (1.41)
  blocking collectives: 0 us -> 30.9 us
  between operations: 0.78 us -> 14.2 us
  waiting for transfers between devices: 39.5 us -> 35 us
    all_gather x0 -> x1, blocking collectives: none -> 30.9 us  [local(): wet_all = lax.all_gather(wet_mask, 'gy', axis=0, tiled=True)]
    all_to_all x1, waiting for transfers between devices: 25 us -> 0.01 us  [local(): lax.all_to_all(sent, ('gx', 'gy'), split_axis=0, concat_axis=0, tiled=True)]
    all_gather x0 -> x1, waiting for transfers between devices: none -> 19.2 us  [local(): wet_all = lax.all_gather(wet_all, 'gx', axis=0, tiled=True)]
    ppermute x1, waiting for transfers between devices: 1.06 us -> 5.03 us  [local(): from_right = lax.ppermute(to_left, 'gy', fall_y)]
    all_to_all x1, waiting for transfers between devices: 4.13 us -> 1.71 us  [local(): lax.all_to_all(outgoing.reshape(devices, message, LANES), ('gx', 'gy'), s...]
  transfers between devices with their start and end apart: 6 -> 7, of which waited for: 6 -> 6; matrix products, arithmetic and copies ran while one was open for 0% -> 0% of each run, Pallas kernels for 13% -> 9%
where the time goes in v6:
time: 136 us
  waiting for transfers between devices  35 us (26%)
  Pallas kernels  33.7 us (25%)
  blocking collectives  30.9 us (23%)
  starting transfers between devices  21 us (15%)
  between operations  14.2 us (10%)
    all_gather x1, blocking collectives, local(): wet_all = lax.all_gather(wet_mask, 'gy', axis=0, tiled=True)  30.9 us
    all_gather x1, waiting for transfers between devices, local(): wet_all = lax.all_gather(wet_all, 'gx', axis=0, tiled=True)  19.2 us
    pallas_call x1, Pallas kernels, remap_back(): pl.pallas_call(functools.partial(remap_back_kernel, capacity, tile_rows),...  9.15 us
    pallas_call x1, Pallas kernels, remap_out(): pl.pallas_call(functools.partial(remap_out_kernel, capacity, grid_y, tile...  8.31 us
    all_to_all x1, starting transfers between devices, local(): lax.all_to_all(outgoing.reshape(devices, message, LANES), ('gx', 'gy'), s...  7.1 us
    pallas_call x1, Pallas kernels, finish(): pl.pallas_call(functools.partial(finish_kernel, levels), out_shape=jax.Sh...  6.85 us
    ppermute x1, waiting for transfers between devices, local(): below = lax.ppermute(edge_up, 'gx', fall_x)  6.77 us
    ppermute x1, waiting for transfers between devices, local(): from_right = lax.ppermute(to_left, 'gy', fall_y)  5.03 us
  transfers between devices with their start and end apart: 7, of which 6 were waited for; matrix products, arithmetic and copies ran while one was open for 0% of the time, Pallas kernels for 9%

profile of v6, /device:TPU:1, one launch (start us, length us, event | category | flops | bytes accessed | tf_op | source)
XLA Modules:
  0.0 135.9 jit_solution(4366001692002594815)
XLA Ops:
  7.2 8.3 %shard_map.115 = f32[2560,128]{1,0:T(8,128)} custom-call(s32[256]{0:T(256)} %block_h.3, s32[256]{0:T(256)} %bitcast.5, s32[256]{0:T(256)} %row_h.3, s32[256]{0:T(256)} %tile_h.3, f32[6,6144]{1,0:T(8,128)} %atm_h.1, bf16[128,128,128]{2,1,0:T(8,128)(2,1)} %weights_h.3), custom_call_target="tpu_custom_call" | custom-call | flops 805306368 | bytes 6291456 | tf_op jit(solution)/shard_map/pallas_call | solution.py:195
  15.5 0.0 copy-start
  15.5 0.0 copy-start.3
  15.5 7.1 %all-to-all-start = ((f32[32,80,128]{2,1,0:T(8,128)}), f32[32,80,128]{2,1,0:T(8,128)S(1)}, u32[]{:S(2)}, u32[]{:S(2)}) async-start(f32[32,80,128]{2,1,0:T(8,128)} %bitcast.4), calls=%async_computation | async-start | bytes 2621440 | tf_op jit(solution)/shard_map/all_to_all | solution.py:741
  22.7 1.0 copy-done.1
  23.7 2.7 %shard_map.113 = (f32[50,64,128]{2,1,0:T(8,128)S(1)}, f32[2,16,64,128]{3,2,1,0:T(8,128)}, f32[50,8,128]{2,1,0:T(8,128)S(1)}, f32[50,8,128]{2,1,0:T(8,128)S(1)}) custom-call(f32[4,16,64,128]{3,2,1,0:T(8,128)S(1)} %copy-done, f32[16,64,128]{2,1,0:T(8,128)S(1)} %copy-done.1, f32[64,128]{1,0:T(8,128)S(1)} %copy-done.3, s32[64,128]{1,0:T(8,128)S(1)} %copy-done.2), custom_call_target="tpu_custom_call" | custom-call | flops 20971520 | bytes 6291456 | tf_op jit(solution)/shard_map/pallas_call | solution.py:285
  26.4 3.5 %collective-permute-start = (f32[50,8,128]{2,1,0:T(8,128)S(1)}, f32[50,8,128]{2,1,0:T(8,128)S(1)}, u32[]{:S(2)}, u32[]{:S(2)}) collective-permute-start(f32[50,8,128]{2,1,0:T(8,128)S(1)} %get-tuple-element.14), channel_id=1, source_target_pairs={{0,4},{4,8},{8,12},{12,16},{16,20},{20,24},{24,28},{1,5},{5,9},{9,... | collective-permute-start | bytes 614408 | tf_op jit(solution)/shard_map/ppermute | solution.py:749
  29.9 1.9 %collective-permute-start.1 = (f32[50,8,128]{2,1,0:T(8,128)S(1)}, f32[50,8,128]{2,1,0:T(8,128)S(1)}, u32[]{:S(2)}, u32[]{:S(2)}) collective-permute-start(f32[50,8,128]{2,1,0:T(8,128)S(1)} %get-tuple-element.15), channel_id=1, source_target_pairs={{4,0},{8,4},{12,8},{16,12},{20,16},{24,20},{28,24},{5,1},{9,5},{13... | collective-permute-start | bytes 614408 | tf_op jit(solution)/shard_map/ppermute | solution.py:750
  31.8 2.1 %collective-permute-done.above = f32[50,8,128]{2,1,0:T(8,128)S(1)} collective-permute-done((f32[50,8,128]{2,1,0:T(8,128)S(1)}, f32[50,8,128]{2,1,0:T(8,128)S(1)}, u32[]{:S(2)}, u32[]{:S(2)}) %collective-permute-start) | collective-permute-done | bytes 204832 | tf_op jit(solution)/shard_map/ppermute | solution.py:749
  33.9 6.8 %collective-permute-done.1.below = f32[50,8,128]{2,1,0:T(8,128)S(1)} collective-permute-done((f32[50,8,128]{2,1,0:T(8,128)S(1)}, f32[50,8,128]{2,1,0:T(8,128)S(1)}, u32[]{:S(2)}, u32[]{:S(2)}) %collective-permute-start.1) | collective-permute-done | bytes 204832 | tf_op jit(solution)/shard_map/ppermute | solution.py:750
  40.7 2.9 %shard_map.114 = (f32[50,80,128]{2,1,0:T(8,128)}, f32[2,80,128]{2,1,0:T(8,128)S(1)}, f32[2,80,128]{2,1,0:T(8,128)S(1)}) custom-call(f32[50,64,128]{2,1,0:T(8,128)S(1)} %get-tuple-element.13.tracer, f32[50,8,128]{2,1,0:T(8,128)S(1)} %collective-permute-done.above, f32[50,8,128]{2,1,0:T(8,128)S(1)} %collective-permute-done.1.below), custom_call_target="tpu_custom_call" | custom-call | flops 8388608 | bytes 4194304 | tf_op jit(solution)/shard_map/pallas_call | solution.py:340
  43.6 2.7 %collective-permute-start.2 = (f32[2,80,128]{2,1,0:T(8,128)S(1)}, f32[2,80,128]{2,1,0:T(8,128)S(1)}, u32[]{:S(2)}, u32[]{:S(2)}) collective-permute-start(f32[2,80,128]{2,1,0:T(8,128)S(1)} %get-tuple-element.19.own_right_h), channel_id=1, source_target_pairs={{0,1},{1,2},{2,3},{4,5},{5,6},{6,7},{8,9},{9,10},{10,11},{12,13},{... | collective-permute-start | bytes 245768 | tf_op jit(solution)/shard_map/ppermute | solution.py:752
  46.3 1.3 collective-permute-start.3
  47.6 0.2 collective-permute-done.2.from_left_h
  47.8 5.0 %collective-permute-done.3.from_right_h = f32[2,80,128]{2,1,0:T(8,128)S(1)} collective-permute-done((f32[2,80,128]{2,1,0:T(8,128)S(1)}, f32[2,80,128]{2,1,0:T(8,128)S(1)}, u32[]{:S(2)}, u32[]{:S(2)}) %collective-permute-start.3) | collective-permute-done | bytes 81952 | tf_op jit(solution)/shard_map/ppermute | solution.py:753
  52.8 1.7 %all-to-all-done.arrived = f32[32,80,128]{2,1,0:T(8,128)S(1)} async-done(((f32[32,80,128]{2,1,0:T(8,128)}), f32[32,80,128]{2,1,0:T(8,128)S(1)}, u32[]{:S(2)}, u32[]{:S(2)}) %all-to-all-start) | async-done | bytes 1310752 | tf_op jit(solution)/shard_map/all_to_all | solution.py:741
  54.5 3.8 %shard_map.116 = (f32[32,64,128]{2,1,0:T(8,128)}, f32[4,80,128]{2,1,0:T(8,128)}, f32[2,80,128]{2,1,0:T(8,128)}, f32[4,80,128]{2,1,0:T(8,128)}) custom-call(f32[32,80,128]{2,1,0:T(8,128)S(1)} %all-to-all-done.arrived, f32[50,80,128]{2,1,0:T(8,128)} %get-tuple-element.16.wide_h, f32[2,16,64,128]{3,2,1,0:T(8,128)} %get-tuple-element.17.currents_h, ...), custom_call_target="tpu_custom_call" | custom-call | flops 209715200 | bytes 4194304 | tf_op jit(solution)/shard_map/pallas_call | solution.py:571
  58.3 4.5 %all-to-all-start.1 = ((f32[32,64,128]{2,1,0:T(8,128)}), f32[32,64,128]{2,1,0:T(8,128)S(1)}, u32[]{:S(2)}, u32[]{:S(2)}) async-start(f32[32,64,128]{2,1,0:T(8,128)} %get-tuple-element.23), calls=%async_computation.1 | async-start | bytes 2097152 | tf_op jit(solution)/shard_map/all_to_all | solution.py:757
  62.8 0.0 all-gather.2.cloned.1.call-start
  62.9 30.9 %all_gather.6 = s32[256,128]{1,0:T(8,128)} all-gather(s32[64,128]{1,0:T(8,128)S(1)} %copy-done.2), channel_id=1, replica_groups=mesh['gx'=8,'gy'=4] {'gy'}, dimensions={0}, use_global_device_ids=true | all-gather | bytes 163840 | tf_op jit(solution)/shard_map/all_gather | solution.py:736
  93.8 0.0 all-gather.2.cloned.1.call-update
  93.8 6.8 %shard_map.117 = f32[4,16,64,128]{3,2,1,0:T(8,128)} custom-call(f32[50,80,128]{2,1,0:T(8,128)} %get-tuple-element.16.wide_h, f32[2,16,64,128]{3,2,1,0:T(8,128)} %get-tuple-element.17.currents_h, f32[4,80,128]{2,1,0:T(8,128)} %get-tuple-element.20.faces_h, f32[4,80,128]{2,1,0:T(8,128)} %get-tuple-element.21.forcing_h, f32[2,80,128]{2,1,0:T(8,128)} %get-tuple-element.22.near_h), custom_call_target="tpu_custom_call" | custom-call | flops 41943040 | bytes 6291456 | tf_op jit(solution)/shard_map/pallas_call | solution.py:631
  100.6 19.2 %all-gather.2.cloned.1.call-done.wet_h = s32[2048,128]{1,0:T(8,128)} async-done(((s32[256,128]{1,0:T(8,128)}), s32[2048,128]{1,0:T(8,128)}) %all-gather.2.cloned.1.call-update) | async-done | bytes 1048592 | tf_op jit(solution)/shard_map/all_gather | solution.py:737
  119.9 9.2 %shard_map.118 = f32[4,6144]{1,0:T(4,128)} custom-call(s32[256]{0:T(256)} %block_h.3, s32[256]{0:T(256)} %tile_h.3, s32[256]{0:T(256)} %bitcast.6, s32[256]{0:T(256)} %row_h.3, f32[2048,128]{1,0:T(8,128)S(1)} %bitcast.3, s32[2048,128]{1,0:T(8,128)} %all-gather.2.cloned.1.call-done.wet_h, bf16[128,128,128]{2,1,0:T(8,128)(2,1)} %weights_h.3), custom_call_target="tpu_custom_call" | custom-call | flops 134217728 | bytes 6291456 | tf_op jit(solution)/shard_map/pallas_call | solution.py:695
  (6 shorter events, 0.0 us)
Async XLA Ops:
  15.5 7.1 %copy-start = (f32[4,16,64,128]{3,2,1,0:T(8,128)S(1)}, f32[4,16,64,128]{3,2,1,0:T(8,128)}, u32[]{:S(2)}) copy-start(f32[4,16,64,128]{3,2,1,0:T(8,128)} %state.1) | copy-start | bytes 6291460
  15.5 7.1 %copy-start.2 = (s32[64,128]{1,0:T(8,128)S(1)}, s32[64,128]{1,0:T(8,128)}, u32[]{:S(2)}) copy-start(s32[64,128]{1,0:T(8,128)} %wet.1) | copy-start | bytes 98308
  15.5 7.1 %copy-start.3 = (f32[64,128]{1,0:T(8,128)S(1)}, f32[64,128]{1,0:T(8,128)}, u32[]{:S(2)}) copy-start(f32[64,128]{1,0:T(8,128)} %horiz.1) | copy-start | bytes 98308
  15.5 39.0 %all-to-all-start = ((f32[32,80,128]{2,1,0:T(8,128)}), f32[32,80,128]{2,1,0:T(8,128)S(1)}, u32[]{:S(2)}, u32[]{:S(2)}) async-start(f32[32,80,128]{2,1,0:T(8,128)} %bitcast.4), calls=%async_computation | async-start | bytes 2621440 | tf_op jit(solution)/shard_map/all_to_all | solution.py:741
  22.6 1.0 copy-start.1
  26.4 7.6 %collective-permute-start = (f32[50,8,128]{2,1,0:T(8,128)S(1)}, f32[50,8,128]{2,1,0:T(8,128)S(1)}, u32[]{:S(2)}, u32[]{:S(2)}) collective-permute-start(f32[50,8,128]{2,1,0:T(8,128)S(1)} %get-tuple-element.14), channel_id=1, source_target_pairs={{0,4},{4,8},{8,12},{12,16},{16,20},{20,24},{24,28},{1,5},{5,9},{9,... | collective-permute-start | bytes 614408 | tf_op jit(solution)/shard_map/ppermute | solution.py:749
  29.9 10.8 %collective-permute-start.1 = (f32[50,8,128]{2,1,0:T(8,128)S(1)}, f32[50,8,128]{2,1,0:T(8,128)S(1)}, u32[]{:S(2)}, u32[]{:S(2)}) collective-permute-start(f32[50,8,128]{2,1,0:T(8,128)S(1)} %get-tuple-element.15), channel_id=1, source_target_pairs={{4,0},{8,4},{12,8},{16,12},{20,16},{24,20},{28,24},{5,1},{9,5},{13... | collective-permute-start | bytes 614408 | tf_op jit(solution)/shard_map/ppermute | solution.py:750
  43.6 4.1 %collective-permute-start.2 = (f32[2,80,128]{2,1,0:T(8,128)S(1)}, f32[2,80,128]{2,1,0:T(8,128)S(1)}, u32[]{:S(2)}, u32[]{:S(2)}) collective-permute-start(f32[2,80,128]{2,1,0:T(8,128)S(1)} %get-tuple-element.19.own_right_h), channel_id=1, source_target_pairs={{0,1},{1,2},{2,3},{4,5},{5,6},{6,7},{8,9},{9,10},{10,11},{12,13},{... | collective-permute-start | bytes 245768 | tf_op jit(solution)/shard_map/ppermute | solution.py:752
  46.3 6.5 %collective-permute-start.3 = (f32[2,80,128]{2,1,0:T(8,128)S(1)}, f32[2,80,128]{2,1,0:T(8,128)S(1)}, u32[]{:S(2)}, u32[]{:S(2)}) collective-permute-start(f32[2,80,128]{2,1,0:T(8,128)S(1)} %get-tuple-element.18.own_left_h), channel_id=1, source_target_pairs={{1,0},{2,1},{3,2},{5,4},{6,5},{7,6},{9,8},{10,9},{11,10},{13,12},{... | collective-permute-start | bytes 245768 | tf_op jit(solution)/shard_map/ppermute | solution.py:753
  58.3 61.5 %all-to-all-start.1 = ((f32[32,64,128]{2,1,0:T(8,128)}), f32[32,64,128]{2,1,0:T(8,128)S(1)}, u32[]{:S(2)}, u32[]{:S(2)}) async-start(f32[32,64,128]{2,1,0:T(8,128)} %get-tuple-element.23), calls=%async_computation.1 | async-start | bytes 2097152 | tf_op jit(solution)/shard_map/all_to_all | solution.py:757
  62.8 57.1 %all-gather.2.cloned.1.call-start = ((), (), s32[]{:S(2)}) async-start(), calls=%async_computation.2 | async-start | bytes 1179648 | tf_op jit(solution)/shard_map/all_gather | solution.py:737
Sparse Core Ops, SparseCore 0:
  93.9 25.9 all-gather.1

commit v7 on v5

--- a/solution.py
+++ b/solution.py
@@ -63,13 +63,12 @@
 
 def remap_out_kernel(
     capacity, grid_y, tile_rows, block_h, owner_h, row_h, tile_h, atm_h, weights_h, out_h,
-    out, block_s, owner_s, row_s, tile_s, atm, weights, flux, every, fill, row_slots, col_slots, rows_acc, cols_acc, sems, weight_sems, out_sems,
+    out, block_s, owner_s, row_s, tile_s, atm, weights, flux, fill, row_slots, col_slots, rows_acc, cols_acc, sems, weight_sems, out_sems,
 ):
     devices = fill.shape[0]
     npairs = block_s.shape[0]
     tiles = weights.shape[0]
-    four = flux.shape[0]
-    nblocks = four // 4
+    nblocks = flux.shape[0]
     message = 4 * capacity + EDGE
     copies = [
         pltpu.make_async_copy(src, dst, sems.at[n])
@@ -99,21 +98,15 @@
     speed = jnp.sqrt(wind_u * wind_u + wind_v * wind_v + 0.25)
     heat = 0.5 * speed * (atm[2:3, :] - atm[5:6, :])
     water = atm[4:5, :] - 0.3 * speed * atm[3:4, :]
-    for f, plane in enumerate([heat, water, 0.2 * speed * wind_u, 0.2 * speed * wind_v]):
-        for b in range(nblocks):
-            flux[f * nblocks + b : f * nblocks + b + 1, :] = plane[:, b * LANES : (b + 1) * LANES]
-    source = flux[...].astype(BF16)
-
-    for n in range(PARTS):
-        loads[n].wait()
-
-        def tile_step(t, carry):
-            every[pl.ds(pl.multiple_of(t * four, 8), four), :] = jnp.dot(
-                source, weights[t], preferred_element_type=F32
-            )
-            return carry
-
-        lax.fori_loop(n * part_tiles, (n + 1) * part_tiles, tile_step, 0, unroll=16)
+    planes = jnp.concatenate(
+        [heat, water, 0.2 * speed * wind_u, 0.2 * speed * wind_v, jnp.zeros((4, wind_u.shape[1]), F32)]
+        + [heat] * 4
+        + [water] * 4,
+        0,
+    ).astype(BF16)
+    for b in range(nblocks):
+        flux[b] = planes[:, b * LANES : (b + 1) * LANES]
+    wait_all(loads)
     for copy in copies[1:]:
         copy.wait()
 
@@ -129,11 +122,9 @@
         row = row_s[p]
         rank = fill[owner]
         fill[owner] = rank + 1
-        first = tile_s[p] * four + block_s[p]
-        lines = [every[pl.ds(first + f * nblocks, 1), :] for f in range(4)]
-        for f in range(4):
-            out[pl.ds(owner * message + 4 * rank + f, 1), :] = lines[f]
-        tracer = jnp.where(sub < 4, lines[0], lines[1])
+        value = jnp.dot(flux[block_s[p]], weights[tile_s[p]], preferred_element_type=F32)
+        out[pl.ds(owner * message + 4 * rank, 4), :] = value[0:4]
+        tracer = value[8:16]
         slot = owner * capacity + rank
         row_slots[slot] = pick(edge_row == row, tracer)
         number = (row + 1).astype(F32)
@@ -195,7 +186,6 @@
     npairs = pair_block.shape[0]
     nblocks = atm_state.shape[1] // LANES
     message = 4 * capacity + EDGE
-    tiles = remap_weight.shape[0]
     return pl.pallas_call(
         functools.partial(remap_out_kernel, capacity, grid_y, tile_rows),
         out_shape=pltpu.HBM((devices * message, LANES), F32),
@@ -206,8 +196,7 @@
         + [
             pltpu.VMEM(atm_state.shape, F32),
             pltpu.VMEM(remap_weight.shape, BF16),
-            pltpu.VMEM((4 * nblocks, LANES), F32),
-            pltpu.VMEM((tiles * 4 * nblocks, LANES), F32),
+            pltpu.VMEM((nblocks, 16, LANES), BF16),
             pltpu.SMEM((devices,), I32),
             pltpu.VMEM((devices * capacity, 8, LANES), F32),
             pltpu.VMEM((devices * capacity, 8, LANES), F32),
@@ -219,7 +208,7 @@
         ],
         compiler_params=pltpu.CompilerParams(vmem_limit_bytes=40 << 20),
         cost_estimate=pl.CostEstimate(
-            flops=2 * tiles * 4 * nblocks * LANES * LANES, bytes_accessed=6 << 20, transcendentals=0
+            flops=2 * npairs * 16 * LANES * LANES, bytes_accessed=6 << 20, transcendentals=0
         ),
     )(*pin(pair_block, owner, pair_row, pair_tile, atm_state, remap_weight))
 
@@ -655,9 +644,38 @@
     )(*pin(wide, currents, faces, forcing, near))
 
 
+def turn_kernel(weights_h, turned_h, weights, turned, sems, out_sems):
+    part_tiles = weights.shape[0] // PARTS
+    parts = [pl.ds(n * part_tiles, part_tiles) for n in range(PARTS)]
+    loads = start_all([(weights_h.at[at], weights.at[at]) for at in parts], sems)
+    stores = []
+    for n, at in enumerate(parts):
+        loads[n].wait()
+
+        def tile_step(t, carry):
+            turned[t] = weights[t].T
+            return carry
+
+        lax.fori_loop(n * part_tiles, (n + 1) * part_tiles, tile_step, 0, unroll=4)
+        stores += start_all([(turned.at[at], turned_h.at[at])], out_sems, n)
+    wait_all(stores)
+
+
+def turn(remap_weight):
+    return pl.pallas_call(
+        turn_kernel,
+        out_shape=pltpu.HBM(remap_weight.shape, BF16),
+        in_specs=[hbm()],
+        out_specs=hbm(),
+        scratch_shapes=[pltpu.VMEM(remap_weight.shape, BF16)] * 2 + [pltpu.SemaphoreType.DMA((PARTS,))] * 2,
+        compiler_params=pltpu.CompilerParams(vmem_limit_bytes=24 << 20),
+        cost_estimate=pl.CostEstimate(flops=8 << 20, bytes_accessed=8 << 20, transcendentals=0),
+    )(*pin(remap_weight))
+
+
 def remap_back_kernel(
     capacity, block_h, tile_h, owner_h, returned, weights_h, out,
-    block_s, tile_s, owner_s, fill, weights, picked, total, sems, weight_sems,
+    block_s, tile_s, owner_s, fill, weights, picked_a, picked_b, total, sems, weight_sems,
 ):
     npairs = block_s.shape[0]
     nblocks = total.shape[0]
@@ -676,28 +694,39 @@
     lax.fori_loop(0, devices, clear_fill, 0, unroll=16)
     wait_all(scalars)
 
-    def gather(p, carry):
+    def gather(p, picked, at):
         owner = owner_s[p]
         rank = fill[owner]
         fill[owner] = rank + 1
         rows = returned[pl.ds(owner * height + 4 * rank, 4), :]
-        mask = returned[pl.ds(owner * height + 4 * capacity + rank, 1), :]
-        high, low = split(jnp.concatenate([rows, mask, jnp.zeros((3, LANES), F32)], 0))
-        picked[p] = jnp.concatenate([high, low], 0)
-        return carry
-
-    lax.fori_loop(0, npairs, gather, 0, unroll=32)
-    wait_all(loads)
-
-    def pair(p, carry):
-        value = lax.dot_general(
-            picked[p], weights[tile_s[p]], (((1,), (1,)), ((), ())), preferred_element_type=F32
-        )
+        mask = returned[pl.ds(owner * height + 4 * capacity + rank - 4, 5), :]
+        high, low = split(jnp.concatenate([rows, mask[4:5], jnp.zeros((3, LANES), F32)], 0))
+        picked[at] = jnp.concatenate([high, low], 0)
+
+    def product(p, picked, at):
+        value = jnp.dot(picked[at], weights[tile_s[p]], preferred_element_type=F32)
         b = block_s[p]
         total[b] = total[b] + (value[0:8] + value[8:16])
-        return carry
-
-    lax.fori_loop(0, npairs, pair, 0, unroll=64)
+
+    half = npairs // 2
+
+    def first(p, carry):
+        gather(p, picked_a, p)
+        return carry
+
+    def both(p, carry):
+        gather(half + p, picked_b, p)
+        product(p, picked_a, p)
+        return carry
+
+    def last(p, carry):
+        product(half + p, picked_b, p)
+        return carry
+
+    lax.fori_loop(0, half, first, 0, unroll=32)
+    wait_all(loads)
+    lax.fori_loop(0, half, both, 0, unroll=64)
+    lax.fori_loop(0, half, last, 0, unroll=64)
     for b in range(nblocks):
         sums = total[b]
         out[:, b * LANES : (b + 1) * LANES] = sums[0:4] / jnp.maximum(sums[4:5], 0.1)
@@ -714,7 +743,8 @@
         + [
             pltpu.SMEM((devices,), I32),
             pltpu.VMEM(remap_weight.shape, BF16),
-            pltpu.VMEM((npairs, 16, LANES), BF16),
+            pltpu.VMEM((npairs // 2, 16, LANES), BF16),
+            pltpu.VMEM((npairs // 2, 16, LANES), BF16),
             pltpu.VMEM((nblocks, 8, LANES), F32),
             pltpu.SemaphoreType.DMA((3,)),
             pltpu.SemaphoreType.DMA((PARTS,)),
@@ -766,8 +796,9 @@
     )
     returned = lax.all_to_all(sent, ("gx", "gy"), split_axis=0, concat_axis=0, tiled=True)
     ocean_next = finish(levels, wide, currents, faces, forcing, near)
+    weights, _ = lax.optimization_barrier((remap_weight, near))
     atm_surface = remap_back(
-        capacity, devices, pair_block, pair_tile, owner, returned.reshape(-1, LANES), remap_weight, nblocks
+        capacity, devices, pair_block, pair_tile, owner, returned.reshape(-1, LANES), turn(weights), nblocks
     )
     return (ocean_next, atm_surface)
 

time: 96.7 us -> 93.8 us (0.970)
  waiting for transfers between devices: 39.5 us -> 34.6 us
  Pallas kernels: 32.7 us -> 34.7 us
    all_to_all x1, waiting for transfers between devices: 25 us -> 20.2 us  [local(): lax.all_to_all(sent, ('gx', 'gy'), split_axis=0, concat_axis=0, tiled=True)]
    pallas_call x0 -> x1, Pallas kernels: none -> 4.8 us  [turn(): pl.pallas_call(turn_kernel, out_shape=pltpu.HBM(remap_weight.shape, BF16)...]
    pallas_call x1, Pallas kernels: 7.86 us -> 5.78 us  [remap_back(): pl.pallas_call(functools.partial(remap_back_kernel, capacity), out_shape=...]
  transfers between devices with their start and end apart: 6 -> 6, of which waited for: 6 -> 6; matrix products, arithmetic and copies ran while one was open for 0% -> 0% of each run, Pallas kernels for 13% -> 19%
where the time goes in v7:
time: 93.8 us; the launch traced here: 93.4 us
  Pallas kernels  34.7 us (37%)
  waiting for transfers between devices  34.6 us (37%)
  starting transfers between devices  22.3 us (24%)
  local copies, waits for them, and re-layouts  1.06 us (1%)
    all_to_all x1, waiting for transfers between devices, local(): lax.all_to_all(sent, ('gx', 'gy'), split_axis=0, concat_axis=0, tiled=True)  20.2 us
    pallas_call x1, Pallas kernels, remap_out(): pl.pallas_call(functools.partial(remap_out_kernel, capacity, grid_y, tile...  7.42 us
    all_to_all x1, starting transfers between devices, local(): lax.all_to_all(outgoing.reshape(devices, message, LANES), ('gx', 'gy'), s...  7.1 us
    pallas_call x1, Pallas kernels, finish(): pl.pallas_call(functools.partial(finish_kernel, levels), out_shape=jax.Sh...  6.85 us
    ppermute x1, waiting for transfers between devices, local(): below = lax.ppermute(edge_up, 'gx', fall_x)  6.42 us
    pallas_call x1, Pallas kernels, remap_back(): pl.pallas_call(functools.partial(remap_back_kernel, capacity), out_shape=...  5.78 us
    pallas_call x1, Pallas kernels, turn(): pl.pallas_call(turn_kernel, out_shape=pltpu.HBM(remap_weight.shape, BF16)...  4.8 us
    all_to_all x1, starting transfers between devices, local(): lax.all_to_all(sent, ('gx', 'gy'), split_axis=0, concat_axis=0, tiled=True)  4.48 us
  transfers between devices with their start and end apart: 6, of which 6 were waited for; matrix products, arithmetic and copies ran while one was open for 0% of the time, Pallas kernels for 19%

profile of v7, /device:TPU:1, one launch (start us, length us, event | category | flops | bytes accessed | tf_op | source)
XLA Modules:
  0.0 93.4 jit_solution(6392327298411384390)
XLA Ops:
  0.6 7.4 %shard_map.115 = f32[2560,128]{1,0:T(8,128)} custom-call(s32[256]{0:T(256)} %block_h.3, s32[256]{0:T(256)} %bitcast.5, s32[256]{0:T(256)} %row_h.1, s32[256]{0:T(256)} %tile_h.3, f32[6,6144]{1,0:T(8,128)} %atm_h.1, bf16[128,128,128]{2,1,0:T(8,128)(2,1)} %weights_h.2), custom_call_target="tpu_custom_call" | custom-call | flops 134217728 | bytes 6291456 | tf_op jit(solution)/shard_map/pallas_call | solution.py:189
  8.1 0.0 copy-start
  8.1 0.0 copy-start.2
  8.1 0.0 copy-start.3
  8.1 7.1 %all-to-all-start = ((f32[32,80,128]{2,1,0:T(8,128)}), f32[32,80,128]{2,1,0:T(8,128)S(1)}, u32[]{:S(2)}, u32[]{:S(2)}) async-start(f32[32,80,128]{2,1,0:T(8,128)} %bitcast.4), calls=%async_computation | async-start | bytes 2621440 | tf_op jit(solution)/shard_map/all_to_all | solution.py:781
  15.2 0.0 copy-start.1
  15.2 1.0 %copy-done.1 = f32[16,64,128]{2,1,0:T(8,128)S(1)} copy-done((f32[16,64,128]{2,1,0:T(8,128)S(1)}, f32[16,64,128]{2,1,0:T(8,128)}, u32[]{:S(2)}) %copy-start.1) | copy-done | bytes 524312
  16.3 2.8 %shard_map.113 = (f32[50,64,128]{2,1,0:T(8,128)S(1)}, f32[2,16,64,128]{3,2,1,0:T(8,128)}, f32[50,8,128]{2,1,0:T(8,128)S(1)}, f32[50,8,128]{2,1,0:T(8,128)S(1)}) custom-call(f32[4,16,64,128]{3,2,1,0:T(8,128)S(1)} %copy-done, f32[16,64,128]{2,1,0:T(8,128)S(1)} %copy-done.1, f32[64,128]{1,0:T(8,128)S(1)} %copy-done.2, s32[64,128]{1,0:T(8,128)S(1)} %copy-done.3), custom_call_target="tpu_custom_call" | custom-call | flops 20971520 | bytes 6291456 | tf_op jit(solution)/shard_map/pallas_call | solution.py:278
  19.1 3.5 %collective-permute-start = (f32[50,8,128]{2,1,0:T(8,128)S(1)}, f32[50,8,128]{2,1,0:T(8,128)S(1)}, u32[]{:S(2)}, u32[]{:S(2)}) collective-permute-start(f32[50,8,128]{2,1,0:T(8,128)S(1)} %get-tuple-element.15), channel_id=1, source_target_pairs={{0,4},{4,8},{8,12},{12,16},{16,20},{20,24},{24,28},{1,5},{5,9},{9,... | collective-permute-start | bytes 614408 | tf_op jit(solution)/shard_map/ppermute | solution.py:789
  22.6 1.9 %collective-permute-start.1 = (f32[50,8,128]{2,1,0:T(8,128)S(1)}, f32[50,8,128]{2,1,0:T(8,128)S(1)}, u32[]{:S(2)}, u32[]{:S(2)}) collective-permute-start(f32[50,8,128]{2,1,0:T(8,128)S(1)} %get-tuple-element.16), channel_id=1, source_target_pairs={{4,0},{8,4},{12,8},{16,12},{20,16},{24,20},{28,24},{5,1},{9,5},{13... | collective-permute-start | bytes 614408 | tf_op jit(solution)/shard_map/ppermute | solution.py:790
  24.5 2.4 %collective-permute-done.above = f32[50,8,128]{2,1,0:T(8,128)S(1)} collective-permute-done((f32[50,8,128]{2,1,0:T(8,128)S(1)}, f32[50,8,128]{2,1,0:T(8,128)S(1)}, u32[]{:S(2)}, u32[]{:S(2)}) %collective-permute-start) | collective-permute-done | bytes 204832 | tf_op jit(solution)/shard_map/ppermute | solution.py:789
  26.9 6.4 %collective-permute-done.1.below = f32[50,8,128]{2,1,0:T(8,128)S(1)} collective-permute-done((f32[50,8,128]{2,1,0:T(8,128)S(1)}, f32[50,8,128]{2,1,0:T(8,128)S(1)}, u32[]{:S(2)}, u32[]{:S(2)}) %collective-permute-start.1) | collective-permute-done | bytes 204832 | tf_op jit(solution)/shard_map/ppermute | solution.py:790
  33.3 2.9 %shard_map.114 = (f32[50,80,128]{2,1,0:T(8,128)}, f32[2,80,128]{2,1,0:T(8,128)S(1)}, f32[2,80,128]{2,1,0:T(8,128)S(1)}) custom-call(f32[50,64,128]{2,1,0:T(8,128)S(1)} %get-tuple-element.14.tracer, f32[50,8,128]{2,1,0:T(8,128)S(1)} %collective-permute-done.above, f32[50,8,128]{2,1,0:T(8,128)S(1)} %collective-permute-done.1.below), custom_call_target="tpu_custom_call" | custom-call | flops 8388608 | bytes 4194304 | tf_op jit(solution)/shard_map/pallas_call | solution.py:333
  36.2 1.3 %collective-permute-start.3 = (f32[2,80,128]{2,1,0:T(8,128)S(1)}, f32[2,80,128]{2,1,0:T(8,128)S(1)}, u32[]{:S(2)}, u32[]{:S(2)}) collective-permute-start(f32[2,80,128]{2,1,0:T(8,128)S(1)} %get-tuple-element.19.own_left_h), channel_id=1, source_target_pairs={{1,0},{2,1},{3,2},{5,4},{6,5},{7,6},{9,8},{10,9},{11,10},{13,12},{... | collective-permute-start | bytes 245768 | tf_op jit(solution)/shard_map/ppermute | solution.py:793
  37.5 4.0 %collective-permute-start.2 = (f32[2,80,128]{2,1,0:T(8,128)S(1)}, f32[2,80,128]{2,1,0:T(8,128)S(1)}, u32[]{:S(2)}, u32[]{:S(2)}) collective-permute-start(f32[2,80,128]{2,1,0:T(8,128)S(1)} %get-tuple-element.20.own_right_h), channel_id=1, source_target_pairs={{0,1},{1,2},{2,3},{4,5},{5,6},{6,7},{8,9},{9,10},{10,11},{12,13},{... | collective-permute-start | bytes 245768 | tf_op jit(solution)/shard_map/ppermute | solution.py:792
  41.5 1.1 %collective-permute-done.3.from_right_h = f32[2,80,128]{2,1,0:T(8,128)S(1)} collective-permute-done((f32[2,80,128]{2,1,0:T(8,128)S(1)}, f32[2,80,128]{2,1,0:T(8,128)S(1)}, u32[]{:S(2)}, u32[]{:S(2)}) %collective-permute-start.3) | collective-permute-done | bytes 81952 | tf_op jit(solution)/shard_map/ppermute | solution.py:793
  42.6 0.4 collective-permute-done.2.from_left_h
  43.0 4.1 %all-to-all-done.arrived = f32[32,80,128]{2,1,0:T(8,128)S(1)} async-done(((f32[32,80,128]{2,1,0:T(8,128)}), f32[32,80,128]{2,1,0:T(8,128)S(1)}, u32[]{:S(2)}, u32[]{:S(2)}) %all-to-all-start) | async-done | bytes 1310752 | tf_op jit(solution)/shard_map/all_to_all | solution.py:781
  47.1 4.1 %shard_map.116 = (f32[32,80,128]{2,1,0:T(8,128)}, f32[4,80,128]{2,1,0:T(8,128)}, f32[2,80,128]{2,1,0:T(8,128)}, f32[4,80,128]{2,1,0:T(8,128)}) custom-call(f32[32,80,128]{2,1,0:T(8,128)S(1)} %all-to-all-done.arrived, f32[50,80,128]{2,1,0:T(8,128)} %get-tuple-element.17.wide_h, f32[2,16,64,128]{3,2,1,0:T(8,128)} %get-tuple-element.18.currents_h, ...), custom_call_target="tpu_custom_call" | custom-call | flops 209715200 | bytes 4194304 | tf_op jit(solution)/shard_map/pallas_call | solution.py:575
  51.2 4.5 %all-to-all-start.1 = ((f32[32,80,128]{2,1,0:T(8,128)}), f32[32,80,128]{2,1,0:T(8,128)S(1)}, u32[]{:S(2)}, u32[]{:S(2)}) async-start(f32[32,80,128]{2,1,0:T(8,128)} %get-tuple-element.24), calls=%async_computation.1 | async-start | bytes 2621440 | tf_op jit(solution)/shard_map/all_to_all | solution.py:797
  55.7 4.8 %shard_map.118.weights_h = bf16[128,128,128]{2,1,0:T(8,128)(2,1)} custom-call(bf16[128,128,128]{2,1,0:T(8,128)(2,1)} %weights_h.2), custom_call_target="tpu_custom_call" | custom-call | flops 8388608 | bytes 8388608 | tf_op jit(solution)/shard_map/pallas_call | solution.py:665
  60.5 6.8 %shard_map.117 = f32[4,16,64,128]{3,2,1,0:T(8,128)} custom-call(f32[50,80,128]{2,1,0:T(8,128)} %get-tuple-element.17.wide_h, f32[2,16,64,128]{3,2,1,0:T(8,128)} %get-tuple-element.18.currents_h, f32[4,80,128]{2,1,0:T(8,128)} %get-tuple-element.21.faces_h, f32[4,80,128]{2,1,0:T(8,128)} %get-tuple-element.22.forcing_h, f32[2,80,128]{2,1,0:T(8,128)} %get-tuple-element.23.near_h), custom_call_target="tpu_custom_call" | custom-call | flops 41943040 | bytes 6291456 | tf_op jit(solution)/shard_map/pallas_call | solution.py:635
  67.4 20.2 %all-to-all-done.1 = f32[32,80,128]{2,1,0:T(8,128)S(1)} async-done(((f32[32,80,128]{2,1,0:T(8,128)}), f32[32,80,128]{2,1,0:T(8,128)S(1)}, u32[]{:S(2)}, u32[]{:S(2)}) %all-to-all-start.1) | async-done | bytes 1310752 | tf_op jit(solution)/shard_map/all_to_all | solution.py:797
  87.6 5.8 %shard_map.119 = f32[4,6144]{1,0:T(4,128)} custom-call(s32[256]{0:T(256)} %block_h.3, s32[256]{0:T(256)} %tile_h.3, s32[256]{0:T(256)} %bitcast.6, f32[2560,128]{1,0:T(8,128)S(1)} %bitcast.3, bf16[128,128,128]{2,1,0:T(8,128)(2,1)} %shard_map.118.weights_h), custom_call_target="tpu_custom_call" | custom-call | flops 134217728 | bytes 6291456 | tf_op jit(solution)/shard_map/pallas_call | solution.py:737
  (3 shorter events, 0.0 us)
Async XLA Ops:
  8.1 7.1 %copy-start = (f32[4,16,64,128]{3,2,1,0:T(8,128)S(1)}, f32[4,16,64,128]{3,2,1,0:T(8,128)}, u32[]{:S(2)}) copy-start(f32[4,16,64,128]{3,2,1,0:T(8,128)} %state.1) | copy-start | bytes 6291460
  8.1 7.1 %copy-start.2 = (f32[64,128]{1,0:T(8,128)S(1)}, f32[64,128]{1,0:T(8,128)}, u32[]{:S(2)}) copy-start(f32[64,128]{1,0:T(8,128)} %horiz.1) | copy-start | bytes 98308
  8.1 7.1 %copy-start.3 = (s32[64,128]{1,0:T(8,128)S(1)}, s32[64,128]{1,0:T(8,128)}, u32[]{:S(2)}) copy-start(s32[64,128]{1,0:T(8,128)} %wet.1) | copy-start | bytes 98308
  8.1 39.0 %all-to-all-start = ((f32[32,80,128]{2,1,0:T(8,128)}), f32[32,80,128]{2,1,0:T(8,128)S(1)}, u32[]{:S(2)}, u32[]{:S(2)}) async-start(f32[32,80,128]{2,1,0:T(8,128)} %bitcast.4), calls=%async_computation | async-start | bytes 2621440 | tf_op jit(solution)/shard_map/all_to_all | solution.py:781
  15.2 1.0 %copy-start.1 = (f32[16,64,128]{2,1,0:T(8,128)S(1)}, f32[16,64,128]{2,1,0:T(8,128)}, u32[]{:S(2)}) copy-start(f32[16,64,128]{2,1,0:T(8,128)} %kappa.1) | copy-start | bytes 1572868
  19.1 7.8 %collective-permute-start = (f32[50,8,128]{2,1,0:T(8,128)S(1)}, f32[50,8,128]{2,1,0:T(8,128)S(1)}, u32[]{:S(2)}, u32[]{:S(2)}) collective-permute-start(f32[50,8,128]{2,1,0:T(8,128)S(1)} %get-tuple-element.15), channel_id=1, source_target_pairs={{0,4},{4,8},{8,12},{12,16},{16,20},{20,24},{24,28},{1,5},{5,9},{9,... | collective-permute-start | bytes 614408 | tf_op jit(solution)/shard_map/ppermute | solution.py:789
  22.6 10.7 %collective-permute-start.1 = (f32[50,8,128]{2,1,0:T(8,128)S(1)}, f32[50,8,128]{2,1,0:T(8,128)S(1)}, u32[]{:S(2)}, u32[]{:S(2)}) collective-permute-start(f32[50,8,128]{2,1,0:T(8,128)S(1)} %get-tuple-element.16), channel_id=1, source_target_pairs={{4,0},{8,4},{12,8},{16,12},{20,16},{24,20},{28,24},{5,1},{9,5},{13... | collective-permute-start | bytes 614408 | tf_op jit(solution)/shard_map/ppermute | solution.py:790
  36.2 6.4 %collective-permute-start.3 = (f32[2,80,128]{2,1,0:T(8,128)S(1)}, f32[2,80,128]{2,1,0:T(8,128)S(1)}, u32[]{:S(2)}, u32[]{:S(2)}) collective-permute-start(f32[2,80,128]{2,1,0:T(8,128)S(1)} %get-tuple-element.19.own_left_h), channel_id=1, source_target_pairs={{1,0},{2,1},{3,2},{5,4},{6,5},{7,6},{9,8},{10,9},{11,10},{13,12},{... | collective-permute-start | bytes 245768 | tf_op jit(solution)/shard_map/ppermute | solution.py:793
  37.5 5.5 %collective-permute-start.2 = (f32[2,80,128]{2,1,0:T(8,128)S(1)}, f32[2,80,128]{2,1,0:T(8,128)S(1)}, u32[]{:S(2)}, u32[]{:S(2)}) collective-permute-start(f32[2,80,128]{2,1,0:T(8,128)S(1)} %get-tuple-element.20.own_right_h), channel_id=1, source_target_pairs={{0,1},{1,2},{2,3},{4,5},{5,6},{6,7},{8,9},{9,10},{10,11},{12,13},{... | collective-permute-start | bytes 245768 | tf_op jit(solution)/shard_map/ppermute | solution.py:792
  51.2 36.4 %all-to-all-start.1 = ((f32[32,80,128]{2,1,0:T(8,128)}), f32[32,80,128]{2,1,0:T(8,128)S(1)}, u32[]{:S(2)}, u32[]{:S(2)}) async-start(f32[32,80,128]{2,1,0:T(8,128)} %get-tuple-element.24), calls=%async_computation.1 | async-start | bytes 2621440 | tf_op jit(solution)/shard_map/all_to_all | solution.py:797

commit v8 on v7

--- a/solution.py
+++ b/solution.py
@@ -17,6 +17,7 @@
 HALO = 8
 NUMBERS = 72
 CORNERS = 112
+SENDS = 8
 PARTS = 8
 
 
@@ -62,8 +63,8 @@
 
 
 def remap_out_kernel(
-    capacity, grid_y, tile_rows, block_h, owner_h, row_h, tile_h, atm_h, weights_h, out_h,
-    out, block_s, owner_s, row_s, tile_s, atm, weights, flux, fill, row_slots, col_slots, rows_acc, cols_acc, sems, weight_sems, out_sems,
+    capacity, grid_y, tile_rows, block_h, owner_h, row_h, tile_h, atm_h, weights_h, out_h, field_h, wet_h,
+    out, block_s, owner_s, row_s, tile_s, slot_s, rank_s, field_s, wet_s, atm, weights, flux, fill, row_slots, col_slots, rows_acc, cols_acc, sems, weight_sems, out_sems,
 ):
     devices = fill.shape[0]
     npairs = block_s.shape[0]
@@ -106,9 +107,23 @@
     ).astype(BF16)
     for b in range(nblocks):
         flux[b] = planes[:, b * LANES : (b + 1) * LANES]
+    wait_all(copies[1:])
+
+    height = back_rows(capacity)
+
+    def place(p, carry):
+        owner = owner_s[p]
+        rank = fill[owner]
+        fill[owner] = rank + 1
+        field_s[p] = owner * height + 4 * rank
+        wet_s[p] = owner * height + 4 * capacity + rank
+        slot_s[p] = owner * capacity + rank
+        rank_s[p] = rank
+        return carry
+
+    lax.fori_loop(0, npairs, place, 0, unroll=32)
+    stores = start_all([(field_s, field_h), (wet_s, wet_h)], out_sems, SENDS)
     wait_all(loads)
-    for copy in copies[1:]:
-        copy.wait()
 
     sub = iota((8, LANES), 0)
     lane = iota((8, LANES), 1)
@@ -118,20 +133,18 @@
     id_rank = jnp.where(sub == 0, lane - NUMBERS, -1)
 
     def pair(p, carry):
-        owner = owner_s[p]
+        slot = slot_s[p]
         row = row_s[p]
-        rank = fill[owner]
-        fill[owner] = rank + 1
+        rank = rank_s[p]
         value = jnp.dot(flux[block_s[p]], weights[tile_s[p]], preferred_element_type=F32)
-        out[pl.ds(owner * message + 4 * rank, 4), :] = value[0:4]
+        out[pl.ds(owner_s[p] * message + 4 * rank, 4), :] = value[0:4]
         tracer = value[8:16]
-        slot = owner * capacity + rank
         row_slots[slot] = pick(edge_row == row, tracer)
         number = (row + 1).astype(F32)
         col_slots[slot] = pick(band == row, pltpu.roll(tracer, row + 2, 1)) + pick(id_rank == rank, number)
         return carry
 
-    lax.fori_loop(0, npairs, pair, 0, unroll=32)
+    lax.fori_loop(0, npairs, pair, 0, unroll=64)
 
     def owner_step(d, carry):
         rows = row_slots[d * capacity]
@@ -157,8 +170,7 @@
     in_band = lane < tile_rows + 4
     in_ids = (sub == 0) & (lane >= NUMBERS) & (lane < NUMBERS + capacity)
     last, first = part == 3, part == 0
-    send = devices // 4
-    stores = []
+    send = devices // SENDS
     for d in range(devices):
         i, j = d // grid_y, d % grid_y
         below = rows_acc[d + grid_y] if i < grid_x - 1 else zero
@@ -188,11 +200,15 @@
     message = 4 * capacity + EDGE
     return pl.pallas_call(
         functools.partial(remap_out_kernel, capacity, grid_y, tile_rows),
-        out_shape=pltpu.HBM((devices * message, LANES), F32),
+        out_shape=(
+            pltpu.HBM((devices * message, LANES), F32),
+            pltpu.HBM((npairs,), I32),
+            pltpu.HBM((npairs,), I32),
+        ),
         in_specs=[hbm()] * 6,
-        out_specs=hbm(),
+        out_specs=(hbm(),) * 3,
         scratch_shapes=[pltpu.VMEM((devices * message, LANES), F32)]
-        + [pltpu.SMEM((npairs,), I32)] * 4
+        + [pltpu.SMEM((npairs,), I32)] * 8
         + [
             pltpu.VMEM(atm_state.shape, F32),
             pltpu.VMEM(remap_weight.shape, BF16),
@@ -204,7 +220,7 @@
             pltpu.VMEM((devices, 8, LANES), F32),
             pltpu.SemaphoreType.DMA((5,)),
             pltpu.SemaphoreType.DMA((PARTS,)),
-            pltpu.SemaphoreType.DMA((4,)),
+            pltpu.SemaphoreType.DMA((SENDS + 2,)),
         ],
         compiler_params=pltpu.CompilerParams(vmem_limit_bytes=40 << 20),
         cost_estimate=pl.CostEstimate(
@@ -474,12 +490,10 @@
     )
 
     row_number = iota((rows_all, LANES), 0).astype(F32) + 1.0
-    lane_field = iota((rows_all, LANES), 1) % 4
     for m in range(groups):
-        hit = numbers[m] == row_number
         for f in range(4):
             placing[f * rows_all : (f + 1) * rows_all, m * LANES : (m + 1) * LANES] = jnp.where(
-                hit & (lane_field == f), 1.0, 0.0
+                pick(lane1 % 4 == f, numbers[m]) == row_number, 1.0, 0.0
             ).astype(BF16)
     edge_rows = jnp.zeros((8, LANES), F32)
     edge_cols = jnp.zeros((8, LANES), F32)
@@ -674,84 +688,73 @@
 
 
 def remap_back_kernel(
-    capacity, block_h, tile_h, owner_h, returned, weights_h, out,
-    block_s, tile_s, owner_s, fill, weights, picked_a, picked_b, total, sems, weight_sems,
+    block_h, tile_h, field_h, wet_h, returned, weights_h, out,
+    block_s, tile_s, field_s, wet_s, weights, picked_a, picked_b, total_0, total_1, total_2, total_3, sems, weight_sems,
 ):
     npairs = block_s.shape[0]
-    nblocks = total.shape[0]
-    devices = fill.shape[0]
-    height = back_rows(capacity)
-    scalars = start_all([(owner_h, owner_s), (block_h, block_s), (tile_h, tile_s)], sems)
+    totals = [total_0, total_1, total_2, total_3]
+    nblocks = total_0.shape[0]
+    scalars = start_all([(field_h, field_s), (wet_h, wet_s), (block_h, block_s), (tile_h, tile_s)], sems)
     part_tiles = weights.shape[0] // PARTS
     parts = [pl.ds(n * part_tiles, part_tiles) for n in range(PARTS)]
     loads = start_all([(weights_h.at[at], weights.at[at]) for at in parts], weight_sems)
-    total[...] = jnp.zeros_like(total)
-
-    def clear_fill(i, carry):
-        fill[i] = 0
-        return carry
-
-    lax.fori_loop(0, devices, clear_fill, 0, unroll=16)
+    for total in totals:
+        total[...] = jnp.zeros_like(total)
     wait_all(scalars)
 
     def gather(p, picked, at):
-        owner = owner_s[p]
-        rank = fill[owner]
-        fill[owner] = rank + 1
-        rows = returned[pl.ds(owner * height + 4 * rank, 4), :]
-        mask = returned[pl.ds(owner * height + 4 * capacity + rank - 4, 5), :]
-        high, low = split(jnp.concatenate([rows, mask[4:5], jnp.zeros((3, LANES), F32)], 0))
+        rows = returned[pl.ds(field_s[p], 4), :]
+        mask = returned[pl.ds(wet_s[p] - 7, 8), :]
+        high, low = split(jnp.concatenate([rows, jnp.zeros((3, LANES), F32), mask[7:8]], 0))
         picked[at] = jnp.concatenate([high, low], 0)
 
-    def product(p, picked, at):
+    def product(p, picked, at, total):
         value = jnp.dot(picked[at], weights[tile_s[p]], preferred_element_type=F32)
         b = block_s[p]
         total[b] = total[b] + (value[0:8] + value[8:16])
 
     half = npairs // 2
+    many = len(totals)
 
     def first(p, carry):
         gather(p, picked_a, p)
         return carry
 
     def both(p, carry):
-        gather(half + p, picked_b, p)
-        product(p, picked_a, p)
+        for n in range(many):
+            gather(half + many * p + n, picked_b, many * p + n)
+            product(many * p + n, picked_a, many * p + n, totals[n])
         return carry
 
     def last(p, carry):
-        product(half + p, picked_b, p)
-        return carry
-
-    lax.fori_loop(0, half, first, 0, unroll=32)
+        for n in range(many):
+            product(half + many * p + n, picked_b, many * p + n, totals[n])
+        return carry
+
+    lax.fori_loop(0, half, first, 0, unroll=64)
     wait_all(loads)
-    lax.fori_loop(0, half, both, 0, unroll=64)
-    lax.fori_loop(0, half, last, 0, unroll=64)
+    lax.fori_loop(0, half // many, both, 0, unroll=32)
+    lax.fori_loop(0, half // many, last, 0, unroll=32)
     for b in range(nblocks):
-        sums = total[b]
-        out[:, b * LANES : (b + 1) * LANES] = sums[0:4] / jnp.maximum(sums[4:5], 0.1)
-
-
-def remap_back(capacity, devices, pair_block, pair_tile, owner, returned, remap_weight, nblocks):
+        sums = (total_0[b] + total_1[b]) + (total_2[b] + total_3[b])
+        out[:, b * LANES : (b + 1) * LANES] = sums[0:4] / jnp.maximum(sums[7:8], 0.1)
+
+
+def remap_back(pair_block, pair_tile, field_at, wet_at, returned, weights, nblocks):
     npairs = pair_block.shape[0]
     return pl.pallas_call(
-        functools.partial(remap_back_kernel, capacity),
+        remap_back_kernel,
         out_shape=jax.ShapeDtypeStruct((4, nblocks * LANES), F32),
-        in_specs=[hbm()] * 3 + [vmem(), hbm()],
+        in_specs=[hbm()] * 4 + [vmem(), hbm()],
         out_specs=vmem(),
-        scratch_shapes=[pltpu.SMEM((npairs,), I32)] * 3
-        + [
-            pltpu.SMEM((devices,), I32),
-            pltpu.VMEM(remap_weight.shape, BF16),
-            pltpu.VMEM((npairs // 2, 16, LANES), BF16),
-            pltpu.VMEM((npairs // 2, 16, LANES), BF16),
-            pltpu.VMEM((nblocks, 8, LANES), F32),
-            pltpu.SemaphoreType.DMA((3,)),
-            pltpu.SemaphoreType.DMA((PARTS,)),
-        ],
+        scratch_shapes=[pltpu.SMEM((npairs,), I32)] * 4
+        + [pltpu.VMEM(weights.shape, BF16)]
+        + [pltpu.VMEM((npairs // 2, 16, LANES), BF16)] * 2
+        + [pltpu.VMEM((nblocks, 8, LANES), F32)] * 4
+        + [pltpu.SemaphoreType.DMA((4,)), pltpu.SemaphoreType.DMA((PARTS,))],
         compiler_params=pltpu.CompilerParams(vmem_limit_bytes=24 << 20),
         cost_estimate=pl.CostEstimate(flops=2 * npairs * 16 * LANES * LANES, bytes_accessed=6 << 20, transcendentals=0),
-    )(*pin(pair_block, pair_tile, owner), returned, *pin(remap_weight))
+    )(*pin(pair_block, pair_tile, field_at, wet_at), returned, *pin(weights))
 
 
 def local(
@@ -775,7 +778,7 @@
     nblocks = atm_state.shape[1] // LANES
     owner = pair_owner.reshape(npairs)
     message = 4 * capacity + EDGE
-    outgoing = remap_out(
+    outgoing, field_at, wet_at = remap_out(
         capacity, grid_y, devices, tile_rows, atm_state, pair_block, owner, pair_row, pair_tile, remap_weight
     )
     arrived = lax.all_to_all(
@@ -798,7 +801,7 @@
     ocean_next = finish(levels, wide, currents, faces, forcing, near)
     weights, _ = lax.optimization_barrier((remap_weight, near))
     atm_surface = remap_back(
-        capacity, devices, pair_block, pair_tile, owner, returned.reshape(-1, LANES), turn(weights), nblocks
+        pair_block, pair_tile, field_at, wet_at, returned.reshape(-1, LANES), turn(weights), nblocks
     )
     return (ocean_next, atm_surface)
 

time: 93.8 us -> 93.5 us (level)
  no operation moved by 1% of the time
where the time goes in v8:
time: 93.5 us; the launch traced here: 93.1 us
  waiting for transfers between devices  34.6 us (37%)
  Pallas kernels  34.4 us (37%)
  starting transfers between devices  22.3 us (24%)
  local copies, waits for them, and re-layouts  1.06 us (1%)
    all_to_all x1, waiting for transfers between devices, local(): lax.all_to_all(sent, ('gx', 'gy'), split_axis=0, concat_axis=0, tiled=True)  20.2 us
    pallas_call x1, Pallas kernels, remap_out(): pl.pallas_call(functools.partial(remap_out_kernel, capacity, grid_y, tile...  7.63 us
    all_to_all x1, starting transfers between devices, local(): lax.all_to_all(outgoing.reshape(devices, message, LANES), ('gx', 'gy'), s...  7.1 us
    pallas_call x1, Pallas kernels, finish(): pl.pallas_call(functools.partial(finish_kernel, levels), out_shape=jax.Sh...  6.85 us
    ppermute x1, waiting for transfers between devices, local(): below = lax.ppermute(edge_up, 'gx', fall_x)  6.38 us
    pallas_call x1, Pallas kernels, remap_back(): pl.pallas_call(remap_back_kernel, out_shape=jax.ShapeDtypeStruct((4, nblo...  5.26 us
    pallas_call x1, Pallas kernels, turn(): pl.pallas_call(turn_kernel, out_shape=pltpu.HBM(remap_weight.shape, BF16)...  4.81 us
    all_to_all x1, starting transfers between devices, local(): lax.all_to_all(sent, ('gx', 'gy'), split_axis=0, concat_axis=0, tiled=True)  4.48 us
  transfers between devices with their start and end apart: 6, of which 6 were waited for; matrix products, arithmetic and copies ran while one was open for 0% of the time, Pallas kernels for 19%

profile of v8, /device:TPU:1, one launch (start us, length us, event | category | flops | bytes accessed | tf_op | source)
XLA Modules:
  0.0 93.1 jit_solution(9834833068857907387)
XLA Ops:
  0.6 7.6 %shard_map.115 = (f32[2560,128]{1,0:T(8,128)}, s32[256]{0:T(256)}, s32[256]{0:T(256)}) custom-call(s32[256]{0:T(256)} %block_h.3, s32[256]{0:T(256)} %bitcast.5, s32[256]{0:T(256)} %row_h.1, s32[256]{0:T(256)} %tile_h.3, f32[6,6144]{1,0:T(8,128)} %atm_h.1, bf16[128,128,128]{2,1,0:T(8,128)(2,1)} %weights_h.2), custom_call_target="tpu_custom_call" | custom-call | flops 134217728 | bytes 6291456 | tf_op jit(solution)/shard_map/pallas_call | solution.py:201
  8.3 0.0 copy-start
  8.3 0.0 copy-start.2
  8.3 0.0 copy-start.3
  8.3 7.1 %all-to-all-start = ((f32[32,80,128]{2,1,0:T(8,128)}), f32[32,80,128]{2,1,0:T(8,128)S(1)}, u32[]{:S(2)}, u32[]{:S(2)}) async-start(f32[32,80,128]{2,1,0:T(8,128)} %bitcast.4), calls=%async_computation | async-start | bytes 2621440 | tf_op jit(solution)/shard_map/all_to_all | solution.py:784
  15.4 0.0 copy-start.1
  15.5 1.0 %copy-done.1 = f32[16,64,128]{2,1,0:T(8,128)S(1)} copy-done((f32[16,64,128]{2,1,0:T(8,128)S(1)}, f32[16,64,128]{2,1,0:T(8,128)}, u32[]{:S(2)}) %copy-start.1) | copy-done | bytes 524312
  16.5 2.8 %shard_map.113 = (f32[50,64,128]{2,1,0:T(8,128)S(1)}, f32[2,16,64,128]{3,2,1,0:T(8,128)}, f32[50,8,128]{2,1,0:T(8,128)S(1)}, f32[50,8,128]{2,1,0:T(8,128)S(1)}) custom-call(f32[4,16,64,128]{3,2,1,0:T(8,128)S(1)} %copy-done, f32[16,64,128]{2,1,0:T(8,128)S(1)} %copy-done.1, f32[64,128]{1,0:T(8,128)S(1)} %copy-done.2, s32[64,128]{1,0:T(8,128)S(1)} %copy-done.3), custom_call_target="tpu_custom_call" | custom-call | flops 20971520 | bytes 6291456 | tf_op jit(solution)/shard_map/pallas_call | solution.py:294
  19.3 3.5 %collective-permute-start = (f32[50,8,128]{2,1,0:T(8,128)S(1)}, f32[50,8,128]{2,1,0:T(8,128)S(1)}, u32[]{:S(2)}, u32[]{:S(2)}) collective-permute-start(f32[50,8,128]{2,1,0:T(8,128)S(1)} %get-tuple-element.18), channel_id=1, source_target_pairs={{0,4},{4,8},{8,12},{12,16},{16,20},{20,24},{24,28},{1,5},{5,9},{9,... | collective-permute-start | bytes 614408 | tf_op jit(solution)/shard_map/ppermute | solution.py:792
  22.8 1.9 %collective-permute-start.1 = (f32[50,8,128]{2,1,0:T(8,128)S(1)}, f32[50,8,128]{2,1,0:T(8,128)S(1)}, u32[]{:S(2)}, u32[]{:S(2)}) collective-permute-start(f32[50,8,128]{2,1,0:T(8,128)S(1)} %get-tuple-element.19), channel_id=1, source_target_pairs={{4,0},{8,4},{12,8},{16,12},{20,16},{24,20},{28,24},{5,1},{9,5},{13... | collective-permute-start | bytes 614408 | tf_op jit(solution)/shard_map/ppermute | solution.py:793
  24.8 2.4 %collective-permute-done.above = f32[50,8,128]{2,1,0:T(8,128)S(1)} collective-permute-done((f32[50,8,128]{2,1,0:T(8,128)S(1)}, f32[50,8,128]{2,1,0:T(8,128)S(1)}, u32[]{:S(2)}, u32[]{:S(2)}) %collective-permute-start) | collective-permute-done | bytes 204832 | tf_op jit(solution)/shard_map/ppermute | solution.py:792
  27.2 6.4 %collective-permute-done.1.below = f32[50,8,128]{2,1,0:T(8,128)S(1)} collective-permute-done((f32[50,8,128]{2,1,0:T(8,128)S(1)}, f32[50,8,128]{2,1,0:T(8,128)S(1)}, u32[]{:S(2)}, u32[]{:S(2)}) %collective-permute-start.1) | collective-permute-done | bytes 204832 | tf_op jit(solution)/shard_map/ppermute | solution.py:793
  33.5 2.9 %shard_map.114 = (f32[50,80,128]{2,1,0:T(8,128)}, f32[2,80,128]{2,1,0:T(8,128)S(1)}, f32[2,80,128]{2,1,0:T(8,128)S(1)}) custom-call(f32[50,64,128]{2,1,0:T(8,128)S(1)} %get-tuple-element.17.tracer, f32[50,8,128]{2,1,0:T(8,128)S(1)} %collective-permute-done.above, f32[50,8,128]{2,1,0:T(8,128)S(1)} %collective-permute-done.1.below), custom_call_target="tpu_custom_call" | custom-call | flops 8388608 | bytes 4194304 | tf_op jit(solution)/shard_map/pallas_call | solution.py:349
  36.5 1.3 %collective-permute-start.3 = (f32[2,80,128]{2,1,0:T(8,128)S(1)}, f32[2,80,128]{2,1,0:T(8,128)S(1)}, u32[]{:S(2)}, u32[]{:S(2)}) collective-permute-start(f32[2,80,128]{2,1,0:T(8,128)S(1)} %get-tuple-element.23.own_left_h), channel_id=1, source_target_pairs={{1,0},{2,1},{3,2},{5,4},{6,5},{7,6},{9,8},{10,9},{11,10},{13,12},{... | collective-permute-start | bytes 245768 | tf_op jit(solution)/shard_map/ppermute | solution.py:796
  37.8 4.0 %collective-permute-start.2 = (f32[2,80,128]{2,1,0:T(8,128)S(1)}, f32[2,80,128]{2,1,0:T(8,128)S(1)}, u32[]{:S(2)}, u32[]{:S(2)}) collective-permute-start(f32[2,80,128]{2,1,0:T(8,128)S(1)} %get-tuple-element.24.own_right_h), channel_id=1, source_target_pairs={{0,1},{1,2},{2,3},{4,5},{5,6},{6,7},{8,9},{9,10},{10,11},{12,13},{... | collective-permute-start | bytes 245768 | tf_op jit(solution)/shard_map/ppermute | solution.py:795
  41.8 1.1 %collective-permute-done.3.from_right_h = f32[2,80,128]{2,1,0:T(8,128)S(1)} collective-permute-done((f32[2,80,128]{2,1,0:T(8,128)S(1)}, f32[2,80,128]{2,1,0:T(8,128)S(1)}, u32[]{:S(2)}, u32[]{:S(2)}) %collective-permute-start.3) | collective-permute-done | bytes 81952 | tf_op jit(solution)/shard_map/ppermute | solution.py:796
  42.8 0.4 collective-permute-done.2.from_left_h
  43.2 4.1 %all-to-all-done.arrived = f32[32,80,128]{2,1,0:T(8,128)S(1)} async-done(((f32[32,80,128]{2,1,0:T(8,128)}), f32[32,80,128]{2,1,0:T(8,128)S(1)}, u32[]{:S(2)}, u32[]{:S(2)}) %all-to-all-start) | async-done | bytes 1310752 | tf_op jit(solution)/shard_map/all_to_all | solution.py:784
  47.3 4.1 %shard_map.116 = (f32[32,80,128]{2,1,0:T(8,128)}, f32[4,80,128]{2,1,0:T(8,128)}, f32[2,80,128]{2,1,0:T(8,128)}, f32[4,80,128]{2,1,0:T(8,128)}) custom-call(f32[32,80,128]{2,1,0:T(8,128)S(1)} %all-to-all-done.arrived, f32[50,80,128]{2,1,0:T(8,128)} %get-tuple-element.20.wide_h, f32[2,16,64,128]{3,2,1,0:T(8,128)} %get-tuple-element.21.currents_h, ...), custom_call_target="tpu_custom_call" | custom-call | flops 209715200 | bytes 4194304 | tf_op jit(solution)/shard_map/pallas_call | solution.py:589
  51.5 4.5 %all-to-all-start.1 = ((f32[32,80,128]{2,1,0:T(8,128)}), f32[32,80,128]{2,1,0:T(8,128)S(1)}, u32[]{:S(2)}, u32[]{:S(2)}) async-start(f32[32,80,128]{2,1,0:T(8,128)} %get-tuple-element.30), calls=%async_computation.1 | async-start | bytes 2621440 | tf_op jit(solution)/shard_map/all_to_all | solution.py:800
  56.0 4.8 %shard_map.118.weights_h = bf16[128,128,128]{2,1,0:T(8,128)(2,1)} custom-call(bf16[128,128,128]{2,1,0:T(8,128)(2,1)} %weights_h.2), custom_call_target="tpu_custom_call" | custom-call | flops 8388608 | bytes 8388608 | tf_op jit(solution)/shard_map/pallas_call | solution.py:679
  60.8 6.8 %shard_map.117 = f32[4,16,64,128]{3,2,1,0:T(8,128)} custom-call(f32[50,80,128]{2,1,0:T(8,128)} %get-tuple-element.20.wide_h, f32[2,16,64,128]{3,2,1,0:T(8,128)} %get-tuple-element.21.currents_h, f32[4,80,128]{2,1,0:T(8,128)} %get-tuple-element.25.faces_h, f32[4,80,128]{2,1,0:T(8,128)} %get-tuple-element.26.forcing_h, f32[2,80,128]{2,1,0:T(8,128)} %get-tuple-element.27.near_h), custom_call_target="tpu_custom_call" | custom-call | flops 41943040 | bytes 6291456 | tf_op jit(solution)/shard_map/pallas_call | solution.py:649
  67.6 20.2 %all-to-all-done.1 = f32[32,80,128]{2,1,0:T(8,128)S(1)} async-done(((f32[32,80,128]{2,1,0:T(8,128)}), f32[32,80,128]{2,1,0:T(8,128)S(1)}, u32[]{:S(2)}, u32[]{:S(2)}) %all-to-all-start.1) | async-done | bytes 1310752 | tf_op jit(solution)/shard_map/all_to_all | solution.py:800
  87.9 5.3 %shard_map.119 = f32[4,6144]{1,0:T(4,128)} custom-call(s32[256]{0:T(256)} %block_h.3, s32[256]{0:T(256)} %tile_h.3, s32[256]{0:T(256)} %get-tuple-element.28.field_h, s32[256]{0:T(256)} %get-tuple-element.29.wet_h, f32[2560,128]{1,0:T(8,128)S(1)} %bitcast.3, bf16[128,128,128]{2,1,0:T(8,128)(2,1)} %shard_map.118.weights_h), custom_call_target="tpu_custom_call" | custom-call | flops 134217728 | bytes 6291456 | tf_op jit(solution)/shard_map/pallas_call | solution.py:745
  (3 shorter events, 0.0 us)
Async XLA Ops:
  8.3 7.1 %copy-start = (f32[4,16,64,128]{3,2,1,0:T(8,128)S(1)}, f32[4,16,64,128]{3,2,1,0:T(8,128)}, u32[]{:S(2)}) copy-start(f32[4,16,64,128]{3,2,1,0:T(8,128)} %state.1) | copy-start | bytes 6291460
  8.3 7.1 %copy-start.2 = (f32[64,128]{1,0:T(8,128)S(1)}, f32[64,128]{1,0:T(8,128)}, u32[]{:S(2)}) copy-start(f32[64,128]{1,0:T(8,128)} %horiz.1) | copy-start | bytes 98308
  8.3 7.1 %copy-start.3 = (s32[64,128]{1,0:T(8,128)S(1)}, s32[64,128]{1,0:T(8,128)}, u32[]{:S(2)}) copy-start(s32[64,128]{1,0:T(8,128)} %wet.1) | copy-start | bytes 98308
  8.3 39.0 %all-to-all-start = ((f32[32,80,128]{2,1,0:T(8,128)}), f32[32,80,128]{2,1,0:T(8,128)S(1)}, u32[]{:S(2)}, u32[]{:S(2)}) async-start(f32[32,80,128]{2,1,0:T(8,128)} %bitcast.4), calls=%async_computation | async-start | bytes 2621440 | tf_op jit(solution)/shard_map/all_to_all | solution.py:784
  15.4 1.0 %copy-start.1 = (f32[16,64,128]{2,1,0:T(8,128)S(1)}, f32[16,64,128]{2,1,0:T(8,128)}, u32[]{:S(2)}) copy-start(f32[16,64,128]{2,1,0:T(8,128)} %kappa.1) | copy-start | bytes 1572868
  19.3 7.9 %collective-permute-start = (f32[50,8,128]{2,1,0:T(8,128)S(1)}, f32[50,8,128]{2,1,0:T(8,128)S(1)}, u32[]{:S(2)}, u32[]{:S(2)}) collective-permute-start(f32[50,8,128]{2,1,0:T(8,128)S(1)} %get-tuple-element.18), channel_id=1, source_target_pairs={{0,4},{4,8},{8,12},{12,16},{16,20},{20,24},{24,28},{1,5},{5,9},{9,... | collective-permute-start | bytes 614408 | tf_op jit(solution)/shard_map/ppermute | solution.py:792
  22.8 10.7 %collective-permute-start.1 = (f32[50,8,128]{2,1,0:T(8,128)S(1)}, f32[50,8,128]{2,1,0:T(8,128)S(1)}, u32[]{:S(2)}, u32[]{:S(2)}) collective-permute-start(f32[50,8,128]{2,1,0:T(8,128)S(1)} %get-tuple-element.19), channel_id=1, source_target_pairs={{4,0},{8,4},{12,8},{16,12},{20,16},{24,20},{28,24},{5,1},{9,5},{13... | collective-permute-start | bytes 614408 | tf_op jit(solution)/shard_map/ppermute | solution.py:793
  36.5 6.4 %collective-permute-start.3 = (f32[2,80,128]{2,1,0:T(8,128)S(1)}, f32[2,80,128]{2,1,0:T(8,128)S(1)}, u32[]{:S(2)}, u32[]{:S(2)}) collective-permute-start(f32[2,80,128]{2,1,0:T(8,128)S(1)} %get-tuple-element.23.own_left_h), channel_id=1, source_target_pairs={{1,0},{2,1},{3,2},{5,4},{6,5},{7,6},{9,8},{10,9},{11,10},{13,12},{... | collective-permute-start | bytes 245768 | tf_op jit(solution)/shard_map/ppermute | solution.py:796
  37.8 5.5 %collective-permute-start.2 = (f32[2,80,128]{2,1,0:T(8,128)S(1)}, f32[2,80,128]{2,1,0:T(8,128)S(1)}, u32[]{:S(2)}, u32[]{:S(2)}) collective-permute-start(f32[2,80,128]{2,1,0:T(8,128)S(1)} %get-tuple-element.24.own_right_h), channel_id=1, source_target_pairs={{0,1},{1,2},{2,3},{4,5},{5,6},{6,7},{8,9},{9,10},{10,11},{12,13},{... | collective-permute-start | bytes 245768 | tf_op jit(solution)/shard_map/ppermute | solution.py:795
  51.5 36.4 %all-to-all-start.1 = ((f32[32,80,128]{2,1,0:T(8,128)}), f32[32,80,128]{2,1,0:T(8,128)S(1)}, u32[]{:S(2)}, u32[]{:S(2)}) async-start(f32[32,80,128]{2,1,0:T(8,128)} %get-tuple-element.30), calls=%async_computation.1 | async-start | bytes 2621440 | tf_op jit(solution)/shard_map/all_to_all | solution.py:800

commit v9 on v8

--- a/solution.py
+++ b/solution.py
@@ -64,7 +64,7 @@
 
 def remap_out_kernel(
     capacity, grid_y, tile_rows, block_h, owner_h, row_h, tile_h, atm_h, weights_h, out_h, field_h, wet_h,
-    out, block_s, owner_s, row_s, tile_s, slot_s, rank_s, field_s, wet_s, atm, weights, flux, fill, row_slots, col_slots, rows_acc, cols_acc, sems, weight_sems, out_sems,
+    out, block_s, owner_s, row_s, tile_s, slot_s, rank_s, field_s, wet_s, atm, weights, atm_rows, flux_rows, flux, fill, row_slots, col_slots, rows_acc, cols_acc, sems, weight_sems, out_sems,
 ):
     devices = fill.shape[0]
     npairs = block_s.shape[0]
@@ -93,25 +93,23 @@
         return carry
 
     lax.fori_loop(0, devices, clear_fill, 0, unroll=16)
-    copies[0].wait()
-    wind_u = atm[0:1, :]
-    wind_v = atm[1:2, :]
+    flux_rows[...] = jnp.zeros_like(flux_rows)
+    wait_all(copies)
+    for b in range(nblocks):
+        atm_rows[8 * b : 8 * b + 6, :] = atm[:, b * LANES : (b + 1) * LANES]
+    wind_u, wind_v, air, dry, rain, sea = [atm_rows[pl.ds(n, nblocks, stride=8), :] for n in range(6)]
     speed = jnp.sqrt(wind_u * wind_u + wind_v * wind_v + 0.25)
-    heat = 0.5 * speed * (atm[2:3, :] - atm[5:6, :])
-    water = atm[4:5, :] - 0.3 * speed * atm[3:4, :]
-    planes = jnp.concatenate(
-        [heat, water, 0.2 * speed * wind_u, 0.2 * speed * wind_v, jnp.zeros((4, wind_u.shape[1]), F32)]
-        + [heat] * 4
-        + [water] * 4,
-        0,
-    ).astype(BF16)
+    heat = 0.5 * speed * (air - sea)
+    water = rain - 0.3 * speed * dry
+    planes = [heat, water, 0.2 * speed * wind_u, 0.2 * speed * wind_v]
+    for n, plane in list(enumerate(planes)) + [(8 + n, heat) for n in range(4)] + [(12 + n, water) for n in range(4)]:
+        flux_rows[pl.ds(n, nblocks, stride=16), :] = plane
     for b in range(nblocks):
-        flux[b] = planes[:, b * LANES : (b + 1) * LANES]
-    wait_all(copies[1:])
+        flux[b] = flux_rows[16 * b : 16 * (b + 1), :].astype(BF16)
 
     height = back_rows(capacity)
 
-    def place(p, carry):
+    for p in range(npairs):
         owner = owner_s[p]
         rank = fill[owner]
         fill[owner] = rank + 1
@@ -119,9 +117,6 @@
         wet_s[p] = owner * height + 4 * capacity + rank
         slot_s[p] = owner * capacity + rank
         rank_s[p] = rank
-        return carry
-
-    lax.fori_loop(0, npairs, place, 0, unroll=32)
     stores = start_all([(field_s, field_h), (wet_s, wet_h)], out_sems, SENDS)
     wait_all(loads)
 
@@ -212,6 +207,8 @@
         + [
             pltpu.VMEM(atm_state.shape, F32),
             pltpu.VMEM(remap_weight.shape, BF16),
+            pltpu.VMEM((nblocks * 8, LANES), F32),
+            pltpu.VMEM((nblocks * 16, LANES), F32),
             pltpu.VMEM((nblocks, 16, LANES), BF16),
             pltpu.SMEM((devices,), I32),
             pltpu.VMEM((devices * capacity, 8, LANES), F32),
@@ -503,12 +500,12 @@
         values[s * span : (s + 1) * span, LANES : 2 * LANES] = low
         edge_rows = edge_rows + arrived[s, span : span + 8, :]
         edge_cols = edge_cols + arrived[s, span + 8 : span + 16, :]
-    total = jnp.dot(placing[...], values[...], preferred_element_type=F32)
-    total = total[:, 0:LANES] + total[:, LANES : 2 * LANES]
-
     wait_all(loads)
     set_faces(levels, top[3], top[4], own_left, own_right, from_left, from_right, faces, packed)
     wet_wide = top[4]
+    total = jnp.dot(placing[...], values[...], preferred_element_type=F32)
+    total = total[:, 0:LANES] + total[:, LANES : 2 * LANES]
+
 
     def plane(f):
         return total[f * rows_all : (f + 1) * rows_all]

time: 93.5 us -> 93.2 us (level)
  no operation moved by 1% of the time
where the time goes in v9:
time: 93.2 us; the launch traced here: 92.9 us
  waiting for transfers between devices  34.6 us (37%)
  Pallas kernels  34.1 us (37%)
  starting transfers between devices  22.3 us (24%)
  local copies, waits for them, and re-layouts  1.06 us (1%)
    all_to_all x1, waiting for transfers between devices, local(): lax.all_to_all(sent, ('gx', 'gy'), split_axis=0, concat_axis=0, tiled=True)  20.2 us
    pallas_call x1, Pallas kernels, remap_out(): pl.pallas_call(functools.partial(remap_out_kernel, capacity, grid_y, tile...  7.57 us
    all_to_all x1, starting transfers between devices, local(): lax.all_to_all(outgoing.reshape(devices, message, LANES), ('gx', 'gy'), s...  7.1 us
    pallas_call x1, Pallas kernels, finish(): pl.pallas_call(functools.partial(finish_kernel, levels), out_shape=jax.Sh...  6.85 us
    ppermute x1, waiting for transfers between devices, local(): below = lax.ppermute(edge_up, 'gx', fall_x)  6.38 us
    pallas_call x1, Pallas kernels, remap_back(): pl.pallas_call(remap_back_kernel, out_shape=jax.ShapeDtypeStruct((4, nblo...  5.27 us
    pallas_call x1, Pallas kernels, turn(): pl.pallas_call(turn_kernel, out_shape=pltpu.HBM(remap_weight.shape, BF16)...  4.81 us
    all_to_all x1, starting transfers between devices, local(): lax.all_to_all(sent, ('gx', 'gy'), split_axis=0, concat_axis=0, tiled=True)  4.48 us
  transfers between devices with their start and end apart: 6, of which 6 were waited for; matrix products, arithmetic and copies ran while one was open for 0% of the time, Pallas kernels for 19%

profile of v9, /device:TPU:1, one launch (start us, length us, event | category | flops | bytes accessed | tf_op | source)
XLA Modules:
  0.0 92.9 jit_solution(2770556445970015027)
XLA Ops:
  0.6 7.6 %shard_map.115 = (f32[2560,128]{1,0:T(8,128)}, s32[256]{0:T(256)}, s32[256]{0:T(256)}) custom-call(s32[256]{0:T(256)} %block_h.3, s32[256]{0:T(256)} %bitcast.5, s32[256]{0:T(256)} %row_h.1, s32[256]{0:T(256)} %tile_h.3, f32[6,6144]{1,0:T(8,128)} %atm_h.1, bf16[128,128,128]{2,1,0:T(8,128)(2,1)} %weights_h.2), custom_call_target="tpu_custom_call" | custom-call | flops 134217728 | bytes 6291456 | tf_op jit(solution)/shard_map/pallas_call | solution.py:196
  8.2 0.0 copy-start
  8.2 0.0 copy-start.2
  8.2 0.0 copy-start.3
  8.2 7.1 %all-to-all-start = ((f32[32,80,128]{2,1,0:T(8,128)}), f32[32,80,128]{2,1,0:T(8,128)S(1)}, u32[]{:S(2)}, u32[]{:S(2)}) async-start(f32[32,80,128]{2,1,0:T(8,128)} %bitcast.4), calls=%async_computation | async-start | bytes 2621440 | tf_op jit(solution)/shard_map/all_to_all | solution.py:781
  15.4 0.0 copy-start.1
  15.4 1.0 %copy-done.1 = f32[16,64,128]{2,1,0:T(8,128)S(1)} copy-done((f32[16,64,128]{2,1,0:T(8,128)S(1)}, f32[16,64,128]{2,1,0:T(8,128)}, u32[]{:S(2)}) %copy-start.1) | copy-done | bytes 524312
  16.4 2.8 %shard_map.113 = (f32[50,64,128]{2,1,0:T(8,128)S(1)}, f32[2,16,64,128]{3,2,1,0:T(8,128)}, f32[50,8,128]{2,1,0:T(8,128)S(1)}, f32[50,8,128]{2,1,0:T(8,128)S(1)}) custom-call(f32[4,16,64,128]{3,2,1,0:T(8,128)S(1)} %copy-done, f32[16,64,128]{2,1,0:T(8,128)S(1)} %copy-done.1, f32[64,128]{1,0:T(8,128)S(1)} %copy-done.2, s32[64,128]{1,0:T(8,128)S(1)} %copy-done.3), custom_call_target="tpu_custom_call" | custom-call | flops 20971520 | bytes 6291456 | tf_op jit(solution)/shard_map/pallas_call | solution.py:291
  19.2 3.5 %collective-permute-start = (f32[50,8,128]{2,1,0:T(8,128)S(1)}, f32[50,8,128]{2,1,0:T(8,128)S(1)}, u32[]{:S(2)}, u32[]{:S(2)}) collective-permute-start(f32[50,8,128]{2,1,0:T(8,128)S(1)} %get-tuple-element.18), channel_id=1, source_target_pairs={{0,4},{4,8},{8,12},{12,16},{16,20},{20,24},{24,28},{1,5},{5,9},{9,... | collective-permute-start | bytes 614408 | tf_op jit(solution)/shard_map/ppermute | solution.py:789
  22.8 1.9 %collective-permute-start.1 = (f32[50,8,128]{2,1,0:T(8,128)S(1)}, f32[50,8,128]{2,1,0:T(8,128)S(1)}, u32[]{:S(2)}, u32[]{:S(2)}) collective-permute-start(f32[50,8,128]{2,1,0:T(8,128)S(1)} %get-tuple-element.19), channel_id=1, source_target_pairs={{4,0},{8,4},{12,8},{16,12},{20,16},{24,20},{28,24},{5,1},{9,5},{13... | collective-permute-start | bytes 614408 | tf_op jit(solution)/shard_map/ppermute | solution.py:790
  24.7 2.4 %collective-permute-done.above = f32[50,8,128]{2,1,0:T(8,128)S(1)} collective-permute-done((f32[50,8,128]{2,1,0:T(8,128)S(1)}, f32[50,8,128]{2,1,0:T(8,128)S(1)}, u32[]{:S(2)}, u32[]{:S(2)}) %collective-permute-start) | collective-permute-done | bytes 204832 | tf_op jit(solution)/shard_map/ppermute | solution.py:789
  27.1 6.4 %collective-permute-done.1.below = f32[50,8,128]{2,1,0:T(8,128)S(1)} collective-permute-done((f32[50,8,128]{2,1,0:T(8,128)S(1)}, f32[50,8,128]{2,1,0:T(8,128)S(1)}, u32[]{:S(2)}, u32[]{:S(2)}) %collective-permute-start.1) | collective-permute-done | bytes 204832 | tf_op jit(solution)/shard_map/ppermute | solution.py:790
  33.5 2.9 %shard_map.114 = (f32[50,80,128]{2,1,0:T(8,128)}, f32[2,80,128]{2,1,0:T(8,128)S(1)}, f32[2,80,128]{2,1,0:T(8,128)S(1)}) custom-call(f32[50,64,128]{2,1,0:T(8,128)S(1)} %get-tuple-element.17.tracer, f32[50,8,128]{2,1,0:T(8,128)S(1)} %collective-permute-done.above, f32[50,8,128]{2,1,0:T(8,128)S(1)} %collective-permute-done.1.below), custom_call_target="tpu_custom_call" | custom-call | flops 8388608 | bytes 4194304 | tf_op jit(solution)/shard_map/pallas_call | solution.py:346
  36.4 1.3 %collective-permute-start.3 = (f32[2,80,128]{2,1,0:T(8,128)S(1)}, f32[2,80,128]{2,1,0:T(8,128)S(1)}, u32[]{:S(2)}, u32[]{:S(2)}) collective-permute-start(f32[2,80,128]{2,1,0:T(8,128)S(1)} %get-tuple-element.23.own_left_h), channel_id=1, source_target_pairs={{1,0},{2,1},{3,2},{5,4},{6,5},{7,6},{9,8},{10,9},{11,10},{13,12},{... | collective-permute-start | bytes 245768 | tf_op jit(solution)/shard_map/ppermute | solution.py:793
  37.7 4.0 %collective-permute-start.2 = (f32[2,80,128]{2,1,0:T(8,128)S(1)}, f32[2,80,128]{2,1,0:T(8,128)S(1)}, u32[]{:S(2)}, u32[]{:S(2)}) collective-permute-start(f32[2,80,128]{2,1,0:T(8,128)S(1)} %get-tuple-element.24.own_right_h), channel_id=1, source_target_pairs={{0,1},{1,2},{2,3},{4,5},{5,6},{6,7},{8,9},{9,10},{10,11},{12,13},{... | collective-permute-start | bytes 245768 | tf_op jit(solution)/shard_map/ppermute | solution.py:792
  41.7 1.1 %collective-permute-done.3.from_right_h = f32[2,80,128]{2,1,0:T(8,128)S(1)} collective-permute-done((f32[2,80,128]{2,1,0:T(8,128)S(1)}, f32[2,80,128]{2,1,0:T(8,128)S(1)}, u32[]{:S(2)}, u32[]{:S(2)}) %collective-permute-start.3) | collective-permute-done | bytes 81952 | tf_op jit(solution)/shard_map/ppermute | solution.py:793
  42.8 0.4 collective-permute-done.2.from_left_h
  43.2 4.1 %all-to-all-done.arrived = f32[32,80,128]{2,1,0:T(8,128)S(1)} async-done(((f32[32,80,128]{2,1,0:T(8,128)}), f32[32,80,128]{2,1,0:T(8,128)S(1)}, u32[]{:S(2)}, u32[]{:S(2)}) %all-to-all-start) | async-done | bytes 1310752 | tf_op jit(solution)/shard_map/all_to_all | solution.py:781
  47.3 3.9 %shard_map.116 = (f32[32,80,128]{2,1,0:T(8,128)}, f32[4,80,128]{2,1,0:T(8,128)}, f32[2,80,128]{2,1,0:T(8,128)}, f32[4,80,128]{2,1,0:T(8,128)}) custom-call(f32[32,80,128]{2,1,0:T(8,128)S(1)} %all-to-all-done.arrived, f32[50,80,128]{2,1,0:T(8,128)} %get-tuple-element.20.wide_h, f32[2,16,64,128]{3,2,1,0:T(8,128)} %get-tuple-element.21.currents_h, ...), custom_call_target="tpu_custom_call" | custom-call | flops 209715200 | bytes 4194304 | tf_op jit(solution)/shard_map/pallas_call | solution.py:586
  51.2 4.5 %all-to-all-start.1 = ((f32[32,80,128]{2,1,0:T(8,128)}), f32[32,80,128]{2,1,0:T(8,128)S(1)}, u32[]{:S(2)}, u32[]{:S(2)}) async-start(f32[32,80,128]{2,1,0:T(8,128)} %get-tuple-element.30), calls=%async_computation.1 | async-start | bytes 2621440 | tf_op jit(solution)/shard_map/all_to_all | solution.py:797
  55.7 4.8 %shard_map.118.weights_h = bf16[128,128,128]{2,1,0:T(8,128)(2,1)} custom-call(bf16[128,128,128]{2,1,0:T(8,128)(2,1)} %weights_h.2), custom_call_target="tpu_custom_call" | custom-call | flops 8388608 | bytes 8388608 | tf_op jit(solution)/shard_map/pallas_call | solution.py:676
  60.5 6.8 %shard_map.117 = f32[4,16,64,128]{3,2,1,0:T(8,128)} custom-call(f32[50,80,128]{2,1,0:T(8,128)} %get-tuple-element.20.wide_h, f32[2,16,64,128]{3,2,1,0:T(8,128)} %get-tuple-element.21.currents_h, f32[4,80,128]{2,1,0:T(8,128)} %get-tuple-element.25.faces_h, f32[4,80,128]{2,1,0:T(8,128)} %get-tuple-element.26.forcing_h, f32[2,80,128]{2,1,0:T(8,128)} %get-tuple-element.27.near_h), custom_call_target="tpu_custom_call" | custom-call | flops 41943040 | bytes 6291456 | tf_op jit(solution)/shard_map/pallas_call | solution.py:646
  67.4 20.2 %all-to-all-done.1 = f32[32,80,128]{2,1,0:T(8,128)S(1)} async-done(((f32[32,80,128]{2,1,0:T(8,128)}), f32[32,80,128]{2,1,0:T(8,128)S(1)}, u32[]{:S(2)}, u32[]{:S(2)}) %all-to-all-start.1) | async-done | bytes 1310752 | tf_op jit(solution)/shard_map/all_to_all | solution.py:797
  87.6 5.3 %shard_map.119 = f32[4,6144]{1,0:T(4,128)} custom-call(s32[256]{0:T(256)} %block_h.3, s32[256]{0:T(256)} %tile_h.3, s32[256]{0:T(256)} %get-tuple-element.28.field_h, s32[256]{0:T(256)} %get-tuple-element.29.wet_h, f32[2560,128]{1,0:T(8,128)S(1)} %bitcast.3, bf16[128,128,128]{2,1,0:T(8,128)(2,1)} %shard_map.118.weights_h), custom_call_target="tpu_custom_call" | custom-call | flops 134217728 | bytes 6291456 | tf_op jit(solution)/shard_map/pallas_call | solution.py:742
  (3 shorter events, 0.0 us)
Async XLA Ops:
  8.2 7.1 %copy-start = (f32[4,16,64,128]{3,2,1,0:T(8,128)S(1)}, f32[4,16,64,128]{3,2,1,0:T(8,128)}, u32[]{:S(2)}) copy-start(f32[4,16,64,128]{3,2,1,0:T(8,128)} %state.1) | copy-start | bytes 6291460
  8.2 7.1 %copy-start.2 = (f32[64,128]{1,0:T(8,128)S(1)}, f32[64,128]{1,0:T(8,128)}, u32[]{:S(2)}) copy-start(f32[64,128]{1,0:T(8,128)} %horiz.1) | copy-start | bytes 98308
  8.2 7.1 %copy-start.3 = (s32[64,128]{1,0:T(8,128)S(1)}, s32[64,128]{1,0:T(8,128)}, u32[]{:S(2)}) copy-start(s32[64,128]{1,0:T(8,128)} %wet.1) | copy-start | bytes 98308
  8.2 39.0 %all-to-all-start = ((f32[32,80,128]{2,1,0:T(8,128)}), f32[32,80,128]{2,1,0:T(8,128)S(1)}, u32[]{:S(2)}, u32[]{:S(2)}) async-start(f32[32,80,128]{2,1,0:T(8,128)} %bitcast.4), calls=%async_computation | async-start | bytes 2621440 | tf_op jit(solution)/shard_map/all_to_all | solution.py:781
  15.4 1.0 %copy-start.1 = (f32[16,64,128]{2,1,0:T(8,128)S(1)}, f32[16,64,128]{2,1,0:T(8,128)}, u32[]{:S(2)}) copy-start(f32[16,64,128]{2,1,0:T(8,128)} %kappa.1) | copy-start | bytes 1572868
  19.2 7.9 %collective-permute-start = (f32[50,8,128]{2,1,0:T(8,128)S(1)}, f32[50,8,128]{2,1,0:T(8,128)S(1)}, u32[]{:S(2)}, u32[]{:S(2)}) collective-permute-start(f32[50,8,128]{2,1,0:T(8,128)S(1)} %get-tuple-element.18), channel_id=1, source_target_pairs={{0,4},{4,8},{8,12},{12,16},{16,20},{20,24},{24,28},{1,5},{5,9},{9,... | collective-permute-start | bytes 614408 | tf_op jit(solution)/shard_map/ppermute | solution.py:789
  22.8 10.7 %collective-permute-start.1 = (f32[50,8,128]{2,1,0:T(8,128)S(1)}, f32[50,8,128]{2,1,0:T(8,128)S(1)}, u32[]{:S(2)}, u32[]{:S(2)}) collective-permute-start(f32[50,8,128]{2,1,0:T(8,128)S(1)} %get-tuple-element.19), channel_id=1, source_target_pairs={{4,0},{8,4},{12,8},{16,12},{20,16},{24,20},{28,24},{5,1},{9,5},{13... | collective-permute-start | bytes 614408 | tf_op jit(solution)/shard_map/ppermute | solution.py:790
  36.4 6.4 %collective-permute-start.3 = (f32[2,80,128]{2,1,0:T(8,128)S(1)}, f32[2,80,128]{2,1,0:T(8,128)S(1)}, u32[]{:S(2)}, u32[]{:S(2)}) collective-permute-start(f32[2,80,128]{2,1,0:T(8,128)S(1)} %get-tuple-element.23.own_left_h), channel_id=1, source_target_pairs={{1,0},{2,1},{3,2},{5,4},{6,5},{7,6},{9,8},{10,9},{11,10},{13,12},{... | collective-permute-start | bytes 245768 | tf_op jit(solution)/shard_map/ppermute | solution.py:793
  37.7 5.5 %collective-permute-start.2 = (f32[2,80,128]{2,1,0:T(8,128)S(1)}, f32[2,80,128]{2,1,0:T(8,128)S(1)}, u32[]{:S(2)}, u32[]{:S(2)}) collective-permute-start(f32[2,80,128]{2,1,0:T(8,128)S(1)} %get-tuple-element.24.own_right_h), channel_id=1, source_target_pairs={{0,1},{1,2},{2,3},{4,5},{5,6},{6,7},{8,9},{9,10},{10,11},{12,13},{... | collective-permute-start | bytes 245768 | tf_op jit(solution)/shard_map/ppermute | solution.py:792
  51.2 36.4 %all-to-all-start.1 = ((f32[32,80,128]{2,1,0:T(8,128)}), f32[32,80,128]{2,1,0:T(8,128)S(1)}, u32[]{:S(2)}, u32[]{:S(2)}) async-start(f32[32,80,128]{2,1,0:T(8,128)} %get-tuple-element.30), calls=%async_computation.1 | async-start | bytes 2621440 | tf_op jit(solution)/shard_map/all_to_all | solution.py:797

commit v10 on v9

--- a/solution.py
+++ b/solution.py
@@ -56,10 +56,6 @@
 def split(value):
     high = value.astype(BF16)
     return high, (value - high.astype(F32)).astype(BF16)
-
-
-def back_rows(capacity):
-    return 4 * capacity + max(8, capacity)
 
 
 def remap_out_kernel(
@@ -107,14 +103,14 @@
     for b in range(nblocks):
         flux[b] = flux_rows[16 * b : 16 * (b + 1), :].astype(BF16)
 
-    height = back_rows(capacity)
+    height = 4 * capacity
 
     for p in range(npairs):
         owner = owner_s[p]
         rank = fill[owner]
         fill[owner] = rank + 1
         field_s[p] = owner * height + 4 * rank
-        wet_s[p] = owner * height + 4 * capacity + rank
+        wet_s[p] = owner * tile_rows + row_s[p]
         slot_s[p] = owner * capacity + rank
         rank_s[p] = rank
     stores = start_all([(field_s, field_h), (wet_s, wet_h)], out_sems, SENDS)
@@ -556,23 +552,12 @@
     lane_t = iota((LANES, 4 * rows_all), 1)
     sub_t = iota((LANES, 4 * rows_all), 0)
     target = jnp.where(sub_t % 4 == lane_t // rows_all, lane_t % rows_all + 1, -1).astype(F32)
-    mask = jnp.concatenate([wet, jnp.zeros((LANES - rows_all, LANES), F32)], 0).astype(BF16)
-    per = LANES // 4
-    slot_number = number_t[pl.ds(0, per, stride=4), :]
-    lane_s = (iota((per, LANES), 1) + 1).astype(F32)
-    height = back_rows(capacity)
     for m in range(groups):
         chosen_rows = jnp.where(number_t[:, m : m + 1] == target, 1.0, 0.0).astype(BF16)
         rows = jnp.dot(chosen_rows, source, preferred_element_type=F32)
         rows = rows[:, 0:LANES] + rows[:, LANES : 2 * LANES]
-        slots = jnp.where(slot_number[:, m : m + 1] == lane_s, 1.0, 0.0).astype(BF16)
-        masks = jnp.dot(slots, mask, preferred_element_type=F32)
         for g in range(group):
-            s = m * group + g
-            sent[s, 0:span, :] = rows[g * span : (g + 1) * span]
-            sent[s, span : span + capacity, :] = masks[g * capacity : (g + 1) * capacity]
-            if height > span + capacity:
-                sent[s, span + capacity : height, :] = jnp.zeros((height - span - capacity, LANES), F32)
+            sent[m * group + g] = rows[g * span : (g + 1) * span]
         at = pl.ds(m * group, group)
         stores += start_all([(sent.at[at], sent_h.at[at])], sent_sems, m)
     wait_all(stores)
@@ -582,7 +567,7 @@
     devices = arrived.shape[0]
     rows = currents.shape[2]
     tall = rows + 2 * HALO
-    height = back_rows(capacity)
+    height = 4 * capacity
     return pl.pallas_call(
         functools.partial(middle_kernel, capacity, levels),
         out_shape=(
@@ -685,13 +670,13 @@
 
 
 def remap_back_kernel(
-    block_h, tile_h, field_h, wet_h, returned, weights_h, out,
-    block_s, tile_s, field_s, wet_s, weights, picked_a, picked_b, total_0, total_1, total_2, total_3, sems, weight_sems,
+    block_h, tile_h, field_h, wet_h, returned, tiles_h, weights_h, out,
+    block_s, tile_s, field_s, wet_s, tiles, weights, picked_a, picked_b, total_0, total_1, total_2, total_3, sems, weight_sems,
 ):
     npairs = block_s.shape[0]
     totals = [total_0, total_1, total_2, total_3]
     nblocks = total_0.shape[0]
-    scalars = start_all([(field_h, field_s), (wet_h, wet_s), (block_h, block_s), (tile_h, tile_s)], sems)
+    scalars = start_all([(field_h, field_s), (wet_h, wet_s), (block_h, block_s), (tile_h, tile_s), (tiles_h, tiles)], sems)
     part_tiles = weights.shape[0] // PARTS
     parts = [pl.ds(n * part_tiles, part_tiles) for n in range(PARTS)]
     loads = start_all([(weights_h.at[at], weights.at[at]) for at in parts], weight_sems)
@@ -701,8 +686,8 @@
 
     def gather(p, picked, at):
         rows = returned[pl.ds(field_s[p], 4), :]
-        mask = returned[pl.ds(wet_s[p] - 7, 8), :]
-        high, low = split(jnp.concatenate([rows, jnp.zeros((3, LANES), F32), mask[7:8]], 0))
+        mask = tiles[pl.ds(wet_s[p], 1), :].astype(F32)
+        high, low = split(jnp.concatenate([rows, mask, jnp.zeros((3, LANES), F32)], 0))
         picked[at] = jnp.concatenate([high, low], 0)
 
     def product(p, picked, at, total):
@@ -734,24 +719,24 @@
     lax.fori_loop(0, half // many, last, 0, unroll=32)
     for b in range(nblocks):
         sums = (total_0[b] + total_1[b]) + (total_2[b] + total_3[b])
-        out[:, b * LANES : (b + 1) * LANES] = sums[0:4] / jnp.maximum(sums[7:8], 0.1)
-
-
-def remap_back(pair_block, pair_tile, field_at, wet_at, returned, weights, nblocks):
+        out[:, b * LANES : (b + 1) * LANES] = sums[0:4] / jnp.maximum(sums[4:5], 0.1)
+
+
+def remap_back(pair_block, pair_tile, field_at, wet_at, returned, tiles, weights, nblocks):
     npairs = pair_block.shape[0]
     return pl.pallas_call(
         remap_back_kernel,
         out_shape=jax.ShapeDtypeStruct((4, nblocks * LANES), F32),
-        in_specs=[hbm()] * 4 + [vmem(), hbm()],
+        in_specs=[hbm()] * 4 + [vmem(), hbm(), hbm()],
         out_specs=vmem(),
         scratch_shapes=[pltpu.SMEM((npairs,), I32)] * 4
-        + [pltpu.VMEM(weights.shape, BF16)]
+        + [pltpu.VMEM(tiles.shape, I32), pltpu.VMEM(weights.shape, BF16)]
         + [pltpu.VMEM((npairs // 2, 16, LANES), BF16)] * 2
         + [pltpu.VMEM((nblocks, 8, LANES), F32)] * 4
-        + [pltpu.SemaphoreType.DMA((4,)), pltpu.SemaphoreType.DMA((PARTS,))],
+        + [pltpu.SemaphoreType.DMA((5,)), pltpu.SemaphoreType.DMA((PARTS,))],
         compiler_params=pltpu.CompilerParams(vmem_limit_bytes=24 << 20),
         cost_estimate=pl.CostEstimate(flops=2 * npairs * 16 * LANES * LANES, bytes_accessed=6 << 20, transcendentals=0),
-    )(*pin(pair_block, pair_tile, field_at, wet_at), returned, *pin(weights))
+    )(*pin(pair_block, pair_tile, field_at, wet_at), returned, *pin(tiles, weights))
 
 
 def local(
@@ -791,6 +776,16 @@
     wide, to_left, to_right = pack(levels, tracer, above, below)
     from_left = lax.ppermute(to_right, "gy", rise_y)
     from_right = lax.ppermute(to_left, "gy", fall_y)
+    line = wet_mask[None]
+    step = 1
+    here = lax.axis_index("gy")
+    while step < grid_y:
+        other = lax.ppermute(line, "gy", [(j, j ^ step) for j in range(grid_y)])
+        lower = (here & step) == 0
+        line = jnp.concatenate([jnp.where(lower, line, other), jnp.where(lower, other, line)], 0)
+        step *= 2
+    arrived, _ = lax.optimization_barrier((arrived, line))
+    wet_all = lax.all_gather(line.reshape(-1, LANES), "gx", axis=0, tiled=True)
     sent, forcing, near, faces = middle(
         capacity, levels, arrived, wide, currents, to_left, to_right, from_left, from_right
     )
@@ -798,7 +793,7 @@
     ocean_next = finish(levels, wide, currents, faces, forcing, near)
     weights, _ = lax.optimization_barrier((remap_weight, near))
     atm_surface = remap_back(
-        pair_block, pair_tile, field_at, wet_at, returned.reshape(-1, LANES), turn(weights), nblocks
+        pair_block, pair_tile, field_at, wet_at, returned.reshape(-1, LANES), wet_all, turn(weights), nblocks
     )
     return (ocean_next, atm_surface)
 

time: 93.2 us -> 129 us (1.38)
  between operations: 0.78 us -> 14.2 us
  waiting for transfers between devices: 34.6 us -> 44.2 us
  starting transfers between devices: 22.3 us -> 28.8 us
  other arithmetic: 0 us -> 2.91 us
  local copies, waits for them, and re-layouts: 1.06 us -> 3.65 us
    ppermute x0 -> x2, waiting for transfers between devices: none -> 20.6 us  [local(): other = lax.ppermute(line, 'gy', [(j, j ^ step) for j in range(grid_y)])]
    all_to_all x1, waiting for transfers between devices: 20.2 us -> 0.01 us  [local(): lax.all_to_all(sent, ('gx', 'gy'), split_axis=0, concat_axis=0, tiled=True)]
    all_gather x0 -> x1, waiting for transfers between devices: none -> 17.6 us  [local(): wet_all = lax.all_gather(line.reshape(-1, LANES), 'gx', axis=0, tiled=True)]
    ppermute x0 -> x2, starting transfers between devices: none -> 5.31 us  [local(): other = lax.ppermute(line, 'gy', [(j, j ^ step) for j in range(grid_y)])]
    all_to_all x1, waiting for transfers between devices: 4.11 us -> 0.01 us  [local(): lax.all_to_all(outgoing.reshape(devices, message, LANES), ('gx', 'gy'), s...]
    unnamed x8 -> x12, local copies, waits for them, and re-layouts: 1.06 us -> 3.65 us
    ppermute x1, waiting for transfers between devices: 2.4 us -> 0.2 us  [local(): above = lax.ppermute(edge_down, 'gx', rise_x)]
    ppermute x1, waiting for transfers between devices: 6.38 us -> 4.29 us  [local(): below = lax.ppermute(edge_up, 'gx', fall_x)]
  transfers between devices with their start and end apart: 6 -> 9, of which waited for: 6 -> 5; matrix products, arithmetic and copies ran while one was open for 0% -> 2% of each run, Pallas kernels for 19% -> 14%
where the time goes in v10:
time: 129 us
  waiting for transfers between devices  44.2 us (34%)
  Pallas kernels  34.8 us (27%)
  starting transfers between devices  28.8 us (22%)
  between operations  14.2 us (11%)
  local copies, waits for them, and re-layouts  3.65 us (3%)
  other arithmetic  2.91 us (2%)
    ppermute x2, waiting for transfers between devices, local(): other = lax.ppermute(line, 'gy', [(j, j ^ step) for j in range(grid_y)])  20.6 us
    all_gather x1, waiting for transfers between devices, local(): wet_all = lax.all_gather(line.reshape(-1, LANES), 'gx', axis=0, tiled=True)  17.6 us
    pallas_call x1, Pallas kernels, remap_out(): pl.pallas_call(functools.partial(remap_out_kernel, capacity, grid_y, tile...  7.46 us
    all_to_all x1, starting transfers between devices, local(): lax.all_to_all(outgoing.reshape(devices, message, LANES), ('gx', 'gy'), s...  7.11 us
    pallas_call x1, Pallas kernels, finish(): pl.pallas_call(functools.partial(finish_kernel, levels), out_shape=jax.Sh...  6.85 us
    pallas_call x1, Pallas kernels, remap_back(): pl.pallas_call(remap_back_kernel, out_shape=jax.ShapeDtypeStruct((4, nblo...  5.7 us
    ppermute x2, starting transfers between devices, local(): other = lax.ppermute(line, 'gy', [(j, j ^ step) for j in range(grid_y)])  5.31 us
    pallas_call x1, Pallas kernels, turn(): pl.pallas_call(turn_kernel, out_shape=pltpu.HBM(remap_weight.shape, BF16)...  4.8 us
  transfers between devices with their start and end apart: 9, of which 5 were waited for; matrix products, arithmetic and copies ran while one was open for 2% of the time, Pallas kernels for 14%

profile of v10, /device:TPU:1, one launch (start us, length us, event | category | flops | bytes accessed | tf_op | source)
XLA Modules:
  0.0 128.6 jit_solution(10151108876510447092)
XLA Ops:
  7.2 7.5 %shard_map.115 = (f32[2560,128]{1,0:T(8,128)}, s32[256]{0:T(256)}, s32[256]{0:T(256)}) custom-call(s32[256]{0:T(256)} %block_h.3, s32[256]{0:T(256)} %bitcast.11, s32[256]{0:T(256)} %row_h.1, s32[256]{0:T(256)} %tile_h.3, f32[6,6144]{1,0:T(8,128)} %atm_h.1, bf16[128,128,128]{2,1,0:T(8,128)(2,1)} %weights_h.2), custom_call_target="tpu_custom_call" | custom-call | flops 134217728 | bytes 6291456 | tf_op jit(solution)/shard_map/pallas_call | solution.py:192
  14.7 7.1 %all-to-all-start = ((f32[32,80,128]{2,1,0:T(8,128)}), f32[32,80,128]{2,1,0:T(8,128)S(1)}, u32[]{:S(2)}, u32[]{:S(2)}) async-start(f32[32,80,128]{2,1,0:T(8,128)} %bitcast.9), calls=%async_computation | async-start | bytes 2621440 | tf_op jit(solution)/shard_map/all_to_all | solution.py:766
  21.8 1.5 %collective-permute-start.2 = (s32[1,64,128]{2,1,0:T(8,128)S(1)}, s32[1,64,128]{2,1,0:T(8,128)}, u32[]{:S(2)}, u32[]{:S(2)}) collective-permute-start(s32[1,64,128]{2,1,0:T(8,128)S(1)} %bitcast.8), channel_id=1, source_target_pairs={{0,1},{1,0},{2,3},{3,2},{4,5},{5,4},{6,7},{7,6},{8,9},{9,8},{10,11... | collective-permute-start | bytes 98312 | tf_op jit(solution)/shard_map/ppermute | solution.py:783
  23.2 20.6 %collective-permute-done.2 = s32[1,64,128]{2,1,0:T(8,128)} collective-permute-done((s32[1,64,128]{2,1,0:T(8,128)S(1)}, s32[1,64,128]{2,1,0:T(8,128)}, u32[]{:S(2)}, u32[]{:S(2)}) %collective-permute-start.2) | collective-permute-done | bytes 32800 | tf_op jit(solution)/shard_map/ppermute | solution.py:783
  43.9 0.8 broadcast_select_fusion.3
  45.3 3.9 %collective-permute-start.3 = (s32[2,64,128]{2,1,0:T(8,128)}, s32[2,64,128]{2,1,0:T(8,128)}, u32[]{:S(2)}, u32[]{:S(2)}) collective-permute-start(s32[2,64,128]{2,1,0:T(8,128)} %pad_add_fusion.1), channel_id=1, source_target_pairs={{0,2},{1,3},{2,0},{3,1},{4,6},{5,7},{6,4},{7,5},{8,10},{9,11},{10,... | collective-permute-start | bytes 196616 | tf_op jit(solution)/shard_map/ppermute | solution.py:783
  49.1 1.0 copy-done.3
  50.2 3.4 %shard_map.113 = (f32[50,64,128]{2,1,0:T(8,128)S(1)}, f32[2,16,64,128]{3,2,1,0:T(8,128)}, f32[50,8,128]{2,1,0:T(8,128)}, f32[50,8,128]{2,1,0:T(8,128)}) custom-call(f32[4,16,64,128]{3,2,1,0:T(8,128)S(1)} %copy-done, f32[16,64,128]{2,1,0:T(8,128)S(1)} %copy-done.3, f32[64,128]{1,0:T(8,128)S(1)} %copy-done.5, s32[64,128]{1,0:T(8,128)S(1)} %copy-done.4), custom_call_target="tpu_custom_call" | custom-call | flops 20971520 | bytes 6291456 | tf_op jit(solution)/shard_map/pallas_call | solution.py:287
  53.6 1.2 copy-done.1
  54.8 4.4 %collective-permute-start = (f32[50,8,128]{2,1,0:T(8,128)}, f32[50,8,128]{2,1,0:T(8,128)S(1)}, u32[]{:S(2)}, u32[]{:S(2)}) collective-permute-start(f32[50,8,128]{2,1,0:T(8,128)} %get-tuple-element.19), channel_id=1, source_target_pairs={{0,4},{4,8},{8,12},{12,16},{16,20},{20,24},{24,28},{1,5},{5,9},{9,... | collective-permute-start | bytes 614408 | tf_op jit(solution)/shard_map/ppermute | solution.py:774
  59.2 1.9 %collective-permute-start.1 = (f32[50,8,128]{2,1,0:T(8,128)}, f32[50,8,128]{2,1,0:T(8,128)S(1)}, u32[]{:S(2)}, u32[]{:S(2)}) collective-permute-start(f32[50,8,128]{2,1,0:T(8,128)} %get-tuple-element.20), channel_id=1, source_target_pairs={{4,0},{8,4},{12,8},{16,12},{20,16},{24,20},{28,24},{5,1},{9,5},{13... | collective-permute-start | bytes 614408 | tf_op jit(solution)/shard_map/ppermute | solution.py:775
  61.2 0.9 broadcast_select_fusion.1
  62.2 4.3 %collective-permute-done.1.below = f32[50,8,128]{2,1,0:T(8,128)S(1)} collective-permute-done((f32[50,8,128]{2,1,0:T(8,128)}, f32[50,8,128]{2,1,0:T(8,128)S(1)}, u32[]{:S(2)}, u32[]{:S(2)}) %collective-permute-start.1) | collective-permute-done | bytes 204832 | tf_op jit(solution)/shard_map/ppermute | solution.py:775
  66.5 1.4 %copy-done.2 = f32[50,64,128]{2,1,0:T(8,128)S(1)} copy-done((f32[50,64,128]{2,1,0:T(8,128)S(1)}, f32[50,64,128]{2,1,0:T(8,128)}, u32[]{:S(2)}) %copy-start.2) | copy-done | bytes 1638424
  67.9 2.9 %shard_map.114 = (f32[50,80,128]{2,1,0:T(8,128)}, f32[2,80,128]{2,1,0:T(8,128)S(1)}, f32[2,80,128]{2,1,0:T(8,128)S(1)}) custom-call(f32[50,64,128]{2,1,0:T(8,128)S(1)} %copy-done.2, f32[50,8,128]{2,1,0:T(8,128)S(1)} %collective-permute-done.above, f32[50,8,128]{2,1,0:T(8,128)S(1)} %collective-permute-done.1.below), custom_call_target="tpu_custom_call" | custom-call | flops 8388608 | bytes 4194304 | tf_op jit(solution)/shard_map/pallas_call | solution.py:342
  70.9 1.3 %collective-permute-start.5 = (f32[2,80,128]{2,1,0:T(8,128)S(1)}, f32[2,80,128]{2,1,0:T(8,128)S(1)}, u32[]{:S(2)}, u32[]{:S(2)}) collective-permute-start(f32[2,80,128]{2,1,0:T(8,128)S(1)} %get-tuple-element.25.own_left_h), channel_id=1, source_target_pairs={{1,0},{2,1},{3,2},{5,4},{6,5},{7,6},{9,8},{10,9},{11,10},{13,12},{... | collective-permute-start | bytes 245768 | tf_op jit(solution)/shard_map/ppermute | solution.py:778
  72.2 4.0 %collective-permute-start.4 = (f32[2,80,128]{2,1,0:T(8,128)S(1)}, f32[2,80,128]{2,1,0:T(8,128)S(1)}, u32[]{:S(2)}, u32[]{:S(2)}) collective-permute-start(f32[2,80,128]{2,1,0:T(8,128)S(1)} %get-tuple-element.26.own_right_h), channel_id=1, source_target_pairs={{0,1},{1,2},{2,3},{4,5},{5,6},{6,7},{8,9},{9,10},{10,11},{12,13},{... | collective-permute-start | bytes 245768 | tf_op jit(solution)/shard_map/ppermute | solution.py:777
  76.8 0.8 collective-permute-done.4.from_left_h
  77.6 3.7 %shard_map.116 = (f32[32,64,128]{2,1,0:T(8,128)}, f32[4,80,128]{2,1,0:T(8,128)}, f32[2,80,128]{2,1,0:T(8,128)}, f32[4,80,128]{2,1,0:T(8,128)}) custom-call(f32[32,80,128]{2,1,0:T(8,128)S(1)} %all-to-all-done.arrived, f32[50,80,128]{2,1,0:T(8,128)} %get-tuple-element.21.wide_h, f32[2,16,64,128]{3,2,1,0:T(8,128)} %get-tuple-element.22.currents_h, ...), custom_call_target="tpu_custom_call" | custom-call | flops 209715200 | bytes 4194304 | tf_op jit(solution)/shard_map/pallas_call | solution.py:571
  81.3 4.7 %all-to-all-start.1 = ((f32[32,64,128]{2,1,0:T(8,128)}), f32[32,64,128]{2,1,0:T(8,128)S(1)}, u32[]{:S(2)}, u32[]{:S(2)}) async-start(f32[32,64,128]{2,1,0:T(8,128)} %get-tuple-element.32), calls=%async_computation.1 | async-start | bytes 2097152 | tf_op jit(solution)/shard_map/all_to_all | solution.py:792
  86.8 4.8 %shard_map.118.weights_h = bf16[128,128,128]{2,1,0:T(8,128)(2,1)} custom-call(bf16[128,128,128]{2,1,0:T(8,128)(2,1)} %weights_h.2), custom_call_target="tpu_custom_call" | custom-call | flops 8388608 | bytes 8388608 | tf_op jit(solution)/shard_map/pallas_call | solution.py:661
  91.6 6.8 %shard_map.117 = f32[4,16,64,128]{3,2,1,0:T(8,128)} custom-call(f32[50,80,128]{2,1,0:T(8,128)} %get-tuple-element.21.wide_h, f32[2,16,64,128]{3,2,1,0:T(8,128)} %get-tuple-element.22.currents_h, f32[4,80,128]{2,1,0:T(8,128)} %get-tuple-element.27.faces_h, f32[4,80,128]{2,1,0:T(8,128)} %get-tuple-element.28.forcing_h, f32[2,80,128]{2,1,0:T(8,128)} %get-tuple-element.29.near_h), custom_call_target="tpu_custom_call" | custom-call | flops 41943040 | bytes 6291456 | tf_op jit(solution)/shard_map/pallas_call | solution.py:631
  98.4 17.6 %all-gather.2.cloned.1.call-done.tiles_h = s32[2048,128]{1,0:T(8,128)} async-done(((s32[256,128]{1,0:T(8,128)}), s32[2048,128]{1,0:T(8,128)}) %all-gather.2.cloned.1.call-update) | async-done | bytes 1048592 | tf_op jit(solution)/shard_map/all_gather | solution.py:788
  116.0 5.7 %shard_map.119 = f32[4,6144]{1,0:T(4,128)} custom-call(s32[256]{0:T(256)} %block_h.3, s32[256]{0:T(256)} %tile_h.3, s32[256]{0:T(256)} %get-tuple-element.30.field_h, s32[256]{0:T(256)} %get-tuple-element.31.wet_h, f32[2048,128]{1,0:T(8,128)S(1)} %bitcast.7, s32[2048,128]{1,0:T(8,128)} %all-gather.2.cloned.1.call-done.tiles_h, ...), custom_call_target="tpu_custom_call" | custom-call | flops 134217728 | bytes 6291456 | tf_op jit(solution)/shard_map/pallas_call | solution.py:727
  (18 shorter events, 2.3 us)
Async XLA Ops:
  14.6 7.2 %copy-start.4 = (s32[64,128]{1,0:T(8,128)S(1)}, s32[64,128]{1,0:T(8,128)}, u32[]{:S(2)}) copy-start(s32[64,128]{1,0:T(8,128)} %wet.1) | copy-start | bytes 98308
  14.6 34.5 %copy-start = (f32[4,16,64,128]{3,2,1,0:T(8,128)S(1)}, f32[4,16,64,128]{3,2,1,0:T(8,128)}, u32[]{:S(2)}) copy-start(f32[4,16,64,128]{3,2,1,0:T(8,128)} %state.1) | copy-start | bytes 6291460
  14.7 34.5 %copy-start.5 = (f32[64,128]{1,0:T(8,128)S(1)}, f32[64,128]{1,0:T(8,128)}, u32[]{:S(2)}) copy-start(f32[64,128]{1,0:T(8,128)} %horiz.1) | copy-start | bytes 98308
  14.7 62.2 %all-to-all-start = ((f32[32,80,128]{2,1,0:T(8,128)}), f32[32,80,128]{2,1,0:T(8,128)S(1)}, u32[]{:S(2)}, u32[]{:S(2)}) async-start(f32[32,80,128]{2,1,0:T(8,128)} %bitcast.9), calls=%async_computation | async-start | bytes 2621440 | tf_op jit(solution)/shard_map/all_to_all | solution.py:766
  21.8 22.1 %collective-permute-start.2 = (s32[1,64,128]{2,1,0:T(8,128)S(1)}, s32[1,64,128]{2,1,0:T(8,128)}, u32[]{:S(2)}, u32[]{:S(2)}) collective-permute-start(s32[1,64,128]{2,1,0:T(8,128)S(1)} %bitcast.8), channel_id=1, source_target_pairs={{0,1},{1,0},{2,3},{3,2},{4,5},{5,4},{6,7},{7,6},{8,9},{9,8},{10,11... | collective-permute-start | bytes 98312 | tf_op jit(solution)/shard_map/ppermute | solution.py:783
  45.3 15.9 %collective-permute-start.3 = (s32[2,64,128]{2,1,0:T(8,128)}, s32[2,64,128]{2,1,0:T(8,128)}, u32[]{:S(2)}, u32[]{:S(2)}) collective-permute-start(s32[2,64,128]{2,1,0:T(8,128)} %pad_add_fusion.1), channel_id=1, source_target_pairs={{0,2},{1,3},{2,0},{3,1},{4,6},{5,7},{6,4},{7,5},{8,10},{9,11},{10,... | collective-permute-start | bytes 196616 | tf_op jit(solution)/shard_map/ppermute | solution.py:783
  49.1 1.0 copy-start.3
  53.6 1.2 copy-start.1
  54.8 7.4 %collective-permute-start = (f32[50,8,128]{2,1,0:T(8,128)}, f32[50,8,128]{2,1,0:T(8,128)S(1)}, u32[]{:S(2)}, u32[]{:S(2)}) collective-permute-start(f32[50,8,128]{2,1,0:T(8,128)} %get-tuple-element.19), channel_id=1, source_target_pairs={{0,4},{4,8},{8,12},{12,16},{16,20},{20,24},{24,28},{1,5},{5,9},{9,... | collective-permute-start | bytes 614408 | tf_op jit(solution)/shard_map/ppermute | solution.py:774
  59.2 7.3 %collective-permute-start.1 = (f32[50,8,128]{2,1,0:T(8,128)}, f32[50,8,128]{2,1,0:T(8,128)S(1)}, u32[]{:S(2)}, u32[]{:S(2)}) collective-permute-start(f32[50,8,128]{2,1,0:T(8,128)} %get-tuple-element.20), channel_id=1, source_target_pairs={{4,0},{8,4},{12,8},{16,12},{20,16},{24,20},{28,24},{5,1},{9,5},{13... | collective-permute-start | bytes 614408 | tf_op jit(solution)/shard_map/ppermute | solution.py:775
  66.5 1.4 %copy-start.2 = (f32[50,64,128]{2,1,0:T(8,128)S(1)}, f32[50,64,128]{2,1,0:T(8,128)}, u32[]{:S(2)}) copy-start(f32[50,64,128]{2,1,0:T(8,128)} %copy-done.1) | copy-start | bytes 4915204
  70.9 6.0 %collective-permute-start.5 = (f32[2,80,128]{2,1,0:T(8,128)S(1)}, f32[2,80,128]{2,1,0:T(8,128)S(1)}, u32[]{:S(2)}, u32[]{:S(2)}) collective-permute-start(f32[2,80,128]{2,1,0:T(8,128)S(1)} %get-tuple-element.25.own_left_h), channel_id=1, source_target_pairs={{1,0},{2,1},{3,2},{5,4},{6,5},{7,6},{9,8},{10,9},{11,10},{13,12},{... | collective-permute-start | bytes 245768 | tf_op jit(solution)/shard_map/ppermute | solution.py:778
  72.2 5.5 %collective-permute-start.4 = (f32[2,80,128]{2,1,0:T(8,128)S(1)}, f32[2,80,128]{2,1,0:T(8,128)S(1)}, u32[]{:S(2)}, u32[]{:S(2)}) collective-permute-start(f32[2,80,128]{2,1,0:T(8,128)S(1)} %get-tuple-element.26.own_right_h), channel_id=1, source_target_pairs={{0,1},{1,2},{2,3},{4,5},{5,6},{6,7},{8,9},{9,10},{10,11},{12,13},{... | collective-permute-start | bytes 245768 | tf_op jit(solution)/shard_map/ppermute | solution.py:777
  81.3 34.7 %all-to-all-start.1 = ((f32[32,64,128]{2,1,0:T(8,128)}), f32[32,64,128]{2,1,0:T(8,128)S(1)}, u32[]{:S(2)}, u32[]{:S(2)}) async-start(f32[32,64,128]{2,1,0:T(8,128)} %get-tuple-element.32), calls=%async_computation.1 | async-start | bytes 2097152 | tf_op jit(solution)/shard_map/all_to_all | solution.py:792
  86.0 30.0 %all-gather.2.cloned.1.call-start = ((), (), s32[]{:S(2)}) async-start(), calls=%async_computation.2 | async-start | bytes 1179648 | tf_op jit(solution)/shard_map/all_gather | solution.py:788
Sparse Core Ops, SparseCore 0:
  88.7 27.2 all-gather.1

commit v11 on v9

--- a/solution.py
+++ b/solution.py
@@ -18,6 +18,7 @@
 NUMBERS = 72
 CORNERS = 112
 SENDS = 8
+AHEAD = 64
 PARTS = 8
 
 
@@ -64,7 +65,7 @@
 
 def remap_out_kernel(
     capacity, grid_y, tile_rows, block_h, owner_h, row_h, tile_h, atm_h, weights_h, out_h, field_h, wet_h,
-    out, block_s, owner_s, row_s, tile_s, slot_s, rank_s, field_s, wet_s, atm, weights, atm_rows, flux_rows, flux, fill, row_slots, col_slots, rows_acc, cols_acc, sems, weight_sems, out_sems,
+    out, block_s, owner_s, row_s, tile_s, rank_s, field_s, wet_s, atm, weights, atm_rows, flux_rows, flux, fill, rows_sum, cols_sum, rows_acc, cols_acc, sems, weight_sems, out_sems,
 ):
     devices = fill.shape[0]
     npairs = block_s.shape[0]
@@ -85,8 +86,8 @@
     for load in loads:
         load.start()
     out[...] = jnp.zeros_like(out)
-    row_slots[...] = jnp.zeros_like(row_slots)
-    col_slots[...] = jnp.zeros_like(col_slots)
+    rows_sum[...] = jnp.zeros_like(rows_sum)
+    cols_sum[...] = jnp.zeros_like(cols_sum)
 
     def clear_fill(i, carry):
         fill[i] = 0
@@ -109,15 +110,17 @@
 
     height = back_rows(capacity)
 
-    for p in range(npairs):
+
+    def place(p):
         owner = owner_s[p]
         rank = fill[owner]
         fill[owner] = rank + 1
         field_s[p] = owner * height + 4 * rank
         wet_s[p] = owner * height + 4 * capacity + rank
-        slot_s[p] = owner * capacity + rank
         rank_s[p] = rank
-    stores = start_all([(field_s, field_h), (wet_s, wet_h)], out_sems, SENDS)
+
+    for p in range(AHEAD):
+        place(p)
     wait_all(loads)
 
     sub = iota((8, LANES), 0)
@@ -127,28 +130,36 @@
     band = ((lane - part) >> 2) * 4 + part
     id_rank = jnp.where(sub == 0, lane - NUMBERS, -1)
 
-    def pair(p, carry):
-        slot = slot_s[p]
+    def pair(p, n):
+        owner = owner_s[p]
         row = row_s[p]
         rank = rank_s[p]
         value = jnp.dot(flux[block_s[p]], weights[tile_s[p]], preferred_element_type=F32)
-        out[pl.ds(owner_s[p] * message + 4 * rank, 4), :] = value[0:4]
+        out[pl.ds(owner * message + 4 * rank, 4), :] = value[0:4]
         tracer = value[8:16]
-        row_slots[slot] = pick(edge_row == row, tracer)
+        rows_sum[n, owner] = rows_sum[n, owner] + pick(edge_row == row, tracer)
         number = (row + 1).astype(F32)
-        col_slots[slot] = pick(band == row, pltpu.roll(tracer, row + 2, 1)) + pick(id_rank == rank, number)
+        cols_sum[n, owner] = cols_sum[n, owner] + (
+            pick(band == row, pltpu.roll(tracer, row + 2, 1)) + pick(id_rank == rank, number)
+        )
+
+    many = rows_sum.shape[0]
+
+    def pairs(more, k, carry):
+        for n in range(many):
+            p = many * k + n
+            if more:
+                place(p + AHEAD)
+            pair(p, n)
         return carry
 
-    lax.fori_loop(0, npairs, pair, 0, unroll=64)
+    lax.fori_loop(0, (npairs - AHEAD) // many, functools.partial(pairs, True), 0, unroll=AHEAD // many)
+    stores = start_all([(field_s, field_h), (wet_s, wet_h)], out_sems, SENDS)
+    lax.fori_loop((npairs - AHEAD) // many, npairs // many, functools.partial(pairs, False), 0, unroll=AHEAD // many)
 
     def owner_step(d, carry):
-        rows = row_slots[d * capacity]
-        cols = col_slots[d * capacity]
-        for r in range(1, capacity):
-            rows = rows + row_slots[d * capacity + r]
-            cols = cols + col_slots[d * capacity + r]
-        rows_acc[d] = rows
-        cols_acc[d] = cols
+        rows_acc[d] = (rows_sum[0, d] + rows_sum[1, d]) + (rows_sum[2, d] + rows_sum[3, d])
+        cols_acc[d] = (cols_sum[0, d] + cols_sum[1, d]) + (cols_sum[2, d] + cols_sum[3, d])
         return carry
 
     lax.fori_loop(0, devices, owner_step, 0, unroll=8)
@@ -203,7 +214,7 @@
         in_specs=[hbm()] * 6,
         out_specs=(hbm(),) * 3,
         scratch_shapes=[pltpu.VMEM((devices * message, LANES), F32)]
-        + [pltpu.SMEM((npairs,), I32)] * 8
+        + [pltpu.SMEM((npairs,), I32)] * 7
         + [
             pltpu.VMEM(atm_state.shape, F32),
             pltpu.VMEM(remap_weight.shape, BF16),
@@ -211,8 +222,8 @@
             pltpu.VMEM((nblocks * 16, LANES), F32),
             pltpu.VMEM((nblocks, 16, LANES), BF16),
             pltpu.SMEM((devices,), I32),
-            pltpu.VMEM((devices * capacity, 8, LANES), F32),
-            pltpu.VMEM((devices * capacity, 8, LANES), F32),
+            pltpu.VMEM((4, devices, 8, LANES), F32),
+            pltpu.VMEM((4, devices, 8, LANES), F32),
             pltpu.VMEM((devices, 8, LANES), F32),
             pltpu.VMEM((devices, 8, LANES), F32),
             pltpu.SemaphoreType.DMA((5,)),
@@ -561,20 +572,22 @@
     slot_number = number_t[pl.ds(0, per, stride=4), :]
     lane_s = (iota((per, LANES), 1) + 1).astype(F32)
     height = back_rows(capacity)
-    for m in range(groups):
-        chosen_rows = jnp.where(number_t[:, m : m + 1] == target, 1.0, 0.0).astype(BF16)
-        rows = jnp.dot(chosen_rows, source, preferred_element_type=F32)
+    many = 4
+    for first in range(0, groups, many):
+        these = range(first, first + many)
+        chosen_rows = [jnp.where(number_t[:, m : m + 1] == target, 1.0, 0.0).astype(BF16) for m in these]
+        rows = jnp.dot(jnp.concatenate(chosen_rows, 0), source, preferred_element_type=F32)
         rows = rows[:, 0:LANES] + rows[:, LANES : 2 * LANES]
-        slots = jnp.where(slot_number[:, m : m + 1] == lane_s, 1.0, 0.0).astype(BF16)
-        masks = jnp.dot(slots, mask, preferred_element_type=F32)
-        for g in range(group):
-            s = m * group + g
+        slots = [jnp.where(slot_number[:, m : m + 1] == lane_s, 1.0, 0.0) for m in these]
+        masks = jnp.dot(jnp.concatenate(slots, 0).astype(BF16), mask, preferred_element_type=F32)
+        for g in range(many * group):
+            s = first * group + g
             sent[s, 0:span, :] = rows[g * span : (g + 1) * span]
             sent[s, span : span + capacity, :] = masks[g * capacity : (g + 1) * capacity]
             if height > span + capacity:
                 sent[s, span + capacity : height, :] = jnp.zeros((height - span - capacity, LANES), F32)
-        at = pl.ds(m * group, group)
-        stores += start_all([(sent.at[at], sent_h.at[at])], sent_sems, m)
+        at = pl.ds(first * group, many * group)
+        stores += start_all([(sent.at[at], sent_h.at[at])], sent_sems, first // many)
     wait_all(stores)
 
 

time: 93.2 us -> 92.8 us (level)
  no operation moved by 1% of the time
where the time goes in v11:
time: 92.8 us; the launch traced here: 92.4 us
  waiting for transfers between devices  34.6 us (37%)
  Pallas kernels  33.7 us (36%)
  starting transfers between devices  22.3 us (24%)
  local copies, waits for them, and re-layouts  1.06 us (1%)
    all_to_all x1, waiting for transfers between devices, local(): lax.all_to_all(sent, ('gx', 'gy'), split_axis=0, concat_axis=0, tiled=True)  20.2 us
    pallas_call x1, Pallas kernels, remap_out(): pl.pallas_call(functools.partial(remap_out_kernel, capacity, grid_y, tile...  7.18 us
    all_to_all x1, starting transfers between devices, local(): lax.all_to_all(outgoing.reshape(devices, message, LANES), ('gx', 'gy'), s...  7.1 us
    pallas_call x1, Pallas kernels, finish(): pl.pallas_call(functools.partial(finish_kernel, levels), out_shape=jax.Sh...  6.85 us
    ppermute x1, waiting for transfers between devices, local(): below = lax.ppermute(edge_up, 'gx', fall_x)  6.38 us
    pallas_call x1, Pallas kernels, remap_back(): pl.pallas_call(remap_back_kernel, out_shape=jax.ShapeDtypeStruct((4, nblo...  5.26 us
    pallas_call x1, Pallas kernels, turn(): pl.pallas_call(turn_kernel, out_shape=pltpu.HBM(remap_weight.shape, BF16)...  4.81 us
    all_to_all x1, starting transfers between devices, local(): lax.all_to_all(sent, ('gx', 'gy'), split_axis=0, concat_axis=0, tiled=True)  4.48 us
  transfers between devices with their start and end apart: 6, of which 6 were waited for; matrix products, arithmetic and copies ran while one was open for 0% of the time, Pallas kernels for 19%

profile of v11, /device:TPU:1, one launch (start us, length us, event | category | flops | bytes accessed | tf_op | source)
XLA Modules:
  0.0 92.4 jit_solution(9154645318712314460)
XLA Ops:
  0.6 7.2 %shard_map.115 = (f32[2560,128]{1,0:T(8,128)}, s32[256]{0:T(256)}, s32[256]{0:T(256)}) custom-call(s32[256]{0:T(256)} %block_h.3, s32[256]{0:T(256)} %bitcast.5, s32[256]{0:T(256)} %row_h.1, s32[256]{0:T(256)} %tile_h.3, f32[6,6144]{1,0:T(8,128)} %atm_h.1, bf16[128,128,128]{2,1,0:T(8,128)(2,1)} %weights_h.2), custom_call_target="tpu_custom_call" | custom-call | flops 134217728 | bytes 6291456 | tf_op jit(solution)/shard_map/pallas_call | solution.py:207
  7.8 0.0 copy-start
  7.8 0.0 copy-start.2
  7.8 0.0 copy-start.3
  7.8 7.1 %all-to-all-start = ((f32[32,80,128]{2,1,0:T(8,128)}), f32[32,80,128]{2,1,0:T(8,128)S(1)}, u32[]{:S(2)}, u32[]{:S(2)}) async-start(f32[32,80,128]{2,1,0:T(8,128)} %bitcast.4), calls=%async_computation | async-start | bytes 2621440 | tf_op jit(solution)/shard_map/all_to_all | solution.py:794
  15.0 0.0 copy-start.1
  15.0 1.0 %copy-done.1 = f32[16,64,128]{2,1,0:T(8,128)S(1)} copy-done((f32[16,64,128]{2,1,0:T(8,128)S(1)}, f32[16,64,128]{2,1,0:T(8,128)}, u32[]{:S(2)}) %copy-start.1) | copy-done | bytes 524312
  16.0 2.8 %shard_map.113 = (f32[50,64,128]{2,1,0:T(8,128)S(1)}, f32[2,16,64,128]{3,2,1,0:T(8,128)}, f32[50,8,128]{2,1,0:T(8,128)S(1)}, f32[50,8,128]{2,1,0:T(8,128)S(1)}) custom-call(f32[4,16,64,128]{3,2,1,0:T(8,128)S(1)} %copy-done, f32[16,64,128]{2,1,0:T(8,128)S(1)} %copy-done.1, f32[64,128]{1,0:T(8,128)S(1)} %copy-done.2, s32[64,128]{1,0:T(8,128)S(1)} %copy-done.3), custom_call_target="tpu_custom_call" | custom-call | flops 20971520 | bytes 6291456 | tf_op jit(solution)/shard_map/pallas_call | solution.py:302
  18.8 3.5 %collective-permute-start = (f32[50,8,128]{2,1,0:T(8,128)S(1)}, f32[50,8,128]{2,1,0:T(8,128)S(1)}, u32[]{:S(2)}, u32[]{:S(2)}) collective-permute-start(f32[50,8,128]{2,1,0:T(8,128)S(1)} %get-tuple-element.18), channel_id=1, source_target_pairs={{0,4},{4,8},{8,12},{12,16},{16,20},{20,24},{24,28},{1,5},{5,9},{9,... | collective-permute-start | bytes 614408 | tf_op jit(solution)/shard_map/ppermute | solution.py:802
  22.4 1.9 %collective-permute-start.1 = (f32[50,8,128]{2,1,0:T(8,128)S(1)}, f32[50,8,128]{2,1,0:T(8,128)S(1)}, u32[]{:S(2)}, u32[]{:S(2)}) collective-permute-start(f32[50,8,128]{2,1,0:T(8,128)S(1)} %get-tuple-element.19), channel_id=1, source_target_pairs={{4,0},{8,4},{12,8},{16,12},{20,16},{24,20},{28,24},{5,1},{9,5},{13... | collective-permute-start | bytes 614408 | tf_op jit(solution)/shard_map/ppermute | solution.py:803
  24.3 2.4 %collective-permute-done.above = f32[50,8,128]{2,1,0:T(8,128)S(1)} collective-permute-done((f32[50,8,128]{2,1,0:T(8,128)S(1)}, f32[50,8,128]{2,1,0:T(8,128)S(1)}, u32[]{:S(2)}, u32[]{:S(2)}) %collective-permute-start) | collective-permute-done | bytes 204832 | tf_op jit(solution)/shard_map/ppermute | solution.py:802
  26.7 6.4 %collective-permute-done.1.below = f32[50,8,128]{2,1,0:T(8,128)S(1)} collective-permute-done((f32[50,8,128]{2,1,0:T(8,128)S(1)}, f32[50,8,128]{2,1,0:T(8,128)S(1)}, u32[]{:S(2)}, u32[]{:S(2)}) %collective-permute-start.1) | collective-permute-done | bytes 204832 | tf_op jit(solution)/shard_map/ppermute | solution.py:803
  33.1 2.9 %shard_map.114 = (f32[50,80,128]{2,1,0:T(8,128)}, f32[2,80,128]{2,1,0:T(8,128)S(1)}, f32[2,80,128]{2,1,0:T(8,128)S(1)}) custom-call(f32[50,64,128]{2,1,0:T(8,128)S(1)} %get-tuple-element.17.tracer, f32[50,8,128]{2,1,0:T(8,128)S(1)} %collective-permute-done.above, f32[50,8,128]{2,1,0:T(8,128)S(1)} %collective-permute-done.1.below), custom_call_target="tpu_custom_call" | custom-call | flops 8388608 | bytes 4194304 | tf_op jit(solution)/shard_map/pallas_call | solution.py:357
  36.0 1.3 %collective-permute-start.3 = (f32[2,80,128]{2,1,0:T(8,128)S(1)}, f32[2,80,128]{2,1,0:T(8,128)S(1)}, u32[]{:S(2)}, u32[]{:S(2)}) collective-permute-start(f32[2,80,128]{2,1,0:T(8,128)S(1)} %get-tuple-element.23.own_left_h), channel_id=1, source_target_pairs={{1,0},{2,1},{3,2},{5,4},{6,5},{7,6},{9,8},{10,9},{11,10},{13,12},{... | collective-permute-start | bytes 245768 | tf_op jit(solution)/shard_map/ppermute | solution.py:806
  37.3 4.0 %collective-permute-start.2 = (f32[2,80,128]{2,1,0:T(8,128)S(1)}, f32[2,80,128]{2,1,0:T(8,128)S(1)}, u32[]{:S(2)}, u32[]{:S(2)}) collective-permute-start(f32[2,80,128]{2,1,0:T(8,128)S(1)} %get-tuple-element.24.own_right_h), channel_id=1, source_target_pairs={{0,1},{1,2},{2,3},{4,5},{5,6},{6,7},{8,9},{9,10},{10,11},{12,13},{... | collective-permute-start | bytes 245768 | tf_op jit(solution)/shard_map/ppermute | solution.py:805
  41.3 1.1 %collective-permute-done.3.from_right_h = f32[2,80,128]{2,1,0:T(8,128)S(1)} collective-permute-done((f32[2,80,128]{2,1,0:T(8,128)S(1)}, f32[2,80,128]{2,1,0:T(8,128)S(1)}, u32[]{:S(2)}, u32[]{:S(2)}) %collective-permute-start.3) | collective-permute-done | bytes 81952 | tf_op jit(solution)/shard_map/ppermute | solution.py:806
  42.4 0.4 collective-permute-done.2.from_left_h
  42.8 4.1 %all-to-all-done.arrived = f32[32,80,128]{2,1,0:T(8,128)S(1)} async-done(((f32[32,80,128]{2,1,0:T(8,128)}), f32[32,80,128]{2,1,0:T(8,128)S(1)}, u32[]{:S(2)}, u32[]{:S(2)}) %all-to-all-start) | async-done | bytes 1310752 | tf_op jit(solution)/shard_map/all_to_all | solution.py:794
  46.9 3.9 %shard_map.116 = (f32[32,80,128]{2,1,0:T(8,128)}, f32[4,80,128]{2,1,0:T(8,128)}, f32[2,80,128]{2,1,0:T(8,128)}, f32[4,80,128]{2,1,0:T(8,128)}) custom-call(f32[32,80,128]{2,1,0:T(8,128)S(1)} %all-to-all-done.arrived, f32[50,80,128]{2,1,0:T(8,128)} %get-tuple-element.20.wide_h, f32[2,16,64,128]{3,2,1,0:T(8,128)} %get-tuple-element.21.currents_h, ...), custom_call_target="tpu_custom_call" | custom-call | flops 209715200 | bytes 4194304 | tf_op jit(solution)/shard_map/pallas_call | solution.py:599
  50.8 4.5 %all-to-all-start.1 = ((f32[32,80,128]{2,1,0:T(8,128)}), f32[32,80,128]{2,1,0:T(8,128)S(1)}, u32[]{:S(2)}, u32[]{:S(2)}) async-start(f32[32,80,128]{2,1,0:T(8,128)} %get-tuple-element.30), calls=%async_computation.1 | async-start | bytes 2621440 | tf_op jit(solution)/shard_map/all_to_all | solution.py:810
  55.2 4.8 %shard_map.118.weights_h = bf16[128,128,128]{2,1,0:T(8,128)(2,1)} custom-call(bf16[128,128,128]{2,1,0:T(8,128)(2,1)} %weights_h.2), custom_call_target="tpu_custom_call" | custom-call | flops 8388608 | bytes 8388608 | tf_op jit(solution)/shard_map/pallas_call | solution.py:689
  60.1 6.8 %shard_map.117 = f32[4,16,64,128]{3,2,1,0:T(8,128)} custom-call(f32[50,80,128]{2,1,0:T(8,128)} %get-tuple-element.20.wide_h, f32[2,16,64,128]{3,2,1,0:T(8,128)} %get-tuple-element.21.currents_h, f32[4,80,128]{2,1,0:T(8,128)} %get-tuple-element.25.faces_h, f32[4,80,128]{2,1,0:T(8,128)} %get-tuple-element.26.forcing_h, f32[2,80,128]{2,1,0:T(8,128)} %get-tuple-element.27.near_h), custom_call_target="tpu_custom_call" | custom-call | flops 41943040 | bytes 6291456 | tf_op jit(solution)/shard_map/pallas_call | solution.py:659
  66.9 20.2 %all-to-all-done.1 = f32[32,80,128]{2,1,0:T(8,128)S(1)} async-done(((f32[32,80,128]{2,1,0:T(8,128)}), f32[32,80,128]{2,1,0:T(8,128)S(1)}, u32[]{:S(2)}, u32[]{:S(2)}) %all-to-all-start.1) | async-done | bytes 1310752 | tf_op jit(solution)/shard_map/all_to_all | solution.py:810
  87.1 5.3 %shard_map.119 = f32[4,6144]{1,0:T(4,128)} custom-call(s32[256]{0:T(256)} %block_h.3, s32[256]{0:T(256)} %tile_h.3, s32[256]{0:T(256)} %get-tuple-element.28.field_h, s32[256]{0:T(256)} %get-tuple-element.29.wet_h, f32[2560,128]{1,0:T(8,128)S(1)} %bitcast.3, bf16[128,128,128]{2,1,0:T(8,128)(2,1)} %shard_map.118.weights_h), custom_call_target="tpu_custom_call" | custom-call | flops 134217728 | bytes 6291456 | tf_op jit(solution)/shard_map/pallas_call | solution.py:755
  (3 shorter events, 0.0 us)
Async XLA Ops:
  7.8 7.1 %copy-start = (f32[4,16,64,128]{3,2,1,0:T(8,128)S(1)}, f32[4,16,64,128]{3,2,1,0:T(8,128)}, u32[]{:S(2)}) copy-start(f32[4,16,64,128]{3,2,1,0:T(8,128)} %state.1) | copy-start | bytes 6291460
  7.8 7.1 %copy-start.2 = (f32[64,128]{1,0:T(8,128)S(1)}, f32[64,128]{1,0:T(8,128)}, u32[]{:S(2)}) copy-start(f32[64,128]{1,0:T(8,128)} %horiz.1) | copy-start | bytes 98308
  7.8 7.1 %copy-start.3 = (s32[64,128]{1,0:T(8,128)S(1)}, s32[64,128]{1,0:T(8,128)}, u32[]{:S(2)}) copy-start(s32[64,128]{1,0:T(8,128)} %wet.1) | copy-start | bytes 98308
  7.8 39.0 %all-to-all-start = ((f32[32,80,128]{2,1,0:T(8,128)}), f32[32,80,128]{2,1,0:T(8,128)S(1)}, u32[]{:S(2)}, u32[]{:S(2)}) async-start(f32[32,80,128]{2,1,0:T(8,128)} %bitcast.4), calls=%async_computation | async-start | bytes 2621440 | tf_op jit(solution)/shard_map/all_to_all | solution.py:794
  15.0 1.0 %copy-start.1 = (f32[16,64,128]{2,1,0:T(8,128)S(1)}, f32[16,64,128]{2,1,0:T(8,128)}, u32[]{:S(2)}) copy-start(f32[16,64,128]{2,1,0:T(8,128)} %kappa.1) | copy-start | bytes 1572868
  18.8 7.9 %collective-permute-start = (f32[50,8,128]{2,1,0:T(8,128)S(1)}, f32[50,8,128]{2,1,0:T(8,128)S(1)}, u32[]{:S(2)}, u32[]{:S(2)}) collective-permute-start(f32[50,8,128]{2,1,0:T(8,128)S(1)} %get-tuple-element.18), channel_id=1, source_target_pairs={{0,4},{4,8},{8,12},{12,16},{16,20},{20,24},{24,28},{1,5},{5,9},{9,... | collective-permute-start | bytes 614408 | tf_op jit(solution)/shard_map/ppermute | solution.py:802
  22.4 10.7 %collective-permute-start.1 = (f32[50,8,128]{2,1,0:T(8,128)S(1)}, f32[50,8,128]{2,1,0:T(8,128)S(1)}, u32[]{:S(2)}, u32[]{:S(2)}) collective-permute-start(f32[50,8,128]{2,1,0:T(8,128)S(1)} %get-tuple-element.19), channel_id=1, source_target_pairs={{4,0},{8,4},{12,8},{16,12},{20,16},{24,20},{28,24},{5,1},{9,5},{13... | collective-permute-start | bytes 614408 | tf_op jit(solution)/shard_map/ppermute | solution.py:803
  36.0 6.4 %collective-permute-start.3 = (f32[2,80,128]{2,1,0:T(8,128)S(1)}, f32[2,80,128]{2,1,0:T(8,128)S(1)}, u32[]{:S(2)}, u32[]{:S(2)}) collective-permute-start(f32[2,80,128]{2,1,0:T(8,128)S(1)} %get-tuple-element.23.own_left_h), channel_id=1, source_target_pairs={{1,0},{2,1},{3,2},{5,4},{6,5},{7,6},{9,8},{10,9},{11,10},{13,12},{... | collective-permute-start | bytes 245768 | tf_op jit(solution)/shard_map/ppermute | solution.py:806
  37.3 5.5 %collective-permute-start.2 = (f32[2,80,128]{2,1,0:T(8,128)S(1)}, f32[2,80,128]{2,1,0:T(8,128)S(1)}, u32[]{:S(2)}, u32[]{:S(2)}) collective-permute-start(f32[2,80,128]{2,1,0:T(8,128)S(1)} %get-tuple-element.24.own_right_h), channel_id=1, source_target_pairs={{0,1},{1,2},{2,3},{4,5},{5,6},{6,7},{8,9},{9,10},{10,11},{12,13},{... | collective-permute-start | bytes 245768 | tf_op jit(solution)/shard_map/ppermute | solution.py:805
  50.8 36.4 %all-to-all-start.1 = ((f32[32,80,128]{2,1,0:T(8,128)}), f32[32,80,128]{2,1,0:T(8,128)S(1)}, u32[]{:S(2)}, u32[]{:S(2)}) async-start(f32[32,80,128]{2,1,0:T(8,128)} %get-tuple-element.30), calls=%async_computation.1 | async-start | bytes 2621440 | tf_op jit(solution)/shard_map/all_to_all | solution.py:810

commit v12 on v11

--- a/solution.py
+++ b/solution.py
@@ -65,7 +65,7 @@
 
 def remap_out_kernel(
     capacity, grid_y, tile_rows, block_h, owner_h, row_h, tile_h, atm_h, weights_h, out_h, field_h, wet_h,
-    out, block_s, owner_s, row_s, tile_s, rank_s, field_s, wet_s, atm, weights, atm_rows, flux_rows, flux, fill, rows_sum, cols_sum, rows_acc, cols_acc, sems, weight_sems, out_sems,
+    out, block_s, owner_s, row_s, tile_s, rank_s, at_s, field_s, wet_s, atm, weights, atm_rows, flux_rows, flux, fill, rows_sum, cols_sum, rows_acc, cols_acc, sems, weight_sems, out_sems,
 ):
     devices = fill.shape[0]
     npairs = block_s.shape[0]
@@ -108,6 +108,7 @@
     for b in range(nblocks):
         flux[b] = flux_rows[16 * b : 16 * (b + 1), :].astype(BF16)
 
+    grid_x = devices // grid_y
     height = back_rows(capacity)
 
 
@@ -115,9 +116,11 @@
         owner = owner_s[p]
         rank = fill[owner]
         fill[owner] = rank + 1
-        field_s[p] = owner * height + 4 * rank
-        wet_s[p] = owner * height + 4 * capacity + rank
+        at = lax.rem(owner, grid_y) * grid_x + lax.div(owner, grid_y)
+        field_s[p] = at * height + 4 * rank
+        wet_s[p] = at * height + 4 * capacity + rank
         rank_s[p] = rank
+        at_s[p] = at
 
     for p in range(AHEAD):
         place(p)
@@ -135,7 +138,7 @@
         row = row_s[p]
         rank = rank_s[p]
         value = jnp.dot(flux[block_s[p]], weights[tile_s[p]], preferred_element_type=F32)
-        out[pl.ds(owner * message + 4 * rank, 4), :] = value[0:4]
+        out[at_s[p], pl.ds(4 * rank, 4), :] = value[0:4]
         tracer = value[8:16]
         rows_sum[n, owner] = rows_sum[n, owner] + pick(edge_row == row, tracer)
         number = (row + 1).astype(F32)
@@ -157,6 +160,9 @@
     stores = start_all([(field_s, field_h), (wet_s, wet_h)], out_sems, SENDS)
     lax.fori_loop((npairs - AHEAD) // many, npairs // many, functools.partial(pairs, False), 0, unroll=AHEAD // many)
 
+    slots = (slice(None), pl.ds(0, 4 * capacity))
+    stores += start_all([(out.at[slots], out_h.at[slots])], out_sems, SENDS + 2)
+
     def owner_step(d, carry):
         rows_acc[d] = (rows_sum[0, d] + rows_sum[1, d]) + (rows_sum[2, d] + rows_sum[3, d])
         cols_acc[d] = (cols_sum[0, d] + cols_sum[1, d]) + (cols_sum[2, d] + cols_sum[3, d])
@@ -164,7 +170,6 @@
 
     lax.fori_loop(0, devices, owner_step, 0, unroll=8)
 
-    grid_x = devices // grid_y
     zero = jnp.zeros((8, LANES), F32)
 
     def columns_of(i, j):
@@ -177,12 +182,13 @@
     in_ids = (sub == 0) & (lane >= NUMBERS) & (lane < NUMBERS + capacity)
     last, first = part == 3, part == 0
     send = devices // SENDS
-    for d in range(devices):
-        i, j = d // grid_y, d % grid_y
+    for at in range(devices):
+        j, i = at // grid_x, at % grid_x
+        d = i * grid_y + j
         below = rows_acc[d + grid_y] if i < grid_x - 1 else zero
         above = rows_acc[d - grid_y] if i > 0 else zero
-        base = d * message + 4 * capacity
-        out[base : base + 8, :] = jnp.where(part < 2, below, above)
+        base = 4 * capacity
+        out[at, base : base + 8, :] = jnp.where(part < 2, below, above)
         tile = pick(in_band, jnp.where(from_left, columns_of(i, j - 1), columns_of(i, j + 1)))
         upper = pick(last & (lane == tile_rows), columns_of(i - 1, j - 1))
         upper = upper + pick(last & (lane == tile_rows + 1), columns_of(i - 1, j + 1))
@@ -190,12 +196,11 @@
         lower = lower + pick(first & (lane == 2), columns_of(i + 1, j + 1))
         tile = tile + pltpu.roll(upper, CORNERS - tile_rows, 1) + pltpu.roll(lower, CORNERS + 1, 1)
         tile = tile + pick(in_ids, cols_acc[d])
-        out[base + 8 : base + 16, :] = tile
-        if d % send == send - 1:
-            n = d // send
-            at = pl.ds(n * send * message, send * message)
-            stores.append(pltpu.make_async_copy(out.at[at], out_h.at[at], out_sems.at[n]))
-            stores[-1].start()
+        out[at, base + 8 : base + 16, :] = tile
+        if at % send == send - 1:
+            n = at // send
+            edges = (pl.ds(n * send, send), pl.ds(base, EDGE))
+            stores += start_all([(out.at[edges], out_h.at[edges])], out_sems, n)
     for store in stores:
         store.wait()
 
@@ -207,14 +212,14 @@
     return pl.pallas_call(
         functools.partial(remap_out_kernel, capacity, grid_y, tile_rows),
         out_shape=(
-            pltpu.HBM((devices * message, LANES), F32),
+            pltpu.HBM((devices, message, LANES), F32),
             pltpu.HBM((npairs,), I32),
             pltpu.HBM((npairs,), I32),
         ),
         in_specs=[hbm()] * 6,
         out_specs=(hbm(),) * 3,
-        scratch_shapes=[pltpu.VMEM((devices * message, LANES), F32)]
-        + [pltpu.SMEM((npairs,), I32)] * 7
+        scratch_shapes=[pltpu.VMEM((devices, message, LANES), F32)]
+        + [pltpu.SMEM((npairs,), I32)] * 8
         + [
             pltpu.VMEM(atm_state.shape, F32),
             pltpu.VMEM(remap_weight.shape, BF16),
@@ -228,7 +233,7 @@
             pltpu.VMEM((devices, 8, LANES), F32),
             pltpu.SemaphoreType.DMA((5,)),
             pltpu.SemaphoreType.DMA((PARTS,)),
-            pltpu.SemaphoreType.DMA((SENDS + 2,)),
+            pltpu.SemaphoreType.DMA((SENDS + 3,)),
         ],
         compiler_params=pltpu.CompilerParams(vmem_limit_bytes=40 << 20),
         cost_estimate=pl.CostEstimate(
@@ -787,12 +792,11 @@
     levels, tile_rows, _ = vert_kappa.shape
     nblocks = atm_state.shape[1] // LANES
     owner = pair_owner.reshape(npairs)
-    message = 4 * capacity + EDGE
     outgoing, field_at, wet_at = remap_out(
         capacity, grid_y, devices, tile_rows, atm_state, pair_block, owner, pair_row, pair_tile, remap_weight
     )
     arrived = lax.all_to_all(
-        outgoing.reshape(devices, message, LANES), ("gx", "gy"), split_axis=0, concat_axis=0, tiled=True
+        outgoing, ("gy", "gx"), split_axis=0, concat_axis=0, tiled=True
     )
     tracer, currents, edge_up, edge_down = solve(ocean_state, vert_kappa, horiz_kappa, wet_mask)
     rise_x = [(i, i + 1) for i in range(grid_x - 1)]
@@ -807,7 +811,7 @@
     sent, forcing, near, faces = middle(
         capacity, levels, arrived, wide, currents, to_left, to_right, from_left, from_right
     )
-    returned = lax.all_to_all(sent, ("gx", "gy"), split_axis=0, concat_axis=0, tiled=True)
+    returned = lax.all_to_all(sent, ("gy", "gx"), split_axis=0, concat_axis=0, tiled=True)
     ocean_next = finish(levels, wide, currents, faces, forcing, near)
     weights, _ = lax.optimization_barrier((remap_weight, near))
     atm_surface = remap_back(

time: 92.8 us -> 94 us (1.013); the launches traced: 92.4 us -> 92.5 us
  waiting for transfers between devices: 34.6 us -> 32.8 us
  starting transfers between devices: 22.3 us -> 23.6 us
    all_to_all x2, waiting for transfers between devices: 24.3 us -> 22.3 us  [the longest x1 19.5 us: local(): lax.all_to_all(sent, ('gy', 'gx'), split_axis=0, concat_axis=0, tiled=True)]
    ppermute x1, waiting for transfers between devices: 1.06 us -> 0.01 us  [local(): from_right = lax.ppermute(to_left, 'gy', fall_y)]
    ppermute x1, waiting for transfers between devices: 0.41 us -> 1.45 us  [local(): from_left = lax.ppermute(to_right, 'gy', rise_y)]
  transfers between devices with their start and end apart: 6 -> 6, of which waited for: 6 -> 5; matrix products, arithmetic and copies ran while one was open for 0% -> 0% of each run, Pallas kernels for 19% -> 19%
where the time goes in v12:
time: 94 us; the launch traced here: 92.5 us
  Pallas kernels  34.2 us (36%)
  waiting for transfers between devices  32.8 us (35%)
  starting transfers between devices  23.6 us (25%)
  local copies, waits for them, and re-layouts  1.06 us (1%)
    all_to_all x1, waiting for transfers between devices, local(): lax.all_to_all(sent, ('gy', 'gx'), split_axis=0, concat_axis=0, tiled=True)  19.5 us
    pallas_call x1, Pallas kernels, remap_out(): pl.pallas_call(functools.partial(remap_out_kernel, capacity, grid_y, tile...  7.67 us
    ppermute x1, waiting for transfers between devices, local(): below = lax.ppermute(edge_up, 'gx', fall_x)  7.22 us
    all_to_all x1, starting transfers between devices, local(): lax.all_to_all(outgoing, ('gy', 'gx'), split_axis=0, concat_axis=0, tiled...  7.1 us
    pallas_call x1, Pallas kernels, finish(): pl.pallas_call(functools.partial(finish_kernel, levels), out_shape=jax.Sh...  6.85 us
    all_to_all x1, starting transfers between devices, local(): lax.all_to_all(sent, ('gy', 'gx'), split_axis=0, concat_axis=0, tiled=True)  5.4 us
    pallas_call x1, Pallas kernels, remap_back(): pl.pallas_call(remap_back_kernel, out_shape=jax.ShapeDtypeStruct((4, nblo...  5.26 us
    pallas_call x1, Pallas kernels, turn(): pl.pallas_call(turn_kernel, out_shape=pltpu.HBM(remap_weight.shape, BF16)...  4.81 us
  transfers between devices with their start and end apart: 6, of which 5 were waited for; matrix products, arithmetic and copies ran while one was open for 0% of the time, Pallas kernels for 19%

profile of v12, /device:TPU:1, one launch (start us, length us, event | category | flops | bytes accessed | tf_op | source)
XLA Modules:
  0.0 92.5 jit_solution(12672343186928294506)
XLA Ops:
  0.6 7.7 %shard_map.115 = (f32[32,80,128]{2,1,0:T(8,128)}, s32[256]{0:T(256)}, s32[256]{0:T(256)}) custom-call(s32[256]{0:T(256)} %block_h.3, s32[256]{0:T(256)} %bitcast.3, s32[256]{0:T(256)} %row_h.1, s32[256]{0:T(256)} %tile_h.3, f32[6,6144]{1,0:T(8,128)} %atm_h.1, bf16[128,128,128]{2,1,0:T(8,128)(2,1)} %weights_h.2), custom_call_target="tpu_custom_call" | custom-call | flops 134217728 | bytes 6291456 | tf_op jit(solution)/shard_map/pallas_call | solution.py:212
  8.3 0.0 copy-start
  8.3 0.0 copy-start.2
  8.3 0.0 copy-start.3
  8.3 7.1 %all-to-all-start = ((f32[32,80,128]{2,1,0:T(8,128)}), f32[32,80,128]{2,1,0:T(8,128)S(1)}, u32[]{:S(2)}, u32[]{:S(2)}) async-start(f32[32,80,128]{2,1,0:T(8,128)} %get-tuple-element.22), calls=%async_computation | async-start | bytes 2621440 | tf_op jit(solution)/shard_map/all_to_all | solution.py:798
  15.5 0.0 copy-start.1
  15.5 1.0 %copy-done.1 = f32[16,64,128]{2,1,0:T(8,128)S(1)} copy-done((f32[16,64,128]{2,1,0:T(8,128)S(1)}, f32[16,64,128]{2,1,0:T(8,128)}, u32[]{:S(2)}) %copy-start.1) | copy-done | bytes 524312
  16.5 2.8 %shard_map.113 = (f32[50,64,128]{2,1,0:T(8,128)S(1)}, f32[2,16,64,128]{3,2,1,0:T(8,128)}, f32[50,8,128]{2,1,0:T(8,128)S(1)}, f32[50,8,128]{2,1,0:T(8,128)S(1)}) custom-call(f32[4,16,64,128]{3,2,1,0:T(8,128)S(1)} %copy-done, f32[16,64,128]{2,1,0:T(8,128)S(1)} %copy-done.1, f32[64,128]{1,0:T(8,128)S(1)} %copy-done.2, s32[64,128]{1,0:T(8,128)S(1)} %copy-done.3), custom_call_target="tpu_custom_call" | custom-call | flops 20971520 | bytes 6291456 | tf_op jit(solution)/shard_map/pallas_call | solution.py:307
  19.3 3.5 %collective-permute-start = (f32[50,8,128]{2,1,0:T(8,128)S(1)}, f32[50,8,128]{2,1,0:T(8,128)S(1)}, u32[]{:S(2)}, u32[]{:S(2)}) collective-permute-start(f32[50,8,128]{2,1,0:T(8,128)S(1)} %get-tuple-element.18), channel_id=1, source_target_pairs={{0,4},{4,8},{8,12},{12,16},{16,20},{20,24},{24,28},{1,5},{5,9},{9,... | collective-permute-start | bytes 614408 | tf_op jit(solution)/shard_map/ppermute | solution.py:806
  22.9 1.9 %collective-permute-start.1 = (f32[50,8,128]{2,1,0:T(8,128)S(1)}, f32[50,8,128]{2,1,0:T(8,128)S(1)}, u32[]{:S(2)}, u32[]{:S(2)}) collective-permute-start(f32[50,8,128]{2,1,0:T(8,128)S(1)} %get-tuple-element.19), channel_id=1, source_target_pairs={{4,0},{8,4},{12,8},{16,12},{20,16},{24,20},{28,24},{5,1},{9,5},{13... | collective-permute-start | bytes 614408 | tf_op jit(solution)/shard_map/ppermute | solution.py:807
  24.8 1.9 %collective-permute-done.above = f32[50,8,128]{2,1,0:T(8,128)S(1)} collective-permute-done((f32[50,8,128]{2,1,0:T(8,128)S(1)}, f32[50,8,128]{2,1,0:T(8,128)S(1)}, u32[]{:S(2)}, u32[]{:S(2)}) %collective-permute-start) | collective-permute-done | bytes 204832 | tf_op jit(solution)/shard_map/ppermute | solution.py:806
  26.7 7.2 %collective-permute-done.1.below = f32[50,8,128]{2,1,0:T(8,128)S(1)} collective-permute-done((f32[50,8,128]{2,1,0:T(8,128)S(1)}, f32[50,8,128]{2,1,0:T(8,128)S(1)}, u32[]{:S(2)}, u32[]{:S(2)}) %collective-permute-start.1) | collective-permute-done | bytes 204832 | tf_op jit(solution)/shard_map/ppermute | solution.py:807
  33.9 2.9 %shard_map.114 = (f32[50,80,128]{2,1,0:T(8,128)}, f32[2,80,128]{2,1,0:T(8,128)S(1)}, f32[2,80,128]{2,1,0:T(8,128)S(1)}) custom-call(f32[50,64,128]{2,1,0:T(8,128)S(1)} %get-tuple-element.17.tracer, f32[50,8,128]{2,1,0:T(8,128)S(1)} %collective-permute-done.above, f32[50,8,128]{2,1,0:T(8,128)S(1)} %collective-permute-done.1.below), custom_call_target="tpu_custom_call" | custom-call | flops 8388608 | bytes 4194304 | tf_op jit(solution)/shard_map/pallas_call | solution.py:362
  36.8 1.3 %collective-permute-start.3 = (f32[2,80,128]{2,1,0:T(8,128)S(1)}, f32[2,80,128]{2,1,0:T(8,128)S(1)}, u32[]{:S(2)}, u32[]{:S(2)}) collective-permute-start(f32[2,80,128]{2,1,0:T(8,128)S(1)} %get-tuple-element.23.own_left_h), channel_id=1, source_target_pairs={{1,0},{2,1},{3,2},{5,4},{6,5},{7,6},{9,8},{10,9},{11,10},{13,12},{... | collective-permute-start | bytes 245768 | tf_op jit(solution)/shard_map/ppermute | solution.py:810
  38.1 4.3 %collective-permute-start.2 = (f32[2,80,128]{2,1,0:T(8,128)S(1)}, f32[2,80,128]{2,1,0:T(8,128)S(1)}, u32[]{:S(2)}, u32[]{:S(2)}) collective-permute-start(f32[2,80,128]{2,1,0:T(8,128)S(1)} %get-tuple-element.24.own_right_h), channel_id=1, source_target_pairs={{0,1},{1,2},{2,3},{4,5},{5,6},{6,7},{8,9},{9,10},{10,11},{12,13},{... | collective-permute-start | bytes 245768 | tf_op jit(solution)/shard_map/ppermute | solution.py:809
  42.5 0.0 collective-permute-done.3.from_right_h
  42.5 1.5 %collective-permute-done.2.from_left_h = f32[2,80,128]{2,1,0:T(8,128)S(1)} collective-permute-done((f32[2,80,128]{2,1,0:T(8,128)S(1)}, f32[2,80,128]{2,1,0:T(8,128)S(1)}, u32[]{:S(2)}, u32[]{:S(2)}) %collective-permute-start.2) | collective-permute-done | bytes 81952 | tf_op jit(solution)/shard_map/ppermute | solution.py:809
  43.9 2.8 %all-to-all-done.arrived = f32[32,80,128]{2,1,0:T(8,128)S(1)} async-done(((f32[32,80,128]{2,1,0:T(8,128)}), f32[32,80,128]{2,1,0:T(8,128)S(1)}, u32[]{:S(2)}, u32[]{:S(2)}) %all-to-all-start) | async-done | bytes 1310752 | tf_op jit(solution)/shard_map/all_to_all | solution.py:798
  46.7 3.9 %shard_map.116 = (f32[32,80,128]{2,1,0:T(8,128)}, f32[4,80,128]{2,1,0:T(8,128)}, f32[2,80,128]{2,1,0:T(8,128)}, f32[4,80,128]{2,1,0:T(8,128)}) custom-call(f32[32,80,128]{2,1,0:T(8,128)S(1)} %all-to-all-done.arrived, f32[50,80,128]{2,1,0:T(8,128)} %get-tuple-element.20.wide_h, f32[2,16,64,128]{3,2,1,0:T(8,128)} %get-tuple-element.21.currents_h, ...), custom_call_target="tpu_custom_call" | custom-call | flops 209715200 | bytes 4194304 | tf_op jit(solution)/shard_map/pallas_call | solution.py:604
  50.6 5.4 %all-to-all-start.1 = ((f32[32,80,128]{2,1,0:T(8,128)}), f32[32,80,128]{2,1,0:T(8,128)S(1)}, u32[]{:S(2)}, u32[]{:S(2)}) async-start(f32[32,80,128]{2,1,0:T(8,128)} %get-tuple-element.30), calls=%async_computation.1 | async-start | bytes 2621440 | tf_op jit(solution)/shard_map/all_to_all | solution.py:814
  56.0 4.8 %shard_map.118.weights_h = bf16[128,128,128]{2,1,0:T(8,128)(2,1)} custom-call(bf16[128,128,128]{2,1,0:T(8,128)(2,1)} %weights_h.2), custom_call_target="tpu_custom_call" | custom-call | flops 8388608 | bytes 8388608 | tf_op jit(solution)/shard_map/pallas_call | solution.py:694
  60.8 6.8 %shard_map.117 = f32[4,16,64,128]{3,2,1,0:T(8,128)} custom-call(f32[50,80,128]{2,1,0:T(8,128)} %get-tuple-element.20.wide_h, f32[2,16,64,128]{3,2,1,0:T(8,128)} %get-tuple-element.21.currents_h, f32[4,80,128]{2,1,0:T(8,128)} %get-tuple-element.25.faces_h, f32[4,80,128]{2,1,0:T(8,128)} %get-tuple-element.26.forcing_h, f32[2,80,128]{2,1,0:T(8,128)} %get-tuple-element.27.near_h), custom_call_target="tpu_custom_call" | custom-call | flops 41943040 | bytes 6291456 | tf_op jit(solution)/shard_map/pallas_call | solution.py:664
  67.6 19.5 %all-to-all-done.1 = f32[32,80,128]{2,1,0:T(8,128)S(1)} async-done(((f32[32,80,128]{2,1,0:T(8,128)}), f32[32,80,128]{2,1,0:T(8,128)S(1)}, u32[]{:S(2)}, u32[]{:S(2)}) %all-to-all-start.1) | async-done | bytes 1310752 | tf_op jit(solution)/shard_map/all_to_all | solution.py:814
  87.2 5.3 %shard_map.119 = f32[4,6144]{1,0:T(4,128)} custom-call(s32[256]{0:T(256)} %block_h.3, s32[256]{0:T(256)} %tile_h.3, s32[256]{0:T(256)} %get-tuple-element.28.field_h, s32[256]{0:T(256)} %get-tuple-element.29.wet_h, f32[2560,128]{1,0:T(8,128)S(1)} %bitcast.2, bf16[128,128,128]{2,1,0:T(8,128)(2,1)} %shard_map.118.weights_h), custom_call_target="tpu_custom_call" | custom-call | flops 134217728 | bytes 6291456 | tf_op jit(solution)/shard_map/pallas_call | solution.py:760
  (3 shorter events, 0.0 us)
Async XLA Ops:
  8.3 7.1 %copy-start = (f32[4,16,64,128]{3,2,1,0:T(8,128)S(1)}, f32[4,16,64,128]{3,2,1,0:T(8,128)}, u32[]{:S(2)}) copy-start(f32[4,16,64,128]{3,2,1,0:T(8,128)} %state.1) | copy-start | bytes 6291460
  8.3 7.1 %copy-start.2 = (f32[64,128]{1,0:T(8,128)S(1)}, f32[64,128]{1,0:T(8,128)}, u32[]{:S(2)}) copy-start(f32[64,128]{1,0:T(8,128)} %horiz.1) | copy-start | bytes 98308
  8.3 7.1 %copy-start.3 = (s32[64,128]{1,0:T(8,128)S(1)}, s32[64,128]{1,0:T(8,128)}, u32[]{:S(2)}) copy-start(s32[64,128]{1,0:T(8,128)} %wet.1) | copy-start | bytes 98308
  8.3 38.3 %all-to-all-start = ((f32[32,80,128]{2,1,0:T(8,128)}), f32[32,80,128]{2,1,0:T(8,128)S(1)}, u32[]{:S(2)}, u32[]{:S(2)}) async-start(f32[32,80,128]{2,1,0:T(8,128)} %get-tuple-element.22), calls=%async_computation | async-start | bytes 2621440 | tf_op jit(solution)/shard_map/all_to_all | solution.py:798
  15.5 1.0 %copy-start.1 = (f32[16,64,128]{2,1,0:T(8,128)S(1)}, f32[16,64,128]{2,1,0:T(8,128)}, u32[]{:S(2)}) copy-start(f32[16,64,128]{2,1,0:T(8,128)} %kappa.1) | copy-start | bytes 1572868
  19.3 7.3 %collective-permute-start = (f32[50,8,128]{2,1,0:T(8,128)S(1)}, f32[50,8,128]{2,1,0:T(8,128)S(1)}, u32[]{:S(2)}, u32[]{:S(2)}) collective-permute-start(f32[50,8,128]{2,1,0:T(8,128)S(1)} %get-tuple-element.18), channel_id=1, source_target_pairs={{0,4},{4,8},{8,12},{12,16},{16,20},{20,24},{24,28},{1,5},{5,9},{9,... | collective-permute-start | bytes 614408 | tf_op jit(solution)/shard_map/ppermute | solution.py:806
  22.9 11.0 %collective-permute-start.1 = (f32[50,8,128]{2,1,0:T(8,128)S(1)}, f32[50,8,128]{2,1,0:T(8,128)S(1)}, u32[]{:S(2)}, u32[]{:S(2)}) collective-permute-start(f32[50,8,128]{2,1,0:T(8,128)S(1)} %get-tuple-element.19), channel_id=1, source_target_pairs={{4,0},{8,4},{12,8},{16,12},{20,16},{24,20},{28,24},{5,1},{9,5},{13... | collective-permute-start | bytes 614408 | tf_op jit(solution)/shard_map/ppermute | solution.py:807
  36.8 5.7 %collective-permute-start.3 = (f32[2,80,128]{2,1,0:T(8,128)S(1)}, f32[2,80,128]{2,1,0:T(8,128)S(1)}, u32[]{:S(2)}, u32[]{:S(2)}) collective-permute-start(f32[2,80,128]{2,1,0:T(8,128)S(1)} %get-tuple-element.23.own_left_h), channel_id=1, source_target_pairs={{1,0},{2,1},{3,2},{5,4},{6,5},{7,6},{9,8},{10,9},{11,10},{13,12},{... | collective-permute-start | bytes 245768 | tf_op jit(solution)/shard_map/ppermute | solution.py:810
  38.1 5.8 %collective-permute-start.2 = (f32[2,80,128]{2,1,0:T(8,128)S(1)}, f32[2,80,128]{2,1,0:T(8,128)S(1)}, u32[]{:S(2)}, u32[]{:S(2)}) collective-permute-start(f32[2,80,128]{2,1,0:T(8,128)S(1)} %get-tuple-element.24.own_right_h), channel_id=1, source_target_pairs={{0,1},{1,2},{2,3},{4,5},{5,6},{6,7},{8,9},{9,10},{10,11},{12,13},{... | collective-permute-start | bytes 245768 | tf_op jit(solution)/shard_map/ppermute | solution.py:809
  50.6 36.6 %all-to-all-start.1 = ((f32[32,80,128]{2,1,0:T(8,128)}), f32[32,80,128]{2,1,0:T(8,128)S(1)}, u32[]{:S(2)}, u32[]{:S(2)}) async-start(f32[32,80,128]{2,1,0:T(8,128)} %get-tuple-element.30), calls=%async_computation.1 | async-start | bytes 2621440 | tf_op jit(solution)/shard_map/all_to_all | solution.py:814

commit v13 on v11

--- a/solution.py
+++ b/solution.py
@@ -18,7 +18,7 @@
 NUMBERS = 72
 CORNERS = 112
 SENDS = 8
-AHEAD = 64
+AHEAD = 32
 PARTS = 8
 
 
@@ -87,6 +87,8 @@
         load.start()
     out[...] = jnp.zeros_like(out)
     rows_sum[...] = jnp.zeros_like(rows_sum)
+    rows_acc[...] = jnp.zeros_like(rows_acc)
+    cols_acc[...] = jnp.zeros_like(cols_acc)
     cols_sum[...] = jnp.zeros_like(cols_sum)
 
     def clear_fill(i, carry):
@@ -157,45 +159,42 @@
     stores = start_all([(field_s, field_h), (wet_s, wet_h)], out_sems, SENDS)
     lax.fori_loop((npairs - AHEAD) // many, npairs // many, functools.partial(pairs, False), 0, unroll=AHEAD // many)
 
+    across = grid_y + 2
+
+    def inside(d):
+        return (lax.div(d, grid_y) + 1) * across + lax.rem(d, grid_y) + 1
+
     def owner_step(d, carry):
-        rows_acc[d] = (rows_sum[0, d] + rows_sum[1, d]) + (rows_sum[2, d] + rows_sum[3, d])
-        cols_acc[d] = (cols_sum[0, d] + cols_sum[1, d]) + (cols_sum[2, d] + cols_sum[3, d])
+        at = inside(d)
+        rows_acc[at] = (rows_sum[0, d] + rows_sum[1, d]) + (rows_sum[2, d] + rows_sum[3, d])
+        cols_acc[at] = (cols_sum[0, d] + cols_sum[1, d]) + (cols_sum[2, d] + cols_sum[3, d])
         return carry
 
     lax.fori_loop(0, devices, owner_step, 0, unroll=8)
-
-    grid_x = devices // grid_y
-    zero = jnp.zeros((8, LANES), F32)
-
-    def columns_of(i, j):
-        if not (0 <= i < grid_x and 0 <= j < grid_y):
-            return zero
-        return cols_acc[i * grid_y + j]
 
     from_left = (lane - sub) % 4 < 2
     in_band = lane < tile_rows + 4
     in_ids = (sub == 0) & (lane >= NUMBERS) & (lane < NUMBERS + capacity)
     last, first = part == 3, part == 0
+    upper_left, upper_right = last & (lane == tile_rows), last & (lane == tile_rows + 1)
+    lower_left, lower_right = first & (lane == 1), first & (lane == 2)
+
+    def edge_step(d, carry):
+        at = inside(d)
+        base = d * message + 4 * capacity
+        out[pl.ds(pl.multiple_of(base, 8), 8), :] = jnp.where(part < 2, rows_acc[at + across], rows_acc[at - across])
+        tile = pick(in_band, jnp.where(from_left, cols_acc[at - 1], cols_acc[at + 1]))
+        upper = pick(upper_left, cols_acc[at - across - 1]) + pick(upper_right, cols_acc[at - across + 1])
+        lower = pick(lower_left, cols_acc[at + across - 1]) + pick(lower_right, cols_acc[at + across + 1])
+        tile = tile + pltpu.roll(upper, CORNERS - tile_rows, 1) + pltpu.roll(lower, CORNERS + 1, 1)
+        out[pl.ds(pl.multiple_of(base + 8, 8), 8), :] = tile + pick(in_ids, cols_acc[at])
+        return carry
+
     send = devices // SENDS
-    for d in range(devices):
-        i, j = d // grid_y, d % grid_y
-        below = rows_acc[d + grid_y] if i < grid_x - 1 else zero
-        above = rows_acc[d - grid_y] if i > 0 else zero
-        base = d * message + 4 * capacity
-        out[base : base + 8, :] = jnp.where(part < 2, below, above)
-        tile = pick(in_band, jnp.where(from_left, columns_of(i, j - 1), columns_of(i, j + 1)))
-        upper = pick(last & (lane == tile_rows), columns_of(i - 1, j - 1))
-        upper = upper + pick(last & (lane == tile_rows + 1), columns_of(i - 1, j + 1))
-        lower = pick(first & (lane == 1), columns_of(i + 1, j - 1))
-        lower = lower + pick(first & (lane == 2), columns_of(i + 1, j + 1))
-        tile = tile + pltpu.roll(upper, CORNERS - tile_rows, 1) + pltpu.roll(lower, CORNERS + 1, 1)
-        tile = tile + pick(in_ids, cols_acc[d])
-        out[base + 8 : base + 16, :] = tile
-        if d % send == send - 1:
-            n = d // send
-            at = pl.ds(n * send * message, send * message)
-            stores.append(pltpu.make_async_copy(out.at[at], out_h.at[at], out_sems.at[n]))
-            stores[-1].start()
+    for n in range(SENDS):
+        lax.fori_loop(n * send, (n + 1) * send, edge_step, 0, unroll=4)
+        piece = pl.ds(n * send * message, send * message)
+        stores += start_all([(out.at[piece], out_h.at[piece])], out_sems, n)
     for store in stores:
         store.wait()
 
@@ -204,6 +203,7 @@
     npairs = pair_block.shape[0]
     nblocks = atm_state.shape[1] // LANES
     message = 4 * capacity + EDGE
+    border = (devices // grid_y + 2) * (grid_y + 2)
     return pl.pallas_call(
         functools.partial(remap_out_kernel, capacity, grid_y, tile_rows),
         out_shape=(
@@ -224,8 +224,8 @@
             pltpu.SMEM((devices,), I32),
             pltpu.VMEM((4, devices, 8, LANES), F32),
             pltpu.VMEM((4, devices, 8, LANES), F32),
-            pltpu.VMEM((devices, 8, LANES), F32),
-            pltpu.VMEM((devices, 8, LANES), F32),
+            pltpu.VMEM((border, 8, LANES), F32),
+            pltpu.VMEM((border, 8, LANES), F32),
             pltpu.SemaphoreType.DMA((5,)),
             pltpu.SemaphoreType.DMA((PARTS,)),
             pltpu.SemaphoreType.DMA((SENDS + 2,)),
@@ -741,10 +741,10 @@
             product(half + many * p + n, picked_b, many * p + n, totals[n])
         return carry
 
-    lax.fori_loop(0, half, first, 0, unroll=64)
+    lax.fori_loop(0, half, first, 0, unroll=32)
     wait_all(loads)
-    lax.fori_loop(0, half // many, both, 0, unroll=32)
-    lax.fori_loop(0, half // many, last, 0, unroll=32)
+    lax.fori_loop(0, half // many, both, 0, unroll=16)
+    lax.fori_loop(0, half // many, last, 0, unroll=16)
     for b in range(nblocks):
         sums = (total_0[b] + total_1[b]) + (total_2[b] + total_3[b])
         out[:, b * LANES : (b + 1) * LANES] = sums[0:4] / jnp.maximum(sums[7:8], 0.1)

time: 92.8 us -> 93.9 us (1.012)
  Pallas kernels: 33.7 us -> 34.8 us
where the time goes in v13:
time: 93.9 us; the launch traced here: 93.6 us
  Pallas kernels  34.8 us (37%)
  waiting for transfers between devices  34.6 us (37%)
  starting transfers between devices  22.3 us (24%)
  local copies, waits for them, and re-layouts  1.06 us (1%)
    all_to_all x1, waiting for transfers between devices, local(): lax.all_to_all(sent, ('gx', 'gy'), split_axis=0, concat_axis=0, tiled=True)  20.2 us
    pallas_call x1, Pallas kernels, remap_out(): pl.pallas_call(functools.partial(remap_out_kernel, capacity, grid_y, tile...  7.95 us
    all_to_all x1, starting transfers between devices, local(): lax.all_to_all(outgoing.reshape(devices, message, LANES), ('gx', 'gy'), s...  7.1 us
    pallas_call x1, Pallas kernels, finish(): pl.pallas_call(functools.partial(finish_kernel, levels), out_shape=jax.Sh...  6.85 us
    ppermute x1, waiting for transfers between devices, local(): below = lax.ppermute(edge_up, 'gx', fall_x)  6.38 us
    pallas_call x1, Pallas kernels, remap_back(): pl.pallas_call(remap_back_kernel, out_shape=jax.ShapeDtypeStruct((4, nblo...  5.65 us
    pallas_call x1, Pallas kernels, turn(): pl.pallas_call(turn_kernel, out_shape=pltpu.HBM(remap_weight.shape, BF16)...  4.81 us
    all_to_all x1, starting transfers between devices, local(): lax.all_to_all(sent, ('gx', 'gy'), split_axis=0, concat_axis=0, tiled=True)  4.48 us
  transfers between devices with their start and end apart: 6, of which 6 were waited for; matrix products, arithmetic and copies ran while one was open for 0% of the time, Pallas kernels for 19%

profile of v13, /device:TPU:1, one launch (start us, length us, event | category | flops | bytes accessed | tf_op | source)
XLA Modules:
  0.0 93.6 jit_solution(7399716905784312973)
XLA Ops:
  0.6 8.0 %shard_map.115 = (f32[2560,128]{1,0:T(8,128)}, s32[256]{0:T(256)}, s32[256]{0:T(256)}) custom-call(s32[256]{0:T(256)} %block_h.3, s32[256]{0:T(256)} %bitcast.5, s32[256]{0:T(256)} %row_h.1, s32[256]{0:T(256)} %tile_h.3, f32[6,6144]{1,0:T(8,128)} %atm_h.1, bf16[128,128,128]{2,1,0:T(8,128)(2,1)} %weights_h.2), custom_call_target="tpu_custom_call" | custom-call | flops 134217728 | bytes 6291456 | tf_op jit(solution)/shard_map/pallas_call | solution.py:207
  8.6 0.0 copy-start
  8.6 0.0 copy-start.2
  8.6 0.0 copy-start.3
  8.6 7.1 %all-to-all-start = ((f32[32,80,128]{2,1,0:T(8,128)}), f32[32,80,128]{2,1,0:T(8,128)S(1)}, u32[]{:S(2)}, u32[]{:S(2)}) async-start(f32[32,80,128]{2,1,0:T(8,128)} %bitcast.4), calls=%async_computation | async-start | bytes 2621440 | tf_op jit(solution)/shard_map/all_to_all | solution.py:794
  15.8 0.0 copy-start.1
  15.8 1.0 %copy-done.1 = f32[16,64,128]{2,1,0:T(8,128)S(1)} copy-done((f32[16,64,128]{2,1,0:T(8,128)S(1)}, f32[16,64,128]{2,1,0:T(8,128)}, u32[]{:S(2)}) %copy-start.1) | copy-done | bytes 524312
  16.8 2.8 %shard_map.113 = (f32[50,64,128]{2,1,0:T(8,128)S(1)}, f32[2,16,64,128]{3,2,1,0:T(8,128)}, f32[50,8,128]{2,1,0:T(8,128)S(1)}, f32[50,8,128]{2,1,0:T(8,128)S(1)}) custom-call(f32[4,16,64,128]{3,2,1,0:T(8,128)S(1)} %copy-done, f32[16,64,128]{2,1,0:T(8,128)S(1)} %copy-done.1, f32[64,128]{1,0:T(8,128)S(1)} %copy-done.2, s32[64,128]{1,0:T(8,128)S(1)} %copy-done.3), custom_call_target="tpu_custom_call" | custom-call | flops 20971520 | bytes 6291456 | tf_op jit(solution)/shard_map/pallas_call | solution.py:302
  19.6 3.5 %collective-permute-start = (f32[50,8,128]{2,1,0:T(8,128)S(1)}, f32[50,8,128]{2,1,0:T(8,128)S(1)}, u32[]{:S(2)}, u32[]{:S(2)}) collective-permute-start(f32[50,8,128]{2,1,0:T(8,128)S(1)} %get-tuple-element.18), channel_id=1, source_target_pairs={{0,4},{4,8},{8,12},{12,16},{16,20},{20,24},{24,28},{1,5},{5,9},{9,... | collective-permute-start | bytes 614408 | tf_op jit(solution)/shard_map/ppermute | solution.py:802
  23.1 1.9 %collective-permute-start.1 = (f32[50,8,128]{2,1,0:T(8,128)S(1)}, f32[50,8,128]{2,1,0:T(8,128)S(1)}, u32[]{:S(2)}, u32[]{:S(2)}) collective-permute-start(f32[50,8,128]{2,1,0:T(8,128)S(1)} %get-tuple-element.19), channel_id=1, source_target_pairs={{4,0},{8,4},{12,8},{16,12},{20,16},{24,20},{28,24},{5,1},{9,5},{13... | collective-permute-start | bytes 614408 | tf_op jit(solution)/shard_map/ppermute | solution.py:803
  25.1 2.4 %collective-permute-done.above = f32[50,8,128]{2,1,0:T(8,128)S(1)} collective-permute-done((f32[50,8,128]{2,1,0:T(8,128)S(1)}, f32[50,8,128]{2,1,0:T(8,128)S(1)}, u32[]{:S(2)}, u32[]{:S(2)}) %collective-permute-start) | collective-permute-done | bytes 204832 | tf_op jit(solution)/shard_map/ppermute | solution.py:802
  27.5 6.4 %collective-permute-done.1.below = f32[50,8,128]{2,1,0:T(8,128)S(1)} collective-permute-done((f32[50,8,128]{2,1,0:T(8,128)S(1)}, f32[50,8,128]{2,1,0:T(8,128)S(1)}, u32[]{:S(2)}, u32[]{:S(2)}) %collective-permute-start.1) | collective-permute-done | bytes 204832 | tf_op jit(solution)/shard_map/ppermute | solution.py:803
  33.9 2.9 %shard_map.114 = (f32[50,80,128]{2,1,0:T(8,128)}, f32[2,80,128]{2,1,0:T(8,128)S(1)}, f32[2,80,128]{2,1,0:T(8,128)S(1)}) custom-call(f32[50,64,128]{2,1,0:T(8,128)S(1)} %get-tuple-element.17.tracer, f32[50,8,128]{2,1,0:T(8,128)S(1)} %collective-permute-done.above, f32[50,8,128]{2,1,0:T(8,128)S(1)} %collective-permute-done.1.below), custom_call_target="tpu_custom_call" | custom-call | flops 8388608 | bytes 4194304 | tf_op jit(solution)/shard_map/pallas_call | solution.py:357
  36.8 1.3 %collective-permute-start.3 = (f32[2,80,128]{2,1,0:T(8,128)S(1)}, f32[2,80,128]{2,1,0:T(8,128)S(1)}, u32[]{:S(2)}, u32[]{:S(2)}) collective-permute-start(f32[2,80,128]{2,1,0:T(8,128)S(1)} %get-tuple-element.23.own_left_h), channel_id=1, source_target_pairs={{1,0},{2,1},{3,2},{5,4},{6,5},{7,6},{9,8},{10,9},{11,10},{13,12},{... | collective-permute-start | bytes 245768 | tf_op jit(solution)/shard_map/ppermute | solution.py:806
  38.1 4.0 %collective-permute-start.2 = (f32[2,80,128]{2,1,0:T(8,128)S(1)}, f32[2,80,128]{2,1,0:T(8,128)S(1)}, u32[]{:S(2)}, u32[]{:S(2)}) collective-permute-start(f32[2,80,128]{2,1,0:T(8,128)S(1)} %get-tuple-element.24.own_right_h), channel_id=1, source_target_pairs={{0,1},{1,2},{2,3},{4,5},{5,6},{6,7},{8,9},{9,10},{10,11},{12,13},{... | collective-permute-start | bytes 245768 | tf_op jit(solution)/shard_map/ppermute | solution.py:805
  42.1 1.1 %collective-permute-done.3.from_right_h = f32[2,80,128]{2,1,0:T(8,128)S(1)} collective-permute-done((f32[2,80,128]{2,1,0:T(8,128)S(1)}, f32[2,80,128]{2,1,0:T(8,128)S(1)}, u32[]{:S(2)}, u32[]{:S(2)}) %collective-permute-start.3) | collective-permute-done | bytes 81952 | tf_op jit(solution)/shard_map/ppermute | solution.py:806
  43.1 0.4 collective-permute-done.2.from_left_h
  43.5 4.1 %all-to-all-done.arrived = f32[32,80,128]{2,1,0:T(8,128)S(1)} async-done(((f32[32,80,128]{2,1,0:T(8,128)}), f32[32,80,128]{2,1,0:T(8,128)S(1)}, u32[]{:S(2)}, u32[]{:S(2)}) %all-to-all-start) | async-done | bytes 1310752 | tf_op jit(solution)/shard_map/all_to_all | solution.py:794
  47.7 3.9 %shard_map.116 = (f32[32,80,128]{2,1,0:T(8,128)}, f32[4,80,128]{2,1,0:T(8,128)}, f32[2,80,128]{2,1,0:T(8,128)}, f32[4,80,128]{2,1,0:T(8,128)}) custom-call(f32[32,80,128]{2,1,0:T(8,128)S(1)} %all-to-all-done.arrived, f32[50,80,128]{2,1,0:T(8,128)} %get-tuple-element.20.wide_h, f32[2,16,64,128]{3,2,1,0:T(8,128)} %get-tuple-element.21.currents_h, ...), custom_call_target="tpu_custom_call" | custom-call | flops 209715200 | bytes 4194304 | tf_op jit(solution)/shard_map/pallas_call | solution.py:599
  51.5 4.5 %all-to-all-start.1 = ((f32[32,80,128]{2,1,0:T(8,128)}), f32[32,80,128]{2,1,0:T(8,128)S(1)}, u32[]{:S(2)}, u32[]{:S(2)}) async-start(f32[32,80,128]{2,1,0:T(8,128)} %get-tuple-element.30), calls=%async_computation.1 | async-start | bytes 2621440 | tf_op jit(solution)/shard_map/all_to_all | solution.py:810
  56.0 4.8 %shard_map.118.weights_h = bf16[128,128,128]{2,1,0:T(8,128)(2,1)} custom-call(bf16[128,128,128]{2,1,0:T(8,128)(2,1)} %weights_h.2), custom_call_target="tpu_custom_call" | custom-call | flops 8388608 | bytes 8388608 | tf_op jit(solution)/shard_map/pallas_call | solution.py:689
  60.8 6.8 %shard_map.117 = f32[4,16,64,128]{3,2,1,0:T(8,128)} custom-call(f32[50,80,128]{2,1,0:T(8,128)} %get-tuple-element.20.wide_h, f32[2,16,64,128]{3,2,1,0:T(8,128)} %get-tuple-element.21.currents_h, f32[4,80,128]{2,1,0:T(8,128)} %get-tuple-element.25.faces_h, f32[4,80,128]{2,1,0:T(8,128)} %get-tuple-element.26.forcing_h, f32[2,80,128]{2,1,0:T(8,128)} %get-tuple-element.27.near_h), custom_call_target="tpu_custom_call" | custom-call | flops 41943040 | bytes 6291456 | tf_op jit(solution)/shard_map/pallas_call | solution.py:659
  67.7 20.2 %all-to-all-done.1 = f32[32,80,128]{2,1,0:T(8,128)S(1)} async-done(((f32[32,80,128]{2,1,0:T(8,128)}), f32[32,80,128]{2,1,0:T(8,128)S(1)}, u32[]{:S(2)}, u32[]{:S(2)}) %all-to-all-start.1) | async-done | bytes 1310752 | tf_op jit(solution)/shard_map/all_to_all | solution.py:810
  87.9 5.6 %shard_map.119 = f32[4,6144]{1,0:T(4,128)} custom-call(s32[256]{0:T(256)} %block_h.3, s32[256]{0:T(256)} %tile_h.3, s32[256]{0:T(256)} %get-tuple-element.28.field_h, s32[256]{0:T(256)} %get-tuple-element.29.wet_h, f32[2560,128]{1,0:T(8,128)S(1)} %bitcast.3, bf16[128,128,128]{2,1,0:T(8,128)(2,1)} %shard_map.118.weights_h), custom_call_target="tpu_custom_call" | custom-call | flops 134217728 | bytes 6291456 | tf_op jit(solution)/shard_map/pallas_call | solution.py:755
  (3 shorter events, 0.0 us)
Async XLA Ops:
  8.6 7.1 %copy-start = (f32[4,16,64,128]{3,2,1,0:T(8,128)S(1)}, f32[4,16,64,128]{3,2,1,0:T(8,128)}, u32[]{:S(2)}) copy-start(f32[4,16,64,128]{3,2,1,0:T(8,128)} %state.1) | copy-start | bytes 6291460
  8.6 7.1 %copy-start.2 = (f32[64,128]{1,0:T(8,128)S(1)}, f32[64,128]{1,0:T(8,128)}, u32[]{:S(2)}) copy-start(f32[64,128]{1,0:T(8,128)} %horiz.1) | copy-start | bytes 98308
  8.6 7.1 %copy-start.3 = (s32[64,128]{1,0:T(8,128)S(1)}, s32[64,128]{1,0:T(8,128)}, u32[]{:S(2)}) copy-start(s32[64,128]{1,0:T(8,128)} %wet.1) | copy-start | bytes 98308
  8.6 39.0 %all-to-all-start = ((f32[32,80,128]{2,1,0:T(8,128)}), f32[32,80,128]{2,1,0:T(8,128)S(1)}, u32[]{:S(2)}, u32[]{:S(2)}) async-start(f32[32,80,128]{2,1,0:T(8,128)} %bitcast.4), calls=%async_computation | async-start | bytes 2621440 | tf_op jit(solution)/shard_map/all_to_all | solution.py:794
  15.8 1.0 %copy-start.1 = (f32[16,64,128]{2,1,0:T(8,128)S(1)}, f32[16,64,128]{2,1,0:T(8,128)}, u32[]{:S(2)}) copy-start(f32[16,64,128]{2,1,0:T(8,128)} %kappa.1) | copy-start | bytes 1572868
  19.6 7.9 %collective-permute-start = (f32[50,8,128]{2,1,0:T(8,128)S(1)}, f32[50,8,128]{2,1,0:T(8,128)S(1)}, u32[]{:S(2)}, u32[]{:S(2)}) collective-permute-start(f32[50,8,128]{2,1,0:T(8,128)S(1)} %get-tuple-element.18), channel_id=1, source_target_pairs={{0,4},{4,8},{8,12},{12,16},{16,20},{20,24},{24,28},{1,5},{5,9},{9,... | collective-permute-start | bytes 614408 | tf_op jit(solution)/shard_map/ppermute | solution.py:802
  23.1 10.7 %collective-permute-start.1 = (f32[50,8,128]{2,1,0:T(8,128)S(1)}, f32[50,8,128]{2,1,0:T(8,128)S(1)}, u32[]{:S(2)}, u32[]{:S(2)}) collective-permute-start(f32[50,8,128]{2,1,0:T(8,128)S(1)} %get-tuple-element.19), channel_id=1, source_target_pairs={{4,0},{8,4},{12,8},{16,12},{20,16},{24,20},{28,24},{5,1},{9,5},{13... | collective-permute-start | bytes 614408 | tf_op jit(solution)/shard_map/ppermute | solution.py:803
  36.8 6.4 %collective-permute-start.3 = (f32[2,80,128]{2,1,0:T(8,128)S(1)}, f32[2,80,128]{2,1,0:T(8,128)S(1)}, u32[]{:S(2)}, u32[]{:S(2)}) collective-permute-start(f32[2,80,128]{2,1,0:T(8,128)S(1)} %get-tuple-element.23.own_left_h), channel_id=1, source_target_pairs={{1,0},{2,1},{3,2},{5,4},{6,5},{7,6},{9,8},{10,9},{11,10},{13,12},{... | collective-permute-start | bytes 245768 | tf_op jit(solution)/shard_map/ppermute | solution.py:806
  38.1 5.5 %collective-permute-start.2 = (f32[2,80,128]{2,1,0:T(8,128)S(1)}, f32[2,80,128]{2,1,0:T(8,128)S(1)}, u32[]{:S(2)}, u32[]{:S(2)}) collective-permute-start(f32[2,80,128]{2,1,0:T(8,128)S(1)} %get-tuple-element.24.own_right_h), channel_id=1, source_target_pairs={{0,1},{1,2},{2,3},{4,5},{5,6},{6,7},{8,9},{9,10},{10,11},{12,13},{... | collective-permute-start | bytes 245768 | tf_op jit(solution)/shard_map/ppermute | solution.py:805
  51.5 36.4 %all-to-all-start.1 = ((f32[32,80,128]{2,1,0:T(8,128)}), f32[32,80,128]{2,1,0:T(8,128)S(1)}, u32[]{:S(2)}, u32[]{:S(2)}) async-start(f32[32,80,128]{2,1,0:T(8,128)} %get-tuple-element.30), calls=%async_computation.1 | async-start | bytes 2621440 | tf_op jit(solution)/shard_map/all_to_all | solution.py:810

commit v14 on v11

--- a/solution.py
+++ b/solution.py
@@ -153,16 +153,16 @@
             pair(p, n)
         return carry
 
-    lax.fori_loop(0, (npairs - AHEAD) // many, functools.partial(pairs, True), 0, unroll=AHEAD // many)
+    lax.fori_loop(0, (npairs - AHEAD) // many, functools.partial(pairs, True), 0, unroll=True)
     stores = start_all([(field_s, field_h), (wet_s, wet_h)], out_sems, SENDS)
-    lax.fori_loop((npairs - AHEAD) // many, npairs // many, functools.partial(pairs, False), 0, unroll=AHEAD // many)
+    lax.fori_loop((npairs - AHEAD) // many, npairs // many, functools.partial(pairs, False), 0, unroll=True)
 
     def owner_step(d, carry):
         rows_acc[d] = (rows_sum[0, d] + rows_sum[1, d]) + (rows_sum[2, d] + rows_sum[3, d])
         cols_acc[d] = (cols_sum[0, d] + cols_sum[1, d]) + (cols_sum[2, d] + cols_sum[3, d])
         return carry
 
-    lax.fori_loop(0, devices, owner_step, 0, unroll=8)
+    lax.fori_loop(0, devices, owner_step, 0, unroll=32)
 
     grid_x = devices // grid_y
     zero = jnp.zeros((8, LANES), F32)
@@ -741,10 +741,10 @@
             product(half + many * p + n, picked_b, many * p + n, totals[n])
         return carry
 
-    lax.fori_loop(0, half, first, 0, unroll=64)
+    lax.fori_loop(0, half, first, 0, unroll=True)
     wait_all(loads)
-    lax.fori_loop(0, half // many, both, 0, unroll=32)
-    lax.fori_loop(0, half // many, last, 0, unroll=32)
+    lax.fori_loop(0, half // many, both, 0, unroll=True)
+    lax.fori_loop(0, half // many, last, 0, unroll=True)
     for b in range(nblocks):
         sums = (total_0[b] + total_1[b]) + (total_2[b] + total_3[b])
         out[:, b * LANES : (b + 1) * LANES] = sums[0:4] / jnp.maximum(sums[7:8], 0.1)

time: 92.8 us -> 91.7 us (0.988)
  Pallas kernels: 33.7 us -> 32.6 us
    pallas_call x1, Pallas kernels: 7.18 us -> 6.12 us  [remap_out(): pl.pallas_call(functools.partial(remap_out_kernel, capacity, grid_y, tile...]
where the time goes in v14:
time: 91.7 us; the launch traced here: 91.3 us
  waiting for transfers between devices  34.6 us (38%)
  Pallas kernels  32.6 us (36%)
  starting transfers between devices  22.3 us (24%)
  local copies, waits for them, and re-layouts  1.06 us (1%)
    all_to_all x1, waiting for transfers between devices, local(): lax.all_to_all(sent, ('gx', 'gy'), split_axis=0, concat_axis=0, tiled=True)  20.2 us
    all_to_all x1, starting transfers between devices, local(): lax.all_to_all(outgoing.reshape(devices, message, LANES), ('gx', 'gy'), s...  7.1 us
    pallas_call x1, Pallas kernels, finish(): pl.pallas_call(functools.partial(finish_kernel, levels), out_shape=jax.Sh...  6.85 us
    ppermute x1, waiting for transfers between devices, local(): below = lax.ppermute(edge_up, 'gx', fall_x)  6.38 us
    pallas_call x1, Pallas kernels, remap_out(): pl.pallas_call(functools.partial(remap_out_kernel, capacity, grid_y, tile...  6.12 us
    pallas_call x1, Pallas kernels, remap_back(): pl.pallas_call(remap_back_kernel, out_shape=jax.ShapeDtypeStruct((4, nblo...  5.26 us
    pallas_call x1, Pallas kernels, turn(): pl.pallas_call(turn_kernel, out_shape=pltpu.HBM(remap_weight.shape, BF16)...  4.81 us
    all_to_all x1, starting transfers between devices, local(): lax.all_to_all(sent, ('gx', 'gy'), split_axis=0, concat_axis=0, tiled=True)  4.48 us
  transfers between devices with their start and end apart: 6, of which 6 were waited for; matrix products, arithmetic and copies ran while one was open for 0% of the time, Pallas kernels for 19%

profile of v14, /device:TPU:1, one launch (start us, length us, event | category | flops | bytes accessed | tf_op | source)
XLA Modules:
  0.0 91.3 jit_solution(15492699289426246968)
XLA Ops:
  0.6 6.1 %shard_map.115 = (f32[2560,128]{1,0:T(8,128)}, s32[256]{0:T(256)}, s32[256]{0:T(256)}) custom-call(s32[256]{0:T(256)} %block_h.3, s32[256]{0:T(256)} %bitcast.5, s32[256]{0:T(256)} %row_h.1, s32[256]{0:T(256)} %tile_h.3, f32[6,6144]{1,0:T(8,128)} %atm_h.1, bf16[128,128,128]{2,1,0:T(8,128)(2,1)} %weights_h.2), custom_call_target="tpu_custom_call" | custom-call | flops 134217728 | bytes 6291456 | tf_op jit(solution)/shard_map/pallas_call | solution.py:207
  6.8 0.0 copy-start
  6.8 0.0 copy-start.2
  6.8 0.0 copy-start.3
  6.8 7.1 %all-to-all-start = ((f32[32,80,128]{2,1,0:T(8,128)}), f32[32,80,128]{2,1,0:T(8,128)S(1)}, u32[]{:S(2)}, u32[]{:S(2)}) async-start(f32[32,80,128]{2,1,0:T(8,128)} %bitcast.4), calls=%async_computation | async-start | bytes 2621440 | tf_op jit(solution)/shard_map/all_to_all | solution.py:794
  13.9 0.0 copy-start.1
  13.9 1.0 %copy-done.1 = f32[16,64,128]{2,1,0:T(8,128)S(1)} copy-done((f32[16,64,128]{2,1,0:T(8,128)S(1)}, f32[16,64,128]{2,1,0:T(8,128)}, u32[]{:S(2)}) %copy-start.1) | copy-done | bytes 524312
  15.0 2.8 %shard_map.113 = (f32[50,64,128]{2,1,0:T(8,128)S(1)}, f32[2,16,64,128]{3,2,1,0:T(8,128)}, f32[50,8,128]{2,1,0:T(8,128)S(1)}, f32[50,8,128]{2,1,0:T(8,128)S(1)}) custom-call(f32[4,16,64,128]{3,2,1,0:T(8,128)S(1)} %copy-done, f32[16,64,128]{2,1,0:T(8,128)S(1)} %copy-done.1, f32[64,128]{1,0:T(8,128)S(1)} %copy-done.2, s32[64,128]{1,0:T(8,128)S(1)} %copy-done.3), custom_call_target="tpu_custom_call" | custom-call | flops 20971520 | bytes 6291456 | tf_op jit(solution)/shard_map/pallas_call | solution.py:302
  17.8 3.5 %collective-permute-start = (f32[50,8,128]{2,1,0:T(8,128)S(1)}, f32[50,8,128]{2,1,0:T(8,128)S(1)}, u32[]{:S(2)}, u32[]{:S(2)}) collective-permute-start(f32[50,8,128]{2,1,0:T(8,128)S(1)} %get-tuple-element.18), channel_id=1, source_target_pairs={{0,4},{4,8},{8,12},{12,16},{16,20},{20,24},{24,28},{1,5},{5,9},{9,... | collective-permute-start | bytes 614408 | tf_op jit(solution)/shard_map/ppermute | solution.py:802
  21.3 1.9 %collective-permute-start.1 = (f32[50,8,128]{2,1,0:T(8,128)S(1)}, f32[50,8,128]{2,1,0:T(8,128)S(1)}, u32[]{:S(2)}, u32[]{:S(2)}) collective-permute-start(f32[50,8,128]{2,1,0:T(8,128)S(1)} %get-tuple-element.19), channel_id=1, source_target_pairs={{4,0},{8,4},{12,8},{16,12},{20,16},{24,20},{28,24},{5,1},{9,5},{13... | collective-permute-start | bytes 614408 | tf_op jit(solution)/shard_map/ppermute | solution.py:803
  23.2 2.4 %collective-permute-done.above = f32[50,8,128]{2,1,0:T(8,128)S(1)} collective-permute-done((f32[50,8,128]{2,1,0:T(8,128)S(1)}, f32[50,8,128]{2,1,0:T(8,128)S(1)}, u32[]{:S(2)}, u32[]{:S(2)}) %collective-permute-start) | collective-permute-done | bytes 204832 | tf_op jit(solution)/shard_map/ppermute | solution.py:802
  25.6 6.4 %collective-permute-done.1.below = f32[50,8,128]{2,1,0:T(8,128)S(1)} collective-permute-done((f32[50,8,128]{2,1,0:T(8,128)S(1)}, f32[50,8,128]{2,1,0:T(8,128)S(1)}, u32[]{:S(2)}, u32[]{:S(2)}) %collective-permute-start.1) | collective-permute-done | bytes 204832 | tf_op jit(solution)/shard_map/ppermute | solution.py:803
  32.0 2.9 %shard_map.114 = (f32[50,80,128]{2,1,0:T(8,128)}, f32[2,80,128]{2,1,0:T(8,128)S(1)}, f32[2,80,128]{2,1,0:T(8,128)S(1)}) custom-call(f32[50,64,128]{2,1,0:T(8,128)S(1)} %get-tuple-element.17.tracer, f32[50,8,128]{2,1,0:T(8,128)S(1)} %collective-permute-done.above, f32[50,8,128]{2,1,0:T(8,128)S(1)} %collective-permute-done.1.below), custom_call_target="tpu_custom_call" | custom-call | flops 8388608 | bytes 4194304 | tf_op jit(solution)/shard_map/pallas_call | solution.py:357
  34.9 1.3 %collective-permute-start.3 = (f32[2,80,128]{2,1,0:T(8,128)S(1)}, f32[2,80,128]{2,1,0:T(8,128)S(1)}, u32[]{:S(2)}, u32[]{:S(2)}) collective-permute-start(f32[2,80,128]{2,1,0:T(8,128)S(1)} %get-tuple-element.23.own_left_h), channel_id=1, source_target_pairs={{1,0},{2,1},{3,2},{5,4},{6,5},{7,6},{9,8},{10,9},{11,10},{13,12},{... | collective-permute-start | bytes 245768 | tf_op jit(solution)/shard_map/ppermute | solution.py:806
  36.2 4.0 %collective-permute-start.2 = (f32[2,80,128]{2,1,0:T(8,128)S(1)}, f32[2,80,128]{2,1,0:T(8,128)S(1)}, u32[]{:S(2)}, u32[]{:S(2)}) collective-permute-start(f32[2,80,128]{2,1,0:T(8,128)S(1)} %get-tuple-element.24.own_right_h), channel_id=1, source_target_pairs={{0,1},{1,2},{2,3},{4,5},{5,6},{6,7},{8,9},{9,10},{10,11},{12,13},{... | collective-permute-start | bytes 245768 | tf_op jit(solution)/shard_map/ppermute | solution.py:805
  40.2 1.1 %collective-permute-done.3.from_right_h = f32[2,80,128]{2,1,0:T(8,128)S(1)} collective-permute-done((f32[2,80,128]{2,1,0:T(8,128)S(1)}, f32[2,80,128]{2,1,0:T(8,128)S(1)}, u32[]{:S(2)}, u32[]{:S(2)}) %collective-permute-start.3) | collective-permute-done | bytes 81952 | tf_op jit(solution)/shard_map/ppermute | solution.py:806
  41.3 0.4 collective-permute-done.2.from_left_h
  41.7 4.1 %all-to-all-done.arrived = f32[32,80,128]{2,1,0:T(8,128)S(1)} async-done(((f32[32,80,128]{2,1,0:T(8,128)}), f32[32,80,128]{2,1,0:T(8,128)S(1)}, u32[]{:S(2)}, u32[]{:S(2)}) %all-to-all-start) | async-done | bytes 1310752 | tf_op jit(solution)/shard_map/all_to_all | solution.py:794
  45.8 3.9 %shard_map.116 = (f32[32,80,128]{2,1,0:T(8,128)}, f32[4,80,128]{2,1,0:T(8,128)}, f32[2,80,128]{2,1,0:T(8,128)}, f32[4,80,128]{2,1,0:T(8,128)}) custom-call(f32[32,80,128]{2,1,0:T(8,128)S(1)} %all-to-all-done.arrived, f32[50,80,128]{2,1,0:T(8,128)} %get-tuple-element.20.wide_h, f32[2,16,64,128]{3,2,1,0:T(8,128)} %get-tuple-element.21.currents_h, ...), custom_call_target="tpu_custom_call" | custom-call | flops 209715200 | bytes 4194304 | tf_op jit(solution)/shard_map/pallas_call | solution.py:599
  49.7 4.5 %all-to-all-start.1 = ((f32[32,80,128]{2,1,0:T(8,128)}), f32[32,80,128]{2,1,0:T(8,128)S(1)}, u32[]{:S(2)}, u32[]{:S(2)}) async-start(f32[32,80,128]{2,1,0:T(8,128)} %get-tuple-element.30), calls=%async_computation.1 | async-start | bytes 2621440 | tf_op jit(solution)/shard_map/all_to_all | solution.py:810
  54.2 4.8 %shard_map.118.weights_h = bf16[128,128,128]{2,1,0:T(8,128)(2,1)} custom-call(bf16[128,128,128]{2,1,0:T(8,128)(2,1)} %weights_h.2), custom_call_target="tpu_custom_call" | custom-call | flops 8388608 | bytes 8388608 | tf_op jit(solution)/shard_map/pallas_call | solution.py:689
  59.0 6.8 %shard_map.117 = f32[4,16,64,128]{3,2,1,0:T(8,128)} custom-call(f32[50,80,128]{2,1,0:T(8,128)} %get-tuple-element.20.wide_h, f32[2,16,64,128]{3,2,1,0:T(8,128)} %get-tuple-element.21.currents_h, f32[4,80,128]{2,1,0:T(8,128)} %get-tuple-element.25.faces_h, f32[4,80,128]{2,1,0:T(8,128)} %get-tuple-element.26.forcing_h, f32[2,80,128]{2,1,0:T(8,128)} %get-tuple-element.27.near_h), custom_call_target="tpu_custom_call" | custom-call | flops 41943040 | bytes 6291456 | tf_op jit(solution)/shard_map/pallas_call | solution.py:659
  65.9 20.2 %all-to-all-done.1 = f32[32,80,128]{2,1,0:T(8,128)S(1)} async-done(((f32[32,80,128]{2,1,0:T(8,128)}), f32[32,80,128]{2,1,0:T(8,128)S(1)}, u32[]{:S(2)}, u32[]{:S(2)}) %all-to-all-start.1) | async-done | bytes 1310752 | tf_op jit(solution)/shard_map/all_to_all | solution.py:810
  86.1 5.3 %shard_map.119 = f32[4,6144]{1,0:T(4,128)} custom-call(s32[256]{0:T(256)} %block_h.3, s32[256]{0:T(256)} %tile_h.3, s32[256]{0:T(256)} %get-tuple-element.28.field_h, s32[256]{0:T(256)} %get-tuple-element.29.wet_h, f32[2560,128]{1,0:T(8,128)S(1)} %bitcast.3, bf16[128,128,128]{2,1,0:T(8,128)(2,1)} %shard_map.118.weights_h), custom_call_target="tpu_custom_call" | custom-call | flops 134217728 | bytes 6291456 | tf_op jit(solution)/shard_map/pallas_call | solution.py:755
  (3 shorter events, 0.0 us)
Async XLA Ops:
  6.8 7.1 %copy-start = (f32[4,16,64,128]{3,2,1,0:T(8,128)S(1)}, f32[4,16,64,128]{3,2,1,0:T(8,128)}, u32[]{:S(2)}) copy-start(f32[4,16,64,128]{3,2,1,0:T(8,128)} %state.1) | copy-start | bytes 6291460
  6.8 7.1 %copy-start.2 = (f32[64,128]{1,0:T(8,128)S(1)}, f32[64,128]{1,0:T(8,128)}, u32[]{:S(2)}) copy-start(f32[64,128]{1,0:T(8,128)} %horiz.1) | copy-start | bytes 98308
  6.8 7.1 %copy-start.3 = (s32[64,128]{1,0:T(8,128)S(1)}, s32[64,128]{1,0:T(8,128)}, u32[]{:S(2)}) copy-start(s32[64,128]{1,0:T(8,128)} %wet.1) | copy-start | bytes 98308
  6.8 39.0 %all-to-all-start = ((f32[32,80,128]{2,1,0:T(8,128)}), f32[32,80,128]{2,1,0:T(8,128)S(1)}, u32[]{:S(2)}, u32[]{:S(2)}) async-start(f32[32,80,128]{2,1,0:T(8,128)} %bitcast.4), calls=%async_computation | async-start | bytes 2621440 | tf_op jit(solution)/shard_map/all_to_all | solution.py:794
  13.9 1.0 %copy-start.1 = (f32[16,64,128]{2,1,0:T(8,128)S(1)}, f32[16,64,128]{2,1,0:T(8,128)}, u32[]{:S(2)}) copy-start(f32[16,64,128]{2,1,0:T(8,128)} %kappa.1) | copy-start | bytes 1572868
  17.8 7.9 %collective-permute-start = (f32[50,8,128]{2,1,0:T(8,128)S(1)}, f32[50,8,128]{2,1,0:T(8,128)S(1)}, u32[]{:S(2)}, u32[]{:S(2)}) collective-permute-start(f32[50,8,128]{2,1,0:T(8,128)S(1)} %get-tuple-element.18), channel_id=1, source_target_pairs={{0,4},{4,8},{8,12},{12,16},{16,20},{20,24},{24,28},{1,5},{5,9},{9,... | collective-permute-start | bytes 614408 | tf_op jit(solution)/shard_map/ppermute | solution.py:802
  21.3 10.7 %collective-permute-start.1 = (f32[50,8,128]{2,1,0:T(8,128)S(1)}, f32[50,8,128]{2,1,0:T(8,128)S(1)}, u32[]{:S(2)}, u32[]{:S(2)}) collective-permute-start(f32[50,8,128]{2,1,0:T(8,128)S(1)} %get-tuple-element.19), channel_id=1, source_target_pairs={{4,0},{8,4},{12,8},{16,12},{20,16},{24,20},{28,24},{5,1},{9,5},{13... | collective-permute-start | bytes 614408 | tf_op jit(solution)/shard_map/ppermute | solution.py:803
  34.9 6.4 %collective-permute-start.3 = (f32[2,80,128]{2,1,0:T(8,128)S(1)}, f32[2,80,128]{2,1,0:T(8,128)S(1)}, u32[]{:S(2)}, u32[]{:S(2)}) collective-permute-start(f32[2,80,128]{2,1,0:T(8,128)S(1)} %get-tuple-element.23.own_left_h), channel_id=1, source_target_pairs={{1,0},{2,1},{3,2},{5,4},{6,5},{7,6},{9,8},{10,9},{11,10},{13,12},{... | collective-permute-start | bytes 245768 | tf_op jit(solution)/shard_map/ppermute | solution.py:806
  36.2 5.5 %collective-permute-start.2 = (f32[2,80,128]{2,1,0:T(8,128)S(1)}, f32[2,80,128]{2,1,0:T(8,128)S(1)}, u32[]{:S(2)}, u32[]{:S(2)}) collective-permute-start(f32[2,80,128]{2,1,0:T(8,128)S(1)} %get-tuple-element.24.own_right_h), channel_id=1, source_target_pairs={{0,1},{1,2},{2,3},{4,5},{5,6},{6,7},{8,9},{9,10},{10,11},{12,13},{... | collective-permute-start | bytes 245768 | tf_op jit(solution)/shard_map/ppermute | solution.py:805
  49.7 36.4 %all-to-all-start.1 = ((f32[32,80,128]{2,1,0:T(8,128)}), f32[32,80,128]{2,1,0:T(8,128)S(1)}, u32[]{:S(2)}, u32[]{:S(2)}) async-start(f32[32,80,128]{2,1,0:T(8,128)} %get-tuple-element.30), calls=%async_computation.1 | async-start | bytes 2621440 | tf_op jit(solution)/shard_map/all_to_all | solution.py:810

commit v15 on v14

--- a/solution.py
+++ b/solution.py
@@ -18,7 +18,7 @@
 NUMBERS = 72
 CORNERS = 112
 SENDS = 8
-AHEAD = 64
+AHEAD = 16
 PARTS = 8
 
 
@@ -723,7 +723,7 @@
         b = block_s[p]
         total[b] = total[b] + (value[0:8] + value[8:16])
 
-    half = npairs // 2
+    early, late = picked_a.shape[0], picked_b.shape[0]
     many = len(totals)
 
     def first(p, carry):
@@ -732,19 +732,25 @@
 
     def both(p, carry):
         for n in range(many):
-            gather(half + many * p + n, picked_b, many * p + n)
+            gather(early + many * p + n, picked_b, many * p + n)
+            product(many * p + n, picked_a, many * p + n, totals[n])
+        return carry
+
+    def rest(p, carry):
+        for n in range(many):
             product(many * p + n, picked_a, many * p + n, totals[n])
         return carry
 
     def last(p, carry):
         for n in range(many):
-            product(half + many * p + n, picked_b, many * p + n, totals[n])
-        return carry
-
-    lax.fori_loop(0, half, first, 0, unroll=True)
+            product(early + many * p + n, picked_b, many * p + n, totals[n])
+        return carry
+
+    lax.fori_loop(0, early, first, 0, unroll=True)
     wait_all(loads)
-    lax.fori_loop(0, half // many, both, 0, unroll=True)
-    lax.fori_loop(0, half // many, last, 0, unroll=True)
+    lax.fori_loop(0, late // many, both, 0, unroll=True)
+    lax.fori_loop(late // many, early // many, rest, 0, unroll=True)
+    lax.fori_loop(0, late // many, last, 0, unroll=True)
     for b in range(nblocks):
         sums = (total_0[b] + total_1[b]) + (total_2[b] + total_3[b])
         out[:, b * LANES : (b + 1) * LANES] = sums[0:4] / jnp.maximum(sums[7:8], 0.1)
@@ -759,7 +765,7 @@
         out_specs=vmem(),
         scratch_shapes=[pltpu.SMEM((npairs,), I32)] * 4
         + [pltpu.VMEM(weights.shape, BF16)]
-        + [pltpu.VMEM((npairs // 2, 16, LANES), BF16)] * 2
+        + [pltpu.VMEM((npairs // 4 * 3, 16, LANES), BF16), pltpu.VMEM((npairs // 4, 16, LANES), BF16)]
         + [pltpu.VMEM((nblocks, 8, LANES), F32)] * 4
         + [pltpu.SemaphoreType.DMA((4,)), pltpu.SemaphoreType.DMA((PARTS,))],
         compiler_params=pltpu.CompilerParams(vmem_limit_bytes=24 << 20),

time: 91.7 us -> 91.7 us (level)
  no operation moved by 1% of the time
where the time goes in v15:
time: 91.7 us; the launch traced here: 91.3 us
  waiting for transfers between devices  34.6 us (38%)
  Pallas kernels  32.6 us (36%)
  starting transfers between devices  22.3 us (24%)
  local copies, waits for them, and re-layouts  1.06 us (1%)
    all_to_all x1, waiting for transfers between devices, local(): lax.all_to_all(sent, ('gx', 'gy'), split_axis=0, concat_axis=0, tiled=True)  20.2 us
    all_to_all x1, starting transfers between devices, local(): lax.all_to_all(outgoing.reshape(devices, message, LANES), ('gx', 'gy'), s...  7.1 us
    pallas_call x1, Pallas kernels, finish(): pl.pallas_call(functools.partial(finish_kernel, levels), out_shape=jax.Sh...  6.85 us
    ppermute x1, waiting for transfers between devices, local(): below = lax.ppermute(edge_up, 'gx', fall_x)  6.38 us
    pallas_call x1, Pallas kernels, remap_out(): pl.pallas_call(functools.partial(remap_out_kernel, capacity, grid_y, tile...  6.09 us
    pallas_call x1, Pallas kernels, remap_back(): pl.pallas_call(remap_back_kernel, out_shape=jax.ShapeDtypeStruct((4, nblo...  5.26 us
    pallas_call x1, Pallas kernels, turn(): pl.pallas_call(turn_kernel, out_shape=pltpu.HBM(remap_weight.shape, BF16)...  4.81 us
    all_to_all x1, starting transfers between devices, local(): lax.all_to_all(sent, ('gx', 'gy'), split_axis=0, concat_axis=0, tiled=True)  4.48 us
  transfers between devices with their start and end apart: 6, of which 6 were waited for; matrix products, arithmetic and copies ran while one was open for 0% of the time, Pallas kernels for 19%

profile of v15, /device:TPU:1, one launch (start us, length us, event | category | flops | bytes accessed | tf_op | source)
XLA Modules:
  0.0 91.3 jit_solution(1651214908452767669)
XLA Ops:
  0.6 6.1 %shard_map.115 = (f32[2560,128]{1,0:T(8,128)}, s32[256]{0:T(256)}, s32[256]{0:T(256)}) custom-call(s32[256]{0:T(256)} %block_h.3, s32[256]{0:T(256)} %bitcast.5, s32[256]{0:T(256)} %row_h.1, s32[256]{0:T(256)} %tile_h.3, f32[6,6144]{1,0:T(8,128)} %atm_h.1, bf16[128,128,128]{2,1,0:T(8,128)(2,1)} %weights_h.2), custom_call_target="tpu_custom_call" | custom-call | flops 134217728 | bytes 6291456 | tf_op jit(solution)/shard_map/pallas_call | solution.py:207
  6.7 0.0 copy-start
  6.7 0.0 copy-start.2
  6.7 0.0 copy-start.3
  6.8 7.1 %all-to-all-start = ((f32[32,80,128]{2,1,0:T(8,128)}), f32[32,80,128]{2,1,0:T(8,128)S(1)}, u32[]{:S(2)}, u32[]{:S(2)}) async-start(f32[32,80,128]{2,1,0:T(8,128)} %bitcast.4), calls=%async_computation | async-start | bytes 2621440 | tf_op jit(solution)/shard_map/all_to_all | solution.py:800
  13.9 0.0 copy-start.1
  13.9 1.0 %copy-done.1 = f32[16,64,128]{2,1,0:T(8,128)S(1)} copy-done((f32[16,64,128]{2,1,0:T(8,128)S(1)}, f32[16,64,128]{2,1,0:T(8,128)}, u32[]{:S(2)}) %copy-start.1) | copy-done | bytes 524312
  14.9 2.8 %shard_map.113 = (f32[50,64,128]{2,1,0:T(8,128)S(1)}, f32[2,16,64,128]{3,2,1,0:T(8,128)}, f32[50,8,128]{2,1,0:T(8,128)S(1)}, f32[50,8,128]{2,1,0:T(8,128)S(1)}) custom-call(f32[4,16,64,128]{3,2,1,0:T(8,128)S(1)} %copy-done, f32[16,64,128]{2,1,0:T(8,128)S(1)} %copy-done.1, f32[64,128]{1,0:T(8,128)S(1)} %copy-done.2, s32[64,128]{1,0:T(8,128)S(1)} %copy-done.3), custom_call_target="tpu_custom_call" | custom-call | flops 20971520 | bytes 6291456 | tf_op jit(solution)/shard_map/pallas_call | solution.py:302
  17.7 3.5 %collective-permute-start = (f32[50,8,128]{2,1,0:T(8,128)S(1)}, f32[50,8,128]{2,1,0:T(8,128)S(1)}, u32[]{:S(2)}, u32[]{:S(2)}) collective-permute-start(f32[50,8,128]{2,1,0:T(8,128)S(1)} %get-tuple-element.18), channel_id=1, source_target_pairs={{0,4},{4,8},{8,12},{12,16},{16,20},{20,24},{24,28},{1,5},{5,9},{9,... | collective-permute-start | bytes 614408 | tf_op jit(solution)/shard_map/ppermute | solution.py:808
  21.3 1.9 %collective-permute-start.1 = (f32[50,8,128]{2,1,0:T(8,128)S(1)}, f32[50,8,128]{2,1,0:T(8,128)S(1)}, u32[]{:S(2)}, u32[]{:S(2)}) collective-permute-start(f32[50,8,128]{2,1,0:T(8,128)S(1)} %get-tuple-element.19), channel_id=1, source_target_pairs={{4,0},{8,4},{12,8},{16,12},{20,16},{24,20},{28,24},{5,1},{9,5},{13... | collective-permute-start | bytes 614408 | tf_op jit(solution)/shard_map/ppermute | solution.py:809
  23.2 2.4 %collective-permute-done.above = f32[50,8,128]{2,1,0:T(8,128)S(1)} collective-permute-done((f32[50,8,128]{2,1,0:T(8,128)S(1)}, f32[50,8,128]{2,1,0:T(8,128)S(1)}, u32[]{:S(2)}, u32[]{:S(2)}) %collective-permute-start) | collective-permute-done | bytes 204832 | tf_op jit(solution)/shard_map/ppermute | solution.py:808
  25.6 6.4 %collective-permute-done.1.below = f32[50,8,128]{2,1,0:T(8,128)S(1)} collective-permute-done((f32[50,8,128]{2,1,0:T(8,128)S(1)}, f32[50,8,128]{2,1,0:T(8,128)S(1)}, u32[]{:S(2)}, u32[]{:S(2)}) %collective-permute-start.1) | collective-permute-done | bytes 204832 | tf_op jit(solution)/shard_map/ppermute | solution.py:809
  32.0 2.9 %shard_map.114 = (f32[50,80,128]{2,1,0:T(8,128)}, f32[2,80,128]{2,1,0:T(8,128)S(1)}, f32[2,80,128]{2,1,0:T(8,128)S(1)}) custom-call(f32[50,64,128]{2,1,0:T(8,128)S(1)} %get-tuple-element.17.tracer, f32[50,8,128]{2,1,0:T(8,128)S(1)} %collective-permute-done.above, f32[50,8,128]{2,1,0:T(8,128)S(1)} %collective-permute-done.1.below), custom_call_target="tpu_custom_call" | custom-call | flops 8388608 | bytes 4194304 | tf_op jit(solution)/shard_map/pallas_call | solution.py:357
  34.9 1.3 %collective-permute-start.3 = (f32[2,80,128]{2,1,0:T(8,128)S(1)}, f32[2,80,128]{2,1,0:T(8,128)S(1)}, u32[]{:S(2)}, u32[]{:S(2)}) collective-permute-start(f32[2,80,128]{2,1,0:T(8,128)S(1)} %get-tuple-element.23.own_left_h), channel_id=1, source_target_pairs={{1,0},{2,1},{3,2},{5,4},{6,5},{7,6},{9,8},{10,9},{11,10},{13,12},{... | collective-permute-start | bytes 245768 | tf_op jit(solution)/shard_map/ppermute | solution.py:812
  36.2 4.0 %collective-permute-start.2 = (f32[2,80,128]{2,1,0:T(8,128)S(1)}, f32[2,80,128]{2,1,0:T(8,128)S(1)}, u32[]{:S(2)}, u32[]{:S(2)}) collective-permute-start(f32[2,80,128]{2,1,0:T(8,128)S(1)} %get-tuple-element.24.own_right_h), channel_id=1, source_target_pairs={{0,1},{1,2},{2,3},{4,5},{5,6},{6,7},{8,9},{9,10},{10,11},{12,13},{... | collective-permute-start | bytes 245768 | tf_op jit(solution)/shard_map/ppermute | solution.py:811
  40.2 1.1 %collective-permute-done.3.from_right_h = f32[2,80,128]{2,1,0:T(8,128)S(1)} collective-permute-done((f32[2,80,128]{2,1,0:T(8,128)S(1)}, f32[2,80,128]{2,1,0:T(8,128)S(1)}, u32[]{:S(2)}, u32[]{:S(2)}) %collective-permute-start.3) | collective-permute-done | bytes 81952 | tf_op jit(solution)/shard_map/ppermute | solution.py:812
  41.3 0.4 collective-permute-done.2.from_left_h
  41.7 4.1 %all-to-all-done.arrived = f32[32,80,128]{2,1,0:T(8,128)S(1)} async-done(((f32[32,80,128]{2,1,0:T(8,128)}), f32[32,80,128]{2,1,0:T(8,128)S(1)}, u32[]{:S(2)}, u32[]{:S(2)}) %all-to-all-start) | async-done | bytes 1310752 | tf_op jit(solution)/shard_map/all_to_all | solution.py:800
  45.8 3.9 %shard_map.116 = (f32[32,80,128]{2,1,0:T(8,128)}, f32[4,80,128]{2,1,0:T(8,128)}, f32[2,80,128]{2,1,0:T(8,128)}, f32[4,80,128]{2,1,0:T(8,128)}) custom-call(f32[32,80,128]{2,1,0:T(8,128)S(1)} %all-to-all-done.arrived, f32[50,80,128]{2,1,0:T(8,128)} %get-tuple-element.20.wide_h, f32[2,16,64,128]{3,2,1,0:T(8,128)} %get-tuple-element.21.currents_h, ...), custom_call_target="tpu_custom_call" | custom-call | flops 209715200 | bytes 4194304 | tf_op jit(solution)/shard_map/pallas_call | solution.py:599
  49.7 4.5 %all-to-all-start.1 = ((f32[32,80,128]{2,1,0:T(8,128)}), f32[32,80,128]{2,1,0:T(8,128)S(1)}, u32[]{:S(2)}, u32[]{:S(2)}) async-start(f32[32,80,128]{2,1,0:T(8,128)} %get-tuple-element.30), calls=%async_computation.1 | async-start | bytes 2621440 | tf_op jit(solution)/shard_map/all_to_all | solution.py:816
  54.2 4.8 %shard_map.118.weights_h = bf16[128,128,128]{2,1,0:T(8,128)(2,1)} custom-call(bf16[128,128,128]{2,1,0:T(8,128)(2,1)} %weights_h.2), custom_call_target="tpu_custom_call" | custom-call | flops 8388608 | bytes 8388608 | tf_op jit(solution)/shard_map/pallas_call | solution.py:689
  59.0 6.8 %shard_map.117 = f32[4,16,64,128]{3,2,1,0:T(8,128)} custom-call(f32[50,80,128]{2,1,0:T(8,128)} %get-tuple-element.20.wide_h, f32[2,16,64,128]{3,2,1,0:T(8,128)} %get-tuple-element.21.currents_h, f32[4,80,128]{2,1,0:T(8,128)} %get-tuple-element.25.faces_h, f32[4,80,128]{2,1,0:T(8,128)} %get-tuple-element.26.forcing_h, f32[2,80,128]{2,1,0:T(8,128)} %get-tuple-element.27.near_h), custom_call_target="tpu_custom_call" | custom-call | flops 41943040 | bytes 6291456 | tf_op jit(solution)/shard_map/pallas_call | solution.py:659
  65.8 20.2 %all-to-all-done.1 = f32[32,80,128]{2,1,0:T(8,128)S(1)} async-done(((f32[32,80,128]{2,1,0:T(8,128)}), f32[32,80,128]{2,1,0:T(8,128)S(1)}, u32[]{:S(2)}, u32[]{:S(2)}) %all-to-all-start.1) | async-done | bytes 1310752 | tf_op jit(solution)/shard_map/all_to_all | solution.py:816
  86.0 5.3 %shard_map.119 = f32[4,6144]{1,0:T(4,128)} custom-call(s32[256]{0:T(256)} %block_h.3, s32[256]{0:T(256)} %tile_h.3, s32[256]{0:T(256)} %get-tuple-element.28.field_h, s32[256]{0:T(256)} %get-tuple-element.29.wet_h, f32[2560,128]{1,0:T(8,128)S(1)} %bitcast.3, bf16[128,128,128]{2,1,0:T(8,128)(2,1)} %shard_map.118.weights_h), custom_call_target="tpu_custom_call" | custom-call | flops 134217728 | bytes 6291456 | tf_op jit(solution)/shard_map/pallas_call | solution.py:761
  (3 shorter events, 0.0 us)
Async XLA Ops:
  6.7 7.2 %copy-start = (f32[4,16,64,128]{3,2,1,0:T(8,128)S(1)}, f32[4,16,64,128]{3,2,1,0:T(8,128)}, u32[]{:S(2)}) copy-start(f32[4,16,64,128]{3,2,1,0:T(8,128)} %state.1) | copy-start | bytes 6291460
  6.7 7.1 %copy-start.2 = (f32[64,128]{1,0:T(8,128)S(1)}, f32[64,128]{1,0:T(8,128)}, u32[]{:S(2)}) copy-start(f32[64,128]{1,0:T(8,128)} %horiz.1) | copy-start | bytes 98308
  6.7 7.1 %copy-start.3 = (s32[64,128]{1,0:T(8,128)S(1)}, s32[64,128]{1,0:T(8,128)}, u32[]{:S(2)}) copy-start(s32[64,128]{1,0:T(8,128)} %wet.1) | copy-start | bytes 98308
  6.8 39.0 %all-to-all-start = ((f32[32,80,128]{2,1,0:T(8,128)}), f32[32,80,128]{2,1,0:T(8,128)S(1)}, u32[]{:S(2)}, u32[]{:S(2)}) async-start(f32[32,80,128]{2,1,0:T(8,128)} %bitcast.4), calls=%async_computation | async-start | bytes 2621440 | tf_op jit(solution)/shard_map/all_to_all | solution.py:800
  13.9 1.0 %copy-start.1 = (f32[16,64,128]{2,1,0:T(8,128)S(1)}, f32[16,64,128]{2,1,0:T(8,128)}, u32[]{:S(2)}) copy-start(f32[16,64,128]{2,1,0:T(8,128)} %kappa.1) | copy-start | bytes 1572868
  17.7 7.9 %collective-permute-start = (f32[50,8,128]{2,1,0:T(8,128)S(1)}, f32[50,8,128]{2,1,0:T(8,128)S(1)}, u32[]{:S(2)}, u32[]{:S(2)}) collective-permute-start(f32[50,8,128]{2,1,0:T(8,128)S(1)} %get-tuple-element.18), channel_id=1, source_target_pairs={{0,4},{4,8},{8,12},{12,16},{16,20},{20,24},{24,28},{1,5},{5,9},{9,... | collective-permute-start | bytes 614408 | tf_op jit(solution)/shard_map/ppermute | solution.py:808
  21.3 10.7 %collective-permute-start.1 = (f32[50,8,128]{2,1,0:T(8,128)S(1)}, f32[50,8,128]{2,1,0:T(8,128)S(1)}, u32[]{:S(2)}, u32[]{:S(2)}) collective-permute-start(f32[50,8,128]{2,1,0:T(8,128)S(1)} %get-tuple-element.19), channel_id=1, source_target_pairs={{4,0},{8,4},{12,8},{16,12},{20,16},{24,20},{28,24},{5,1},{9,5},{13... | collective-permute-start | bytes 614408 | tf_op jit(solution)/shard_map/ppermute | solution.py:809
  34.9 6.4 %collective-permute-start.3 = (f32[2,80,128]{2,1,0:T(8,128)S(1)}, f32[2,80,128]{2,1,0:T(8,128)S(1)}, u32[]{:S(2)}, u32[]{:S(2)}) collective-permute-start(f32[2,80,128]{2,1,0:T(8,128)S(1)} %get-tuple-element.23.own_left_h), channel_id=1, source_target_pairs={{1,0},{2,1},{3,2},{5,4},{6,5},{7,6},{9,8},{10,9},{11,10},{13,12},{... | collective-permute-start | bytes 245768 | tf_op jit(solution)/shard_map/ppermute | solution.py:812
  36.2 5.5 %collective-permute-start.2 = (f32[2,80,128]{2,1,0:T(8,128)S(1)}, f32[2,80,128]{2,1,0:T(8,128)S(1)}, u32[]{:S(2)}, u32[]{:S(2)}) collective-permute-start(f32[2,80,128]{2,1,0:T(8,128)S(1)} %get-tuple-element.24.own_right_h), channel_id=1, source_target_pairs={{0,1},{1,2},{2,3},{4,5},{5,6},{6,7},{8,9},{9,10},{10,11},{12,13},{... | collective-permute-start | bytes 245768 | tf_op jit(solution)/shard_map/ppermute | solution.py:811
  49.7 36.4 %all-to-all-start.1 = ((f32[32,80,128]{2,1,0:T(8,128)}), f32[32,80,128]{2,1,0:T(8,128)S(1)}, u32[]{:S(2)}, u32[]{:S(2)}) async-start(f32[32,80,128]{2,1,0:T(8,128)} %get-tuple-element.30), calls=%async_computation.1 | async-start | bytes 2621440 | tf_op jit(solution)/shard_map/all_to_all | solution.py:816

commit v16 on v15

--- a/solution.py
+++ b/solution.py
@@ -17,9 +17,9 @@
 HALO = 8
 NUMBERS = 72
 CORNERS = 112
-SENDS = 8
+SENDS = 16
 AHEAD = 16
-PARTS = 8
+PARTS = 16
 
 
 def hbm():

time: 91.7 us -> 91.9 us (level)
  no operation moved by 1% of the time
where the time goes in v16:
time: 91.9 us; the launch traced here: 91.5 us
  waiting for transfers between devices  34.6 us (38%)
  Pallas kernels  32.7 us (36%)
  starting transfers between devices  22.3 us (24%)
  local copies, waits for them, and re-layouts  1.06 us (1%)
    all_to_all x1, waiting for transfers between devices, local(): lax.all_to_all(sent, ('gx', 'gy'), split_axis=0, concat_axis=0, tiled=True)  20.3 us
    all_to_all x1, starting transfers between devices, local(): lax.all_to_all(outgoing.reshape(devices, message, LANES), ('gx', 'gy'), s...  7.1 us
    pallas_call x1, Pallas kernels, finish(): pl.pallas_call(functools.partial(finish_kernel, levels), out_shape=jax.Sh...  6.85 us
    ppermute x1, waiting for transfers between devices, local(): below = lax.ppermute(edge_up, 'gx', fall_x)  6.38 us
    pallas_call x1, Pallas kernels, remap_out(): pl.pallas_call(functools.partial(remap_out_kernel, capacity, grid_y, tile...  6.21 us
    pallas_call x1, Pallas kernels, remap_back(): pl.pallas_call(remap_back_kernel, out_shape=jax.ShapeDtypeStruct((4, nblo...  5.32 us
    pallas_call x1, Pallas kernels, turn(): pl.pallas_call(turn_kernel, out_shape=pltpu.HBM(remap_weight.shape, BF16)...  4.77 us
    all_to_all x1, starting transfers between devices, local(): lax.all_to_all(sent, ('gx', 'gy'), split_axis=0, concat_axis=0, tiled=True)  4.48 us
  transfers between devices with their start and end apart: 6, of which 6 were waited for; matrix products, arithmetic and copies ran while one was open for 0% of the time, Pallas kernels for 19%

profile of v16, /device:TPU:1, one launch (start us, length us, event | category | flops | bytes accessed | tf_op | source)
XLA Modules:
  0.0 91.5 jit_solution(16976739087436680468)
XLA Ops:
  0.6 6.2 %shard_map.115 = (f32[2560,128]{1,0:T(8,128)}, s32[256]{0:T(256)}, s32[256]{0:T(256)}) custom-call(s32[256]{0:T(256)} %block_h.3, s32[256]{0:T(256)} %bitcast.5, s32[256]{0:T(256)} %row_h.1, s32[256]{0:T(256)} %tile_h.3, f32[6,6144]{1,0:T(8,128)} %atm_h.1, bf16[128,128,128]{2,1,0:T(8,128)(2,1)} %weights_h.2), custom_call_target="tpu_custom_call" | custom-call | flops 134217728 | bytes 6291456 | tf_op jit(solution)/shard_map/pallas_call | solution.py:207
  6.9 0.0 copy-start
  6.9 0.0 copy-start.2
  6.9 0.0 copy-start.3
  6.9 7.1 %all-to-all-start = ((f32[32,80,128]{2,1,0:T(8,128)}), f32[32,80,128]{2,1,0:T(8,128)S(1)}, u32[]{:S(2)}, u32[]{:S(2)}) async-start(f32[32,80,128]{2,1,0:T(8,128)} %bitcast.4), calls=%async_computation | async-start | bytes 2621440 | tf_op jit(solution)/shard_map/all_to_all | solution.py:800
  14.0 0.0 copy-start.1
  14.0 1.0 %copy-done.1 = f32[16,64,128]{2,1,0:T(8,128)S(1)} copy-done((f32[16,64,128]{2,1,0:T(8,128)S(1)}, f32[16,64,128]{2,1,0:T(8,128)}, u32[]{:S(2)}) %copy-start.1) | copy-done | bytes 524312
  15.1 2.8 %shard_map.113 = (f32[50,64,128]{2,1,0:T(8,128)S(1)}, f32[2,16,64,128]{3,2,1,0:T(8,128)}, f32[50,8,128]{2,1,0:T(8,128)S(1)}, f32[50,8,128]{2,1,0:T(8,128)S(1)}) custom-call(f32[4,16,64,128]{3,2,1,0:T(8,128)S(1)} %copy-done, f32[16,64,128]{2,1,0:T(8,128)S(1)} %copy-done.1, f32[64,128]{1,0:T(8,128)S(1)} %copy-done.2, s32[64,128]{1,0:T(8,128)S(1)} %copy-done.3), custom_call_target="tpu_custom_call" | custom-call | flops 20971520 | bytes 6291456 | tf_op jit(solution)/shard_map/pallas_call | solution.py:302
  17.9 3.5 %collective-permute-start = (f32[50,8,128]{2,1,0:T(8,128)S(1)}, f32[50,8,128]{2,1,0:T(8,128)S(1)}, u32[]{:S(2)}, u32[]{:S(2)}) collective-permute-start(f32[50,8,128]{2,1,0:T(8,128)S(1)} %get-tuple-element.18), channel_id=1, source_target_pairs={{0,4},{4,8},{8,12},{12,16},{16,20},{20,24},{24,28},{1,5},{5,9},{9,... | collective-permute-start | bytes 614408 | tf_op jit(solution)/shard_map/ppermute | solution.py:808
  21.4 1.9 %collective-permute-start.1 = (f32[50,8,128]{2,1,0:T(8,128)S(1)}, f32[50,8,128]{2,1,0:T(8,128)S(1)}, u32[]{:S(2)}, u32[]{:S(2)}) collective-permute-start(f32[50,8,128]{2,1,0:T(8,128)S(1)} %get-tuple-element.19), channel_id=1, source_target_pairs={{4,0},{8,4},{12,8},{16,12},{20,16},{24,20},{28,24},{5,1},{9,5},{13... | collective-permute-start | bytes 614408 | tf_op jit(solution)/shard_map/ppermute | solution.py:809
  23.3 2.4 %collective-permute-done.above = f32[50,8,128]{2,1,0:T(8,128)S(1)} collective-permute-done((f32[50,8,128]{2,1,0:T(8,128)S(1)}, f32[50,8,128]{2,1,0:T(8,128)S(1)}, u32[]{:S(2)}, u32[]{:S(2)}) %collective-permute-start) | collective-permute-done | bytes 204832 | tf_op jit(solution)/shard_map/ppermute | solution.py:808
  25.7 6.4 %collective-permute-done.1.below = f32[50,8,128]{2,1,0:T(8,128)S(1)} collective-permute-done((f32[50,8,128]{2,1,0:T(8,128)S(1)}, f32[50,8,128]{2,1,0:T(8,128)S(1)}, u32[]{:S(2)}, u32[]{:S(2)}) %collective-permute-start.1) | collective-permute-done | bytes 204832 | tf_op jit(solution)/shard_map/ppermute | solution.py:809
  32.1 2.9 %shard_map.114 = (f32[50,80,128]{2,1,0:T(8,128)}, f32[2,80,128]{2,1,0:T(8,128)S(1)}, f32[2,80,128]{2,1,0:T(8,128)S(1)}) custom-call(f32[50,64,128]{2,1,0:T(8,128)S(1)} %get-tuple-element.17.tracer, f32[50,8,128]{2,1,0:T(8,128)S(1)} %collective-permute-done.above, f32[50,8,128]{2,1,0:T(8,128)S(1)} %collective-permute-done.1.below), custom_call_target="tpu_custom_call" | custom-call | flops 8388608 | bytes 4194304 | tf_op jit(solution)/shard_map/pallas_call | solution.py:357
  35.0 1.3 %collective-permute-start.3 = (f32[2,80,128]{2,1,0:T(8,128)S(1)}, f32[2,80,128]{2,1,0:T(8,128)S(1)}, u32[]{:S(2)}, u32[]{:S(2)}) collective-permute-start(f32[2,80,128]{2,1,0:T(8,128)S(1)} %get-tuple-element.23.own_left_h), channel_id=1, source_target_pairs={{1,0},{2,1},{3,2},{5,4},{6,5},{7,6},{9,8},{10,9},{11,10},{13,12},{... | collective-permute-start | bytes 245768 | tf_op jit(solution)/shard_map/ppermute | solution.py:812
  36.3 4.0 %collective-permute-start.2 = (f32[2,80,128]{2,1,0:T(8,128)S(1)}, f32[2,80,128]{2,1,0:T(8,128)S(1)}, u32[]{:S(2)}, u32[]{:S(2)}) collective-permute-start(f32[2,80,128]{2,1,0:T(8,128)S(1)} %get-tuple-element.24.own_right_h), channel_id=1, source_target_pairs={{0,1},{1,2},{2,3},{4,5},{5,6},{6,7},{8,9},{9,10},{10,11},{12,13},{... | collective-permute-start | bytes 245768 | tf_op jit(solution)/shard_map/ppermute | solution.py:811
  40.3 1.1 %collective-permute-done.3.from_right_h = f32[2,80,128]{2,1,0:T(8,128)S(1)} collective-permute-done((f32[2,80,128]{2,1,0:T(8,128)S(1)}, f32[2,80,128]{2,1,0:T(8,128)S(1)}, u32[]{:S(2)}, u32[]{:S(2)}) %collective-permute-start.3) | collective-permute-done | bytes 81952 | tf_op jit(solution)/shard_map/ppermute | solution.py:812
  41.4 0.4 collective-permute-done.2.from_left_h
  41.8 4.1 %all-to-all-done.arrived = f32[32,80,128]{2,1,0:T(8,128)S(1)} async-done(((f32[32,80,128]{2,1,0:T(8,128)}), f32[32,80,128]{2,1,0:T(8,128)S(1)}, u32[]{:S(2)}, u32[]{:S(2)}) %all-to-all-start) | async-done | bytes 1310752 | tf_op jit(solution)/shard_map/all_to_all | solution.py:800
  45.9 3.9 %shard_map.116 = (f32[32,80,128]{2,1,0:T(8,128)}, f32[4,80,128]{2,1,0:T(8,128)}, f32[2,80,128]{2,1,0:T(8,128)}, f32[4,80,128]{2,1,0:T(8,128)}) custom-call(f32[32,80,128]{2,1,0:T(8,128)S(1)} %all-to-all-done.arrived, f32[50,80,128]{2,1,0:T(8,128)} %get-tuple-element.20.wide_h, f32[2,16,64,128]{3,2,1,0:T(8,128)} %get-tuple-element.21.currents_h, ...), custom_call_target="tpu_custom_call" | custom-call | flops 209715200 | bytes 4194304 | tf_op jit(solution)/shard_map/pallas_call | solution.py:599
  49.8 4.5 %all-to-all-start.1 = ((f32[32,80,128]{2,1,0:T(8,128)}), f32[32,80,128]{2,1,0:T(8,128)S(1)}, u32[]{:S(2)}, u32[]{:S(2)}) async-start(f32[32,80,128]{2,1,0:T(8,128)} %get-tuple-element.30), calls=%async_computation.1 | async-start | bytes 2621440 | tf_op jit(solution)/shard_map/all_to_all | solution.py:816
  54.3 4.8 %shard_map.118.weights_h = bf16[128,128,128]{2,1,0:T(8,128)(2,1)} custom-call(bf16[128,128,128]{2,1,0:T(8,128)(2,1)} %weights_h.2), custom_call_target="tpu_custom_call" | custom-call | flops 8388608 | bytes 8388608 | tf_op jit(solution)/shard_map/pallas_call | solution.py:689
  59.1 6.8 %shard_map.117 = f32[4,16,64,128]{3,2,1,0:T(8,128)} custom-call(f32[50,80,128]{2,1,0:T(8,128)} %get-tuple-element.20.wide_h, f32[2,16,64,128]{3,2,1,0:T(8,128)} %get-tuple-element.21.currents_h, f32[4,80,128]{2,1,0:T(8,128)} %get-tuple-element.25.faces_h, f32[4,80,128]{2,1,0:T(8,128)} %get-tuple-element.26.forcing_h, f32[2,80,128]{2,1,0:T(8,128)} %get-tuple-element.27.near_h), custom_call_target="tpu_custom_call" | custom-call | flops 41943040 | bytes 6291456 | tf_op jit(solution)/shard_map/pallas_call | solution.py:659
  65.9 20.3 %all-to-all-done.1 = f32[32,80,128]{2,1,0:T(8,128)S(1)} async-done(((f32[32,80,128]{2,1,0:T(8,128)}), f32[32,80,128]{2,1,0:T(8,128)S(1)}, u32[]{:S(2)}, u32[]{:S(2)}) %all-to-all-start.1) | async-done | bytes 1310752 | tf_op jit(solution)/shard_map/all_to_all | solution.py:816
  86.2 5.3 %shard_map.119 = f32[4,6144]{1,0:T(4,128)} custom-call(s32[256]{0:T(256)} %block_h.3, s32[256]{0:T(256)} %tile_h.3, s32[256]{0:T(256)} %get-tuple-element.28.field_h, s32[256]{0:T(256)} %get-tuple-element.29.wet_h, f32[2560,128]{1,0:T(8,128)S(1)} %bitcast.3, bf16[128,128,128]{2,1,0:T(8,128)(2,1)} %shard_map.118.weights_h), custom_call_target="tpu_custom_call" | custom-call | flops 134217728 | bytes 6291456 | tf_op jit(solution)/shard_map/pallas_call | solution.py:761
  (3 shorter events, 0.0 us)
Async XLA Ops:
  6.9 7.1 %copy-start = (f32[4,16,64,128]{3,2,1,0:T(8,128)S(1)}, f32[4,16,64,128]{3,2,1,0:T(8,128)}, u32[]{:S(2)}) copy-start(f32[4,16,64,128]{3,2,1,0:T(8,128)} %state.1) | copy-start | bytes 6291460
  6.9 7.1 %copy-start.2 = (f32[64,128]{1,0:T(8,128)S(1)}, f32[64,128]{1,0:T(8,128)}, u32[]{:S(2)}) copy-start(f32[64,128]{1,0:T(8,128)} %horiz.1) | copy-start | bytes 98308
  6.9 7.1 %copy-start.3 = (s32[64,128]{1,0:T(8,128)S(1)}, s32[64,128]{1,0:T(8,128)}, u32[]{:S(2)}) copy-start(s32[64,128]{1,0:T(8,128)} %wet.1) | copy-start | bytes 98308
  6.9 39.0 %all-to-all-start = ((f32[32,80,128]{2,1,0:T(8,128)}), f32[32,80,128]{2,1,0:T(8,128)S(1)}, u32[]{:S(2)}, u32[]{:S(2)}) async-start(f32[32,80,128]{2,1,0:T(8,128)} %bitcast.4), calls=%async_computation | async-start | bytes 2621440 | tf_op jit(solution)/shard_map/all_to_all | solution.py:800
  14.0 1.0 %copy-start.1 = (f32[16,64,128]{2,1,0:T(8,128)S(1)}, f32[16,64,128]{2,1,0:T(8,128)}, u32[]{:S(2)}) copy-start(f32[16,64,128]{2,1,0:T(8,128)} %kappa.1) | copy-start | bytes 1572868
  17.9 7.9 %collective-permute-start = (f32[50,8,128]{2,1,0:T(8,128)S(1)}, f32[50,8,128]{2,1,0:T(8,128)S(1)}, u32[]{:S(2)}, u32[]{:S(2)}) collective-permute-start(f32[50,8,128]{2,1,0:T(8,128)S(1)} %get-tuple-element.18), channel_id=1, source_target_pairs={{0,4},{4,8},{8,12},{12,16},{16,20},{20,24},{24,28},{1,5},{5,9},{9,... | collective-permute-start | bytes 614408 | tf_op jit(solution)/shard_map/ppermute | solution.py:808
  21.4 10.7 %collective-permute-start.1 = (f32[50,8,128]{2,1,0:T(8,128)S(1)}, f32[50,8,128]{2,1,0:T(8,128)S(1)}, u32[]{:S(2)}, u32[]{:S(2)}) collective-permute-start(f32[50,8,128]{2,1,0:T(8,128)S(1)} %get-tuple-element.19), channel_id=1, source_target_pairs={{4,0},{8,4},{12,8},{16,12},{20,16},{24,20},{28,24},{5,1},{9,5},{13... | collective-permute-start | bytes 614408 | tf_op jit(solution)/shard_map/ppermute | solution.py:809
  35.0 6.4 %collective-permute-start.3 = (f32[2,80,128]{2,1,0:T(8,128)S(1)}, f32[2,80,128]{2,1,0:T(8,128)S(1)}, u32[]{:S(2)}, u32[]{:S(2)}) collective-permute-start(f32[2,80,128]{2,1,0:T(8,128)S(1)} %get-tuple-element.23.own_left_h), channel_id=1, source_target_pairs={{1,0},{2,1},{3,2},{5,4},{6,5},{7,6},{9,8},{10,9},{11,10},{13,12},{... | collective-permute-start | bytes 245768 | tf_op jit(solution)/shard_map/ppermute | solution.py:812
  36.3 5.5 %collective-permute-start.2 = (f32[2,80,128]{2,1,0:T(8,128)S(1)}, f32[2,80,128]{2,1,0:T(8,128)S(1)}, u32[]{:S(2)}, u32[]{:S(2)}) collective-permute-start(f32[2,80,128]{2,1,0:T(8,128)S(1)} %get-tuple-element.24.own_right_h), channel_id=1, source_target_pairs={{0,1},{1,2},{2,3},{4,5},{5,6},{6,7},{8,9},{9,10},{10,11},{12,13},{... | collective-permute-start | bytes 245768 | tf_op jit(solution)/shard_map/ppermute | solution.py:811
  49.8 36.4 %all-to-all-start.1 = ((f32[32,80,128]{2,1,0:T(8,128)}), f32[32,80,128]{2,1,0:T(8,128)S(1)}, u32[]{:S(2)}, u32[]{:S(2)}) async-start(f32[32,80,128]{2,1,0:T(8,128)} %get-tuple-element.30), calls=%async_computation.1 | async-start | bytes 2621440 | tf_op jit(solution)/shard_map/all_to_all | solution.py:816
